TPU v7x, 32 devices: a whole 2x2x4 slice. The times are simulated.
32 devices in a mesh: lon: 4 (over y, x), lat: 8 (over z, core).
Axes of the slice: x: 2, y: 2, z: 4, core: 2. Of those that a mesh axis runs over, the one named last changes fastest.
Arguments:
- tracers: float32 [2, 16, 256, 512], P(None, None, 'lat', 'lon'), may hold values from -6 to 6
- velocity: float32 [2, 16, 256, 512], P(None, None, 'lat', 'lon'), may hold values from -3 to 3
- land_mask: int32 [256, 512], P('lat', 'lon'), may hold values 0 or 1
- mixing: float32 [256, 512], P('lat', 'lon'), may hold values from 0.05 to 0.25
- owners: int32 [1024, 1], P(('lon', 'lat')), may hold values from 0 to 31; in each aligned block of 32 rows (0 to 31, 32 to 63, ...) at most 2 rows name the same one
- atm_row: int32 [1024], P(('lon', 'lat')), may hold values from 0 to 31
Outputs:
- tracers_out: float32 [2, 16, 256, 512], P(None, None, 'lat', 'lon')
- velocity_out: float32 [2, 16, 256, 512], P(None, None, 'lat', 'lon')
- atm_surface: float32 [4, 1024, 128], P(None, ('lon', 'lat'))
- atm_cover: float32 [1024, 128], P(('lon', 'lat'))
Inputs may be any that keep to these rules, and one draw needn't show every extreme that they name: `owners`: among the 32 blocks of one device at most 2 name the same owner, and in every draw some owner is named by exactly 2 blocks of some device.
All inputs are finite; a program needn't handle non-finite values. No bound on the sum of `land_mask` on one device may be relied on, other than what follows from the above.
Results may differ from a plain program's by a relative error of at most 0.00007.
Values sent between devices are 32-bit elements; how exact they have to be, the bound alone decides.
No kernel may reach another device: no remote copies, remote signals or barrier semaphores. Data moves between devices by JAX's collectives and lax.ppermute only.
A program may use at most 64 MiB of HBM per device.

v0:
```python
import math

import jax
import jax.numpy as jnp
from jax import lax
from jax.sharding import PartitionSpec as P

STEPS = 2
ATM_ROWS = 32


THERMAL = 0.2
HALINE = 0.15
GRAVITY = 0.2
TIMESTEP = 0.8
VERTICAL_MIX = 0.1
VISCOSITY = 0.2
CORIOLIS_MAX = 0.3


def extended(shard, sides, width, wrap):
    for axis, dim in sides:
        count, length = (lax.axis_size(axis), shard.shape[dim])
        up = [(i, (i + 1) % count) for i in range(count if wrap else count - 1)]
        down = [(j, i) for i, j in up]
        last = lax.slice_in_dim(shard, length - width, length, axis=dim)
        leading = lax.slice_in_dim(shard, 0, width, axis=dim)
        before = lax.ppermute(last, axis, up)
        after = lax.ppermute(leading, axis, down)
        shard = jnp.concatenate([before, shard, after], axis=dim)
    return shard


def from_partner(shard, axis, distance):
    return lax.ppermute(shard, axis, [(i, i ^ 1 << distance) for i in range(lax.axis_size(axis))])


def pressure(fields):
    density = HALINE * fields[1] - THERMAL * fields[0]
    return GRAVITY * (jnp.cumsum(density, axis=0) - 0.5 * density)


def coriolis_table(latitude, total_rows):
    return CORIOLIS_MAX * jnp.sin(math.pi * (-0.43 + 0.93 * (latitude + 0.5) / total_rows))


def neighbour(center, edge_value, axis, shift, position):
    rolled = jnp.roll(center, shift, axis=axis)
    return jnp.where(position, jnp.expand_dims(edge_value, axis), rolled)


def level_shift(fields, shift, at_end):
    rolled = jnp.roll(fields, shift, axis=1)
    return jnp.where(at_end, fields, rolled)


def local(tracers, velocity, land_mask, mixing, owners, atm_row):
    wet_mask = land_mask.astype(jnp.float32)
    levels = tracers.shape[1]
    rows_local, cols_local = land_mask.shape
    field_rows = jnp.concatenate(
        [
            (tracers * wet_mask).reshape(2 * levels, rows_local, cols_local),
            (velocity * wet_mask).reshape(2 * levels, rows_local, cols_local),
        ],
        axis=0,
    )
    sign_rows = jnp.concatenate(
        [
            jnp.ones((2 * levels,), jnp.float32),
            -jnp.ones((2 * levels,), jnp.float32),
            jnp.ones((1,), jnp.float32),
        ]
    )[:, None]
    lat_count = lax.axis_size("lat")
    lon_count = lax.axis_size("lon")
    lat_index = lax.axis_index("lat")
    latitude = (lat_index * rows_local + jnp.arange(rows_local)).astype(jnp.float32)
    coriolis = coriolis_table(latitude, lat_count * rows_local)[:, None]
    is_top = lat_index == lat_count - 1
    bit_total = lon_count.bit_length() - 1
    column_id = jnp.arange(cols_local, dtype=jnp.int32)[None, :]
    row_id = jnp.arange(rows_local, dtype=jnp.int32)[:, None]
    first_col = column_id == 0
    last_col = column_id == cols_local - 1
    first_row = row_id == 0
    last_row = row_id == rows_local - 1
    level_id = jnp.arange(levels, dtype=jnp.int32)[None, :, None, None]
    top_level = level_id == 0
    bottom_level = level_id == levels - 1
    for step_index in range(STEPS):
        col_edges = jnp.concatenate(
            [
                jnp.concatenate([field_rows[:, :, :1], field_rows[:, :, -1:]], axis=2),
                jnp.stack([wet_mask[:, 0], wet_mask[:, -1]], axis=1)[None],
            ],
            axis=0,
        )
        row_edges = jnp.concatenate(
            [
                jnp.stack([field_rows[:, 0, :], field_rows[:, -1, :]], axis=1),
                jnp.stack([wet_mask[0], wet_mask[-1]], axis=0)[None],
            ],
            axis=0,
        )
        lon_padded = extended(col_edges, (("lon", 2),), 1, True)
        lat_padded = extended(row_edges, (("lat", 1),), 1, False)
        mirror = row_edges[:, 1, :]
        for bit_index in range(bit_total):
            mirror = from_partner(mirror, "lon", bit_index)
        fold_row = sign_rows * mirror[:, ::-1]
        west_edge = lon_padded[:, :, 0]
        east_edge = lon_padded[:, :, 3]
        south_edge = lat_padded[:, 0, :]
        north_edge = jnp.where(is_top, fold_row, lat_padded[:, 3, :])
        east_rows = neighbour(field_rows, east_edge[:-1], 2, -1, last_col)
        west_rows = neighbour(field_rows, west_edge[:-1], 2, 1, first_col)
        north_rows = neighbour(field_rows, north_edge[:-1], 1, -1, last_row)
        south_rows = neighbour(field_rows, south_edge[:-1], 1, 1, first_row)
        wet_east = neighbour(wet_mask, east_edge[-1], 1, -1, last_col)
        wet_west = neighbour(wet_mask, west_edge[-1], 1, 1, first_col)
        wet_north = neighbour(wet_mask, north_edge[-1], 0, -1, last_row)
        wet_south = neighbour(wet_mask, south_edge[-1], 0, 1, first_row)
        shape_four = (4, levels, rows_local, cols_local)
        fields = field_rows.reshape(shape_four)
        fields_east = east_rows.reshape(shape_four)
        fields_west = west_rows.reshape(shape_four)
        fields_north = north_rows.reshape(shape_four)
        fields_south = south_rows.reshape(shape_four)
        laplace = wet_east * (fields_east - fields) + wet_west * (fields_west - fields)
        laplace = (
            laplace + wet_north * (fields_north - fields) + wet_south * (fields_south - fields)
        )
        zonal_vel = fields[2]
        merid_vel = fields[3]
        advect = 0.5 * (
            zonal_vel * (fields_east - fields_west) + merid_vel * (fields_north - fields_south)
        )
        level_above = level_shift(fields, 1, top_level)
        level_below = level_shift(fields, -1, bottom_level)
        vertical = level_above + level_below - 2.0 * fields
        grad_east = 0.5 * (pressure(fields_east) - pressure(fields_west))
        grad_north = 0.5 * (pressure(fields_north) - pressure(fields_south))
        tend_temp = -advect[0] + mixing * laplace[0] + VERTICAL_MIX * vertical[0]
        tend_salt = -advect[1] + mixing * laplace[1] + VERTICAL_MIX * vertical[1]
        tend_zonal = (
            -advect[2]
            + coriolis * merid_vel
            - grad_east
            + VISCOSITY * laplace[2]
            + VERTICAL_MIX * vertical[2]
        )
        tend_merid = (
            -advect[3]
            - coriolis * zonal_vel
            - grad_north
            + VISCOSITY * laplace[3]
            + VERTICAL_MIX * vertical[3]
        )
        tendency = jnp.stack([tend_temp, tend_salt, tend_zonal, tend_merid])
        updated = wet_mask * (fields + TIMESTEP * tendency)
        field_rows = updated.reshape(4 * levels, rows_local, cols_local)
    fields = field_rows.reshape(4, levels, rows_local, cols_local)
    surface = jnp.concatenate([fields[:, 0], wet_mask[None]], axis=0)
    blocks = (
        surface.reshape(5, rows_local, cols_local // 128, 128)
        .transpose(1, 2, 0, 3)
        .reshape(-1, 5, 128)
    )
    block_count = blocks.shape[0]
    devices = lon_count * lat_count
    capacity = max(2, 2 * block_count // devices)
    owner_ids = owners[:, 0]
    onehot = (owner_ids[:, None] == jnp.arange(devices, dtype=jnp.int32)[None, :]).astype(jnp.int32)
    position = jnp.sum((jnp.cumsum(onehot, axis=0) - 1) * onehot, axis=1)
    slot_index = owner_ids * capacity + position
    outgoing = jnp.zeros((devices * capacity, 5, 128), jnp.float32).at[slot_index].set(blocks)
    outgoing_rows = jnp.full((devices * capacity,), -1, jnp.int32).at[slot_index].set(atm_row)
    incoming, incoming_rows = (
        lax.all_to_all(outgoing, ("lon", "lat"), split_axis=0, concat_axis=0, tiled=True),
        lax.all_to_all(outgoing_rows, ("lon", "lat"), split_axis=0, concat_axis=0, tiled=True),
    )
    row_onehot = (incoming_rows[:, None] == jnp.arange(ATM_ROWS, dtype=jnp.int32)[None, :]).astype(
        jnp.float32
    )
    totals = lax.dot_general(
        row_onehot,
        incoming.reshape(devices * capacity, 640),
        (((0,), (0,)), ((), ())),
        precision=lax.Precision.HIGHEST,
        preferred_element_type=jnp.float32,
    )
    totals = totals.reshape(ATM_ROWS, 5, 128)
    ocean_count = totals[:, 4]
    atm_surface = (totals[:, :4] / jnp.maximum(ocean_count, 1.0)[:, None]).transpose(1, 0, 2)
    return (fields[:2], fields[2:], atm_surface, ocean_count)


def solution(mesh):
    in_specs = (
        P(None, None, "lat", "lon"),
        P(None, None, "lat", "lon"),
        P("lat", "lon"),
        P("lat", "lon"),
        P(("lon", "lat"), None),
        P(("lon", "lat")),
    )
    out_specs = (
        P(None, None, "lat", "lon"),
        P(None, None, "lat", "lon"),
        P(None, ("lon", "lat"), None),
        P(("lon", "lat"), None),
    )
    return jax.shard_map(local, mesh=mesh, in_specs=in_specs, out_specs=out_specs, check_vma=False)
```

profile of v0, /device:TPU:0, one launch (start us, length us, event | category | flops | bytes accessed | tf_op | source)
XLA Modules:
  0.0 183.2 jit_solution(9223048833857527386)
XLA Ops:
  0.6 1.3 convert_bitcast_fusion
  2.0 1.8 copy_multiply_fusion
  8.7 3.9 %collective-permute-start = (f32[65,32,1]{0,1,2:T(8,128)}, f32[65,32,1]{0,1,2:T(8,128)}, u32[]{:S(2)}, u32[]{:S(2)}) collective-permute-start(f32[65,32,1]{0,1,2:T(8,128)} %get-tuple-element.69), channel_id=1, source_target_pairs={{8,0},{16,8},{24,16},{0,24},{9,1},{17,9},{25,17},{1,25},{10,2},{18... | collective-permute-start | bytes 24968 | tf_op jit(solution)/shard_map/ppermute | solution.py:29
  14.4 2.0 %collective-permute-start.2 = (f32[65,128]{1,0:T(8,128)}, f32[65,128]{1,0:T(8,128)}, u32[]{:S(2)}, u32[]{:S(2)}) collective-permute-start(f32[65,128]{1,0:T(8,128)} %get-tuple-element.56), channel_id=1, source_target_pairs={{0,8},{8,0},{16,24},{24,16},{1,9},{9,1},{17,25},{25,17},{2,10},{10... | collective-permute-start | bytes 99848 | tf_op jit(solution)/shard_map/ppermute | solution.py:35
  16.3 1.3 collective-permute-start.4
  17.6 3.6 %collective-permute-start.5 = (f32[65,1,128]{2,0,1:T(8,128)}, f32[65,1,128]{2,0,1:T(8,128)}, u32[]{:S(2)}, u32[]{:S(2)}) collective-permute-start(f32[65,1,128]{2,0,1:T(8,128)} %get-tuple-element.58), channel_id=1, source_target_pairs={{0,1},{1,2},{2,3},{3,4},{4,5},{5,6},{6,7},{8,9},{9,10},{10,11},{11... | collective-permute-start | bytes 99848 | tf_op jit(solution)/shard_map/ppermute | solution.py:28
  23.1 5.4 %all-to-all-start = ((s32[32,2,1]{1,2,0:T(1,128)}), s32[32,2,1]{1,2,0:T(1,128)}, u32[]{:S(2)}, u32[]{:S(2)}) async-start(s32[32,2,1]{1,2,0:T(1,128)} %bitcast.69), calls=%async_computation | async-start | bytes 32768 | tf_op jit(solution)/shard_map/all_to_all | solution.py:181
  29.9 1.6 fusion.104
  33.7 1.6 fusion.106
  35.9 2.0 %fusion.12 = f32[4,16,32,128]{3,1,2,0:T(8,128)S(1)} fusion(pred[16]{0:T(512)(128)(4,1)S(1)} %get-tuple-element.93, pred[16]{0:T(512)(128)(4,1)S(1)} %get-tuple-element.94, f32[4,16,32,128]{3,1,0,2:T(8,128)S(1)} %bitcast.151, f32[4,15,32,128]{3,1,0,2:T(8,128)} %get-tuple-element.48, f32[4,1,32,128]{3,1,0,2:T(1,128)S(1)} %get-tuple-element.50, ...), kind=kLoop, calls=%fused_computation.22 | loop fusion | flops 1835008 | bytes 4194336 | tf_op jit(solution)/shard_map/sub | solution.py:141
  37.9 1.0 copy-done.17
  39.5 2.4 %copy.257 = f32[64,32,1]{1,0,2:T(8,128)} copy(f32[64,32,1]{2,0,1:T(8,128)} %copy-done.4) | data formatting | bytes 16384 | tf_op jit(solution)/shard_map/slice | solution.py:94
  41.9 2.4 %copy.262 = f32[64,32,1]{1,0,2:T(8,128)} copy(f32[64,32,1]{2,0,1:T(8,128)} %copy-done.5) | data formatting | bytes 16384 | tf_op jit(solution)/shard_map/slice | solution.py:94
  44.3 1.6 copy.249
  45.8 2.2 %copy.259 = f32[4,16,32,1]{3,1,2,0:T(8,128)} copy(f32[4,16,32,1]{2,1,0,3:T(8,128)} %bitcast.194) | data formatting | bytes 16384 | tf_op jit(solution)/shard_map/jit(_roll_static)/concatenate | solution.py:48
  48.0 2.2 %copy.263 = f32[4,16,32,1]{3,1,2,0:T(8,128)} copy(f32[4,16,32,1]{2,1,0,3:T(8,128)} %bitcast.193) | data formatting | bytes 16384 | tf_op jit(solution)/shard_map/jit(_roll_static)/concatenate | solution.py:48
  50.2 1.3 slice_bitcast_fusion.13
  51.6 1.3 slice_bitcast_fusion.12
  53.5 2.5 %maximum_select_fusion.6 = (f32[64,32,128]{2,0,1:T(8,128)S(1)}, f32[64,32,128]{2,0,1:T(8,128)S(1)}) fusion(f32[64,32,1]{2,0,1:T(8,128)} %copy-done.4, f32[64,32,127]{2,0,1:T(8,128)S(1)} %get-tuple-element.40, f32[64,32]{0,1:T(8,128)S(1)} %get-tuple-element.77, pred[128]{0:T(512)(128)(4,1)S(1)} %copy-done.75, f32[64,32,127]{2,0,1:T(8,128)S(1)} %get-tuple-element.41, ...), kind=kLoop, calls=%fused_computation.24 | loop fusion | flops 1048576 | bytes 4210944 | tf_op jit(solution)/shard_map/jit(_where)/select_n | solution.py:49
  56.2 0.9 fusion.63
  62.7 1.4 copy.397
  64.1 1.5 copy.261
  65.6 1.4 slice_bitcast_fusion.15
  67.6 1.3 maximum_select_fusion.9
  69.0 1.0 copy-done.19
  71.5 1.5 collective-permute-start.3
  73.7 2.1 %collective-permute-done.3 = f32[65,128]{1,0:T(8,128)} collective-permute-done((f32[65,128]{1,0:T(8,128)}, f32[65,128]{1,0:T(8,128)}, u32[]{:S(2)}, u32[]{:S(2)}) %collective-permute-start.3) | collective-permute-done | bytes 33312 | tf_op jit(solution)/shard_map/ppermute | solution.py:35
  75.7 1.5 rev.6
  77.2 0.9 bitcast_select_fusion.1
  78.2 1.5 maximum_select_fusion.8
  81.8 2.6 %add_multiply_fusion.2 = f32[4,16,32,128]{3,1,2,0:T(8,128)S(1)} fusion(f32[4,16,1,128]{3,1,2,0:T(8,128)S(1)} %bitcast.175, f32[4,16,1,128]{3,1,2,0:T(8,128)S(1)} %bitcast.173, f32[4,16,128]{2,1,0:T(8,128)} %bitcast.191, f32[4,16,128]{2,1,0:T(8,128)S(1)} %bitcast.187, f32[16,32,128]{2,0,1:T(8,128)S(1)} %copy-done.34, f32[16,32,128]{2,0,1:T(8,128)S(1)} %copy-done.33, ...), kind=kLoop, calls=%fused_computation.50 | loop fusion | flops 3670016 | bytes 5849408 | tf_op jit(solution)/shard_map/mul | solution.py:136
  84.6 1.5 multiply_add_fusion.1
  89.6 1.8 fusion.97
  91.4 1.3 fusion.96
  92.7 1.6 fusion.98
  95.8 1.5 fusion.99
  97.4 1.6 copy.321
  99.0 1.6 copy.322
  100.7 2.7 %collective-permute-start.6 = (f32[65,32,1]{0,1,2:T(8,128)S(1)}, f32[65,32,1]{0,1,2:T(8,128)S(1)}, u32[]{:S(2)}, u32[]{:S(2)}) collective-permute-start(f32[65,32,1]{0,1,2:T(8,128)S(1)} %get-tuple-element.67), channel_id=1, source_target_pairs={{8,0},{16,8},{24,16},{0,24},{9,1},{17,9},{25,17},{1,25},{10,2},{18... | collective-permute-start | bytes 24968 | tf_op jit(solution)/shard_map/ppermute | solution.py:29
  105.3 1.9 %collective-permute-start.11 = (f32[65,1,128]{2,0,1:T(8,128)}, f32[65,1,128]{2,0,1:T(8,128)}, u32[]{:S(2)}, u32[]{:S(2)}) collective-permute-start(f32[65,1,128]{2,0,1:T(8,128)} %copy.547), channel_id=1, source_target_pairs={{0,1},{1,2},{2,3},{3,4},{4,5},{5,6},{6,7},{8,9},{9,10},{10,11},{11... | collective-permute-start | bytes 99848 | tf_op jit(solution)/shard_map/ppermute | solution.py:28
  107.2 2.0 %collective-permute-start.8 = (f32[65,128]{1,0:T(8,128)}, f32[65,128]{1,0:T(8,128)}, u32[]{:S(2)}, u32[]{:S(2)}) collective-permute-start(f32[65,128]{1,0:T(8,128)} %bitcast.135.clone.2), channel_id=1, source_target_pairs={{0,8},{8,0},{16,24},{24,16},{1,9},{9,1},{17,25},{25,17},{2,10},{10... | collective-permute-start | bytes 99848 | tf_op jit(solution)/shard_map/ppermute | solution.py:35
  109.3 1.3 collective-permute-start.10
  111.2 3.4 %fusion.14 = f32[4,16,32,128]{3,1,2,0:T(8,128)} fusion(f32[4,15,32,128]{3,1,2,0:T(8,128)} %get-tuple-element.32, f32[4,1,32,128]{3,1,2,0:T(1,128)S(1)} %get-tuple-element.34, f32[4,1,32,128]{3,1,2,0:T(1,128)S(1)} %get-tuple-element.33, f32[4,15,32,128]{3,1,2,0:T(8,128)} %get-tuple-element.31, pred[16]{0:T(512)(128)(4,1)S(1)} %copy-done.88, ...), kind=kLoop, calls=%fused_computation.35 | loop fusion | flops 1835008 | bytes 4194336 | tf_op jit(solution)/shard_map/sub | solution.py:141
  114.7 1.8 copy.326
  116.4 1.8 copy.331
  118.2 1.5 copy.328
  119.7 1.5 copy.332
  121.1 3.0 %copy.372 = f32[64,31,128]{2,1,0:T(8,128)} copy(f32[64,31,128]{2,0,1:T(8,128)} %get-tuple-element.30) | data formatting | bytes 2031616 | tf_op jit(solution)/shard_map/jit(_roll_static)/slice | solution.py:48
  128.3 0.9 copy-done.25
  134.4 1.4 slice_bitcast_fusion.14
  136.4 1.3 maximum_select_fusion.19
  139.2 1.5 collective-permute-start.9
  141.3 2.1 %collective-permute-done.9 = f32[65,128]{1,0:T(8,128)} collective-permute-done((f32[65,128]{1,0:T(8,128)}, f32[65,128]{1,0:T(8,128)}, u32[]{:S(2)}, u32[]{:S(2)}) %collective-permute-start.9) | collective-permute-done | bytes 33312 | tf_op jit(solution)/shard_map/ppermute | solution.py:35
  143.5 1.4 rev.7
  144.9 0.9 bitcast_select_fusion
  146.7 1.6 maximum_select_fusion.18
  148.5 1.1 copy-done.1
  149.7 2.8 %add_multiply_fusion = f32[4,16,32,128]{3,1,2,0:T(8,128)S(1)} fusion(f32[4,16,1,128]{3,1,2,0:T(8,128)S(1)} %bitcast.178, f32[4,16,1,128]{3,1,2,0:T(8,128)S(1)} %bitcast.182, f32[4,16,128]{2,1,0:T(8,128)S(1)} %bitcast.189, f32[4,16,128]{2,1,0:T(8,128)S(1)} %bitcast.185, f32[16,32,128]{2,0,1:T(8,128)S(1)} %copy-done.32, f32[16,32,128]{2,0,1:T(8,128)S(1)} %copy-done.31, ...), kind=kLoop, calls=%fused_computation.47 | loop fusion | flops 3670016 | bytes 5849408 | tf_op jit(solution)/shard_map/mul | solution.py:136
  152.6 3.5 %multiply_add_fusion = f32[4,16,32,128]{3,1,2,0:T(8,128)S(1)} fusion(f32[4,16,1,128]{3,1,2,0:T(8,128)S(1)} %bitcast.179, f32[4,16,1,128]{3,1,2,0:T(8,128)S(1)} %bitcast.183, f32[32,128]{1,0:T(8,128)S(1)} %copy-done.60, f32[32,128]{1,0:T(8,128)S(1)} %fusion.82, f32[32,128]{1,0:T(8,128)S(1)} %copy-done.57, f32[32,128]{1,0:T(8,128)S(1)} %copy-done.56, ...), kind=kLoop, calls=%fused_computation.46 | loop fusion | flops 4980736 | bytes 6439232 | tf_op jit(solution)/shard_map/add | solution.py:132
  161.1 3.5 %scatter_fusion = f32[64,5,128]{2,1,0:T(8,128)} fusion(f32[64,5,128]{2,1,0:T(8,128)} %broadcast_in_dim.390, s32[32]{0:T(128)S(1)} %copy-done.93, f32[32,5,128]{2,1,0:T(8,128)S(1)} %copy.382), kind=kCustom, calls=%fused_computation.1 | custom fusion | bytes 245888 | tf_op jit(solution)/shard_map/scatter | solution.py:177
  164.6 6.8 %all-to-all-start.1 = ((f32[64,5,128]{2,1,0:T(8,128)}), f32[64,5,128]{2,1,0:T(8,128)S(1)}, u32[]{:S(2)}, u32[]{:S(2)}) async-start(f32[64,5,128]{2,1,0:T(8,128)} %scatter_fusion), calls=%async_computation.1 | async-start | bytes 524288 | tf_op jit(solution)/shard_map/all_to_all | solution.py:180
  171.9 1.4 reduce.11
  173.4 1.0 fusion.94
  174.5 7.3 %all-to-all-done.1 = f32[64,5,128]{2,1,0:T(8,128)S(1)} async-done(((f32[64,5,128]{2,1,0:T(8,128)}), f32[64,5,128]{2,1,0:T(8,128)S(1)}, u32[]{:S(2)}, u32[]{:S(2)}) %all-to-all-start.1) | async-done | bytes 163872 | tf_op jit(solution)/shard_map/all_to_all | solution.py:180
  (307 shorter events, 52.2 us)
Async XLA Ops:
  2.0 56.8 %copy-start.46 = (f32[32,1]{1,0:T(8,128)}, f32[32,1]{1,0:T(8,128)S(1)}, u32[]{:S(2)}) copy-start(f32[32,1]{1,0:T(8,128)S(1)} %get-tuple-element.83) | copy-start | bytes 388
  2.0 58.4 %copy-start.44 = (f32[32,1]{1,0:T(8,128)}, f32[32,1]{1,0:T(8,128)S(1)}, u32[]{:S(2)}) copy-start(f32[32,1]{1,0:T(8,128)S(1)} %get-tuple-element.84) | copy-start | bytes 388
  8.7 41.6 %collective-permute-start = (f32[65,32,1]{0,1,2:T(8,128)}, f32[65,32,1]{0,1,2:T(8,128)}, u32[]{:S(2)}, u32[]{:S(2)}) collective-permute-start(f32[65,32,1]{0,1,2:T(8,128)} %get-tuple-element.69), channel_id=1, source_target_pairs={{8,0},{16,8},{24,16},{0,24},{9,1},{17,9},{25,17},{1,25},{10,2},{18... | collective-permute-start | bytes 24968 | tf_op jit(solution)/shard_map/ppermute | solution.py:29
  12.6 39.0 %collective-permute-start.1 = (f32[65,32,1]{0,1,2:T(8,128)}, f32[65,32,1]{0,1,2:T(8,128)}, u32[]{:S(2)}, u32[]{:S(2)}) collective-permute-start(f32[65,32,1]{0,1,2:T(8,128)} %get-tuple-element.70), channel_id=1, source_target_pairs={{0,8},{8,16},{16,24},{24,0},{1,9},{9,17},{17,25},{25,1},{2,10},{10... | collective-permute-start | bytes 24968 | tf_op jit(solution)/shard_map/ppermute | solution.py:28
  14.4 57.1 %collective-permute-start.2 = (f32[65,128]{1,0:T(8,128)}, f32[65,128]{1,0:T(8,128)}, u32[]{:S(2)}, u32[]{:S(2)}) collective-permute-start(f32[65,128]{1,0:T(8,128)} %get-tuple-element.56), channel_id=1, source_target_pairs={{0,8},{8,0},{16,24},{24,16},{1,9},{9,1},{17,25},{25,17},{2,10},{10... | collective-permute-start | bytes 99848 | tf_op jit(solution)/shard_map/ppermute | solution.py:35
  16.3 60.9 %collective-permute-start.4 = (f32[65,1,128]{2,0,1:T(8,128)}, f32[65,1,128]{2,0,1:T(8,128)}, u32[]{:S(2)}, u32[]{:S(2)}) collective-permute-start(f32[65,1,128]{2,0,1:T(8,128)} %get-tuple-element.57), channel_id=1, source_target_pairs={{1,0},{2,1},{3,2},{4,3},{5,4},{6,5},{7,6},{9,8},{10,9},{11,10},{12... | collective-permute-start | bytes 99848 | tf_op jit(solution)/shard_map/ppermute | solution.py:29
  17.6 3.6 %copy-start.91 = (s32[32,1]{0,1:T(1,128)S(1)}, s32[32,1]{0,1:T(1,128)}, u32[]{:S(2)}) copy-start(s32[32,1]{0,1:T(1,128)} %param.10) | copy-start | bytes 388
  17.6 47.9 %collective-permute-start.5 = (f32[65,1,128]{2,0,1:T(8,128)}, f32[65,1,128]{2,0,1:T(8,128)}, u32[]{:S(2)}, u32[]{:S(2)}) collective-permute-start(f32[65,1,128]{2,0,1:T(8,128)} %get-tuple-element.58), channel_id=1, source_target_pairs={{0,1},{1,2},{2,3},{3,4},{4,5},{5,6},{6,7},{8,9},{9,10},{10,11},{11... | collective-permute-start | bytes 99848 | tf_op jit(solution)/shard_map/ppermute | solution.py:28
  23.1 141.5 %all-to-all-start = ((s32[32,2,1]{1,2,0:T(1,128)}), s32[32,2,1]{1,2,0:T(1,128)}, u32[]{:S(2)}, u32[]{:S(2)}) async-start(s32[32,2,1]{1,2,0:T(1,128)} %bitcast.69), calls=%async_computation | async-start | bytes 32768 | tf_op jit(solution)/shard_map/all_to_all | solution.py:181
  29.9 1.6 copy-start.15
  33.7 25.1 %copy-start.50 = (f32[32,127]{1,0:T(8,128)}, f32[32,127]{1,0:T(8,128)S(1)}, u32[]{:S(2)}) copy-start(f32[32,127]{1,0:T(8,128)S(1)} %get-tuple-element.81) | copy-start | bytes 48772
  33.7 26.7 %copy-start.48 = (f32[32,127]{1,0:T(8,128)}, f32[32,127]{1,0:T(8,128)S(1)}, u32[]{:S(2)}) copy-start(f32[32,127]{1,0:T(8,128)S(1)} %get-tuple-element.82) | copy-start | bytes 48772
  70.0 3.0 %copy-start.52 = (f32[31,128]{1,0:T(8,128)S(1)}, f32[31,128]{1,0:T(8,128)}, u32[]{:S(2)}) copy-start(f32[31,128]{1,0:T(8,128)} %get-tuple-element.86) | copy-start | bytes 47620
  71.5 1.5 copy-start.82
  71.5 4.3 %collective-permute-start.3 = (f32[65,128]{1,0:T(8,128)}, f32[65,128]{1,0:T(8,128)}, u32[]{:S(2)}, u32[]{:S(2)}) collective-permute-start(f32[65,128]{1,0:T(8,128)} %collective-permute-done.2), channel_id=1, source_target_pairs={{0,16},{8,24},{16,0},{24,8},{1,17},{9,25},{17,1},{25,9},{2,18},{10... | collective-permute-start | bytes 99848 | tf_op jit(solution)/shard_map/ppermute | solution.py:35
  77.2 3.9 %copy-start.34 = (f32[16,32,128]{2,0,1:T(8,128)S(1)}, f32[16,32,128]{2,0,1:T(8,128)}, u32[]{:S(2)}) copy-start(f32[16,32,128]{2,0,1:T(8,128)} %get-tuple-element.53) | copy-start | bytes 786436
  78.1 3.0 %copy-start.8 = (f32[64,31,128]{2,0,1:T(8,128)S(1)}, f32[64,31,128]{2,0,1:T(8,128)}, u32[]{:S(2)}) copy-start(f32[64,31,128]{2,0,1:T(8,128)} %get-tuple-element.45) | copy-start | bytes 3047428
  78.2 3.0 %copy-start.12 = (f32[4,16,32,1]{3,1,2,0:T(8,128)S(1)}, f32[4,16,32,1]{3,1,2,0:T(8,128)}, u32[]{:S(2)}) copy-start(f32[4,16,32,1]{3,1,2,0:T(8,128)} %copy.259) | copy-start | bytes 24580
  79.7 1.5 copy-start.7
  79.8 1.4 copy-start.33
  81.8 2.6 %copy-start.13 = (f32[4,16,32,1]{3,1,2,0:T(8,128)S(1)}, f32[4,16,32,1]{3,1,2,0:T(8,128)}, u32[]{:S(2)}) copy-start(f32[4,16,32,1]{3,1,2,0:T(8,128)} %copy.263) | copy-start | bytes 24580
  81.8 2.7 %copy-start.41 = (f32[64,1,128]{2,0,1:T(8,128)S(1)}, f32[64,1,128]{2,0,1:T(8,128)}, u32[]{:S(2)}) copy-start(f32[64,1,128]{2,0,1:T(8,128)} %get-tuple-element.64) | copy-start | bytes 98308
  81.8 2.7 %copy-start.58 = (f32[32,128]{1,0:T(8,128)S(1)}, f32[32,128]{1,0:T(8,128)}, u32[]{:S(2)}) copy-start(f32[32,128]{1,0:T(8,128)} %broadcast_select_fusion.3) | copy-start | bytes 49156
  81.8 2.7 %copy-start.59 = (f32[32,128]{1,0:T(8,128)S(1)}, f32[32,128]{1,0:T(8,128)}, u32[]{:S(2)}) copy-start(f32[32,128]{1,0:T(8,128)} %broadcast_select_fusion.2) | copy-start | bytes 49156
  81.8 2.7 %copy-start.61 = (f32[32,128]{1,0:T(8,128)S(1)}, f32[32,128]{1,0:T(8,128)}, u32[]{:S(2)}) copy-start(f32[32,128]{1,0:T(8,128)} %fusion.81) | copy-start | bytes 49156
  84.5 1.6 copy-start.16
  84.5 1.6 copy-start.18
  84.5 1.7 copy-start.20
  84.5 1.7 copy-start.30
  84.5 1.7 copy-start.54
  84.5 1.7 copy-start.85
  99.0 1.6 copy-start.43
  100.7 23.4 %collective-permute-start.6 = (f32[65,32,1]{0,1,2:T(8,128)S(1)}, f32[65,32,1]{0,1,2:T(8,128)S(1)}, u32[]{:S(2)}, u32[]{:S(2)}) collective-permute-start(f32[65,32,1]{0,1,2:T(8,128)S(1)} %get-tuple-element.67), channel_id=1, source_target_pairs={{8,0},{16,8},{24,16},{0,24},{9,1},{17,9},{25,17},{1,25},{10,2},{18... | collective-permute-start | bytes 24968 | tf_op jit(solution)/shard_map/ppermute | solution.py:29
  103.4 22.9 %collective-permute-start.7 = (f32[65,32,1]{0,1,2:T(8,128)S(1)}, f32[65,32,1]{0,1,2:T(8,128)S(1)}, u32[]{:S(2)}, u32[]{:S(2)}) collective-permute-start(f32[65,32,1]{0,1,2:T(8,128)S(1)} %get-tuple-element.68), channel_id=1, source_target_pairs={{0,8},{8,16},{16,24},{24,0},{1,9},{9,17},{17,25},{25,1},{2,10},{10... | collective-permute-start | bytes 24968 | tf_op jit(solution)/shard_map/ppermute | solution.py:28
  105.3 29.0 %collective-permute-start.11 = (f32[65,1,128]{2,0,1:T(8,128)}, f32[65,1,128]{2,0,1:T(8,128)}, u32[]{:S(2)}, u32[]{:S(2)}) collective-permute-start(f32[65,1,128]{2,0,1:T(8,128)} %copy.547), channel_id=1, source_target_pairs={{0,1},{1,2},{2,3},{3,4},{4,5},{5,6},{6,7},{8,9},{9,10},{10,11},{11... | collective-permute-start | bytes 99848 | tf_op jit(solution)/shard_map/ppermute | solution.py:28
  107.2 31.9 %collective-permute-start.8 = (f32[65,128]{1,0:T(8,128)}, f32[65,128]{1,0:T(8,128)}, u32[]{:S(2)}, u32[]{:S(2)}) collective-permute-start(f32[65,128]{1,0:T(8,128)} %bitcast.135.clone.2), channel_id=1, source_target_pairs={{0,8},{8,0},{16,24},{24,16},{1,9},{9,1},{17,25},{25,17},{2,10},{10... | collective-permute-start | bytes 99848 | tf_op jit(solution)/shard_map/ppermute | solution.py:35
  109.3 35.7 %collective-permute-start.10 = (f32[65,1,128]{2,1,0:T(1,128)}, f32[65,1,128]{2,1,0:T(1,128)}, u32[]{:S(2)}, u32[]{:S(2)}) collective-permute-start(f32[65,1,128]{2,1,0:T(1,128)} %get-tuple-element.60), channel_id=1, source_target_pairs={{1,0},{2,1},{3,2},{4,3},{5,4},{6,5},{7,6},{9,8},{10,9},{11,10},{12... | collective-permute-start | bytes 99848 | tf_op jit(solution)/shard_map/ppermute | solution.py:29
  121.1 3.0 %copy-start.3 = (f32[64,32,1]{2,0,1:T(8,128)S(1)}, f32[64,32,1]{2,0,1:T(8,128)}, u32[]{:S(2)}) copy-start(f32[64,32,1]{2,0,1:T(8,128)} %get-tuple-element.27) | copy-start | bytes 24580
  124.8 2.1 %copy-start.2 = (f32[64,32,1]{2,0,1:T(8,128)S(1)}, f32[64,32,1]{2,0,1:T(8,128)}, u32[]{:S(2)}) copy-start(f32[64,32,1]{2,0,1:T(8,128)} %get-tuple-element.28) | copy-start | bytes 24580
  125.4 2.8 %copy-start.23 = (f32[64,32,128]{2,0,1:T(8,128)}, f32[64,32,128]{2,0,1:T(8,128)S(1)}, u32[]{:S(2)}) copy-start(f32[64,32,128]{2,0,1:T(8,128)S(1)} %maximum_select_fusion.16) | copy-start | bytes 3145732
  125.4 1.8 copy-start
  128.2 1.9 %copy-start.51 = (f32[32,127]{1,0:T(8,128)S(1)}, f32[32,127]{1,0:T(8,128)}, u32[]{:S(2)}) copy-start(f32[32,127]{1,0:T(8,128)} %copy-done.50) | copy-start | bytes 48772
  128.2 3.3 %copy-start.49 = (f32[32,127]{1,0:T(8,128)S(1)}, f32[32,127]{1,0:T(8,128)}, u32[]{:S(2)}) copy-start(f32[32,127]{1,0:T(8,128)} %copy-done.48) | copy-start | bytes 48772
  137.7 2.9 %copy-start.53 = (f32[31,128]{1,0:T(8,128)S(1)}, f32[31,128]{1,0:T(8,128)}, u32[]{:S(2)}) copy-start(f32[31,128]{1,0:T(8,128)} %get-tuple-element.86) | copy-start | bytes 47620
  138.5 2.2 %copy-start.83 = (f32[1,128]{1,0:T(1,128)S(1)}, f32[1,128]{1,0:T(1,128)}, u32[]{:S(2)}) copy-start(f32[1,128]{1,0:T(1,128)} %copy-done.81) | copy-start | bytes 1540
  139.2 4.3 %collective-permute-start.9 = (f32[65,128]{1,0:T(8,128)}, f32[65,128]{1,0:T(8,128)}, u32[]{:S(2)}, u32[]{:S(2)}) collective-permute-start(f32[65,128]{1,0:T(8,128)} %collective-permute-done.8), channel_id=1, source_target_pairs={{0,16},{8,24},{16,0},{24,8},{1,17},{9,25},{17,1},{25,9},{2,18},{10... | collective-permute-start | bytes 99848 | tf_op jit(solution)/shard_map/ppermute | solution.py:35
  144.9 3.5 %copy-start.32 = (f32[16,32,128]{2,0,1:T(8,128)S(1)}, f32[16,32,128]{2,0,1:T(8,128)}, u32[]{:S(2)}) copy-start(f32[16,32,128]{2,0,1:T(8,128)} %get-tuple-element.24) | copy-start | bytes 786436
  146.6 1.8 copy-start.6
  146.6 1.8 %copy-start.9 = (f32[64,31,128]{2,0,1:T(8,128)S(1)}, f32[64,31,128]{2,0,1:T(8,128)}, u32[]{:S(2)}) copy-start(f32[64,31,128]{2,0,1:T(8,128)} %get-tuple-element.30) | copy-start | bytes 3047428
  146.6 1.8 %copy-start.38 = (f32[4,16,32]{1,2,0:T(8,128)S(1)}, f32[4,16,32]{1,2,0:T(8,128)}, u32[]{:S(2)}) copy-start(f32[4,16,32]{1,2,0:T(8,128)} %copy.330) | copy-start | bytes 24580
  146.6 1.8 copy-start.40
  149.6 2.9 %copy-start.10 = (f32[4,16,32,1]{3,1,2,0:T(8,128)S(1)}, f32[4,16,32,1]{3,1,2,0:T(8,128)}, u32[]{:S(2)}) copy-start(f32[4,16,32,1]{3,1,2,0:T(8,128)} %copy.328) | copy-start | bytes 24580
  149.6 2.9 %copy-start.11 = (f32[4,16,32,1]{3,1,2,0:T(8,128)S(1)}, f32[4,16,32,1]{3,1,2,0:T(8,128)}, u32[]{:S(2)}) copy-start(f32[4,16,32,1]{3,1,2,0:T(8,128)} %copy.332) | copy-start | bytes 24580
  149.6 2.9 %copy-start.56 = (f32[32,128]{1,0:T(8,128)S(1)}, f32[32,128]{1,0:T(8,128)}, u32[]{:S(2)}) copy-start(f32[32,128]{1,0:T(8,128)} %broadcast_select_fusion.1) | copy-start | bytes 49156
  149.6 2.9 %copy-start.57 = (f32[32,128]{1,0:T(8,128)S(1)}, f32[32,128]{1,0:T(8,128)}, u32[]{:S(2)}) copy-start(f32[32,128]{1,0:T(8,128)} %broadcast_select_fusion) | copy-start | bytes 49156
  149.6 2.9 %copy-start.60 = (f32[32,128]{1,0:T(8,128)S(1)}, f32[32,128]{1,0:T(8,128)}, u32[]{:S(2)}) copy-start(f32[32,128]{1,0:T(8,128)} %fusion.80) | copy-start | bytes 49156
  152.5 3.6 %copy-start.21 = (f32[4,16,32,128]{3,1,2,0:T(8,128)S(1)}, f32[4,16,32,128]{3,1,2,0:T(8,128)}, u32[]{:S(2)}) copy-start(f32[4,16,32,128]{3,1,2,0:T(8,128)} %fusion.14) | copy-start | bytes 3145732
  152.5 3.6 %copy-start.24 = (f32[64,32,128]{2,0,1:T(8,128)S(1)}, f32[64,32,128]{2,0,1:T(8,128)}, u32[]{:S(2)}) copy-start(f32[64,32,128]{2,0,1:T(8,128)} %copy-done.23) | copy-start | bytes 3145732
  152.5 3.6 %copy-start.26 = (f32[64,32,128]{2,0,1:T(8,128)S(1)}, f32[64,32,128]{2,0,1:T(8,128)}, u32[]{:S(2)}) copy-start(f32[64,32,128]{2,0,1:T(8,128)} %copy-done.25) | copy-start | bytes 3145732
  152.5 3.6 %copy-start.28 = (f32[16,32,128]{2,1,0:T(8,128)S(1)}, f32[16,32,128]{2,1,0:T(8,128)}, u32[]{:S(2)}) copy-start(f32[16,32,128]{2,1,0:T(8,128)} %fusion.53) | copy-start | bytes 786436
  152.6 3.6 %copy-start.29 = (f32[16,32,128]{2,1,0:T(8,128)S(1)}, f32[16,32,128]{2,1,0:T(8,128)}, u32[]{:S(2)}) copy-start(f32[16,32,128]{2,1,0:T(8,128)} %fusion.50) | copy-start | bytes 786436
  152.6 3.6 %copy-start.55 = (f32[32,128]{1,0:T(8,128)S(1)}, f32[32,128]{1,0:T(8,128)}, u32[]{:S(2)}) copy-start(f32[32,128]{1,0:T(8,128)} %param.9) | copy-start | bytes 49156
  152.6 3.6 %copy-start.86 = (f32[32]{0:T(128)S(1)}, f32[32]{0:T(128)}, u32[]{:S(2)}) copy-start(f32[32]{0:T(128)} %sine_multiply_fusion) | copy-start | bytes 388
  164.6 17.1 %all-to-all-start.1 = ((f32[64,5,128]{2,1,0:T(8,128)}), f32[64,5,128]{2,1,0:T(8,128)S(1)}, u32[]{:S(2)}, u32[]{:S(2)}) async-start(f32[64,5,128]{2,1,0:T(8,128)} %scatter_fusion), calls=%async_computation.1 | async-start | bytes 524288 | tf_op jit(solution)/shard_map/all_to_all | solution.py:180
  (45 other events, 38.5 us)
where the time goes:
time: 186 us; the launch traced here: 183 us
  local copies, waits for them, and re-layouts  85.5 us (46%)
  other arithmetic  50.3 us (27%)
  starting transfers between devices  33.8 us (18%)
  waiting for transfers between devices  11.5 us (6%)
  between operations  1.92 us (1%)
    unnamed x194, local copies, waits for them, and re-layouts  20.2 us
    select_n x15, other arithmetic, neighbour(): return jnp.where(position, jnp.expand_dims(edge_value, axis), rolled)  15.1 us
    broadcast_in_dim x12, local copies, waits for them, and re-layouts, neighbour(): return jnp.where(position, jnp.expand_dims(edge_value, axis), rolled)  10.4 us
    ppermute x4, starting transfers between devices, extended(): after = lax.ppermute(leading, axis, down)  9.15 us
    slice x7, local copies, waits for them, and re-layouts, neighbour(): rolled = jnp.roll(center, shift, axis=axis)  8.58 us
    slice x6, local copies, waits for them, and re-layouts, local(): field_rows[:, :, :1]  8.22 us
    concatenate x4, local copies, waits for them, and re-layouts, neighbour(): rolled = jnp.roll(center, shift, axis=axis)  7.35 us
    all_to_all x1, waiting for transfers between devices, local(): lax.all_to_all(outgoing, ('lon', 'lat'), split_axis=0, concat_axis=0, til...  7.32 us
  transfers between devices with their start and end apart: 14, of which 3 were waited for; matrix products, arithmetic and copies ran while one was open for 60% of the time, Pallas kernels for 0%

commit v1 on v0

v1 whole, which is shorter than its diff:
```python
import functools
import math

import jax
import jax.numpy as jnp
from jax import lax
from jax.experimental import pallas as pl
from jax.experimental.pallas import tpu as pltpu
from jax.sharding import PartitionSpec as P

ATM_ROWS = 32
CAP = 2

THERMAL = 0.2
HALINE = 0.15
GRAVITY = 0.2
TIMESTEP = 0.8
VERTICAL_MIX = 0.1
VISCOSITY = 0.2
CORIOLIS_MAX = 0.3

LANES = 128
PAD = 8
EXACT = lax.Precision.HIGHEST
F32 = jnp.float32
VMEM_LIMIT = 48 * 1024 * 1024


def iota(shape, dim):
    return lax.broadcasted_iota(jnp.int32, shape, dim)


def dot(a, b, dims=(((1,), (0,)), ((), ()))):
    return lax.dot_general(a, b, dims, precision=EXACT, preferred_element_type=F32)


def is_lower():
    return lax.axis_index("lon") < lax.axis_size("lon") // 2


def pack_kernel(rows, fields, devices, tr, ve, mask, mix, own, arow, east, west, up, down, info):
    half = fields // 2
    wet = mask[...].astype(F32)
    lane = iota((rows, LANES), 1)
    pair = lane >> 1

    def columns(ref, base, carry):
        def body(f, carry):
            to_east, to_west = carry
            x = ref[pl.ds(pl.multiple_of(f * rows, rows), rows), :] * wet
            keep = pair == base + f
            low = 2 * (base + f)
            to_east = jnp.where(keep, pltpu.roll(x, (low + 2) & (LANES - 1), 1), to_east)
            to_west = jnp.where(keep, pltpu.roll(x, low, 1), to_west)
            return to_east, to_west

        return lax.fori_loop(0, half, body, carry, unroll=8)

    zero = jnp.zeros((rows, LANES), F32)
    to_east, to_west = columns(ve, half, columns(tr, 0, (zero, zero)))
    east[0:rows, :] = to_east
    west[0:rows, :] = to_west
    mixing = mix[...]
    east[rows : 2 * rows, :] = jnp.where(
        lane == 0,
        pltpu.roll(wet, 1, 1),
        jnp.where(lane == 1, pltpu.roll(wet, 3, 1), pltpu.roll(mixing, 3, 1)),
    )
    west[rows : 2 * rows, :] = jnp.where(lane <= 1, wet, pltpu.roll(mixing, 2, 1))

    lower = is_lower()
    top, bottom = (rows - 1, rows - 2), (0, 1)
    for buf, first, second in ((up, top, bottom), (down, bottom, top)):
        near = jnp.where(lower, first[0], second[0])
        far = jnp.where(lower, first[1], second[1])
        for place, line in ((0, near), (fields, far)):
            row_wet = mask[pl.ds(line, 1), :].astype(F32)
            buf[place : place + half, :] = tr[pl.ds(line, half, stride=rows), :] * row_wet
            buf[place + half : place + fields, :] = ve[pl.ds(line, half, stride=rows), :] * row_wet
        buf[2 * fields : 2 * fields + 8, :] = jnp.zeros((8, LANES), F32)
        buf[2 * fields : 2 * fields + 1, :] = mask[pl.ds(near, 1), :].astype(F32)
        buf[2 * fields + 1 : 2 * fields + 2, :] = mask[pl.ds(far, 1), :].astype(F32)
        buf[2 * fields + 2 : 2 * fields + 3, :] = mix[pl.ds(near, 1), :]

    blocks = own.shape[1]
    info[0:rows, :] = mask[...]
    info[rows : rows + 8, :] = jnp.zeros((8, LANES), jnp.int32)
    info[rows : rows + 1, 0:blocks] = own[...]
    info[rows + 1 : rows + 2, 0:blocks] = arow[...]


def corner_kernel(rows, up_in, down_in, from_east, from_west, up, down):
    lower = is_lower()
    lane = iota((1, LANES), 1)
    for src, dst, first, second in ((up_in, up, rows - 1, 0), (down_in, down, 0, rows - 1)):
        near = jnp.where(lower, first, second)
        dst[...] = src[...]
        dst[3:4, :] = jnp.where(
            (lane & 1) == 0, from_east[pl.ds(near, 1), :], from_west[pl.ds(near, 1), :]
        )
        wet_east = from_east[pl.ds(rows + near, 1), :]
        wet_west = from_west[pl.ds(rows + near, 1), :]
        dst[4:5, :] = jnp.where(
            lane == 0,
            jnp.broadcast_to(wet_east[:, 0:1], (1, LANES)),
            jnp.broadcast_to(wet_west[:, 0:1], (1, LANES)),
        )


def level_matrix(kind, levels, source, target):
    if kind == "mix":
        above = (source == jnp.maximum(target - 1, 0)).astype(F32)
        below = (source == jnp.minimum(target + 1, levels - 1)).astype(F32)
        return above + below - 2.0 * (source == target).astype(F32)
    full = jnp.where(source < target, 1.0, jnp.where(source == target, 0.5, 0.0))
    return (0.5 * GRAVITY) * full


def density_weight(group):
    return jnp.where(group == 0, -THERMAL, jnp.where(group == 1, HALINE, 0.0)).astype(F32)


def advance_columns(levels, mid, outer, inner, corner_n, corner_s, wets, mixing, coriolis):
    rows = mid.shape[0]
    wet_mid, wet_out, wet_in, wet_corner_n, wet_corner_s = wets
    lane = iota((rows, LANES), 1)
    row = iota((rows, LANES), 0)
    even = (lane & 1) == 0
    group = lane // (2 * levels)

    def sides(outside, inside):
        return jnp.where(even, outside, inside), jnp.where(even, inside, outside)

    def shifted(x, north, south):
        n = jnp.where(row == rows - 1, north, pltpu.roll(x, rows - 1, 0))
        s = jnp.where(row == 0, south, pltpu.roll(x, 1, 0))
        return n, s

    e, w = sides(outer, inner)
    wet_e, wet_w = sides(wet_out, wet_in)
    n, s = shifted(mid, corner_n, corner_s)
    wet_n, wet_s = shifted(wet_mid, wet_corner_n, wet_corner_s)
    lap = wet_e * (e - mid) + wet_w * (w - mid) + wet_n * (n - mid) + wet_s * (s - mid)
    de, dn = e - w, n - s
    span = 2 * levels
    one, two, three = (pltpu.roll(mid, i * span, 1) for i in (1, 2, 3))

    def pick(a, b, c, d):
        return jnp.where(group == 0, a, jnp.where(group == 1, b, jnp.where(group == 2, c, d)))

    u = pick(two, three, mid, one)
    v = pick(one, two, three, mid)
    adv = 0.5 * (u * de + v * dn)
    src, dst = iota((LANES, LANES), 0), iota((LANES, LANES), 1)
    src_group, dst_group = src // span, dst // span
    src_level, dst_level = (src // 2) % levels, (dst // 2) % levels
    same_side = (src & 1) == (dst & 1)
    mix_map = jnp.where(
        same_side & (src_group == dst_group), level_matrix("mix", levels, src_level, dst_level), 0.0
    )
    press = level_matrix("pressure", levels, src_level, dst_level) * density_weight(src_group)
    press_x = jnp.where(same_side & (dst_group == 2), press, 0.0)
    press_y = jnp.where(same_side & (dst_group == 3), press, 0.0)
    vertical = dot(mid, mix_map)
    grad = dot(de, press_x) + dot(dn, press_y)
    zero = jnp.zeros_like(mid)
    turn = pick(zero, zero, coriolis * v, -coriolis * u)
    kappa = jnp.where(group < 2, mixing, VISCOSITY)
    tend = turn - adv - grad + kappa * lap + VERTICAL_MIX * vertical
    return wet_mid * (mid + TIMESTEP * tend)


def advance_row(levels, north_side, mid, outer, inner, corner_e, corner_w, wets, mixing, coriolis):
    fields = mid.shape[0]
    wet_mid, wet_out, wet_in, wet_corner_e, wet_corner_w = wets
    lane = iota((fields, LANES), 1)
    lane8 = iota((8, LANES), 1)

    def sides(x, east, west, at):
        e = jnp.where(at == LANES - 1, east, pltpu.roll(x, LANES - 1, 1))
        w = jnp.where(at == 0, west, pltpu.roll(x, 1, 1))
        return e, w

    e, w = sides(mid, corner_e, corner_w, lane)
    wet_e, wet_w = sides(
        jnp.broadcast_to(wet_mid, (8, LANES)), wet_corner_e, wet_corner_w, lane8
    )
    wet_e, wet_w = wet_e[0:1], wet_w[0:1]
    n, s = (outer, inner) if north_side else (inner, outer)
    wet_n, wet_s = (wet_out, wet_in) if north_side else (wet_in, wet_out)
    lap = wet_e * (e - mid) + wet_w * (w - mid) + wet_n * (n - mid) + wet_s * (s - mid)
    de, dn = e - w, n - s
    u, v = mid[2 * levels : 3 * levels], mid[3 * levels :]
    adv = 0.5 * (jnp.concatenate([u] * 4, axis=0) * de + jnp.concatenate([v] * 4, axis=0) * dn)
    dst, src = iota((fields, fields), 0), iota((fields, fields), 1)
    mix_map = jnp.where(
        dst // levels == src // levels, level_matrix("mix", levels, src % levels, dst % levels), 0.0
    )
    dst, src = iota((levels, fields), 0), iota((levels, fields), 1)
    press = level_matrix("pressure", levels, src % levels, dst) * density_weight(src // levels)
    vertical = dot(mix_map, mid)
    zero = jnp.zeros((2 * levels, LANES), F32)
    turn = jnp.concatenate(
        [zero, coriolis * v - dot(press, de), -coriolis * u - dot(press, dn)], axis=0
    )
    kappa = jnp.concatenate(
        [jnp.broadcast_to(mixing, (2 * levels, LANES)), jnp.full((2 * levels, LANES), VISCOSITY)],
        axis=0,
    )
    tend = turn - adv + kappa * lap + VERTICAL_MIX * vertical
    return wet_mid * (mid + TIMESTEP * tend)


def advance_level(k, count, levels, rows, src, sides, wets, mixing, coriolis, acc):
    pitch = rows + 2 * PAD
    wet, wet_e, wet_w, wet_n, wet_s = wets
    lane = iota((rows, LANES), 1)
    first, last = lane == 0, lane == LANES - 1
    above_k = jnp.maximum(k - 1, 0)
    below_k = jnp.minimum(k + 1, levels - 1)

    def load(q, level, shift):
        return src[pl.ds((q * count + level) * pitch + PAD + shift, rows), :]

    center, lap, de, dn, vertical = [], [], [], [], []
    for q in range(4):
        c = load(q, k, 0)
        n, s = load(q, k, 1), load(q, k, -1)
        edge = pltpu.roll(sides, (LANES - 1 - 2 * (q * levels + k)) & (LANES - 1), 1)
        e = jnp.where(last, edge, pltpu.roll(c, LANES - 1, 1))
        w = jnp.where(first, edge, pltpu.roll(c, 1, 1))
        center.append(c)
        lap.append(wet_e * (e - c) + wet_w * (w - c) + wet_n * (n - c) + wet_s * (s - c))
        de.append(e - w)
        dn.append(n - s)
        vertical.append(load(q, above_k, 0) + load(q, below_k, 0) - 2.0 * c)
    u, v = center[2], center[3]
    dens_x = HALINE * de[1] - THERMAL * de[0]
    dens_y = HALINE * dn[1] - THERMAL * dn[0]
    acc_x, acc_y = acc
    grad_x = (0.5 * GRAVITY) * (acc_x + 0.5 * dens_x)
    grad_y = (0.5 * GRAVITY) * (acc_y + 0.5 * dens_y)
    extra = (None, None, coriolis * v - grad_x, -coriolis * u - grad_y)
    new = []
    for q in range(4):
        tend = (mixing if q < 2 else VISCOSITY) * lap[q] - 0.5 * (u * de[q] + v * dn[q])
        tend = tend + VERTICAL_MIX * vertical[q]
        if extra[q] is not None:
            tend = tend + extra[q]
        new.append(wet * (center[q] + TIMESTEP * tend))
    return new, (acc_x + dens_x, acc_y + dens_y)


class Halo:
    def __init__(self, rows, fields):
        at = 0
        for name, size in (
            ("side0", rows), ("side1", rows), ("north0", fields), ("south0", fields),
            ("north1", fields), ("south1", fields), ("wet_e", rows), ("wet_w", rows),
            ("wet_n", rows), ("wet_s", rows), ("coriolis", rows),
        ):
            setattr(self, name, slice(at, at + size))
            at += size
        self.size = at


def surface_kernel(
    rows, levels, lat_count,
    tr, ve, mask, mix, east, west, from_east, from_west, from_up, from_down, up, down, own,
    halo, out, now, later, wet_pad, stage,
):
    fields = 4 * levels
    at = Halo(rows, fields)
    lat = lax.axis_index("lat")
    lower = is_lower()
    fold = lat == lat_count - 1
    wet = mask[...].astype(F32)
    mixing = mix[...]
    lane = iota((rows, LANES), 1)
    even = (lane & 1) == 0

    latitude = lat * rows - PAD + iota((rows + 2 * PAD, LANES), 0)
    total = lat_count * rows
    latitude = jnp.where(latitude >= total, 2 * total - 1 - latitude, latitude).astype(F32)
    table = CORIOLIS_MAX * jnp.sin(math.pi * (-0.43 + 0.93 * (latitude + 0.5) / total))
    coriolis = table[PAD : PAD + rows]

    got_up, got_down = from_up[...], from_down[...]
    north, south = jnp.where(lower, got_down, got_up), jnp.where(lower, got_up, got_down)
    length = 2 * fields + 8
    back = jnp.broadcast_to(LANES - 1 - iota((8, LANES), 1), (8, LANES))
    flipped = jnp.concatenate(
        [
            jnp.take_along_axis(north[i : i + 8], back, axis=1)
            * (-1.0 if i < 2 * fields and i % fields >= fields // 2 else 1.0)
            for i in range(0, length, 8)
        ],
        axis=0,
    )
    straight = north
    north = jnp.where(fold, flipped, straight)
    lane1 = iota((1, LANES), 1)
    even1 = (lane1 & 1) == 0
    tail_n, tail_s = straight[2 * fields :], south[2 * fields :]
    swapped = jnp.where(
        iota((8, LANES), 1) & 1 == 0, pltpu.roll(tail_n, LANES - 1, 1), pltpu.roll(tail_n, 1, 1)
    )
    sign = jnp.where(lane1 >= LANES // 2, -1.0, 1.0)
    corner_n = jnp.where(fold, swapped[3:4] * sign, tail_n[3:4])
    corner_s = tail_s[3:4]
    wet_corner_n = jnp.where(fold, swapped[4:5], tail_n[4:5])
    wet_corner_s = tail_s[4:5]

    def corner_wet(x):
        east_wet = jnp.broadcast_to(x[:, 0:1], (1, LANES))
        west_wet = jnp.broadcast_to(x[:, 1:2], (1, LANES))
        return east_wet, west_wet, jnp.where(even1, east_wet, west_wet)

    wet_ne, wet_nw, wet_n_lanes = corner_wet(wet_corner_n)
    wet_se, wet_sw, wet_s_lanes = corner_wet(wet_corner_s)

    north_rows = (north[0:fields], north[fields : 2 * fields], north[2 * fields :])
    south_rows = (south[0:fields], south[fields : 2 * fields], south[2 * fields :])
    halo[at.north0] = north_rows[0]
    halo[at.south0] = south_rows[0]

    wet_pad[PAD : PAD + rows, :] = wet
    wet_pad[PAD - 1 : PAD, :] = south_rows[2][0:1]
    wet_pad[PAD + rows : PAD + rows + 1, :] = north_rows[2][0:1]
    wet_n = wet_pad[PAD + 1 : PAD + 1 + rows, :]
    wet_s = wet_pad[PAD - 1 : PAD - 1 + rows, :]

    def spread(x, i):
        return jnp.broadcast_to(x[:, i : i + 1], (rows, LANES))

    aux_e, aux_w = from_east[rows:, :], from_west[rows:, :]
    wet_col_e, wet_col_w = spread(aux_e, 0), spread(aux_w, 0)
    wet_e = jnp.where(lane == LANES - 1, wet_col_e, pltpu.roll(wet, LANES - 1, 1))
    wet_w = jnp.where(lane == 0, wet_col_w, pltpu.roll(wet, 1, 1))
    halo[at.wet_e] = wet_e
    halo[at.wet_w] = wet_w
    halo[at.wet_n] = wet_n
    halo[at.wet_s] = wet_s
    halo[at.coriolis] = coriolis

    got_e, got_w = from_east[0:rows, :], from_west[0:rows, :]
    side = jnp.where(even, got_e, got_w)
    outer = jnp.where(even, pltpu.roll(got_e, LANES - 1, 1), pltpu.roll(got_w, 1, 1))
    inner = jnp.where(
        even, pltpu.roll(east[0:rows, :], LANES - 1, 1), pltpu.roll(west[0:rows, :], 1, 1)
    )
    halo[at.side0] = side
    side_new = advance_columns(
        levels, side, outer, inner, corner_n, corner_s,
        (
            jnp.where(even, wet_col_e, wet_col_w),
            jnp.where(even, spread(aux_e, 1), spread(aux_w, 1)),
            jnp.where(even, spread(wet, LANES - 1), spread(wet, 0)),
            wet_n_lanes,
            wet_s_lanes,
        ),
        jnp.where(even, spread(aux_e, 2), spread(aux_w, 2)),
        coriolis,
    )
    halo[at.side1] = side_new

    field_lane = iota((fields, LANES), 1)
    field_id = iota((fields, LANES), 0)

    def to_sublanes(x, parity):
        here = field_lane == 2 * field_id + parity
        return jnp.sum(jnp.where(here, x, 0.0), axis=1, keepdims=True)

    own_up, own_down = up[...], down[...]
    for north_side, (mid, outside, tail), inside, corner, corner_wets, line, lat_row, place in (
        (
            True, north_rows, jnp.where(lower, own_up, own_down), corner_n, (wet_ne, wet_nw),
            rows - 1, PAD + rows, at.north1,
        ),
        (
            False, south_rows, jnp.where(lower, own_down, own_up), corner_s, (wet_se, wet_sw),
            0, PAD - 1, at.south1,
        ),
    ):
        halo[place] = advance_row(
            levels, north_side, mid, outside, inside,
            to_sublanes(corner, 0), to_sublanes(corner, 1),
            (tail[0:1], tail[1:2], wet[line : line + 1], *corner_wets),
            tail[2:3], table[lat_row : lat_row + 1],
        )

    count = now.shape[0] // (4 * (rows + 2 * PAD))
    pitch = rows + 2 * PAD
    for q in range(4):
        ref = tr if q < 2 else ve
        for k in range(count):
            base = (q * count + k) * pitch
            field = q * levels + k
            now[base + PAD : base + PAD + rows, :] = ref[q % 2, k * rows : (k + 1) * rows, :] * wet
            for buf, north_at, south_at in (
                (now, at.north0, at.south0),
                (later, at.north1, at.south1),
            ):
                n, s = north_at.start + field, south_at.start + field
                buf[base + PAD + rows : base + PAD + rows + 1, :] = halo[n : n + 1, :]
                buf[base + PAD - 1 : base + PAD, :] = halo[s : s + 1, :]
    wets = (wet, wet_e, wet_w, wet_n, wet_s)
    none = jnp.zeros((rows, LANES), F32)
    acc = (none, none)
    for k in range(count - 1):
        new, acc = advance_level(
            k, count, levels, rows, now, side, wets, mixing, coriolis, acc
        )
        for q in range(4):
            base = (q * count + k) * pitch + PAD
            later[base : base + rows, :] = new[q]
    new, _ = advance_level(
        0, count, levels, rows, later, side_new, wets, mixing, coriolis, (none, none)
    )
    for q in range(4):
        stage[pl.ds(q, rows, stride=4), :] = new[q]

    out[...] = jnp.zeros(out.shape, F32)
    for r in range(rows):
        place = pl.multiple_of(own[r] * (4 * CAP), 4 * CAP)
        out[pl.ds(place, 4), :] = stage[4 * r : 4 * r + 4, :]
    for r in reversed(range(rows)):
        place = pl.multiple_of(own[r] * (4 * CAP), 4 * CAP)
        out[pl.ds(place + 4, 4), :] = stage[4 * r : 4 * r + 4, :]


def main_kernel(
    rows, levels, devices, tr, ve, mask, mix, halo, info, tr_out, ve_out, slots, cover, now, later
):
    fields = 4 * levels
    half = fields // 2
    pitch = rows + 2 * PAD
    at = Halo(rows, fields)
    wet = mask[...].astype(F32)
    mixing = mix[...]
    wets = (wet, halo[at.wet_e], halo[at.wet_w], halo[at.wet_n], halo[at.wet_s])
    coriolis = halo[at.coriolis]
    for buf, north, south in ((now, at.north0, at.south0), (later, at.north1, at.south1)):
        buf[pl.ds(PAD - 1, fields, stride=pitch), :] = halo[south]
        buf[pl.ds(PAD + rows, fields, stride=pitch), :] = halo[north]

    for ref, base in ((tr, 0), (ve, half)):

        def fill(f, carry, ref=ref, base=base):
            x = ref[pl.ds(pl.multiple_of(f * rows, rows), rows), :] * wet
            now[pl.ds(pl.multiple_of((base + f) * pitch + PAD, 8), rows), :] = x
            return carry

        lax.fori_loop(0, half, fill, 0, unroll=4)

    none = jnp.zeros((rows, LANES), F32)

    def first(k, acc):
        new, acc = advance_level(
            k, levels, levels, rows, now, halo[at.side0], wets, mixing, coriolis, acc
        )
        for q in range(4):
            place = pl.multiple_of((q * levels + k) * pitch + PAD, 8)
            later[pl.ds(place, rows), :] = new[q]
        return acc

    def second(k, acc):
        new, acc = advance_level(
            k, levels, levels, rows, later, halo[at.side1], wets, mixing, coriolis, acc
        )
        for q in range(4):
            ref = tr_out if q < 2 else ve_out
            place = pl.multiple_of(((q % 2) * levels + k) * rows, 8)
            ref[pl.ds(place, rows), :] = new[q]
        return acc

    lax.fori_loop(0, levels, first, (none, none))
    lax.fori_loop(0, levels, second, (none, none))

    me = lax.axis_index("lon") * lax.axis_size("lat") + lax.axis_index("lat")
    pitch = rows + 8
    owner = info[pl.ds(rows, devices, stride=pitch), :]
    target = info[pl.ds(rows + 1, devices, stride=pitch), :]
    lane = iota((devices, LANES), 1)
    mine = (owner == me) & (lane < rows)
    last = jnp.max(jnp.where(mine, lane, -1), axis=1, keepdims=True)
    start = jnp.min(jnp.where(mine, lane, LANES), axis=1, keepdims=True)
    for i, block in enumerate((last, start)):
        line = jnp.sum(jnp.where(lane == block, target, 0), axis=1, keepdims=True)
        keep = (last >= 0) if i == 0 else (last > start)
        slots[i * devices : (i + 1) * devices, :] = ((lane == line) & keep).astype(F32)

    atm_row = iota((ATM_ROWS, rows), 0)

    def count(d, total):
        base = pl.multiple_of(d * pitch, 8)
        extra = info[pl.ds(base + rows, 8), :]
        here = (extra[1:2, 0:rows] == atm_row) & (extra[0:1, 0:rows] == me)
        wet_rows = info[pl.ds(base, rows), :].astype(F32)
        return total + jnp.dot(
            here.astype(F32).astype(jnp.bfloat16), wet_rows.astype(jnp.bfloat16),
            preferred_element_type=F32,
        )

    cover[...] = lax.fori_loop(0, devices, count, jnp.zeros((ATM_ROWS, LANES), F32), unroll=4)


def reduce_kernel(devices, data, slots, cover, surface, cover_out):
    ocean = cover[...]
    cover_out[...] = ocean
    share = 1.0 / jnp.maximum(ocean, 1.0)
    totals = None
    for i in range(CAP):
        fields = [data[pl.ds(4 * i + q, devices, stride=4 * CAP), :] for q in range(4)]
        to_rows = slots[i * devices : (i + 1) * devices, :]
        part = dot(to_rows, jnp.concatenate(fields, axis=1), (((0,), (0,)), ((), ())))
        totals = part if totals is None else totals + part
    for q in range(4):
        surface[q] = totals[0:ATM_ROWS, q * LANES : (q + 1) * LANES] * share


def call(kernel, out_shape, **kwargs):
    return pl.pallas_call(
        kernel,
        out_shape=out_shape,
        compiler_params=pltpu.CompilerParams(vmem_limit_bytes=VMEM_LIMIT),
        **kwargs,
    )


def shaped(*shape, dtype=F32):
    return jax.ShapeDtypeStruct(shape, dtype)


def local(tracers, velocity, land_mask, mixing, owners, atm_row):
    levels = tracers.shape[1]
    rows, cols = land_mask.shape
    fields = 4 * levels
    lon_count, lat_count = lax.axis_size("lon"), lax.axis_size("lat")
    devices = lon_count * lat_count
    assert cols == LANES and rows % 8 == 0 and 2 * fields == LANES and lon_count % 2 == 0
    tr = tracers.reshape(2, levels * rows, cols)
    ve = velocity.reshape(2, levels * rows, cols)
    tr_flat, ve_flat = tr.reshape(-1, cols), ve.reshape(-1, cols)
    owner_list = owners.reshape(rows)
    length = 2 * fields + 8

    east, west, up, down, info = call(
        functools.partial(pack_kernel, rows, fields, devices),
        [
            shaped(2 * rows, cols),
            shaped(2 * rows, cols),
            shaped(length, cols),
            shaped(length, cols),
            shaped(rows + 8, cols, dtype=jnp.int32),
        ],
    )(tr_flat, ve_flat, land_mask, mixing, owners.reshape(1, rows), atm_row.reshape(1, rows))
    info = lax.all_gather(info, ("lon", "lat"), axis=0, tiled=True)

    ring = [(i, (i + 1) % lon_count) for i in range(lon_count)]
    from_west = lax.ppermute(east, "lon", ring)
    from_east = lax.ppermute(west, "lon", [(j, i) for i, j in ring])

    tail = pl.BlockSpec((8, cols), lambda i: (length // 8 - 1, 0))
    whole = pl.BlockSpec((2 * rows, cols), lambda i: (0, 0))
    up, down = call(
        functools.partial(corner_kernel, rows),
        [shaped(length, cols), shaped(length, cols)],
        grid=(1,),
        in_specs=[tail, tail, whole, whole],
        out_specs=[tail, tail],
        input_output_aliases={0: 0, 1: 1},
    )(up, down, from_east, from_west)

    path = []
    for i in range(lon_count // 2):
        line = [i * lat_count + a for a in range(lat_count)]
        line += [(lon_count - 1 - i) * lat_count + a for a in reversed(range(lat_count))]
        path += list(zip(line[:-1], line[1:]))
    from_up = lax.ppermute(up, ("lon", "lat"), path)
    from_down = lax.ppermute(down, ("lon", "lat"), [(j, i) for i, j in path])

    at = Halo(rows, fields)
    count = min(3, levels)
    pitch = rows + 2 * PAD

    def full(*shape):
        return pl.BlockSpec(shape, lambda i: (0,) * len(shape))

    top = full(2, count * rows, cols)
    halo, outgoing = call(
        functools.partial(surface_kernel, rows, levels, lat_count),
        [shaped(at.size, cols), shaped(devices * CAP * 4, cols)],
        grid=(1,),
        in_specs=[top, top, full(rows, cols), full(rows, cols)]
        + [full(2 * rows, cols)] * 4
        + [full(length, cols)] * 2
        + [full(fields, cols)] * 2
        + [pl.BlockSpec(memory_space=pltpu.SMEM)],
        out_specs=[full(at.size, cols), full(devices * CAP * 4, cols)],
        scratch_shapes=[
            pltpu.VMEM((4 * count * pitch, cols), F32),
            pltpu.VMEM((4 * count * pitch, cols), F32),
            pltpu.VMEM((pitch, cols), F32),
            pltpu.VMEM((4 * rows, cols), F32),
        ],
    )(tr, ve, land_mask, mixing, east, west, from_east, from_west, from_up, from_down, up, down,
      owner_list)
    incoming = lax.all_to_all(
        outgoing.reshape(devices, CAP * 4, cols), ("lon", "lat"), 0, 0, tiled=True
    ).reshape(devices * CAP * 4, cols)

    tr_out, ve_out, slots, cover = call(
        functools.partial(main_kernel, rows, levels, devices),
        [
            shaped(2 * levels * rows, cols),
            shaped(2 * levels * rows, cols),
            shaped(CAP * devices, cols),
            shaped(ATM_ROWS, cols),
        ],
        scratch_shapes=[
            pltpu.VMEM((fields * pitch, cols), F32),
            pltpu.VMEM((fields * pitch, cols), F32),
        ],
        cost_estimate=pl.CostEstimate(
            flops=80 * fields * rows * cols, bytes_accessed=5 << 20, transcendentals=0
        ),
    )(tr_flat, ve_flat, land_mask, mixing, halo, info)
    surface, cover = call(
        functools.partial(reduce_kernel, devices),
        [shaped(4, ATM_ROWS, cols), shaped(ATM_ROWS, cols)],
    )(incoming, slots, cover)
    shape = (2, levels, rows, cols)
    return tr_out.reshape(shape), ve_out.reshape(shape), surface, cover


def solution(mesh):
    in_specs = (
        P(None, None, "lat", "lon"),
        P(None, None, "lat", "lon"),
        P("lat", "lon"),
        P("lat", "lon"),
        P(("lon", "lat"), None),
        P(("lon", "lat")),
    )
    out_specs = (
        P(None, None, "lat", "lon"),
        P(None, None, "lat", "lon"),
        P(None, ("lon", "lat"), None),
        P(("lon", "lat"), None),
    )
    return jax.shard_map(local, mesh=mesh, in_specs=in_specs, out_specs=out_specs, check_vma=False)
```

time: 186 us -> 81.8 us (0.44); the launches traced: 183 us -> 81.4 us
  local copies, waits for them, and re-layouts: 85.5 us -> 4.19 us
  other arithmetic: 50.3 us -> 0 us
  blocking collectives: 0 us -> 44.5 us
  starting transfers between devices: 33.8 us -> 13.9 us
  Pallas kernels: 0 us -> 11.4 us
  waiting for transfers between devices: 11.5 us -> 6.55 us
    all_gather x0 -> x1, blocking collectives: none -> 44.5 us  [local(): info = lax.all_gather(info, ('lon', 'lat'), axis=0, tiled=True)]
    slice x42 -> x0, local copies, waits for them, and re-layouts: 32.5 us -> none  [the longest x7 8.58 us: neighbour(): rolled = jnp.roll(center, shift, axis=axis)]
    select_n x18 -> x0, other arithmetic: 17 us -> none  [the longest x15 15.1 us: neighbour(): return jnp.where(position, jnp.expand_dims(edge_value, axis), rolled)]
    unnamed x194 -> x20, local copies, waits for them, and re-layouts: 20.2 us -> 4.19 us
    ppermute x12 -> x4, starting transfers between devices: 21.7 us -> 6.59 us  [the longest x1 2.99 us: local(): from_west = lax.ppermute(east, 'lon', ring)]
    pallas_call x0 -> x5, Pallas kernels: none -> 11.4 us  [the longest x1 6.87 us: local(): call(functools.partial(main_kernel, rows, levels, devices), [shaped(2 * l...]
    broadcast_in_dim x14 -> x0, local copies, waits for them, and re-layouts: 11.2 us -> none  [the longest x12 10.4 us: neighbour(): return jnp.where(position, jnp.expand_dims(edge_value, axis), rolled)]
    mul x10 -> x0, other arithmetic: 10.8 us -> none  [the longest x2 5.4 us: local(): 0.5 * (zonal_vel * (fields_east - fields_west) + merid_vel * (fields_nort...]
  transfers between devices with their start and end apart: 14 -> 5, of which waited for: 3 -> 3; matrix products, arithmetic and copies ran while one was open for 60% -> 0% of each run, Pallas kernels for 0% -> 8%
where the time goes in v1:
time: 81.8 us; the launch traced here: 81.4 us
  blocking collectives  44.5 us (54%)
  starting transfers between devices  13.9 us (17%)
  Pallas kernels  11.4 us (14%)
  waiting for transfers between devices  6.55 us (8%)
  local copies, waits for them, and re-layouts  4.19 us (5%)
    all_gather x1, blocking collectives, local(): info = lax.all_gather(info, ('lon', 'lat'), axis=0, tiled=True)  44.5 us
    all_to_all x1, starting transfers between devices, local(): lax.all_to_all(outgoing.reshape(devices, CAP * 4, cols), ('lon', 'lat'),...  7.36 us
    pallas_call x1, Pallas kernels, local(): call(functools.partial(main_kernel, rows, levels, devices), [shaped(2 * l...  6.87 us
    unnamed x20, local copies, waits for them, and re-layouts  4.19 us
    ppermute x1, waiting for transfers between devices, local(): from_down = lax.ppermute(down, ('lon', 'lat'), [(j, i) for i, j in path])  3.65 us
    ppermute x1, starting transfers between devices, local(): from_west = lax.ppermute(east, 'lon', ring)  2.99 us
    pallas_call x1, Pallas kernels, local(): call(functools.partial(surface_kernel, rows, levels, lat_count), [shaped(...  2.06 us
    ppermute x1, waiting for transfers between devices, local(): from_west = lax.ppermute(east, 'lon', ring)  1.83 us
  transfers between devices with their start and end apart: 5, of which 3 were waited for; matrix products, arithmetic and copies ran while one was open for 0% of the time, Pallas kernels for 8%

profile of v1, /device:TPU:0, one launch (start us, length us, event | category | flops | bytes accessed | tf_op | source)
XLA Modules:
  0.0 81.4 jit_solution(14815706608930109322)
XLA Ops:
  0.6 0.0 copy-start.8
  0.6 0.0 copy-start.9
  0.7 0.6 copy-done.8
  1.3 0.0 copy-done.9
  1.3 0.0 copy-start
  1.3 1.0 %copy-done = f32[2,16,32,128]{3,2,1,0:T(8,128)S(1)} copy-done((f32[2,16,32,128]{3,2,1,0:T(8,128)S(1)}, f32[2,16,32,128]{3,2,1,0:T(8,128)}, u32[]{:S(2)}) %copy-start) | copy-done | bytes 524312
  2.3 0.0 copy-start.2
  2.3 1.0 %copy-done.2 = f32[2,16,32,128]{3,2,1,0:T(8,128)S(1)} copy-done((f32[2,16,32,128]{3,2,1,0:T(8,128)S(1)}, f32[2,16,32,128]{3,2,1,0:T(8,128)}, u32[]{:S(2)}) %copy-start.2) | copy-done | bytes 524312
  3.4 0.0 copy-start.4
  3.4 0.7 copy-done.4
  4.1 0.0 copy-start.6
  4.1 0.7 copy-done.6
  4.8 0.0 copy-start.1
  4.8 1.2 %shard_map.93 = (f32[64,128]{1,0:T(8,128)S(1)}, f32[64,128]{1,0:T(8,128)S(1)}, f32[136,128]{1,0:T(8,128)S(1)}, f32[136,128]{1,0:T(8,128)S(1)}, s32[40,128]{1,0:T(8,128)S(1)}) custom-call(f32[1024,128]{1,0:T(8,128)S(1)} %bitcast.11, f32[1024,128]{1,0:T(8,128)S(1)} %bitcast.14, s32[32,128]{1,0:T(8,128)S(1)} %copy-done.4, f32[32,128]{1,0:T(8,128)S(1)} %copy-done.6, ...), custom_call_target="tpu_custom_call" | custom-call | tf_op jit(solution)/shard_map/pallas_call | solution.py:548
  6.1 3.0 %collective-permute-start.1 = (f32[64,128]{1,0:T(8,128)S(1)}, f32[64,128]{1,0:T(8,128)S(1)}, u32[]{:S(2)}, u32[]{:S(2)}) collective-permute-start(f32[64,128]{1,0:T(8,128)S(1)} %get-tuple-element.19.east), channel_id=1, source_target_pairs={{0,8},{8,16},{16,24},{24,0},{1,9},{9,17},{17,25},{25,1},{2,10},{10... | collective-permute-start | bytes 98312 | tf_op jit(solution)/shard_map/ppermute | solution.py:561
  9.1 1.0 %collective-permute-start = (f32[64,128]{1,0:T(8,128)S(1)}, f32[64,128]{1,0:T(8,128)S(1)}, u32[]{:S(2)}, u32[]{:S(2)}) collective-permute-start(f32[64,128]{1,0:T(8,128)S(1)} %get-tuple-element.20.west), channel_id=1, source_target_pairs={{8,0},{16,8},{24,16},{0,24},{9,1},{17,9},{25,17},{1,25},{10,2},{18... | collective-permute-start | bytes 98312 | tf_op jit(solution)/shard_map/ppermute | solution.py:562
  10.1 1.8 %collective-permute-done.1.from_west = f32[64,128]{1,0:T(8,128)S(1)} collective-permute-done((f32[64,128]{1,0:T(8,128)S(1)}, f32[64,128]{1,0:T(8,128)S(1)}, u32[]{:S(2)}, u32[]{:S(2)}) %collective-permute-start.1) | collective-permute-done | bytes 32800 | tf_op jit(solution)/shard_map/ppermute | solution.py:561
  11.9 1.1 %collective-permute-done.from_east = f32[64,128]{1,0:T(8,128)S(1)} collective-permute-done((f32[64,128]{1,0:T(8,128)S(1)}, f32[64,128]{1,0:T(8,128)S(1)}, u32[]{:S(2)}, u32[]{:S(2)}) %collective-permute-start) | collective-permute-done | bytes 32800 | tf_op jit(solution)/shard_map/ppermute | solution.py:562
  13.0 0.1 shard_map.94
  13.0 1.3 %collective-permute-start.2 = (f32[136,128]{1,0:T(8,128)S(1)}, f32[136,128]{1,0:T(8,128)S(1)}, u32[]{:S(2)}, u32[]{:S(2)}) collective-permute-start(f32[136,128]{1,0:T(8,128)S(1)} %get-tuple-element.23.up), channel_id=1, source_target_pairs={{0,1},{1,2},{2,3},{3,4},{4,5},{5,6},{6,7},{7,31},{31,30},{30,29},{... | collective-permute-start | bytes 208904 | tf_op jit(solution)/shard_map/ppermute | solution.py:580
  14.3 1.3 %collective-permute-start.3 = (f32[136,128]{1,0:T(8,128)S(1)}, f32[136,128]{1,0:T(8,128)S(1)}, u32[]{:S(2)}, u32[]{:S(2)}) collective-permute-start(f32[136,128]{1,0:T(8,128)S(1)} %get-tuple-element.24.down), channel_id=1, source_target_pairs={{1,0},{2,1},{3,2},{4,3},{5,4},{6,5},{7,6},{31,7},{30,31},{29,30},{... | collective-permute-start | bytes 208904 | tf_op jit(solution)/shard_map/ppermute | solution.py:581
  15.6 0.0 collective-permute-done.2.from_up
  15.6 3.7 %collective-permute-done.3.from_down = f32[136,128]{1,0:T(8,128)S(1)} collective-permute-done((f32[136,128]{1,0:T(8,128)S(1)}, f32[136,128]{1,0:T(8,128)S(1)}, u32[]{:S(2)}, u32[]{:S(2)}) %collective-permute-start.3) | collective-permute-done | bytes 69664 | tf_op jit(solution)/shard_map/ppermute | solution.py:581
  19.3 0.0 copy-done.1
  19.3 2.1 %shard_map.95 = (f32[480,128]{1,0:T(8,128)S(1)}, f32[256,128]{1,0:T(8,128)}) custom-call(f32[2,512,128]{2,1,0:T(8,128)S(1)} %bitcast.12, f32[2,512,128]{2,1,0:T(8,128)S(1)} %bitcast.15, s32[32,128]{1,0:T(8,128)S(1)} %copy-done.4, f32[32,128]{1,0:T(8,128)S(1)} %copy-done.6, f32[64,128]{1,0:T(8,128)S(1)} %get-tuple-element.19.east, ...), custom_call_target="tpu_custom_call" | custom-call | tf_op jit(solution)/shard_map/pallas_call | solution.py:591
  21.4 0.0 copy-start.3
  21.4 7.4 %all-to-all-start = ((f32[32,8,128]{2,1,0:T(8,128)}), f32[32,8,128]{2,1,0:T(8,128)S(1)}, u32[]{:S(2)}, u32[]{:S(2)}) async-start(f32[32,8,128]{2,1,0:T(8,128)} %bitcast.9), calls=%async_computation | async-start | bytes 262144 | tf_op jit(solution)/shard_map/all_to_all | solution.py:609
  28.7 0.0 copy-start.5
  28.7 0.0 copy-start.7
  28.7 44.5 %all_gather.3.info = s32[1280,128]{1,0:T(8,128)S(1)} all-gather(s32[40,128]{1,0:T(8,128)S(1)} %get-tuple-element.26), channel_id=1, replica_groups=mesh['lon'=4,'lat'=8] {'lon','lat'}, dimensions={0}, use_global_device_ids=true | all-gather | bytes 675840 | tf_op jit(solution)/shard_map/all_gather | solution.py:558
  73.3 0.0 copy-done.3
  73.3 0.0 copy-done.5
  73.3 0.0 copy-done.7
  73.3 6.9 %shard_map.96 = (f32[1024,128]{1,0:T(8,128)}, f32[1024,128]{1,0:T(8,128)}, f32[64,128]{1,0:T(8,128)S(1)}, f32[32,128]{1,0:T(8,128)S(1)}) custom-call(f32[1024,128]{1,0:T(8,128)S(1)} %bitcast.13, f32[1024,128]{1,0:T(8,128)S(1)} %bitcast.16, s32[32,128]{1,0:T(8,128)S(1)} %copy-done.5, f32[32,128]{1,0:T(8,128)S(1)} %copy-done.7, ...), custom_call_target="tpu_custom_call" | custom-call | flops 20971520 | bytes 5242880 | tf_op jit(solution)/shard_map/pallas_call | solution.py:613
  80.2 0.0 all-to-all-done
  80.2 1.2 %shard_map.97 = (f32[4,32,128]{2,1,0:T(8,128)}, f32[32,128]{1,0:T(8,128)}) custom-call(f32[256,128]{1,0:T(8,128)S(1)} %bitcast.17, f32[64,128]{1,0:T(8,128)S(1)} %get-tuple-element.30.slots, f32[32,128]{1,0:T(8,128)S(1)} %get-tuple-element.31.cover), custom_call_target="tpu_custom_call" | custom-call | tf_op jit(solution)/shard_map/pallas_call | solution.py:629
Async XLA Ops:
  0.6 0.7 copy-start.8
  0.6 0.7 copy-start.9
  1.3 1.0 %copy-start = (f32[2,16,32,128]{3,2,1,0:T(8,128)S(1)}, f32[2,16,32,128]{3,2,1,0:T(8,128)}, u32[]{:S(2)}) copy-start(f32[2,16,32,128]{3,2,1,0:T(8,128)} %param.6) | copy-start | bytes 1572868
  2.3 1.0 %copy-start.2 = (f32[2,16,32,128]{3,2,1,0:T(8,128)S(1)}, f32[2,16,32,128]{3,2,1,0:T(8,128)}, u32[]{:S(2)}) copy-start(f32[2,16,32,128]{3,2,1,0:T(8,128)} %param.7) | copy-start | bytes 1572868
  3.4 0.7 copy-start.4
  4.1 0.7 copy-start.6
  4.8 14.5 %copy-start.1 = (f32[2,16,32,128]{3,2,1,0:T(8,128)S(1)}, f32[2,16,32,128]{3,2,1,0:T(8,128)}, u32[]{:S(2)}) copy-start(f32[2,16,32,128]{3,2,1,0:T(8,128)} %param.6) | copy-start | bytes 1572868
  6.1 5.8 %collective-permute-start.1 = (f32[64,128]{1,0:T(8,128)S(1)}, f32[64,128]{1,0:T(8,128)S(1)}, u32[]{:S(2)}, u32[]{:S(2)}) collective-permute-start(f32[64,128]{1,0:T(8,128)S(1)} %get-tuple-element.19.east), channel_id=1, source_target_pairs={{0,8},{8,16},{16,24},{24,0},{1,9},{9,17},{17,25},{25,1},{2,10},{10... | collective-permute-start | bytes 98312 | tf_op jit(solution)/shard_map/ppermute | solution.py:561
  9.1 3.9 %collective-permute-start = (f32[64,128]{1,0:T(8,128)S(1)}, f32[64,128]{1,0:T(8,128)S(1)}, u32[]{:S(2)}, u32[]{:S(2)}) collective-permute-start(f32[64,128]{1,0:T(8,128)S(1)} %get-tuple-element.20.west), channel_id=1, source_target_pairs={{8,0},{16,8},{24,16},{0,24},{9,1},{17,9},{25,17},{1,25},{10,2},{18... | collective-permute-start | bytes 98312 | tf_op jit(solution)/shard_map/ppermute | solution.py:562
  13.0 2.6 %collective-permute-start.2 = (f32[136,128]{1,0:T(8,128)S(1)}, f32[136,128]{1,0:T(8,128)S(1)}, u32[]{:S(2)}, u32[]{:S(2)}) collective-permute-start(f32[136,128]{1,0:T(8,128)S(1)} %get-tuple-element.23.up), channel_id=1, source_target_pairs={{0,1},{1,2},{2,3},{3,4},{4,5},{5,6},{6,7},{7,31},{31,30},{30,29},{... | collective-permute-start | bytes 208904 | tf_op jit(solution)/shard_map/ppermute | solution.py:580
  14.3 5.0 %collective-permute-start.3 = (f32[136,128]{1,0:T(8,128)S(1)}, f32[136,128]{1,0:T(8,128)S(1)}, u32[]{:S(2)}, u32[]{:S(2)}) collective-permute-start(f32[136,128]{1,0:T(8,128)S(1)} %get-tuple-element.24.down), channel_id=1, source_target_pairs={{1,0},{2,1},{3,2},{4,3},{5,4},{6,5},{7,6},{31,7},{30,31},{29,30},{... | collective-permute-start | bytes 208904 | tf_op jit(solution)/shard_map/ppermute | solution.py:581
  21.4 51.9 %copy-start.3 = (f32[2,16,32,128]{3,2,1,0:T(8,128)S(1)}, f32[2,16,32,128]{3,2,1,0:T(8,128)}, u32[]{:S(2)}) copy-start(f32[2,16,32,128]{3,2,1,0:T(8,128)} %param.7) | copy-start | bytes 1572868
  21.4 58.8 %all-to-all-start = ((f32[32,8,128]{2,1,0:T(8,128)}), f32[32,8,128]{2,1,0:T(8,128)S(1)}, u32[]{:S(2)}, u32[]{:S(2)}) async-start(f32[32,8,128]{2,1,0:T(8,128)} %bitcast.9), calls=%async_computation | async-start | bytes 262144 | tf_op jit(solution)/shard_map/all_to_all | solution.py:609
  28.7 44.6 %copy-start.5 = (s32[32,128]{1,0:T(8,128)S(1)}, s32[32,128]{1,0:T(8,128)}, u32[]{:S(2)}) copy-start(s32[32,128]{1,0:T(8,128)} %mask.5) | copy-start | bytes 49156
  28.7 44.6 %copy-start.7 = (f32[32,128]{1,0:T(8,128)S(1)}, f32[32,128]{1,0:T(8,128)}, u32[]{:S(2)}) copy-start(f32[32,128]{1,0:T(8,128)} %mix.5) | copy-start | bytes 49156

commit v2 on v1

v2 whole, which is shorter than its diff:
```python
import functools
import math

import jax
import jax.numpy as jnp
from jax import lax
from jax.experimental import pallas as pl
from jax.experimental.pallas import tpu as pltpu
from jax.sharding import PartitionSpec as P

ATM_ROWS = 32
CAP = 2

THERMAL = 0.2
HALINE = 0.15
GRAVITY = 0.2
TIMESTEP = 0.8
VERTICAL_MIX = 0.1
VISCOSITY = 0.2
CORIOLIS_MAX = 0.3

LANES = 128
PAD = 8
EXACT = lax.Precision.HIGHEST
F32 = jnp.float32
VMEM_LIMIT = 48 * 1024 * 1024


def iota(shape, dim):
    return lax.broadcasted_iota(jnp.int32, shape, dim)


def dot(a, b, dims=(((1,), (0,)), ((), ()))):
    return lax.dot_general(a, b, dims, precision=EXACT, preferred_element_type=F32)


def is_even(axis):
    return lax.rem(lax.axis_index(axis), 2) == 0


def start_copies(pairs, sems):
    copies = [pltpu.make_async_copy(src, dst, sems.at[i]) for i, (src, dst) in enumerate(pairs)]
    for copy in copies:
        copy.start()
    return copies


def pack_kernel(
    rows, fields, chunks,
    tr_hbm, ve_hbm, mask_hbm, mix_hbm,
    lon_a, lon_b, lat_a, lat_b, state, wet_out, mix,
    tr, ve, mask, sems,
):
    half = fields // 2
    size = half // chunks
    pairs = [(mask_hbm, mask), (mix_hbm, mix)]
    for src, dst in ((tr_hbm, tr), (ve_hbm, ve)):
        for i in range(chunks):
            part = slice(i * size * rows, (i + 1) * size * rows)
            pairs.append((src.at[part], dst.at[part]))
    copies = start_copies(pairs, sems)
    copies[0].wait()
    copies[1].wait()
    wet = mask[...].astype(F32)
    wet_out[...] = wet
    lane = iota((rows, LANES), 1)
    pair = lane >> 1

    def columns(ref, base, carry):
        def body(f, carry):
            to_east, to_west = carry
            x = ref[pl.ds(pl.multiple_of(f * rows, rows), rows), :] * wet
            state[pl.ds(pl.multiple_of((base + f) * rows, 8), rows), :] = x
            keep = pair == base + f
            low = 2 * (base + f)
            to_east = jnp.where(keep, pltpu.roll(x, (low + 2) & (LANES - 1), 1), to_east)
            to_west = jnp.where(keep, pltpu.roll(x, low, 1), to_west)
            return to_east, to_west

        return body

    carry = (jnp.zeros((rows, LANES), F32), jnp.zeros((rows, LANES), F32))
    for n, (ref, base) in enumerate(((tr, 0), (ve, half))):
        for i in range(chunks):
            copies[2 + n * chunks + i].wait()
            carry = lax.fori_loop(
                i * size, (i + 1) * size, columns(ref, base, carry), carry, unroll=8
            )
    to_east, to_west = carry
    mixing = mix[...]
    aux_east = jnp.where(
        lane == 0,
        pltpu.roll(wet, 1, 1),
        jnp.where(lane == 1, pltpu.roll(wet, 3, 1), pltpu.roll(mixing, 3, 1)),
    )
    aux_west = jnp.where(lane <= 1, wet, pltpu.roll(mixing, 2, 1))
    even = is_even("lon")
    lon_a[0:rows, :] = jnp.where(even, to_east, to_west)
    lon_b[0:rows, :] = jnp.where(even, to_west, to_east)
    lon_a[rows : 2 * rows, :] = jnp.where(even, aux_east, aux_west)
    lon_b[rows : 2 * rows, :] = jnp.where(even, aux_west, aux_east)

    even = is_even("lat")
    top, bottom = (rows - 1, rows - 2), (0, 1)
    for buf, first, second in ((lat_a, top, bottom), (lat_b, bottom, top)):
        near = jnp.where(even, first[0], second[0])
        far = jnp.where(even, first[1], second[1])
        for place, line in ((0, near), (fields, far)):
            buf[place : place + fields, :] = state[pl.ds(line, fields, stride=rows), :]
        buf[2 * fields : 2 * fields + 8, :] = jnp.zeros((8, LANES), F32)
        buf[2 * fields : 2 * fields + 1, :] = wet_out[pl.ds(near, 1), :]
        buf[2 * fields + 1 : 2 * fields + 2, :] = wet_out[pl.ds(far, 1), :]
        buf[2 * fields + 2 : 2 * fields + 3, :] = mix[pl.ds(near, 1), :]


def corner_kernel(rows, a_in, b_in, got_a, got_b, a_out, b_out):
    even, even_lon = is_even("lat"), is_even("lon")
    lane = iota((1, LANES), 1)
    for src, dst, first, second in ((a_in, a_out, rows - 1, 0), (b_in, b_out, 0, rows - 1)):
        near = jnp.where(even, first, second)
        dst[...] = src[...]

        def sides(line):
            a, b = got_a[pl.ds(line, 1), :], got_b[pl.ds(line, 1), :]
            return jnp.where(even_lon, a, b), jnp.where(even_lon, b, a)

        east, west = sides(near)
        dst[3:4, :] = jnp.where((lane & 1) == 0, east, west)
        east, west = sides(rows + near)
        dst[4:5, :] = jnp.where(
            lane == 0,
            jnp.broadcast_to(east[:, 0:1], (1, LANES)),
            jnp.broadcast_to(west[:, 0:1], (1, LANES)),
        )


def level_matrix(kind, levels, source, target):
    if kind == "mix":
        above = (source == jnp.maximum(target - 1, 0)).astype(F32)
        below = (source == jnp.minimum(target + 1, levels - 1)).astype(F32)
        return above + below - 2.0 * (source == target).astype(F32)
    full = jnp.where(source < target, 1.0, jnp.where(source == target, 0.5, 0.0))
    return (0.5 * GRAVITY) * full


def density_weight(group):
    return jnp.where(group == 0, -THERMAL, jnp.where(group == 1, HALINE, 0.0)).astype(F32)


def advance_columns(levels, mid, outer, inner, corner_n, corner_s, wets, mixing, coriolis):
    rows = mid.shape[0]
    wet_mid, wet_out, wet_in, wet_corner_n, wet_corner_s = wets
    lane = iota((rows, LANES), 1)
    row = iota((rows, LANES), 0)
    even = (lane & 1) == 0
    group = lane // (2 * levels)

    def sides(outside, inside):
        return jnp.where(even, outside, inside), jnp.where(even, inside, outside)

    def shifted(x, north, south):
        n = jnp.where(row == rows - 1, north, pltpu.roll(x, rows - 1, 0))
        s = jnp.where(row == 0, south, pltpu.roll(x, 1, 0))
        return n, s

    e, w = sides(outer, inner)
    wet_e, wet_w = sides(wet_out, wet_in)
    n, s = shifted(mid, corner_n, corner_s)
    wet_n, wet_s = shifted(wet_mid, wet_corner_n, wet_corner_s)
    lap = wet_e * (e - mid) + wet_w * (w - mid) + wet_n * (n - mid) + wet_s * (s - mid)
    de, dn = e - w, n - s
    span = 2 * levels
    one, two, three = (pltpu.roll(mid, i * span, 1) for i in (1, 2, 3))

    def pick(a, b, c, d):
        return jnp.where(group == 0, a, jnp.where(group == 1, b, jnp.where(group == 2, c, d)))

    u = pick(two, three, mid, one)
    v = pick(one, two, three, mid)
    adv = 0.5 * (u * de + v * dn)
    src, dst = iota((LANES, LANES), 0), iota((LANES, LANES), 1)
    src_group, dst_group = src // span, dst // span
    src_level, dst_level = (src // 2) % levels, (dst // 2) % levels
    same_side = (src & 1) == (dst & 1)
    mix_map = jnp.where(
        same_side & (src_group == dst_group), level_matrix("mix", levels, src_level, dst_level), 0.0
    )
    press = level_matrix("pressure", levels, src_level, dst_level) * density_weight(src_group)
    press_x = jnp.where(same_side & (dst_group == 2), press, 0.0)
    press_y = jnp.where(same_side & (dst_group == 3), press, 0.0)
    vertical = dot(mid, mix_map)
    grad = dot(de, press_x) + dot(dn, press_y)
    zero = jnp.zeros_like(mid)
    turn = pick(zero, zero, coriolis * v, -coriolis * u)
    kappa = jnp.where(group < 2, mixing, VISCOSITY)
    tend = turn - adv - grad + kappa * lap + VERTICAL_MIX * vertical
    return wet_mid * (mid + TIMESTEP * tend)


def advance_row(levels, north_side, mid, outer, inner, corner_e, corner_w, wets, mixing, coriolis):
    fields = mid.shape[0]
    wet_mid, wet_out, wet_in, wet_corner_e, wet_corner_w = wets
    lane = iota((fields, LANES), 1)
    lane8 = iota((8, LANES), 1)

    def sides(x, east, west, at):
        e = jnp.where(at == LANES - 1, east, pltpu.roll(x, LANES - 1, 1))
        w = jnp.where(at == 0, west, pltpu.roll(x, 1, 1))
        return e, w

    e, w = sides(mid, corner_e, corner_w, lane)
    wet_e, wet_w = sides(
        jnp.broadcast_to(wet_mid, (8, LANES)), wet_corner_e, wet_corner_w, lane8
    )
    wet_e, wet_w = wet_e[0:1], wet_w[0:1]
    n, s = (outer, inner) if north_side else (inner, outer)
    wet_n, wet_s = (wet_out, wet_in) if north_side else (wet_in, wet_out)
    lap = wet_e * (e - mid) + wet_w * (w - mid) + wet_n * (n - mid) + wet_s * (s - mid)
    de, dn = e - w, n - s
    u, v = mid[2 * levels : 3 * levels], mid[3 * levels :]
    adv = 0.5 * (jnp.concatenate([u] * 4, axis=0) * de + jnp.concatenate([v] * 4, axis=0) * dn)
    dst, src = iota((fields, fields), 0), iota((fields, fields), 1)
    mix_map = jnp.where(
        dst // levels == src // levels, level_matrix("mix", levels, src % levels, dst % levels), 0.0
    )
    dst, src = iota((levels, fields), 0), iota((levels, fields), 1)
    press = level_matrix("pressure", levels, src % levels, dst) * density_weight(src // levels)
    vertical = dot(mix_map, mid)
    zero = jnp.zeros((2 * levels, LANES), F32)
    turn = jnp.concatenate(
        [zero, coriolis * v - dot(press, de), -coriolis * u - dot(press, dn)], axis=0
    )
    kappa = jnp.concatenate(
        [jnp.broadcast_to(mixing, (2 * levels, LANES)), jnp.full((2 * levels, LANES), VISCOSITY)],
        axis=0,
    )
    tend = turn - adv + kappa * lap + VERTICAL_MIX * vertical
    return wet_mid * (mid + TIMESTEP * tend)


COEFFICIENTS = ("te", "tw", "tn", "ts", "tc", "ve", "vw", "vn", "vs", "vc", "adv", "mix", "turn")


class Halo:
    def __init__(self, rows, fields):
        at = 0
        sizes = [("side0", rows), ("side1", rows)]
        sizes += [(name, fields) for name in ("north0", "south0", "north1", "south1")]
        for name, size in sizes + [(name, rows) for name in COEFFICIENTS]:
            setattr(self, name, slice(at, at + size))
            at += size
        self.size = at


def coefficients(wet, neighbours, mixing, coriolis):
    made = {}
    for name, kappa in (("t", mixing), ("v", VISCOSITY)):
        rest = wet * (1.0 - 2.0 * TIMESTEP * VERTICAL_MIX)
        for side, wet_n in zip("ewns", neighbours):
            made[name + side] = TIMESTEP * kappa * wet * wet_n
            rest = rest - made[name + side]
        made[name + "c"] = rest
    made["adv"] = (0.5 * TIMESTEP) * wet
    made["mix"] = (TIMESTEP * VERTICAL_MIX) * wet
    made["turn"] = TIMESTEP * coriolis * wet
    return made


def advance_level(k, count, levels, rows, src, sides, coef, acc):
    pitch = rows + 2 * PAD
    lane = iota((rows, LANES), 1)
    first, last = lane == 0, lane == LANES - 1
    above_k = jnp.maximum(k - 1, 0)
    below_k = jnp.minimum(k + 1, levels - 1)

    def load(q, level, shift):
        return src[pl.ds((q * count + level) * pitch + PAD + shift, rows), :]

    def base(q):
        return pl.multiple_of((q * count + k) * pitch + PAD, 8)

    center = [load(q, k, 0) for q in range(4)]
    u, v = coef("adv") * center[2], coef("adv") * center[3]
    sums, de, dn = [], [], []
    for q in range(4):
        c = center[q]
        n, s = load(q, k, 1), load(q, k, -1)
        edge = pltpu.roll(sides, (LANES - 1 - 2 * (q * levels + k)) & (LANES - 1), 1)
        e = jnp.where(last, edge, pltpu.roll(c, LANES - 1, 1))
        w = jnp.where(first, edge, pltpu.roll(c, 1, 1))
        kind = "t" if q < 2 else "v"
        lap = coef(kind + "c") * c + coef(kind + "e") * e + coef(kind + "w") * w
        lap = lap + coef(kind + "n") * n + coef(kind + "s") * s
        de.append(e - w)
        dn.append(n - s)
        sums.append(lap - (u * de[q] + v * dn[q]))
    scale = 0.5 * GRAVITY / VERTICAL_MIX
    dens_x = (scale * HALINE) * de[1] - (scale * THERMAL) * de[0]
    dens_y = (scale * HALINE) * dn[1] - (scale * THERMAL) * dn[0]
    acc_x, acc_y = acc
    grad = (None, None, acc_x + 0.5 * dens_x, acc_y + 0.5 * dens_y)
    turn = (None, None, coef("turn") * center[3], -coef("turn") * center[2])
    new = []
    for q in range(4):
        vertical = load(q, above_k, 0) + load(q, below_k, 0)
        if grad[q] is not None:
            vertical = vertical - grad[q]
        total = sums[q] + coef("mix") * vertical
        new.append(total if turn[q] is None else total + turn[q])
    return new, (acc_x + dens_x, acc_y + dens_y)


def surface_kernel(
    rows, levels, lat_count, devices,
    state, wet_in, mix_in, lon_a, lon_b, got_lon_a, got_lon_b, lat_a, lat_b, got_lat_a, got_lat_b,
    own, atm_row,
    halo, out, now, later, wet_pad, stage, used,
):
    fields = 4 * levels
    pitch = rows + 2 * PAD
    at = Halo(rows, fields)
    lat = lax.axis_index("lat")
    even_lat, even_lon = is_even("lat"), is_even("lon")
    fold = lat == lat_count - 1
    wet = wet_in[...]
    mixing = mix_in[...]
    lane = iota((rows, LANES), 1)
    even = (lane & 1) == 0

    def ordered(flag, a, b):
        return jnp.where(flag, a, b), jnp.where(flag, b, a)

    slot_rows = out.shape[0] // (devices * CAP)

    def clear(d, carry):
        used[d] = 0
        return carry

    lax.fori_loop(0, devices, clear, 0, unroll=8)
    out[...] = jnp.zeros(out.shape, F32)
    stage[...] = jnp.zeros(stage.shape, F32)
    stage[pl.ds(4, rows, stride=slot_rows), :] = wet
    for r in range(rows):
        line = jnp.full((1, LANES), atm_row[r], jnp.int32)
        stage[r * slot_rows + 5 : r * slot_rows + 6, :] = line.astype(F32)

    latitude = lat * rows - PAD + iota((rows + 2 * PAD, LANES), 0)
    total = lat_count * rows
    latitude = jnp.where(latitude >= total, 2 * total - 1 - latitude, latitude).astype(F32)
    table = CORIOLIS_MAX * jnp.sin(math.pi * (-0.43 + 0.93 * (latitude + 0.5) / total))
    coriolis = table[PAD : PAD + rows]

    north, south = ordered(even_lat, got_lat_a[...], got_lat_b[...])
    length = 2 * fields + 8
    back = LANES - 1 - iota((8, LANES), 1)
    flipped = jnp.concatenate(
        [
            jnp.take_along_axis(north[i : i + 8], back, axis=1)
            * (-1.0 if i < 2 * fields and i % fields >= fields // 2 else 1.0)
            for i in range(0, length, 8)
        ],
        axis=0,
    )
    straight = north
    north = jnp.where(fold, flipped, straight)
    lane1 = iota((1, LANES), 1)
    even1 = (lane1 & 1) == 0
    tail_n, tail_s = straight[2 * fields :], south[2 * fields :]
    swapped = jnp.where(
        iota((8, LANES), 1) & 1 == 0, pltpu.roll(tail_n, LANES - 1, 1), pltpu.roll(tail_n, 1, 1)
    )
    sign = jnp.where(lane1 >= LANES // 2, -1.0, 1.0)
    corner_n = jnp.where(fold, swapped[3:4] * sign, tail_n[3:4])
    corner_s = tail_s[3:4]
    wet_corner_n = jnp.where(fold, swapped[4:5], tail_n[4:5])
    wet_corner_s = tail_s[4:5]

    def corner_wet(x):
        east_wet = jnp.broadcast_to(x[:, 0:1], (1, LANES))
        west_wet = jnp.broadcast_to(x[:, 1:2], (1, LANES))
        return east_wet, west_wet, jnp.where(even1, east_wet, west_wet)

    wet_ne, wet_nw, wet_n_lanes = corner_wet(wet_corner_n)
    wet_se, wet_sw, wet_s_lanes = corner_wet(wet_corner_s)

    north_rows = (north[0:fields], north[fields : 2 * fields], north[2 * fields :])
    south_rows = (south[0:fields], south[fields : 2 * fields], south[2 * fields :])
    halo[at.north0] = north_rows[0]
    halo[at.south0] = south_rows[0]

    wet_pad[PAD : PAD + rows, :] = wet
    wet_pad[PAD - 1 : PAD, :] = south_rows[2][0:1]
    wet_pad[PAD + rows : PAD + rows + 1, :] = north_rows[2][0:1]
    wet_n = wet_pad[PAD + 1 : PAD + 1 + rows, :]
    wet_s = wet_pad[PAD - 1 : PAD - 1 + rows, :]

    def spread(x, i):
        return jnp.broadcast_to(x[:, i : i + 1], (rows, LANES))

    aux_e, aux_w = ordered(even_lon, got_lon_a[rows:, :], got_lon_b[rows:, :])
    wet_col_e, wet_col_w = spread(aux_e, 0), spread(aux_w, 0)
    wet_e = jnp.where(lane == LANES - 1, wet_col_e, pltpu.roll(wet, LANES - 1, 1))
    wet_w = jnp.where(lane == 0, wet_col_w, pltpu.roll(wet, 1, 1))
    made = coefficients(wet, (wet_e, wet_w, wet_n, wet_s), mixing, coriolis)
    for name in COEFFICIENTS:
        halo[getattr(at, name)] = made[name]

    def coef(name):
        return halo[getattr(at, name)]

    got_e, got_w = ordered(even_lon, got_lon_a[0:rows, :], got_lon_b[0:rows, :])
    sent_e, sent_w = ordered(even_lon, lon_a[0:rows, :], lon_b[0:rows, :])
    side = jnp.where(even, got_e, got_w)
    outer = jnp.where(even, pltpu.roll(got_e, LANES - 1, 1), pltpu.roll(got_w, 1, 1))
    inner = jnp.where(even, pltpu.roll(sent_e, LANES - 1, 1), pltpu.roll(sent_w, 1, 1))
    halo[at.side0] = side
    halo[at.side1] = advance_columns(
        levels, side, outer, inner, corner_n, corner_s,
        (
            jnp.where(even, wet_col_e, wet_col_w),
            jnp.where(even, spread(aux_e, 1), spread(aux_w, 1)),
            jnp.where(even, spread(wet, LANES - 1), spread(wet, 0)),
            wet_n_lanes,
            wet_s_lanes,
        ),
        jnp.where(even, spread(aux_e, 2), spread(aux_w, 2)),
        coriolis,
    )

    field_lane = iota((fields, LANES), 1)
    field_id = iota((fields, LANES), 0)

    def to_sublanes(x, parity):
        here = field_lane == 2 * field_id + parity
        return jnp.sum(jnp.where(here, x, 0.0), axis=1, keepdims=True)

    inside_n, inside_s = ordered(even_lat, lat_a[0:fields, :], lat_b[0:fields, :])
    for north_side, (mid, outside, tail), inside, corner, corner_wets, line, lat_row, place in (
        (True, north_rows, inside_n, corner_n, (wet_ne, wet_nw), rows - 1, PAD + rows, at.north1),
        (False, south_rows, inside_s, corner_s, (wet_se, wet_sw), 0, PAD - 1, at.south1),
    ):
        halo[place] = advance_row(
            levels, north_side, mid, outside, inside,
            to_sublanes(corner, 0), to_sublanes(corner, 1),
            (tail[0:1], tail[1:2], wet[line : line + 1], *corner_wets),
            tail[2:3], table[lat_row : lat_row + 1],
        )

    count = now.shape[0] // (4 * pitch)

    def put(buf, q, k, value, north, south):
        base = (q * count + k) * pitch + PAD
        n, s = north.start + q * levels + k, south.start + q * levels + k
        buf[base : base + rows, :] = value
        buf[base + rows : base + rows + 1, :] = halo[n : n + 1, :]
        buf[base - 1 : base, :] = halo[s : s + 1, :]

    for q in range(4):
        for k in range(count):
            field = (q * levels + k) * rows
            put(now, q, k, state[field : field + rows, :], at.north0, at.south0)
    none = jnp.zeros((rows, LANES), F32)
    acc = (none, none)
    for k in range(count - 1):
        new, acc = advance_level(k, count, levels, rows, now, halo[at.side0], coef, acc)
        for q in range(4):
            put(later, q, k, new[q], at.north1, at.south1)
    new, _ = advance_level(0, count, levels, rows, later, halo[at.side1], coef, (none, none))
    for q in range(4):
        stage[pl.ds(q, rows, stride=slot_rows), :] = new[q]
    for r in range(rows):
        owner = own[r]
        slot = used[owner]
        used[owner] = slot + 1
        place = pl.multiple_of((owner * CAP + slot) * slot_rows, 8)
        out[pl.ds(place, slot_rows), :] = stage[r * slot_rows : (r + 1) * slot_rows, :]


def main_kernel(
    rows, levels, chunks, state, halo, tr_hbm, ve_hbm, now, later, tr_out, ve_out, sems
):
    fields = 4 * levels
    pitch = rows + 2 * PAD
    at = Halo(rows, fields)
    for buf, north, south in ((now, at.north0, at.south0), (later, at.north1, at.south1)):
        buf[pl.ds(PAD - 1, fields, stride=pitch), :] = halo[south]
        buf[pl.ds(PAD + rows, fields, stride=pitch), :] = halo[north]

    def fill(f, carry):
        x = state[pl.ds(pl.multiple_of(f * rows, 8), rows), :]
        now[pl.ds(pl.multiple_of(f * pitch + PAD, 8), rows), :] = x
        return carry

    lax.fori_loop(0, fields, fill, 0, unroll=8)

    def coef(name):
        return halo[getattr(at, name)]

    def first(k, acc):
        new, acc = advance_level(k, levels, levels, rows, now, halo[at.side0], coef, acc)
        for q in range(4):
            place = pl.multiple_of((q * levels + k) * pitch + PAD, 8)
            later[pl.ds(place, rows), :] = new[q]
        return acc

    def second(k, acc):
        new, acc = advance_level(k, levels, levels, rows, later, halo[at.side1], coef, acc)
        for q in range(4):
            ref = tr_out if q < 2 else ve_out
            place = pl.multiple_of(((q % 2) * levels + k) * rows, 8)
            ref[pl.ds(place, rows), :] = new[q]
        return acc

    none = jnp.zeros((rows, LANES), F32)
    lax.fori_loop(0, levels, first, (none, none), unroll=2)
    acc = (none, none)
    size = levels // chunks
    copies = []
    for i in range(chunks):
        acc = lax.fori_loop(i * size, (i + 1) * size, second, acc, unroll=2)
        for src, dst in ((tr_out, tr_hbm), (ve_out, ve_hbm)):
            for q in range(2):
                start = (q * levels + i * size) * rows
                part = slice(start, start + size * rows)
                copy = pltpu.make_async_copy(src.at[part], dst.at[part], sems.at[len(copies)])
                copy.start()
                copies.append(copy)
    for copy in copies:
        copy.wait()


def reduce_kernel(devices, data, surface, cover):
    slot_rows = data.shape[0] // (devices * CAP)
    slots = devices * CAP
    lines = data[pl.ds(5, slots, stride=slot_rows), :]
    to_rows = (lines == iota((slots, LANES), 1).astype(F32)).astype(F32)
    values = [data[pl.ds(q, slots, stride=slot_rows), :] for q in range(5)]
    totals = dot(to_rows, jnp.concatenate(values, axis=1), (((0,), (0,)), ((), ())))
    totals = totals[0:ATM_ROWS]
    ocean = totals[:, 4 * LANES :]
    cover[...] = ocean
    share = jnp.maximum(ocean, 1.0)
    for q in range(4):
        surface[q] = totals[:, q * LANES : (q + 1) * LANES] / share


def call(kernel, out_shape, **kwargs):
    return pl.pallas_call(
        kernel,
        out_shape=out_shape,
        compiler_params=pltpu.CompilerParams(vmem_limit_bytes=VMEM_LIMIT),
        **kwargs,
    )


def shaped(*shape, dtype=F32):
    return jax.ShapeDtypeStruct(shape, dtype)


def pairs_of(lon_count, lat_count):
    lon_a = [(i, i ^ 1) for i in range(lon_count)]
    lon_b = [(i, (i + 1 if i % 2 else i - 1) % lon_count) for i in range(lon_count)]
    lat_a, lat_b = [], []
    for i in range(lon_count):
        for a in range(lat_count):
            here = i * lat_count + a
            lat_a.append((here, i * lat_count + (a ^ 1)))
            if a == lat_count - 1:
                lat_b.append((here, (lon_count - 1 - i) * lat_count + a))
            elif a > 0:
                lat_b.append((here, here + 1 if a % 2 else here - 1))
    return lon_a, lon_b, lat_a, lat_b


def local(tracers, velocity, land_mask, mixing, owners, atm_row):
    levels = tracers.shape[1]
    rows, cols = land_mask.shape
    fields = 4 * levels
    lon_count, lat_count = lax.axis_size("lon"), lax.axis_size("lat")
    devices = lon_count * lat_count
    assert cols == LANES and rows % 8 == 0 and 2 * fields == LANES
    assert lon_count % 2 == 0 and lat_count % 2 == 0
    length = 2 * fields + 8
    pitch = rows + 2 * PAD
    flat = 2 * levels * rows
    hbm = pl.BlockSpec(memory_space=pltpu.HBM)
    smem = pl.BlockSpec(memory_space=pltpu.SMEM)
    vmem = pl.BlockSpec(memory_space=pltpu.VMEM)

    chunks = 2
    lon_a, lon_b, lat_a, lat_b, state, wet, mix = call(
        functools.partial(pack_kernel, rows, fields, chunks),
        [shaped(2 * rows, cols)] * 2
        + [shaped(length, cols)] * 2
        + [shaped(fields * rows, cols), shaped(rows, cols), shaped(rows, cols)],
        in_specs=[hbm] * 4,
        scratch_shapes=[
            pltpu.VMEM((flat, cols), F32),
            pltpu.VMEM((flat, cols), F32),
            pltpu.VMEM((rows, cols), jnp.int32),
            pltpu.SemaphoreType.DMA((2 + 2 * chunks,)),
        ],
    )(tracers.reshape(flat, cols), velocity.reshape(flat, cols), land_mask, mixing)

    swaps = pairs_of(lon_count, lat_count)
    got_lon_a = lax.ppermute(lon_a, "lon", swaps[0])
    got_lon_b = lax.ppermute(lon_b, "lon", swaps[1])

    tail = pl.BlockSpec((8, cols), lambda i: (length // 8 - 1, 0))
    whole = pl.BlockSpec((2 * rows, cols), lambda i: (0, 0))
    lat_a, lat_b = call(
        functools.partial(corner_kernel, rows),
        [shaped(length, cols), shaped(length, cols)],
        grid=(1,),
        in_specs=[tail, tail, whole, whole],
        out_specs=[tail, tail],
        input_output_aliases={0: 0, 1: 1},
    )(lat_a, lat_b, got_lon_a, got_lon_b)
    got_lat_a = lax.ppermute(lat_a, ("lon", "lat"), swaps[2])
    got_lat_b = lax.ppermute(lat_b, ("lon", "lat"), swaps[3])

    at = Halo(rows, fields)
    slot_rows = 8
    count = min(3, levels)
    halo, outgoing = call(
        functools.partial(surface_kernel, rows, levels, lat_count, devices),
        [shaped(at.size, cols), shaped(devices * CAP * slot_rows, cols)],
        in_specs=[vmem] * 11 + [smem] * 2,
        scratch_shapes=[
            pltpu.VMEM((4 * count * pitch, cols), F32),
            pltpu.VMEM((4 * count * pitch, cols), F32),
            pltpu.VMEM((pitch, cols), F32),
            pltpu.VMEM((rows * slot_rows, cols), F32),
            pltpu.SMEM((devices,), jnp.int32),
        ],
    )(state, wet, mix, lon_a, lon_b, got_lon_a, got_lon_b, lat_a, lat_b, got_lat_a, got_lat_b,
      owners.reshape(rows), atm_row)
    incoming = lax.all_to_all(
        outgoing.reshape(devices, CAP * slot_rows, cols), ("lon", "lat"), 0, 0, tiled=True
    )

    chunks = 4
    tr_out, ve_out = call(
        functools.partial(main_kernel, rows, levels, chunks),
        [shaped(flat, cols), shaped(flat, cols)],
        in_specs=[vmem] * 2,
        out_specs=[hbm] * 2,
        scratch_shapes=[
            pltpu.VMEM((fields * pitch, cols), F32),
            pltpu.VMEM((fields * pitch, cols), F32),
            pltpu.VMEM((flat, cols), F32),
            pltpu.VMEM((flat, cols), F32),
            pltpu.SemaphoreType.DMA((4 * chunks,)),
        ],
        cost_estimate=pl.CostEstimate(
            flops=80 * fields * rows * cols, bytes_accessed=5 << 20, transcendentals=0
        ),
    )(state, halo)
    surface, cover = call(
        functools.partial(reduce_kernel, devices),
        [shaped(4, ATM_ROWS, cols), shaped(ATM_ROWS, cols)],
    )(incoming.reshape(devices * CAP * slot_rows, cols))
    shape = (2, levels, rows, cols)
    return tr_out.reshape(shape), ve_out.reshape(shape), surface, cover


def solution(mesh):
    in_specs = (
        P(None, None, "lat", "lon"),
        P(None, None, "lat", "lon"),
        P("lat", "lon"),
        P("lat", "lon"),
        P(("lon", "lat"), None),
        P(("lon", "lat")),
    )
    out_specs = (
        P(None, None, "lat", "lon"),
        P(None, None, "lat", "lon"),
        P(None, ("lon", "lat"), None),
        P(("lon", "lat"), None),
    )
    return jax.shard_map(local, mesh=mesh, in_specs=in_specs, out_specs=out_specs, check_vma=False)
```

time: 81.8 us -> 39.2 us (0.48)
  blocking collectives: 44.5 us -> 0 us
  waiting for transfers between devices: 6.55 us -> 10.3 us
  Pallas kernels: 11.4 us -> 8.78 us
  starting transfers between devices: 13.9 us -> 14.9 us
    all_gather x1 -> x0, blocking collectives: 44.5 us -> none  [local(): info = lax.all_gather(info, ('lon', 'lat'), axis=0, tiled=True)]
    all_to_all x1, waiting for transfers between devices: 0.01 us -> 6.38 us  [local(): lax.all_to_all(outgoing.reshape(devices, CAP * slot_rows, cols), ('lon',...]
    ppermute x4, waiting for transfers between devices: 6.55 us -> 3.9 us  [the longest x1 2.92 us: local(): got_lon_b = lax.ppermute(lon_b, 'lon', swaps[1])]
    pallas_call x3, Pallas kernels: 10.1 us -> 7.6 us  [the longest x1 4 us: local(): call(functools.partial(main_kernel, rows, levels, chunks), [shaped(flat,...]
    all_to_all x1, starting transfers between devices: 7.36 us -> 9.71 us  [local(): lax.all_to_all(outgoing.reshape(devices, CAP * slot_rows, cols), ('lon',...]
    ppermute x4, starting transfers between devices: 6.59 us -> 5.17 us  [the longest x1 3 us: local(): got_lon_a = lax.ppermute(lon_a, 'lon', swaps[0])]
    unnamed x20 -> x12, local copies, waits for them, and re-layouts: 4.19 us -> 4.18 us
  transfers between devices with their start and end apart: 5 -> 5, of which waited for: 3 -> 4; matrix products, arithmetic and copies ran while one was open for 0% -> 0% of each run, Pallas kernels for 8% -> 10%
where the time goes in v2:
time: 39.2 us; the launch traced here: 38.8 us
  starting transfers between devices  14.9 us (38%)
  waiting for transfers between devices  10.3 us (26%)
  Pallas kernels  8.78 us (22%)
  local copies, waits for them, and re-layouts  4.18 us (11%)
  between operations  0.69 us (2%)
    all_to_all x1, starting transfers between devices, local(): lax.all_to_all(outgoing.reshape(devices, CAP * slot_rows, cols), ('lon',...  9.71 us
    all_to_all x1, waiting for transfers between devices, local(): lax.all_to_all(outgoing.reshape(devices, CAP * slot_rows, cols), ('lon',...  6.38 us
    unnamed x12, local copies, waits for them, and re-layouts  4.18 us
    pallas_call x1, Pallas kernels, local(): call(functools.partial(main_kernel, rows, levels, chunks), [shaped(flat,...  4 us
    ppermute x1, starting transfers between devices, local(): got_lon_a = lax.ppermute(lon_a, 'lon', swaps[0])  3 us
    ppermute x1, waiting for transfers between devices, local(): got_lon_b = lax.ppermute(lon_b, 'lon', swaps[1])  2.92 us
    pallas_call x1, Pallas kernels, local(): call(functools.partial(surface_kernel, rows, levels, lat_count, devices),...  2.21 us
    ppermute x1, starting transfers between devices, local(): got_lon_b = lax.ppermute(lon_b, 'lon', swaps[1])  1.49 us
  transfers between devices with their start and end apart: 5, of which 4 were waited for; matrix products, arithmetic and copies ran while one was open for 0% of the time, Pallas kernels for 10%

profile of v2, /device:TPU:0, one launch (start us, length us, event | category | flops | bytes accessed | tf_op | source)
XLA Modules:
  0.0 38.8 jit_solution(476807074362235907)
XLA Ops:
  0.6 0.0 copy-start
  0.6 1.0 %copy-done = f32[2,16,32,128]{3,2,1,0:T(8,128)S(1)} copy-done((f32[2,16,32,128]{3,2,1,0:T(8,128)S(1)}, f32[2,16,32,128]{3,2,1,0:T(8,128)}, u32[]{:S(2)}) %copy-start) | copy-done | bytes 524312
  1.7 0.0 copy-start.1
  1.7 1.0 %copy-done.1 = f32[2,16,32,128]{3,2,1,0:T(8,128)S(1)} copy-done((f32[2,16,32,128]{3,2,1,0:T(8,128)S(1)}, f32[2,16,32,128]{3,2,1,0:T(8,128)}, u32[]{:S(2)}) %copy-start.1) | copy-done | bytes 524312
  2.7 0.0 copy-start.2
  2.7 0.7 %copy-done.2 = s32[32,128]{1,0:T(8,128)S(1)} copy-done((s32[32,128]{1,0:T(8,128)S(1)}, s32[32,128]{1,0:T(8,128)}, u32[]{:S(2)}) %copy-start.2) | copy-done | bytes 16408
  3.4 0.0 copy-start.3
  3.4 0.7 %copy-done.3 = f32[32,128]{1,0:T(8,128)S(1)} copy-done((f32[32,128]{1,0:T(8,128)S(1)}, f32[32,128]{1,0:T(8,128)}, u32[]{:S(2)}) %copy-start.3) | copy-done | bytes 16408
  4.2 1.4 %shard_map.93 = (f32[64,128]{1,0:T(8,128)S(1)}, f32[64,128]{1,0:T(8,128)S(1)}, f32[136,128]{1,0:T(8,128)S(1)}, f32[136,128]{1,0:T(8,128)S(1)}, f32[2048,128]{1,0...) custom-call(f32[1024,128]{1,0:T(8,128)S(1)} %bitcast.8, f32[1024,128]{1,0:T(8,128)S(1)} %bitcast.9, ...), custom_call_target="tpu_custom_call" | custom-call | tf_op jit(solution)/shard_map/pallas_call | solution.py:591
  5.6 3.0 %collective-permute-start = (f32[64,128]{1,0:T(8,128)S(1)}, f32[64,128]{1,0:T(8,128)S(1)}, u32[]{:S(2)}, u32[]{:S(2)}) collective-permute-start(f32[64,128]{1,0:T(8,128)S(1)} %get-tuple-element.22.lon_a), channel_id=1, source_target_pairs={{0,8},{8,0},{16,24},{24,16},{1,9},{9,1},{17,25},{25,17},{2,10},{10... | collective-permute-start | bytes 98312 | tf_op jit(solution)/shard_map/ppermute | solution.py:606
  8.6 1.5 %collective-permute-start.1 = (f32[64,128]{1,0:T(8,128)S(1)}, f32[64,128]{1,0:T(8,128)S(1)}, u32[]{:S(2)}, u32[]{:S(2)}) collective-permute-start(f32[64,128]{1,0:T(8,128)S(1)} %get-tuple-element.23.lon_b), channel_id=1, source_target_pairs={{0,24},{8,16},{16,8},{24,0},{1,25},{9,17},{17,9},{25,1},{2,26},{10... | collective-permute-start | bytes 98312 | tf_op jit(solution)/shard_map/ppermute | solution.py:607
  10.1 0.4 %collective-permute-done.got_a.got_lon_a = f32[64,128]{1,0:T(8,128)S(1)} collective-permute-done((f32[64,128]{1,0:T(8,128)S(1)}, f32[64,128]{1,0:T(8,128)S(1)}, u32[]{:S(2)}, u32[]{:S(2)}) %collective-permute-start) | collective-permute-done | bytes 32800 | tf_op jit(solution)/shard_map/ppermute | solution.py:606
  10.5 2.9 %collective-permute-done.1.got_b.got_lon_b = f32[64,128]{1,0:T(8,128)S(1)} collective-permute-done((f32[64,128]{1,0:T(8,128)S(1)}, f32[64,128]{1,0:T(8,128)S(1)}, u32[]{:S(2)}, u32[]{:S(2)}) %collective-permute-start.1) | collective-permute-done | bytes 32800 | tf_op jit(solution)/shard_map/ppermute | solution.py:607
  13.4 0.1 shard_map.94
  13.5 0.0 collective-permute-start.2
  13.5 0.7 %collective-permute-start.3 = (f32[136,128]{1,0:T(8,128)S(1)}, f32[136,128]{1,0:T(8,128)S(1)}, u32[]{:S(2)}, u32[]{:S(2)}) collective-permute-start(f32[136,128]{1,0:T(8,128)S(1)} %get-tuple-element.27.lat_b), channel_id=1, source_target_pairs={{1,2},{2,1},{3,4},{4,3},{5,6},{6,5},{7,31},{9,10},{10,9},{11,12},{... | collective-permute-start | bytes 208904 | tf_op jit(solution)/shard_map/ppermute | solution.py:620
  14.1 0.6 %collective-permute-done.2.got_lat_a = f32[136,128]{1,0:T(8,128)S(1)} collective-permute-done((f32[136,128]{1,0:T(8,128)S(1)}, f32[136,128]{1,0:T(8,128)S(1)}, u32[]{:S(2)}, u32[]{:S(2)}) %collective-permute-start.2) | collective-permute-done | bytes 69664 | tf_op jit(solution)/shard_map/ppermute | solution.py:619
  14.7 0.0 collective-permute-done.3.got_lat_b
  14.7 0.0 copy-start.4
  14.7 0.0 copy-start.5
  14.7 0.7 %copy-done.4 = s32[32,1]{0,1:T(1,128)S(1)} copy-done((s32[32,1]{0,1:T(1,128)S(1)}, s32[32,1]{0,1:T(1,128)}, u32[]{:S(2)}) %copy-start.4) | copy-done | bytes 152
  15.4 0.0 copy-done.5
  15.4 2.2 %shard_map.95 = (f32[736,128]{1,0:T(8,128)S(1)}, f32[512,128]{1,0:T(8,128)}) custom-call(f32[2048,128]{1,0:T(8,128)S(1)} %get-tuple-element.19.state, f32[32,128]{1,0:T(8,128)S(1)} %get-tuple-element.20.wet_in, f32[32,128]{1,0:T(8,128)S(1)} %get-tuple-element.21.mix_in, f32[64,128]{1,0:T(8,128)S(1)} %get-tuple-element.22.lon_a, ...), custom_call_target="tpu_custom_call" | custom-call | tf_op jit(solution)/shard_map/pallas_call | solution.py:625
  17.6 9.7 %all-to-all-start = ((f32[32,16,128]{2,1,0:T(8,128)}), f32[32,16,128]{2,1,0:T(8,128)S(1)}, u32[]{:S(2)}, u32[]{:S(2)}) async-start(f32[32,16,128]{2,1,0:T(8,128)} %bitcast.5), calls=%async_computation | async-start | bytes 524288 | tf_op jit(solution)/shard_map/all_to_all | solution.py:638
  27.3 4.0 %shard_map.96 = (f32[1024,128]{1,0:T(8,128)}, f32[1024,128]{1,0:T(8,128)}) custom-call(f32[2048,128]{1,0:T(8,128)S(1)} %get-tuple-element.19.state, f32[736,128]{1,0:T(8,128)S(1)} %get-tuple-element.28.halo), custom_call_target="tpu_custom_call" | custom-call | flops 20971520 | bytes 5242880 | tf_op jit(solution)/shard_map/pallas_call | solution.py:643
  31.3 6.4 %all-to-all-done = f32[32,16,128]{2,1,0:T(8,128)S(1)} async-done(((f32[32,16,128]{2,1,0:T(8,128)}), f32[32,16,128]{2,1,0:T(8,128)S(1)}, u32[]{:S(2)}, u32[]{:S(2)}) %all-to-all-start) | async-done | bytes 262176 | tf_op jit(solution)/shard_map/all_to_all | solution.py:638
  37.7 1.1 %shard_map.97 = (f32[4,32,128]{2,1,0:T(8,128)}, f32[32,128]{1,0:T(8,128)}) custom-call(f32[512,128]{1,0:T(8,128)S(1)} %bitcast.7), custom_call_target="tpu_custom_call" | custom-call | tf_op jit(solution)/shard_map/pallas_call | solution.py:659
Async XLA Ops:
  0.6 1.0 %copy-start = (f32[2,16,32,128]{3,2,1,0:T(8,128)S(1)}, f32[2,16,32,128]{3,2,1,0:T(8,128)}, u32[]{:S(2)}) copy-start(f32[2,16,32,128]{3,2,1,0:T(8,128)} %param.6) | copy-start | bytes 1572868
  1.7 1.0 %copy-start.1 = (f32[2,16,32,128]{3,2,1,0:T(8,128)S(1)}, f32[2,16,32,128]{3,2,1,0:T(8,128)}, u32[]{:S(2)}) copy-start(f32[2,16,32,128]{3,2,1,0:T(8,128)} %param.7) | copy-start | bytes 1572868
  2.7 0.7 %copy-start.2 = (s32[32,128]{1,0:T(8,128)S(1)}, s32[32,128]{1,0:T(8,128)}, u32[]{:S(2)}) copy-start(s32[32,128]{1,0:T(8,128)} %mask_hbm.1) | copy-start | bytes 49156
  3.4 0.7 %copy-start.3 = (f32[32,128]{1,0:T(8,128)S(1)}, f32[32,128]{1,0:T(8,128)}, u32[]{:S(2)}) copy-start(f32[32,128]{1,0:T(8,128)} %mix_hbm.1) | copy-start | bytes 49156
  5.6 4.9 %collective-permute-start = (f32[64,128]{1,0:T(8,128)S(1)}, f32[64,128]{1,0:T(8,128)S(1)}, u32[]{:S(2)}, u32[]{:S(2)}) collective-permute-start(f32[64,128]{1,0:T(8,128)S(1)} %get-tuple-element.22.lon_a), channel_id=1, source_target_pairs={{0,8},{8,0},{16,24},{24,16},{1,9},{9,1},{17,25},{25,17},{2,10},{10... | collective-permute-start | bytes 98312 | tf_op jit(solution)/shard_map/ppermute | solution.py:606
  8.6 4.8 %collective-permute-start.1 = (f32[64,128]{1,0:T(8,128)S(1)}, f32[64,128]{1,0:T(8,128)S(1)}, u32[]{:S(2)}, u32[]{:S(2)}) collective-permute-start(f32[64,128]{1,0:T(8,128)S(1)} %get-tuple-element.23.lon_b), channel_id=1, source_target_pairs={{0,24},{8,16},{16,8},{24,0},{1,25},{9,17},{17,9},{25,1},{2,26},{10... | collective-permute-start | bytes 98312 | tf_op jit(solution)/shard_map/ppermute | solution.py:607
  13.5 1.3 %collective-permute-start.2 = (f32[136,128]{1,0:T(8,128)S(1)}, f32[136,128]{1,0:T(8,128)S(1)}, u32[]{:S(2)}, u32[]{:S(2)}) collective-permute-start(f32[136,128]{1,0:T(8,128)S(1)} %get-tuple-element.26.lat_a), channel_id=1, source_target_pairs={{0,1},{1,0},{2,3},{3,2},{4,5},{5,4},{6,7},{7,6},{8,9},{9,8},{10,11... | collective-permute-start | bytes 208904 | tf_op jit(solution)/shard_map/ppermute | solution.py:619
  13.5 1.2 %collective-permute-start.3 = (f32[136,128]{1,0:T(8,128)S(1)}, f32[136,128]{1,0:T(8,128)S(1)}, u32[]{:S(2)}, u32[]{:S(2)}) collective-permute-start(f32[136,128]{1,0:T(8,128)S(1)} %get-tuple-element.27.lat_b), channel_id=1, source_target_pairs={{1,2},{2,1},{3,4},{4,3},{5,6},{6,5},{7,31},{9,10},{10,9},{11,12},{... | collective-permute-start | bytes 208904 | tf_op jit(solution)/shard_map/ppermute | solution.py:620
  14.7 0.7 %copy-start.4 = (s32[32,1]{0,1:T(1,128)S(1)}, s32[32,1]{0,1:T(1,128)}, u32[]{:S(2)}) copy-start(s32[32,1]{0,1:T(1,128)} %param.10) | copy-start | bytes 388
  14.7 0.7 %copy-start.5 = (s32[32]{0:T(128)S(1)}, s32[32]{0:T(128)}, u32[]{:S(2)}) copy-start(s32[32]{0:T(128)} %atm_row.1) | copy-start | bytes 388
  17.6 20.1 %all-to-all-start = ((f32[32,16,128]{2,1,0:T(8,128)}), f32[32,16,128]{2,1,0:T(8,128)S(1)}, u32[]{:S(2)}, u32[]{:S(2)}) async-start(f32[32,16,128]{2,1,0:T(8,128)} %bitcast.5), calls=%async_computation | async-start | bytes 524288 | tf_op jit(solution)/shard_map/all_to_all | solution.py:638

commit v3 on v2

--- a/solution.py
+++ b/solution.py
@@ -23,7 +23,8 @@
 PAD = 8
 EXACT = lax.Precision.HIGHEST
 F32 = jnp.float32
-VMEM_LIMIT = 48 * 1024 * 1024
+VMEM_LIMIT = 32 * 1024 * 1024
+VMEM_ALL = 63 * 1024 * 1024
 
 
 def iota(shape, dim):
@@ -46,10 +47,7 @@
 
 
 def pack_kernel(
-    rows, fields, chunks,
-    tr_hbm, ve_hbm, mask_hbm, mix_hbm,
-    lon_a, lon_b, lat_a, lat_b, state, wet_out, mix,
-    tr, ve, mask, sems,
+    rows, fields, chunks, tr_hbm, ve_hbm, mask_hbm, mix_hbm, lon_a, lon_b, tr, ve, mask, mix, sems
 ):
     half = fields // 2
     size = half // chunks
@@ -62,15 +60,13 @@
     copies[0].wait()
     copies[1].wait()
     wet = mask[...].astype(F32)
-    wet_out[...] = wet
     lane = iota((rows, LANES), 1)
     pair = lane >> 1
 
-    def columns(ref, base, carry):
+    def columns(ref, base):
         def body(f, carry):
             to_east, to_west = carry
-            x = ref[pl.ds(pl.multiple_of(f * rows, rows), rows), :] * wet
-            state[pl.ds(pl.multiple_of((base + f) * rows, 8), rows), :] = x
+            x = ref[pl.ds(pl.multiple_of(f * rows, rows), rows), :]
             keep = pair == base + f
             low = 2 * (base + f)
             to_east = jnp.where(keep, pltpu.roll(x, (low + 2) & (LANES - 1), 1), to_east)
@@ -83,10 +79,7 @@
     for n, (ref, base) in enumerate(((tr, 0), (ve, half))):
         for i in range(chunks):
             copies[2 + n * chunks + i].wait()
-            carry = lax.fori_loop(
-                i * size, (i + 1) * size, columns(ref, base, carry), carry, unroll=8
-            )
-    to_east, to_west = carry
+            carry = lax.fori_loop(i * size, (i + 1) * size, columns(ref, base), carry, unroll=8)
     mixing = mix[...]
     aux_east = jnp.where(
         lane == 0,
@@ -94,11 +87,37 @@
         jnp.where(lane == 1, pltpu.roll(wet, 3, 1), pltpu.roll(mixing, 3, 1)),
     )
     aux_west = jnp.where(lane <= 1, wet, pltpu.roll(mixing, 2, 1))
+
+    def spread(x, i):
+        return jnp.broadcast_to(x[:, i : i + 1], (rows, LANES))
+
+    odd = (lane & 1) == 1
+    to_east = carry[0] * jnp.where(odd, spread(wet, LANES - 1), spread(wet, LANES - 2))
+    to_west = carry[1] * jnp.where(odd, spread(wet, 1), spread(wet, 0))
     even = is_even("lon")
     lon_a[0:rows, :] = jnp.where(even, to_east, to_west)
     lon_b[0:rows, :] = jnp.where(even, to_west, to_east)
     lon_a[rows : 2 * rows, :] = jnp.where(even, aux_east, aux_west)
     lon_b[rows : 2 * rows, :] = jnp.where(even, aux_west, aux_east)
+
+
+def prepare_kernel(
+    rows, levels, devices, tr, ve, mask, mix, own, atm_row,
+    state, lat_a, lat_b, base, col_map, row_map, out, ids, used,
+):
+    fields = 4 * levels
+    half = fields // 2
+    wet = mask[...].astype(F32)
+    base[0:rows, :] = wet
+    base[rows : 2 * rows, :] = mix[...]
+    for ref, first in ((tr, 0), (ve, half)):
+
+        def fill(f, carry, ref=ref, first=first):
+            x = ref[pl.ds(pl.multiple_of(f * rows, 8), rows), :] * wet
+            state[pl.ds(pl.multiple_of((first + f) * rows, 8), rows), :] = x
+            return carry
+
+        lax.fori_loop(0, half, fill, 0, unroll=8)
 
     even = is_even("lat")
     top, bottom = (rows - 1, rows - 2), (0, 1)
@@ -108,9 +127,56 @@
         for place, line in ((0, near), (fields, far)):
             buf[place : place + fields, :] = state[pl.ds(line, fields, stride=rows), :]
         buf[2 * fields : 2 * fields + 8, :] = jnp.zeros((8, LANES), F32)
-        buf[2 * fields : 2 * fields + 1, :] = wet_out[pl.ds(near, 1), :]
-        buf[2 * fields + 1 : 2 * fields + 2, :] = wet_out[pl.ds(far, 1), :]
-        buf[2 * fields + 2 : 2 * fields + 3, :] = mix[pl.ds(near, 1), :]
+        buf[2 * fields : 2 * fields + 1, :] = base[pl.ds(near, 1), :]
+        buf[2 * fields + 1 : 2 * fields + 2, :] = base[pl.ds(far, 1), :]
+        buf[2 * fields + 2 : 2 * fields + 3, :] = base[pl.ds(rows + near, 1), :]
+
+    total = lax.axis_size("lat") * rows
+    latitude = lax.axis_index("lat") * rows - PAD + iota((rows + 2 * PAD, LANES), 0)
+    latitude = jnp.where(latitude >= total, 2 * total - 1 - latitude, latitude).astype(F32)
+    table = CORIOLIS_MAX * jnp.sin(math.pi * (-0.43 + 0.93 * (latitude + 0.5) / total))
+    base[2 * rows :, :] = table
+
+    span = 2 * levels
+    src, dst = iota((LANES, LANES), 0), iota((LANES, LANES), 1)
+    src_group, dst_group = src // span, dst // span
+    src_level, dst_level = (src // 2) % levels, (dst // 2) % levels
+    same_side = (src & 1) == (dst & 1)
+    mixes = VERTICAL_MIX * level_matrix("mix", levels, src_level, dst_level)
+    press = level_matrix("pressure", levels, src_level, dst_level) * density_weight(src_group)
+    col_map[0:LANES, :] = jnp.where(same_side & (src_group == dst_group), mixes, 0.0)
+    col_map[LANES : 2 * LANES, :] = jnp.where(same_side & (dst_group == 2), -press, 0.0)
+    col_map[2 * LANES :, :] = jnp.where(same_side & (dst_group == 3), -press, 0.0)
+
+    dst, src = iota((fields, fields), 0), iota((fields, fields), 1)
+    mixes = VERTICAL_MIX * level_matrix("mix", levels, src % levels, dst % levels)
+    row_map[0:fields, 0:fields] = jnp.where(dst // levels == src // levels, mixes, 0.0)
+    dst, src = iota((levels, fields), 0), iota((levels, fields), 1)
+    press = level_matrix("pressure", levels, src % levels, dst) * density_weight(src // levels)
+    row_map[fields:, 0:fields] = press
+
+    slot_rows = out.shape[0] // devices
+
+    def clear(d, carry):
+        used[d] = 0
+        return carry
+
+    lax.fori_loop(0, devices, clear, 0, unroll=8)
+    out[...] = jnp.zeros(out.shape, F32)
+    lane1 = iota((1, LANES), 1)
+    places = jnp.zeros((1, LANES), jnp.int32)
+    for r in range(rows):
+        owner = own[r]
+        slot = used[owner]
+        used[owner] = slot + 1
+        start = owner * slot_rows
+        places = jnp.where(lane1 == r, start + 4 * slot, places)
+        out[pl.ds(start + 4 * CAP + slot, 1), :] = base[r : r + 1, :]
+        line = out[pl.ds(start + 5 * CAP, 1), :]
+        target = jnp.full((1, LANES), atm_row[r], jnp.int32).astype(F32)
+        out[pl.ds(start + 5 * CAP, 1), :] = jnp.where(lane1 // (LANES // CAP) == slot, target, line)
+    ids[...] = jnp.zeros(ids.shape, jnp.int32)
+    ids[0:1, :] = places
 
 
 def corner_kernel(rows, a_in, b_in, got_a, got_b, a_out, b_out):
@@ -147,13 +213,14 @@
     return jnp.where(group == 0, -THERMAL, jnp.where(group == 1, HALINE, 0.0)).astype(F32)
 
 
-def advance_columns(levels, mid, outer, inner, corner_n, corner_s, wets, mixing, coriolis):
+def advance_columns(mid, outer, inner, corner_n, corner_s, wets, mixing, coriolis, level_map):
     rows = mid.shape[0]
     wet_mid, wet_out, wet_in, wet_corner_n, wet_corner_s = wets
     lane = iota((rows, LANES), 1)
     row = iota((rows, LANES), 0)
     even = (lane & 1) == 0
-    group = lane // (2 * levels)
+    span = LANES // 4
+    group = lane // span
 
     def sides(outside, inside):
         return jnp.where(even, outside, inside), jnp.where(even, inside, outside)
@@ -169,7 +236,6 @@
     wet_n, wet_s = shifted(wet_mid, wet_corner_n, wet_corner_s)
     lap = wet_e * (e - mid) + wet_w * (w - mid) + wet_n * (n - mid) + wet_s * (s - mid)
     de, dn = e - w, n - s
-    span = 2 * levels
     one, two, three = (pltpu.roll(mid, i * span, 1) for i in (1, 2, 3))
 
     def pick(a, b, c, d):
@@ -178,28 +244,16 @@
     u = pick(two, three, mid, one)
     v = pick(one, two, three, mid)
     adv = 0.5 * (u * de + v * dn)
-    src, dst = iota((LANES, LANES), 0), iota((LANES, LANES), 1)
-    src_group, dst_group = src // span, dst // span
-    src_level, dst_level = (src // 2) % levels, (dst // 2) % levels
-    same_side = (src & 1) == (dst & 1)
-    mix_map = jnp.where(
-        same_side & (src_group == dst_group), level_matrix("mix", levels, src_level, dst_level), 0.0
-    )
-    press = level_matrix("pressure", levels, src_level, dst_level) * density_weight(src_group)
-    press_x = jnp.where(same_side & (dst_group == 2), press, 0.0)
-    press_y = jnp.where(same_side & (dst_group == 3), press, 0.0)
-    vertical = dot(mid, mix_map)
-    grad = dot(de, press_x) + dot(dn, press_y)
+    linear = dot(jnp.concatenate([mid, de, dn], axis=1), level_map)
     zero = jnp.zeros_like(mid)
     turn = pick(zero, zero, coriolis * v, -coriolis * u)
     kappa = jnp.where(group < 2, mixing, VISCOSITY)
-    tend = turn - adv - grad + kappa * lap + VERTICAL_MIX * vertical
+    tend = turn - adv + kappa * lap + linear
     return wet_mid * (mid + TIMESTEP * tend)
 
 
-def advance_row(levels, north_side, mid, outer, inner, corner_e, corner_w, wets, mixing, coriolis):
-    fields = mid.shape[0]
-    wet_mid, wet_out, wet_in, wet_corner_e, wet_corner_w = wets
+def advance_rows(levels, parts, level_map):
+    fields = 4 * levels
     lane = iota((fields, LANES), 1)
     lane8 = iota((8, LANES), 1)
 
@@ -208,34 +262,36 @@
         w = jnp.where(at == 0, west, pltpu.roll(x, 1, 1))
         return e, w
 
-    e, w = sides(mid, corner_e, corner_w, lane)
-    wet_e, wet_w = sides(
-        jnp.broadcast_to(wet_mid, (8, LANES)), wet_corner_e, wet_corner_w, lane8
-    )
-    wet_e, wet_w = wet_e[0:1], wet_w[0:1]
-    n, s = (outer, inner) if north_side else (inner, outer)
-    wet_n, wet_s = (wet_out, wet_in) if north_side else (wet_in, wet_out)
-    lap = wet_e * (e - mid) + wet_w * (w - mid) + wet_n * (n - mid) + wet_s * (s - mid)
-    de, dn = e - w, n - s
-    u, v = mid[2 * levels : 3 * levels], mid[3 * levels :]
-    adv = 0.5 * (jnp.concatenate([u] * 4, axis=0) * de + jnp.concatenate([v] * 4, axis=0) * dn)
-    dst, src = iota((fields, fields), 0), iota((fields, fields), 1)
-    mix_map = jnp.where(
-        dst // levels == src // levels, level_matrix("mix", levels, src % levels, dst % levels), 0.0
-    )
-    dst, src = iota((levels, fields), 0), iota((levels, fields), 1)
-    press = level_matrix("pressure", levels, src % levels, dst) * density_weight(src // levels)
-    vertical = dot(mix_map, mid)
-    zero = jnp.zeros((2 * levels, LANES), F32)
-    turn = jnp.concatenate(
-        [zero, coriolis * v - dot(press, de), -coriolis * u - dot(press, dn)], axis=0
-    )
-    kappa = jnp.concatenate(
-        [jnp.broadcast_to(mixing, (2 * levels, LANES)), jnp.full((2 * levels, LANES), VISCOSITY)],
-        axis=0,
-    )
-    tend = turn - adv + kappa * lap + VERTICAL_MIX * vertical
-    return wet_mid * (mid + TIMESTEP * tend)
+    mids, gaps = [], []
+    for mid, n, s, (corner_e, corner_w), *_ in parts:
+        e, w = sides(mid, corner_e, corner_w, lane)
+        mids.append((mid, e, w, n, s))
+        gaps += [e - w, n - s]
+    vertical = dot(level_map[0:fields, 0:fields], jnp.concatenate([m[0] for m in mids], axis=1))
+    grads = dot(level_map[fields:, 0:fields], jnp.concatenate(gaps, axis=1))
+    done = []
+    for i, (mid, e, w, n, s) in enumerate(mids):
+        *_, wets, mixing, coriolis = parts[i]
+        wet_mid, wet_n, wet_s, wet_corner_e, wet_corner_w = wets
+        wet_e, wet_w = sides(
+            jnp.broadcast_to(wet_mid, (8, LANES)), wet_corner_e, wet_corner_w, lane8
+        )
+        lap = wet_e[0:1] * (e - mid) + wet_w[0:1] * (w - mid)
+        lap = lap + wet_n * (n - mid) + wet_s * (s - mid)
+        de, dn = gaps[2 * i], gaps[2 * i + 1]
+        u, v = mid[2 * levels : 3 * levels], mid[3 * levels :]
+        adv = jnp.concatenate([u] * 4, axis=0) * de + jnp.concatenate([v] * 4, axis=0) * dn
+        grad_x = grads[:, 2 * i * LANES : (2 * i + 1) * LANES]
+        grad_y = grads[:, (2 * i + 1) * LANES : (2 * i + 2) * LANES]
+        zero = jnp.zeros((2 * levels, LANES), F32)
+        turn = jnp.concatenate([zero, coriolis * v - grad_x, -coriolis * u - grad_y], axis=0)
+        kappa = jnp.concatenate(
+            [jnp.broadcast_to(mixing, (2 * levels, LANES)), jnp.full(zero.shape, VISCOSITY)],
+            axis=0,
+        )
+        tend = turn - 0.5 * adv + kappa * lap + vertical[:, i * LANES : (i + 1) * LANES]
+        done.append(wet_mid * (mid + TIMESTEP * tend))
+    return done
 
 
 COEFFICIENTS = ("te", "tw", "tn", "ts", "tc", "ve", "vw", "vn", "vs", "vc", "adv", "mix", "turn")
@@ -311,44 +367,29 @@
 
 
 def surface_kernel(
-    rows, levels, lat_count, devices,
-    state, wet_in, mix_in, lon_a, lon_b, got_lon_a, got_lon_b, lat_a, lat_b, got_lat_a, got_lat_b,
-    own, atm_row,
-    halo, out, now, later, wet_pad, stage, used,
+    rows, levels, lat_count,
+    state, base, col_map, row_map, lon_a, lon_b, got_lon_a, got_lon_b, lat_a, lat_b, got_lat_a,
+    got_lat_b, out_in, ids,
+    halo, out, now, later, wet_pad, stage, places, sem,
 ):
     fields = 4 * levels
     pitch = rows + 2 * PAD
     at = Halo(rows, fields)
+    to_scalars = pltpu.make_async_copy(ids, places, sem)
+    to_scalars.start()
+    out[...] = out_in[...]
     lat = lax.axis_index("lat")
     even_lat, even_lon = is_even("lat"), is_even("lon")
     fold = lat == lat_count - 1
-    wet = wet_in[...]
-    mixing = mix_in[...]
+    wet = base[0:rows, :]
+    mixing = base[rows : 2 * rows, :]
+    table = base[2 * rows :, :]
+    coriolis = table[PAD : PAD + rows]
     lane = iota((rows, LANES), 1)
     even = (lane & 1) == 0
 
     def ordered(flag, a, b):
         return jnp.where(flag, a, b), jnp.where(flag, b, a)
-
-    slot_rows = out.shape[0] // (devices * CAP)
-
-    def clear(d, carry):
-        used[d] = 0
-        return carry
-
-    lax.fori_loop(0, devices, clear, 0, unroll=8)
-    out[...] = jnp.zeros(out.shape, F32)
-    stage[...] = jnp.zeros(stage.shape, F32)
-    stage[pl.ds(4, rows, stride=slot_rows), :] = wet
-    for r in range(rows):
-        line = jnp.full((1, LANES), atm_row[r], jnp.int32)
-        stage[r * slot_rows + 5 : r * slot_rows + 6, :] = line.astype(F32)
-
-    latitude = lat * rows - PAD + iota((rows + 2 * PAD, LANES), 0)
-    total = lat_count * rows
-    latitude = jnp.where(latitude >= total, 2 * total - 1 - latitude, latitude).astype(F32)
-    table = CORIOLIS_MAX * jnp.sin(math.pi * (-0.43 + 0.93 * (latitude + 0.5) / total))
-    coriolis = table[PAD : PAD + rows]
 
     north, south = ordered(even_lat, got_lat_a[...], got_lat_b[...])
     length = 2 * fields + 8
@@ -415,7 +456,7 @@
     inner = jnp.where(even, pltpu.roll(sent_e, LANES - 1, 1), pltpu.roll(sent_w, 1, 1))
     halo[at.side0] = side
     halo[at.side1] = advance_columns(
-        levels, side, outer, inner, corner_n, corner_s,
+        side, outer, inner, corner_n, corner_s,
         (
             jnp.where(even, wet_col_e, wet_col_w),
             jnp.where(even, spread(aux_e, 1), spread(aux_w, 1)),
@@ -424,7 +465,7 @@
             wet_s_lanes,
         ),
         jnp.where(even, spread(aux_e, 2), spread(aux_w, 2)),
-        coriolis,
+        coriolis, col_map[...],
     )
 
     field_lane = iota((fields, LANES), 1)
@@ -435,16 +476,21 @@
         return jnp.sum(jnp.where(here, x, 0.0), axis=1, keepdims=True)
 
     inside_n, inside_s = ordered(even_lat, lat_a[0:fields, :], lat_b[0:fields, :])
-    for north_side, (mid, outside, tail), inside, corner, corner_wets, line, lat_row, place in (
-        (True, north_rows, inside_n, corner_n, (wet_ne, wet_nw), rows - 1, PAD + rows, at.north1),
-        (False, south_rows, inside_s, corner_s, (wet_se, wet_sw), 0, PAD - 1, at.south1),
+    parts = []
+    for north_side, (mid, outside, tail), inside, corner, corner_wets, line, lat_row in (
+        (True, north_rows, inside_n, corner_n, (wet_ne, wet_nw), rows - 1, PAD + rows),
+        (False, south_rows, inside_s, corner_s, (wet_se, wet_sw), 0, PAD - 1),
     ):
-        halo[place] = advance_row(
-            levels, north_side, mid, outside, inside,
-            to_sublanes(corner, 0), to_sublanes(corner, 1),
-            (tail[0:1], tail[1:2], wet[line : line + 1], *corner_wets),
-            tail[2:3], table[lat_row : lat_row + 1],
+        pair = (outside, inside), (tail[1:2], wet[line : line + 1])
+        (n, s), (wet_n1, wet_s1) = pair if north_side else [x[::-1] for x in pair]
+        parts.append(
+            (
+                mid, n, s, (to_sublanes(corner, 0), to_sublanes(corner, 1)),
+                (tail[0:1], wet_n1, wet_s1, *corner_wets),
+                tail[2:3], table[lat_row : lat_row + 1],
+            )
         )
+    halo[at.north1], halo[at.south1] = advance_rows(levels, parts, row_map[...])
 
     count = now.shape[0] // (4 * pitch)
 
@@ -467,13 +513,10 @@
             put(later, q, k, new[q], at.north1, at.south1)
     new, _ = advance_level(0, count, levels, rows, later, halo[at.side1], coef, (none, none))
     for q in range(4):
-        stage[pl.ds(q, rows, stride=slot_rows), :] = new[q]
+        stage[pl.ds(q, rows, stride=4), :] = new[q]
+    to_scalars.wait()
     for r in range(rows):
-        owner = own[r]
-        slot = used[owner]
-        used[owner] = slot + 1
-        place = pl.multiple_of((owner * CAP + slot) * slot_rows, 8)
-        out[pl.ds(place, slot_rows), :] = stage[r * slot_rows : (r + 1) * slot_rows, :]
+        out[pl.ds(places[0, r], 4), :] = stage[4 * r : 4 * r + 4, :]
 
 
 def main_kernel(
@@ -530,13 +573,22 @@
 
 
 def reduce_kernel(devices, data, surface, cover):
-    slot_rows = data.shape[0] // (devices * CAP)
-    slots = devices * CAP
-    lines = data[pl.ds(5, slots, stride=slot_rows), :]
-    to_rows = (lines == iota((slots, LANES), 1).astype(F32)).astype(F32)
-    values = [data[pl.ds(q, slots, stride=slot_rows), :] for q in range(5)]
-    totals = dot(to_rows, jnp.concatenate(values, axis=1), (((0,), (0,)), ((), ())))
-    totals = totals[0:ATM_ROWS]
+    slot_rows = data.shape[0] // devices
+
+    def rows_of(i):
+        return data[pl.ds(i, devices, stride=slot_rows), :]
+
+    width = LANES // CAP
+    lines = rows_of(5 * CAP)
+    named = (lines == (iota((devices, LANES), 1) % width).astype(F32)).astype(F32)
+    to_rows, values = [], []
+    for slot in range(CAP):
+        to_rows.append(named[:, slot * width : slot * width + ATM_ROWS])
+        parts = [rows_of(4 * slot + q) for q in range(4)] + [rows_of(4 * CAP + slot)]
+        values.append(jnp.concatenate(parts, axis=1))
+    totals = dot(
+        jnp.concatenate(to_rows, axis=0), jnp.concatenate(values, axis=0), (((0,), (0,)), ((), ()))
+    )
     ocean = totals[:, 4 * LANES :]
     cover[...] = ocean
     share = jnp.maximum(ocean, 1.0)
@@ -544,11 +596,11 @@
         surface[q] = totals[:, q * LANES : (q + 1) * LANES] / share
 
 
-def call(kernel, out_shape, **kwargs):
+def call(kernel, out_shape, limit=VMEM_LIMIT, **kwargs):
     return pl.pallas_call(
         kernel,
         out_shape=out_shape,
-        compiler_params=pltpu.CompilerParams(vmem_limit_bytes=VMEM_LIMIT),
+        compiler_params=pltpu.CompilerParams(vmem_limit_bytes=limit),
         **kwargs,
     )
 
@@ -588,19 +640,36 @@
     vmem = pl.BlockSpec(memory_space=pltpu.VMEM)
 
     chunks = 2
-    lon_a, lon_b, lat_a, lat_b, state, wet, mix = call(
+    tr, ve = tracers.reshape(flat, cols), velocity.reshape(flat, cols)
+    lon_a, lon_b = call(
         functools.partial(pack_kernel, rows, fields, chunks),
-        [shaped(2 * rows, cols)] * 2
-        + [shaped(length, cols)] * 2
-        + [shaped(fields * rows, cols), shaped(rows, cols), shaped(rows, cols)],
+        [shaped(2 * rows, cols)] * 2,
+        limit=VMEM_ALL,
         in_specs=[hbm] * 4,
         scratch_shapes=[
             pltpu.VMEM((flat, cols), F32),
             pltpu.VMEM((flat, cols), F32),
             pltpu.VMEM((rows, cols), jnp.int32),
+            pltpu.VMEM((rows, cols), F32),
             pltpu.SemaphoreType.DMA((2 + 2 * chunks,)),
         ],
-    )(tracers.reshape(flat, cols), velocity.reshape(flat, cols), land_mask, mixing)
+    )(tr, ve, land_mask, mixing)
+
+    slot_rows = 5 * CAP + 1
+    state, lat_a, lat_b, base, col_map, row_map, outgoing, ids = call(
+        functools.partial(prepare_kernel, rows, levels, devices),
+        [shaped(fields * rows, cols)]
+        + [shaped(length, cols)] * 2
+        + [
+            shaped(2 * rows + pitch, cols),
+            shaped(3 * cols, cols),
+            shaped(fields + levels, cols),
+            shaped(devices * slot_rows, cols),
+            shaped(8, cols, dtype=jnp.int32),
+        ],
+        in_specs=[vmem] * 4 + [smem] * 2,
+        scratch_shapes=[pltpu.SMEM((devices,), jnp.int32)],
+    )(tr, ve, land_mask, mixing, owners.reshape(rows), atm_row)
 
     swaps = pairs_of(lon_count, lat_count)
     got_lon_a = lax.ppermute(lon_a, "lon", swaps[0])
@@ -620,24 +689,24 @@
     got_lat_b = lax.ppermute(lat_b, ("lon", "lat"), swaps[3])
 
     at = Halo(rows, fields)
-    slot_rows = 8
     count = min(3, levels)
     halo, outgoing = call(
-        functools.partial(surface_kernel, rows, levels, lat_count, devices),
-        [shaped(at.size, cols), shaped(devices * CAP * slot_rows, cols)],
-        in_specs=[vmem] * 11 + [smem] * 2,
+        functools.partial(surface_kernel, rows, levels, lat_count),
+        [shaped(at.size, cols), shaped(devices * slot_rows, cols)],
+        in_specs=[vmem] * 14,
         scratch_shapes=[
             pltpu.VMEM((4 * count * pitch, cols), F32),
             pltpu.VMEM((4 * count * pitch, cols), F32),
             pltpu.VMEM((pitch, cols), F32),
-            pltpu.VMEM((rows * slot_rows, cols), F32),
-            pltpu.SMEM((devices,), jnp.int32),
+            pltpu.VMEM((4 * rows, cols), F32),
+            pltpu.SMEM((8, cols), jnp.int32),
+            pltpu.SemaphoreType.DMA,
         ],
-    )(state, wet, mix, lon_a, lon_b, got_lon_a, got_lon_b, lat_a, lat_b, got_lat_a, got_lat_b,
-      owners.reshape(rows), atm_row)
+    )(state, base, col_map, row_map, lon_a, lon_b, got_lon_a, got_lon_b, lat_a, lat_b, got_lat_a,
+      got_lat_b, outgoing, ids)
     incoming = lax.all_to_all(
-        outgoing.reshape(devices, CAP * slot_rows, cols), ("lon", "lat"), 0, 0, tiled=True
-    )
+        outgoing.reshape(devices, slot_rows, 1, cols), ("lon", "lat"), 0, 0, tiled=True
+    ).reshape(devices * slot_rows, cols)
 
     chunks = 4
     tr_out, ve_out = call(
@@ -659,7 +728,7 @@
     surface, cover = call(
         functools.partial(reduce_kernel, devices),
         [shaped(4, ATM_ROWS, cols), shaped(ATM_ROWS, cols)],
-    )(incoming.reshape(devices * CAP * slot_rows, cols))
+    )(incoming)
     shape = (2, levels, rows, cols)
     return tr_out.reshape(shape), ve_out.reshape(shape), surface, cover
 

time: 39.2 us -> 34.4 us (0.88)
  waiting for transfers between devices: 10.3 us -> 6.47 us
  local copies, waits for them, and re-layouts: 4.18 us -> 1.06 us
  Pallas kernels: 8.78 us -> 10.7 us
    unnamed x12 -> x16, local copies, waits for them, and re-layouts: 4.18 us -> 1.06 us
    all_to_all x1, waiting for transfers between devices: 6.38 us -> 4.6 us  [local(): lax.all_to_all(outgoing.reshape(devices, slot_rows, 1, cols), ('lon', 'la...]
    ppermute x1, waiting for transfers between devices: 2.92 us -> 1.29 us  [local(): got_lon_b = lax.ppermute(lon_b, 'lon', swaps[1])]
    pallas_call x1, Pallas kernels: 1.4 us -> 2.89 us  [local(): call(functools.partial(pack_kernel, rows, fields, chunks), [shaped(2 * ro...]
    pallas_call x1 -> x2, Pallas kernels: 2.21 us -> 2.79 us  [the longest x1 1.63 us: local(): call(functools.partial(surface_kernel, rows, levels, lat_count), [shaped(...]
    ppermute x1, waiting for transfers between devices: 0.4 us -> 0.01 us  [local(): got_lon_a = lax.ppermute(lon_a, 'lon', swaps[0])]
  transfers between devices with their start and end apart: 5 -> 5, of which waited for: 4 -> 3; matrix products, arithmetic and copies ran while one was open for 0% -> 0% of each run, Pallas kernels for 10% -> 15%
where the time goes in v3:
time: 34.4 us; the launch traced here: 33.9 us
  starting transfers between devices  14.9 us (43%)
  Pallas kernels  10.7 us (31%)
  waiting for transfers between devices  6.47 us (19%)
  local copies, waits for them, and re-layouts  1.06 us (3%)
  between operations  0.75 us (2%)
    all_to_all x1, starting transfers between devices, local(): lax.all_to_all(outgoing.reshape(devices, slot_rows, 1, cols), ('lon', 'la...  9.71 us
    all_to_all x1, waiting for transfers between devices, local(): lax.all_to_all(outgoing.reshape(devices, slot_rows, 1, cols), ('lon', 'la...  4.6 us
    pallas_call x1, Pallas kernels, local(): call(functools.partial(main_kernel, rows, levels, chunks), [shaped(flat,...  4 us
    ppermute x1, starting transfers between devices, local(): got_lon_a = lax.ppermute(lon_a, 'lon', swaps[0])  3 us
    pallas_call x1, Pallas kernels, local(): call(functools.partial(pack_kernel, rows, fields, chunks), [shaped(2 * ro...  2.89 us
    pallas_call x1, Pallas kernels, local(): call(functools.partial(surface_kernel, rows, levels, lat_count), [shaped(...  1.63 us
    ppermute x1, starting transfers between devices, local(): got_lon_b = lax.ppermute(lon_b, 'lon', swaps[1])  1.49 us
    ppermute x1, waiting for transfers between devices, local(): got_lon_b = lax.ppermute(lon_b, 'lon', swaps[1])  1.29 us
  transfers between devices with their start and end apart: 5, of which 3 were waited for; matrix products, arithmetic and copies ran while one was open for 0% of the time, Pallas kernels for 15%

profile of v3, /device:TPU:0, one launch (start us, length us, event | category | flops | bytes accessed | tf_op | source)
XLA Modules:
  0.0 33.9 jit_solution(14382283643524866045)
XLA Ops:
  0.6 0.0 copy-start
  0.6 0.0 copy-start.2
  0.7 0.0 copy-start.3
  0.7 2.9 %shard_map.94 = (f32[64,128]{1,0:T(8,128)}, f32[64,128]{1,0:T(8,128)}) custom-call(f32[1024,128]{1,0:T(8,128)} %bitcast.7, f32[1024,128]{1,0:T(8,128)} %bitcast.9, s32[32,128]{1,0:T(8,128)} %mask_hbm.1, f32[32,128]{1,0:T(8,128)} %mix_hbm.1), custom_call_target="tpu_custom_call" | custom-call | tf_op jit(solution)/shard_map/pallas_call | solution.py:644
  3.6 3.0 %collective-permute-start = (f32[64,128]{1,0:T(8,128)}, f32[64,128]{1,0:T(8,128)S(1)}, u32[]{:S(2)}, u32[]{:S(2)}) collective-permute-start(f32[64,128]{1,0:T(8,128)} %get-tuple-element.26.lon_a), channel_id=1, source_target_pairs={{0,8},{8,0},{16,24},{24,16},{1,9},{9,1},{17,25},{25,17},{2,10},{10... | collective-permute-start | bytes 98312 | tf_op jit(solution)/shard_map/ppermute | solution.py:675
  6.6 0.0 copy-start.6
  6.6 0.0 copy-start.7
  6.6 1.5 %collective-permute-start.1 = (f32[64,128]{1,0:T(8,128)}, f32[64,128]{1,0:T(8,128)S(1)}, u32[]{:S(2)}, u32[]{:S(2)}) collective-permute-start(f32[64,128]{1,0:T(8,128)} %get-tuple-element.27.lon_b), channel_id=1, source_target_pairs={{0,24},{8,16},{16,8},{24,0},{1,25},{9,17},{17,9},{25,1},{2,26},{10... | collective-permute-start | bytes 98312 | tf_op jit(solution)/shard_map/ppermute | solution.py:676
  8.1 0.0 copy-done
  8.1 0.0 copy-done.2
  8.1 0.0 copy-done.3
  8.1 0.0 copy-done.6
  8.1 0.0 copy-done.7
  8.1 0.0 copy-start.1
  8.1 1.0 %copy-done.1 = f32[2,16,32,128]{3,2,1,0:T(8,128)S(1)} copy-done((f32[2,16,32,128]{3,2,1,0:T(8,128)S(1)}, f32[2,16,32,128]{3,2,1,0:T(8,128)}, u32[]{:S(2)}) %copy-start.1) | copy-done | bytes 524312
  9.1 1.2 %shard_map.93 = (f32[2048,128]{1,0:T(8,128)S(1)}, f32[136,128]{1,0:T(8,128)S(1)}, f32[136,128]{1,0:T(8,128)S(1)}, f32[112,128]{1,0:T(8,128)S(1)}, f32[384,128]{1...) custom-call(f32[1024,128]{1,0:T(8,128)S(1)} %bitcast.8, ...), custom_call_target="tpu_custom_call" | custom-call | tf_op jit(solution)/shard_map/pallas_call | solution.py:659
  10.3 0.0 collective-permute-done.got_a.got_lon_a
  10.3 1.3 %collective-permute-done.1.got_b.got_lon_b = f32[64,128]{1,0:T(8,128)S(1)} collective-permute-done((f32[64,128]{1,0:T(8,128)}, f32[64,128]{1,0:T(8,128)S(1)}, u32[]{:S(2)}, u32[]{:S(2)}) %collective-permute-start.1) | collective-permute-done | bytes 32800 | tf_op jit(solution)/shard_map/ppermute | solution.py:676
  11.6 0.0 copy-start.4
  11.6 0.0 copy-start.5
  11.6 0.1 shard_map.95
  11.7 0.0 collective-permute-start.2
  11.7 0.7 %collective-permute-start.3 = (f32[136,128]{1,0:T(8,128)S(1)}, f32[136,128]{1,0:T(8,128)S(1)}, u32[]{:S(2)}, u32[]{:S(2)}) collective-permute-start(f32[136,128]{1,0:T(8,128)S(1)} %get-tuple-element.31.lat_b), channel_id=1, source_target_pairs={{1,2},{2,1},{3,4},{4,3},{5,6},{6,5},{7,31},{9,10},{10,9},{11,12},{... | collective-permute-start | bytes 208904 | tf_op jit(solution)/shard_map/ppermute | solution.py:689
  12.4 0.6 %collective-permute-done.2.got_lat_a = f32[136,128]{1,0:T(8,128)S(1)} collective-permute-done((f32[136,128]{1,0:T(8,128)S(1)}, f32[136,128]{1,0:T(8,128)S(1)}, u32[]{:S(2)}, u32[]{:S(2)}) %collective-permute-start.2) | collective-permute-done | bytes 69664 | tf_op jit(solution)/shard_map/ppermute | solution.py:688
  13.0 0.0 collective-permute-done.3.got_lat_b
  13.0 0.0 copy-done.4
  13.0 0.0 copy-done.5
  13.0 1.6 %shard_map.96 = (f32[736,128]{1,0:T(8,128)S(1)}, f32[352,128]{1,0:T(8,128)}) custom-call(f32[2048,128]{1,0:T(8,128)S(1)} %get-tuple-element.22.state, f32[112,128]{1,0:T(8,128)S(1)} %get-tuple-element.23.base, f32[384,128]{1,0:T(8,128)S(1)} %get-tuple-element.24.col_map, f32[80,128]{1,0:T(8,128)S(1)} %get-tuple-element.25.row_map, f32[64,128]{1,0:T(8,128)S(1)} %copy-done.4, ...), custom_call_target="tpu_custom_call" | custom-call | tf_op jit(solution)/shard_map/pallas_call | solution.py:693
  14.6 9.7 %all-to-all-start = ((f32[32,11,1,128]{3,2,1,0:T(1,128)}), f32[32,11,1,128]{3,2,1,0:T(1,128)S(1)}, u32[]{:S(2)}, u32[]{:S(2)}) async-start(f32[32,11,1,128]{3,2,1,0:T(1,128)} %bitcast.5), calls=%async_computation | async-start | bytes 360448 | tf_op jit(solution)/shard_map/all_to_all | solution.py:707
  24.3 4.0 %shard_map.97 = (f32[1024,128]{1,0:T(8,128)}, f32[1024,128]{1,0:T(8,128)}) custom-call(f32[2048,128]{1,0:T(8,128)S(1)} %get-tuple-element.22.state, f32[736,128]{1,0:T(8,128)S(1)} %get-tuple-element.34.halo), custom_call_target="tpu_custom_call" | custom-call | flops 20971520 | bytes 5242880 | tf_op jit(solution)/shard_map/pallas_call | solution.py:712
  28.3 4.6 %all-to-all-done = f32[32,11,1,128]{3,2,1,0:T(1,128)S(1)} async-done(((f32[32,11,1,128]{3,2,1,0:T(1,128)}), f32[32,11,1,128]{3,2,1,0:T(1,128)S(1)}, u32[]{:S(2)}, u32[]{:S(2)}) %all-to-all-start) | async-done | bytes 180256 | tf_op jit(solution)/shard_map/all_to_all | solution.py:707
  32.9 1.0 %shard_map.98 = (f32[4,32,128]{2,1,0:T(8,128)}, f32[32,128]{1,0:T(8,128)}) custom-call(f32[352,128]{1,0:T(8,128)S(1)} %bitcast.11), custom_call_target="tpu_custom_call" | custom-call | tf_op jit(solution)/shard_map/pallas_call | solution.py:728
Async XLA Ops:
  0.6 7.4 %copy-start = (f32[2,16,32,128]{3,2,1,0:T(8,128)S(1)}, f32[2,16,32,128]{3,2,1,0:T(8,128)}, u32[]{:S(2)}) copy-start(f32[2,16,32,128]{3,2,1,0:T(8,128)} %param.6) | copy-start | bytes 1572868
  0.6 7.4 %copy-start.2 = (s32[32,128]{1,0:T(8,128)S(1)}, s32[32,128]{1,0:T(8,128)}, u32[]{:S(2)}) copy-start(s32[32,128]{1,0:T(8,128)} %mask_hbm.1) | copy-start | bytes 49156
  0.7 7.4 %copy-start.3 = (f32[32,128]{1,0:T(8,128)S(1)}, f32[32,128]{1,0:T(8,128)}, u32[]{:S(2)}) copy-start(f32[32,128]{1,0:T(8,128)} %mix_hbm.1) | copy-start | bytes 49156
  3.6 6.7 %collective-permute-start = (f32[64,128]{1,0:T(8,128)}, f32[64,128]{1,0:T(8,128)S(1)}, u32[]{:S(2)}, u32[]{:S(2)}) collective-permute-start(f32[64,128]{1,0:T(8,128)} %get-tuple-element.26.lon_a), channel_id=1, source_target_pairs={{0,8},{8,0},{16,24},{24,16},{1,9},{9,1},{17,25},{25,17},{2,10},{10... | collective-permute-start | bytes 98312 | tf_op jit(solution)/shard_map/ppermute | solution.py:675
  6.6 1.5 %copy-start.6 = (s32[32,1]{0,1:T(1,128)S(1)}, s32[32,1]{0,1:T(1,128)}, u32[]{:S(2)}) copy-start(s32[32,1]{0,1:T(1,128)} %param.10) | copy-start | bytes 388
  6.6 1.5 %copy-start.7 = (s32[32]{0:T(128)S(1)}, s32[32]{0:T(128)}, u32[]{:S(2)}) copy-start(s32[32]{0:T(128)} %atm_row.1) | copy-start | bytes 388
  6.6 5.0 %collective-permute-start.1 = (f32[64,128]{1,0:T(8,128)}, f32[64,128]{1,0:T(8,128)S(1)}, u32[]{:S(2)}, u32[]{:S(2)}) collective-permute-start(f32[64,128]{1,0:T(8,128)} %get-tuple-element.27.lon_b), channel_id=1, source_target_pairs={{0,24},{8,16},{16,8},{24,0},{1,25},{9,17},{17,9},{25,1},{2,26},{10... | collective-permute-start | bytes 98312 | tf_op jit(solution)/shard_map/ppermute | solution.py:676
  8.1 1.0 %copy-start.1 = (f32[2,16,32,128]{3,2,1,0:T(8,128)S(1)}, f32[2,16,32,128]{3,2,1,0:T(8,128)}, u32[]{:S(2)}) copy-start(f32[2,16,32,128]{3,2,1,0:T(8,128)} %param.7) | copy-start | bytes 1572868
  11.6 1.4 %copy-start.4 = (f32[64,128]{1,0:T(8,128)S(1)}, f32[64,128]{1,0:T(8,128)}, u32[]{:S(2)}) copy-start(f32[64,128]{1,0:T(8,128)} %get-tuple-element.26.lon_a) | copy-start | bytes 98308
  11.6 1.4 %copy-start.5 = (f32[64,128]{1,0:T(8,128)S(1)}, f32[64,128]{1,0:T(8,128)}, u32[]{:S(2)}) copy-start(f32[64,128]{1,0:T(8,128)} %get-tuple-element.27.lon_b) | copy-start | bytes 98308
  11.7 1.3 %collective-permute-start.2 = (f32[136,128]{1,0:T(8,128)S(1)}, f32[136,128]{1,0:T(8,128)S(1)}, u32[]{:S(2)}, u32[]{:S(2)}) collective-permute-start(f32[136,128]{1,0:T(8,128)S(1)} %get-tuple-element.30.lat_a), channel_id=1, source_target_pairs={{0,1},{1,0},{2,3},{3,2},{4,5},{5,4},{6,7},{7,6},{8,9},{9,8},{10,11... | collective-permute-start | bytes 208904 | tf_op jit(solution)/shard_map/ppermute | solution.py:688
  11.7 1.2 %collective-permute-start.3 = (f32[136,128]{1,0:T(8,128)S(1)}, f32[136,128]{1,0:T(8,128)S(1)}, u32[]{:S(2)}, u32[]{:S(2)}) collective-permute-start(f32[136,128]{1,0:T(8,128)S(1)} %get-tuple-element.31.lat_b), channel_id=1, source_target_pairs={{1,2},{2,1},{3,4},{4,3},{5,6},{6,5},{7,31},{9,10},{10,9},{11,12},{... | collective-permute-start | bytes 208904 | tf_op jit(solution)/shard_map/ppermute | solution.py:689
  14.6 18.3 %all-to-all-start = ((f32[32,11,1,128]{3,2,1,0:T(1,128)}), f32[32,11,1,128]{3,2,1,0:T(1,128)S(1)}, u32[]{:S(2)}, u32[]{:S(2)}) async-start(f32[32,11,1,128]{3,2,1,0:T(1,128)} %bitcast.5), calls=%async_computation | async-start | bytes 360448 | tf_op jit(solution)/shard_map/all_to_all | solution.py:707

commit v4 on v3

--- a/solution.py
+++ b/solution.py
@@ -46,19 +46,35 @@
     return copies
 
 
-def pack_kernel(
-    rows, fields, chunks, tr_hbm, ve_hbm, mask_hbm, mix_hbm, lon_a, lon_b, tr, ve, mask, mix, sems
-):
+def edge_kernel(rows, fields, tr_hbm, ve_hbm, mask_hbm, mix_hbm, lat_a, lat_b, edges, mask, mix, sems):
     half = fields // 2
-    size = half // chunks
     pairs = [(mask_hbm, mask), (mix_hbm, mix)]
-    for src, dst in ((tr_hbm, tr), (ve_hbm, ve)):
-        for i in range(chunks):
-            part = slice(i * size * rows, (i + 1) * size * rows)
-            pairs.append((src.at[part], dst.at[part]))
-    copies = start_copies(pairs, sems)
-    copies[0].wait()
-    copies[1].wait()
+    for n, src in enumerate((tr_hbm, ve_hbm)):
+        for side, first in enumerate((0, rows - 8)):
+            part = edges.at[side, n * half : (n + 1) * half]
+            pairs.append((src.at[:, first : first + 8, :], part))
+    for copy in start_copies(pairs, sems):
+        copy.wait()
+    flat = edges.reshape(2 * fields * 8, LANES)
+    even = is_even("lat")
+    top = ((rows - 1, 8 * fields + 7), (rows - 2, 8 * fields + 6))
+    bottom = ((0, 0), (1, 1))
+    for buf, first, second in ((lat_a, top, bottom), (lat_b, bottom, top)):
+        (near, near_at), (far, far_at) = [
+            [jnp.where(even, x, y) for x, y in zip(one, other)] for one, other in zip(first, second)
+        ]
+        wet_near = mask[pl.ds(near, 1), :].astype(F32)
+        wet_far = mask[pl.ds(far, 1), :].astype(F32)
+        buf[0:fields, :] = flat[pl.ds(near_at, fields, stride=8), :] * wet_near
+        buf[fields : 2 * fields, :] = flat[pl.ds(far_at, fields, stride=8), :] * wet_far
+        buf[2 * fields : 2 * fields + 8, :] = jnp.zeros((8, LANES), F32)
+        buf[2 * fields : 2 * fields + 1, :] = wet_near
+        buf[2 * fields + 1 : 2 * fields + 2, :] = wet_far
+        buf[2 * fields + 2 : 2 * fields + 3, :] = mix[pl.ds(near, 1), :]
+
+
+def pack_kernel(rows, fields, tr, ve, mask, mix, lon_a, lon_b):
+    half = fields // 2
     wet = mask[...].astype(F32)
     lane = iota((rows, LANES), 1)
     pair = lane >> 1
@@ -76,10 +92,8 @@
         return body
 
     carry = (jnp.zeros((rows, LANES), F32), jnp.zeros((rows, LANES), F32))
-    for n, (ref, base) in enumerate(((tr, 0), (ve, half))):
-        for i in range(chunks):
-            copies[2 + n * chunks + i].wait()
-            carry = lax.fori_loop(i * size, (i + 1) * size, columns(ref, base), carry, unroll=8)
+    for ref, base in ((tr, 0), (ve, half)):
+        carry = lax.fori_loop(0, half, columns(ref, base), carry, unroll=8)
     mixing = mix[...]
     aux_east = jnp.where(
         lane == 0,
@@ -103,7 +117,7 @@
 
 def prepare_kernel(
     rows, levels, devices, tr, ve, mask, mix, own, atm_row,
-    state, lat_a, lat_b, base, col_map, row_map, out, ids, used,
+    state, base, col_map, row_map, out, ids, used,
 ):
     fields = 4 * levels
     half = fields // 2
@@ -118,18 +132,6 @@
             return carry
 
         lax.fori_loop(0, half, fill, 0, unroll=8)
-
-    even = is_even("lat")
-    top, bottom = (rows - 1, rows - 2), (0, 1)
-    for buf, first, second in ((lat_a, top, bottom), (lat_b, bottom, top)):
-        near = jnp.where(even, first[0], second[0])
-        far = jnp.where(even, first[1], second[1])
-        for place, line in ((0, near), (fields, far)):
-            buf[place : place + fields, :] = state[pl.ds(line, fields, stride=rows), :]
-        buf[2 * fields : 2 * fields + 8, :] = jnp.zeros((8, LANES), F32)
-        buf[2 * fields : 2 * fields + 1, :] = base[pl.ds(near, 1), :]
-        buf[2 * fields + 1 : 2 * fields + 2, :] = base[pl.ds(far, 1), :]
-        buf[2 * fields + 2 : 2 * fields + 3, :] = base[pl.ds(rows + near, 1), :]
 
     total = lax.axis_size("lat") * rows
     latitude = lax.axis_index("lat") * rows - PAD + iota((rows + 2 * PAD, LANES), 0)
@@ -179,25 +181,33 @@
     ids[0:1, :] = places
 
 
-def corner_kernel(rows, a_in, b_in, got_a, got_b, a_out, b_out):
-    even, even_lon = is_even("lat"), is_even("lon")
-    lane = iota((1, LANES), 1)
-    for src, dst, first, second in ((a_in, a_out, rows - 1, 0), (b_in, b_out, 0, rows - 1)):
-        near = jnp.where(even, first, second)
-        dst[...] = src[...]
-
-        def sides(line):
-            a, b = got_a[pl.ds(line, 1), :], got_b[pl.ds(line, 1), :]
-            return jnp.where(even_lon, a, b), jnp.where(even_lon, b, a)
-
-        east, west = sides(near)
-        dst[3:4, :] = jnp.where((lane & 1) == 0, east, west)
-        east, west = sides(rows + near)
-        dst[4:5, :] = jnp.where(
-            lane == 0,
-            jnp.broadcast_to(east[:, 0:1], (1, LANES)),
-            jnp.broadcast_to(west[:, 0:1], (1, LANES)),
+def corner_kernel(lat_count, fields, got_a, got_b, north, south, corners):
+    fold = lax.axis_index("lat") == lat_count - 1
+    even = is_even("lat")
+    a, b = got_a[...], got_b[...]
+    straight = jnp.where(even, a, b)
+    south[...] = jnp.where(even, b, a)
+    back = LANES - 1 - iota((8, LANES), 1)
+    flipped = jnp.concatenate(
+        [
+            jnp.take_along_axis(straight[i : i + 8], back, axis=1)
+            * (-1.0 if i < 2 * fields and i % fields >= fields // 2 else 1.0)
+            for i in range(0, straight.shape[0], 8)
+        ],
+        axis=0,
+    )
+    north[...] = jnp.where(fold, flipped, straight)
+    lane, field = iota((fields, LANES), 1), iota((fields, LANES), 0)
+    lane1 = iota((1, LANES), 1)
+    corners[...] = jnp.zeros(corners.shape, F32)
+    for i, ref in enumerate((north, south)):
+        near = ref[0:fields, :]
+        ends = jnp.where(
+            lane == 2 * field, near[:, 0:1], jnp.where(lane == 2 * field + 1, near[:, LANES - 1 :], 0.0)
         )
+        corners[i : i + 1, :] = jnp.sum(ends, axis=0, keepdims=True)
+        wet = ref[2 * fields : 2 * fields + 1, :]
+        corners[2 + i : 3 + i, :] = jnp.where(lane1 == 0, wet[:, 0:1], wet[:, LANES - 1 :])
 
 
 def level_matrix(kind, levels, source, target):
@@ -297,15 +307,9 @@
 COEFFICIENTS = ("te", "tw", "tn", "ts", "tc", "ve", "vw", "vn", "vs", "vc", "adv", "mix", "turn")
 
 
-class Halo:
-    def __init__(self, rows, fields):
-        at = 0
-        sizes = [("side0", rows), ("side1", rows)]
-        sizes += [(name, fields) for name in ("north0", "south0", "north1", "south1")]
-        for name, size in sizes + [(name, rows) for name in COEFFICIENTS]:
-            setattr(self, name, slice(at, at + size))
-            at += size
-        self.size = at
+def place_of(name, rows):
+    i = COEFFICIENTS.index(name)
+    return slice(i * rows, (i + 1) * rows)
 
 
 def coefficients(wet, neighbours, mixing, coriolis):
@@ -366,106 +370,103 @@
     return new, (acc_x + dens_x, acc_y + dens_y)
 
 
-def surface_kernel(
-    rows, levels, lat_count,
-    state, base, col_map, row_map, lon_a, lon_b, got_lon_a, got_lon_b, lat_a, lat_b, got_lat_a,
-    got_lat_b, out_in, ids,
-    halo, out, now, later, wet_pad, stage, places, sem,
+def ordered(flag, a, b):
+    return jnp.where(flag, a, b), jnp.where(flag, b, a)
+
+
+def padded(buf, count, levels, rows, q, k, value, north, south):
+    at = (q * count + k) * (rows + 2 * PAD) + PAD
+    field = q * levels + k
+    buf[at : at + rows, :] = value
+    buf[at + rows : at + rows + 1, :] = north[field : field + 1, :]
+    buf[at - 1 : at, :] = south[field : field + 1, :]
+
+
+def first_kernel(
+    rows, levels, state, base, got_lon_a, got_lon_b, north, south, coef, side, top, now, wet_pad
 ):
     fields = 4 * levels
-    pitch = rows + 2 * PAD
-    at = Halo(rows, fields)
+    even_lon = is_even("lon")
+    wet = base[0:rows, :]
+    mixing = base[rows : 2 * rows, :]
+    coriolis = base[2 * rows + PAD : 3 * rows + PAD, :]
+    lane = iota((rows, LANES), 1)
+    wet_pad[PAD : PAD + rows, :] = wet
+    wet_pad[PAD - 1 : PAD, :] = south[2 * fields : 2 * fields + 1, :]
+    wet_pad[PAD + rows : PAD + rows + 1, :] = north[2 * fields : 2 * fields + 1, :]
+    wet_n = wet_pad[PAD + 1 : PAD + 1 + rows, :]
+    wet_s = wet_pad[PAD - 1 : PAD - 1 + rows, :]
+    aux_e, aux_w = ordered(even_lon, got_lon_a[rows:, :], got_lon_b[rows:, :])
+    wet_e = jnp.where(lane == LANES - 1, aux_e[:, 0:1], pltpu.roll(wet, LANES - 1, 1))
+    wet_w = jnp.where(lane == 0, aux_w[:, 0:1], pltpu.roll(wet, 1, 1))
+    made = coefficients(wet, (wet_e, wet_w, wet_n, wet_s), mixing, coriolis)
+    for name in COEFFICIENTS:
+        coef[place_of(name, rows)] = made[name]
+    got_e, got_w = ordered(even_lon, got_lon_a[0:rows, :], got_lon_b[0:rows, :])
+    side[...] = jnp.where((lane & 1) == 0, got_e, got_w)
+
+    count = now.shape[0] // (4 * (rows + 2 * PAD))
+    for q in range(4):
+        for k in range(count):
+            field = (q * levels + k) * rows
+            padded(now, count, levels, rows, q, k, state[field : field + rows, :], north, south)
+    none = jnp.zeros((rows, LANES), F32)
+    acc = (none, none)
+    for k in range(count - 1):
+        new, acc = advance_level(
+            k, count, levels, rows, now, side[...], lambda x: coef[place_of(x, rows)], acc
+        )
+        for q in range(4):
+            at = (q * (count - 1) + k) * rows
+            top[at : at + rows, :] = new[q]
+
+
+def surface_kernel(
+    rows, levels,
+    state, base, col_map, row_map, coef, side, top, lon_a, lon_b, got_lon_a, got_lon_b, north, south,
+    got_corner_a, got_corner_b, out_in, ids,
+    side_new, north_new, south_new, out, later, stage, places, sem,
+):
+    fields = 4 * levels
     to_scalars = pltpu.make_async_copy(ids, places, sem)
     to_scalars.start()
     out[...] = out_in[...]
-    lat = lax.axis_index("lat")
-    even_lat, even_lon = is_even("lat"), is_even("lon")
-    fold = lat == lat_count - 1
+    even_lon = is_even("lon")
     wet = base[0:rows, :]
-    mixing = base[rows : 2 * rows, :]
     table = base[2 * rows :, :]
-    coriolis = table[PAD : PAD + rows]
     lane = iota((rows, LANES), 1)
     even = (lane & 1) == 0
-
-    def ordered(flag, a, b):
-        return jnp.where(flag, a, b), jnp.where(flag, b, a)
-
-    north, south = ordered(even_lat, got_lat_a[...], got_lat_b[...])
-    length = 2 * fields + 8
-    back = LANES - 1 - iota((8, LANES), 1)
-    flipped = jnp.concatenate(
-        [
-            jnp.take_along_axis(north[i : i + 8], back, axis=1)
-            * (-1.0 if i < 2 * fields and i % fields >= fields // 2 else 1.0)
-            for i in range(0, length, 8)
-        ],
-        axis=0,
-    )
-    straight = north
-    north = jnp.where(fold, flipped, straight)
     lane1 = iota((1, LANES), 1)
     even1 = (lane1 & 1) == 0
-    tail_n, tail_s = straight[2 * fields :], south[2 * fields :]
-    swapped = jnp.where(
-        iota((8, LANES), 1) & 1 == 0, pltpu.roll(tail_n, LANES - 1, 1), pltpu.roll(tail_n, 1, 1)
-    )
-    sign = jnp.where(lane1 >= LANES // 2, -1.0, 1.0)
-    corner_n = jnp.where(fold, swapped[3:4] * sign, tail_n[3:4])
-    corner_s = tail_s[3:4]
-    wet_corner_n = jnp.where(fold, swapped[4:5], tail_n[4:5])
-    wet_corner_s = tail_s[4:5]
-
-    def corner_wet(x):
-        east_wet = jnp.broadcast_to(x[:, 0:1], (1, LANES))
-        west_wet = jnp.broadcast_to(x[:, 1:2], (1, LANES))
-        return east_wet, west_wet, jnp.where(even1, east_wet, west_wet)
-
-    wet_ne, wet_nw, wet_n_lanes = corner_wet(wet_corner_n)
-    wet_se, wet_sw, wet_s_lanes = corner_wet(wet_corner_s)
-
-    north_rows = (north[0:fields], north[fields : 2 * fields], north[2 * fields :])
-    south_rows = (south[0:fields], south[fields : 2 * fields], south[2 * fields :])
-    halo[at.north0] = north_rows[0]
-    halo[at.south0] = south_rows[0]
-
-    wet_pad[PAD : PAD + rows, :] = wet
-    wet_pad[PAD - 1 : PAD, :] = south_rows[2][0:1]
-    wet_pad[PAD + rows : PAD + rows + 1, :] = north_rows[2][0:1]
-    wet_n = wet_pad[PAD + 1 : PAD + 1 + rows, :]
-    wet_s = wet_pad[PAD - 1 : PAD - 1 + rows, :]
+
+    corner_e, corner_w = ordered(even_lon, got_corner_a[...], got_corner_b[...])
+
+    def corner(i):
+        wets = corner_e[2 + i : 3 + i, 0:1], corner_w[2 + i : 3 + i, 1:2]
+        return jnp.where(even1, corner_e[i : i + 1], corner_w[i : i + 1]), *wets
+
+    corner_n, wet_ne, wet_nw = corner(0)
+    corner_s, wet_se, wet_sw = corner(1)
 
     def spread(x, i):
         return jnp.broadcast_to(x[:, i : i + 1], (rows, LANES))
 
     aux_e, aux_w = ordered(even_lon, got_lon_a[rows:, :], got_lon_b[rows:, :])
-    wet_col_e, wet_col_w = spread(aux_e, 0), spread(aux_w, 0)
-    wet_e = jnp.where(lane == LANES - 1, wet_col_e, pltpu.roll(wet, LANES - 1, 1))
-    wet_w = jnp.where(lane == 0, wet_col_w, pltpu.roll(wet, 1, 1))
-    made = coefficients(wet, (wet_e, wet_w, wet_n, wet_s), mixing, coriolis)
-    for name in COEFFICIENTS:
-        halo[getattr(at, name)] = made[name]
-
-    def coef(name):
-        return halo[getattr(at, name)]
-
     got_e, got_w = ordered(even_lon, got_lon_a[0:rows, :], got_lon_b[0:rows, :])
     sent_e, sent_w = ordered(even_lon, lon_a[0:rows, :], lon_b[0:rows, :])
-    side = jnp.where(even, got_e, got_w)
     outer = jnp.where(even, pltpu.roll(got_e, LANES - 1, 1), pltpu.roll(got_w, 1, 1))
     inner = jnp.where(even, pltpu.roll(sent_e, LANES - 1, 1), pltpu.roll(sent_w, 1, 1))
-    halo[at.side0] = side
-    halo[at.side1] = advance_columns(
-        side, outer, inner, corner_n, corner_s,
+    side_new[...] = advance_columns(
+        side[...], outer, inner, corner_n, corner_s,
         (
-            jnp.where(even, wet_col_e, wet_col_w),
+            jnp.where(even, spread(aux_e, 0), spread(aux_w, 0)),
             jnp.where(even, spread(aux_e, 1), spread(aux_w, 1)),
             jnp.where(even, spread(wet, LANES - 1), spread(wet, 0)),
-            wet_n_lanes,
-            wet_s_lanes,
+            jnp.where(even1, wet_ne, wet_nw),
+            jnp.where(even1, wet_se, wet_sw),
         ),
         jnp.where(even, spread(aux_e, 2), spread(aux_w, 2)),
-        coriolis, col_map[...],
+        table[PAD : PAD + rows], col_map[...],
     )
 
     field_lane = iota((fields, LANES), 1)
@@ -475,43 +476,35 @@
         here = field_lane == 2 * field_id + parity
         return jnp.sum(jnp.where(here, x, 0.0), axis=1, keepdims=True)
 
-    inside_n, inside_s = ordered(even_lat, lat_a[0:fields, :], lat_b[0:fields, :])
     parts = []
-    for north_side, (mid, outside, tail), inside, corner, corner_wets, line, lat_row in (
-        (True, north_rows, inside_n, corner_n, (wet_ne, wet_nw), rows - 1, PAD + rows),
-        (False, south_rows, inside_s, corner_s, (wet_se, wet_sw), 0, PAD - 1),
+    for north_side, ref, ends, corner_wets, line, lat_row in (
+        (True, north, corner_n, (wet_ne, wet_nw), rows - 1, PAD + rows),
+        (False, south, corner_s, (wet_se, wet_sw), 0, PAD - 1),
     ):
-        pair = (outside, inside), (tail[1:2], wet[line : line + 1])
-        (n, s), (wet_n1, wet_s1) = pair if north_side else [x[::-1] for x in pair]
+        inside = state[pl.ds(line, fields, stride=rows), :]
+        tail = ref[2 * fields :, :]
+        pair = (ref[fields : 2 * fields, :], inside), (tail[1:2], wet[line : line + 1])
+        (n, s), (wet_n, wet_s) = pair if north_side else [x[::-1] for x in pair]
         parts.append(
             (
-                mid, n, s, (to_sublanes(corner, 0), to_sublanes(corner, 1)),
-                (tail[0:1], wet_n1, wet_s1, *corner_wets),
+                ref[0:fields, :], n, s, (to_sublanes(ends, 0), to_sublanes(ends, 1)),
+                (tail[0:1], wet_n, wet_s, *corner_wets),
                 tail[2:3], table[lat_row : lat_row + 1],
             )
         )
-    halo[at.north1], halo[at.south1] = advance_rows(levels, parts, row_map[...])
-
-    count = now.shape[0] // (4 * pitch)
-
-    def put(buf, q, k, value, north, south):
-        base = (q * count + k) * pitch + PAD
-        n, s = north.start + q * levels + k, south.start + q * levels + k
-        buf[base : base + rows, :] = value
-        buf[base + rows : base + rows + 1, :] = halo[n : n + 1, :]
-        buf[base - 1 : base, :] = halo[s : s + 1, :]
-
+    north_new[...], south_new[...] = advance_rows(levels, parts, row_map[...])
+
+    count = later.shape[0] // (4 * (rows + 2 * PAD))
     for q in range(4):
         for k in range(count):
-            field = (q * levels + k) * rows
-            put(now, q, k, state[field : field + rows, :], at.north0, at.south0)
+            at = (q * count + k) * rows
+            padded(
+                later, count, levels, rows, q, k, top[at : at + rows, :], north_new, south_new
+            )
     none = jnp.zeros((rows, LANES), F32)
-    acc = (none, none)
-    for k in range(count - 1):
-        new, acc = advance_level(k, count, levels, rows, now, halo[at.side0], coef, acc)
-        for q in range(4):
-            put(later, q, k, new[q], at.north1, at.south1)
-    new, _ = advance_level(0, count, levels, rows, later, halo[at.side1], coef, (none, none))
+    new, _ = advance_level(
+        0, count, levels, rows, later, side_new[...], lambda x: coef[place_of(x, rows)], (none, none)
+    )
     for q in range(4):
         stage[pl.ds(q, rows, stride=4), :] = new[q]
     to_scalars.wait()
@@ -520,14 +513,15 @@
 
 
 def main_kernel(
-    rows, levels, chunks, state, halo, tr_hbm, ve_hbm, now, later, tr_out, ve_out, sems
+    rows, levels, chunks,
+    state, coefs, side, side_new, north, south, north_new, south_new,
+    tr_hbm, ve_hbm, now, later, tr_out, ve_out, sems,
 ):
     fields = 4 * levels
     pitch = rows + 2 * PAD
-    at = Halo(rows, fields)
-    for buf, north, south in ((now, at.north0, at.south0), (later, at.north1, at.south1)):
-        buf[pl.ds(PAD - 1, fields, stride=pitch), :] = halo[south]
-        buf[pl.ds(PAD + rows, fields, stride=pitch), :] = halo[north]
+    for buf, n, s in ((now, north, south), (later, north_new, south_new)):
+        buf[pl.ds(PAD - 1, fields, stride=pitch), :] = s[0:fields, :]
+        buf[pl.ds(PAD + rows, fields, stride=pitch), :] = n[0:fields, :]
 
     def fill(f, carry):
         x = state[pl.ds(pl.multiple_of(f * rows, 8), rows), :]
@@ -537,17 +531,17 @@
     lax.fori_loop(0, fields, fill, 0, unroll=8)
 
     def coef(name):
-        return halo[getattr(at, name)]
+        return coefs[place_of(name, rows)]
 
     def first(k, acc):
-        new, acc = advance_level(k, levels, levels, rows, now, halo[at.side0], coef, acc)
+        new, acc = advance_level(k, levels, levels, rows, now, side[...], coef, acc)
         for q in range(4):
             place = pl.multiple_of((q * levels + k) * pitch + PAD, 8)
             later[pl.ds(place, rows), :] = new[q]
         return acc
 
     def second(k, acc):
-        new, acc = advance_level(k, levels, levels, rows, later, halo[at.side1], coef, acc)
+        new, acc = advance_level(k, levels, levels, rows, later, side_new[...], coef, acc)
         for q in range(4):
             ref = tr_out if q < 2 else ve_out
             place = pl.multiple_of(((q % 2) * levels + k) * rows, 8)
@@ -639,28 +633,37 @@
     smem = pl.BlockSpec(memory_space=pltpu.SMEM)
     vmem = pl.BlockSpec(memory_space=pltpu.VMEM)
 
-    chunks = 2
-    tr, ve = tracers.reshape(flat, cols), velocity.reshape(flat, cols)
-    lon_a, lon_b = call(
-        functools.partial(pack_kernel, rows, fields, chunks),
-        [shaped(2 * rows, cols)] * 2,
+    deep = (2 * levels, rows, cols)
+    lat_a, lat_b = call(
+        functools.partial(edge_kernel, rows, fields),
+        [shaped(length, cols)] * 2,
         limit=VMEM_ALL,
         in_specs=[hbm] * 4,
         scratch_shapes=[
-            pltpu.VMEM((flat, cols), F32),
-            pltpu.VMEM((flat, cols), F32),
+            pltpu.VMEM((2, fields, 8, cols), F32),
             pltpu.VMEM((rows, cols), jnp.int32),
             pltpu.VMEM((rows, cols), F32),
-            pltpu.SemaphoreType.DMA((2 + 2 * chunks,)),
+            pltpu.SemaphoreType.DMA((6,)),
         ],
+    )(tracers.reshape(deep), velocity.reshape(deep), land_mask, mixing)
+    swaps = pairs_of(lon_count, lat_count)
+    got_lat_b = lax.ppermute(lat_b, ("lon", "lat"), swaps[3])
+    got_lat_a = lax.ppermute(lat_a, ("lon", "lat"), swaps[2])
+
+    tr, ve = tracers.reshape(flat, cols), velocity.reshape(flat, cols)
+    lon_a, lon_b = call(
+        functools.partial(pack_kernel, rows, fields),
+        [shaped(2 * rows, cols)] * 2,
+        in_specs=[vmem] * 4,
     )(tr, ve, land_mask, mixing)
+    got_lon_a = lax.ppermute(lon_a, "lon", swaps[0])
+    got_lon_b = lax.ppermute(lon_b, "lon", swaps[1])
 
     slot_rows = 5 * CAP + 1
-    state, lat_a, lat_b, base, col_map, row_map, outgoing, ids = call(
+    state, base, col_map, row_map, outgoing, ids = call(
         functools.partial(prepare_kernel, rows, levels, devices),
-        [shaped(fields * rows, cols)]
-        + [shaped(length, cols)] * 2
-        + [
+        [
+            shaped(fields * rows, cols),
             shaped(2 * rows + pitch, cols),
             shaped(3 * cols, cols),
             shaped(fields + levels, cols),
@@ -671,39 +674,43 @@
         scratch_shapes=[pltpu.SMEM((devices,), jnp.int32)],
     )(tr, ve, land_mask, mixing, owners.reshape(rows), atm_row)
 
-    swaps = pairs_of(lon_count, lat_count)
-    got_lon_a = lax.ppermute(lon_a, "lon", swaps[0])
-    got_lon_b = lax.ppermute(lon_b, "lon", swaps[1])
-
-    tail = pl.BlockSpec((8, cols), lambda i: (length // 8 - 1, 0))
-    whole = pl.BlockSpec((2 * rows, cols), lambda i: (0, 0))
-    lat_a, lat_b = call(
-        functools.partial(corner_kernel, rows),
-        [shaped(length, cols), shaped(length, cols)],
-        grid=(1,),
-        in_specs=[tail, tail, whole, whole],
-        out_specs=[tail, tail],
-        input_output_aliases={0: 0, 1: 1},
-    )(lat_a, lat_b, got_lon_a, got_lon_b)
-    got_lat_a = lax.ppermute(lat_a, ("lon", "lat"), swaps[2])
-    got_lat_b = lax.ppermute(lat_b, ("lon", "lat"), swaps[3])
-
-    at = Halo(rows, fields)
+    north, south, corners = call(
+        functools.partial(corner_kernel, lat_count, fields),
+        [shaped(length, cols), shaped(length, cols), shaped(8, cols)],
+    )(got_lat_a, got_lat_b)
+    got_corner_a = lax.ppermute(corners, "lon", swaps[0])
+    got_corner_b = lax.ppermute(corners, "lon", swaps[1])
+
     count = min(3, levels)
-    halo, outgoing = call(
-        functools.partial(surface_kernel, rows, levels, lat_count),
-        [shaped(at.size, cols), shaped(devices * slot_rows, cols)],
-        in_specs=[vmem] * 14,
+    coefs, side, top = call(
+        functools.partial(first_kernel, rows, levels),
+        [
+            shaped(len(COEFFICIENTS) * rows, cols),
+            shaped(rows, cols),
+            shaped(4 * (count - 1) * rows, cols),
+        ],
         scratch_shapes=[
             pltpu.VMEM((4 * count * pitch, cols), F32),
-            pltpu.VMEM((4 * count * pitch, cols), F32),
             pltpu.VMEM((pitch, cols), F32),
+        ],
+    )(state, base, got_lon_a, got_lon_b, north, south)
+
+    side_new, north_new, south_new, outgoing = call(
+        functools.partial(surface_kernel, rows, levels),
+        [
+            shaped(rows, cols),
+            shaped(fields, cols),
+            shaped(fields, cols),
+            shaped(devices * slot_rows, cols),
+        ],
+        scratch_shapes=[
+            pltpu.VMEM((4 * (count - 1) * pitch, cols), F32),
             pltpu.VMEM((4 * rows, cols), F32),
             pltpu.SMEM((8, cols), jnp.int32),
             pltpu.SemaphoreType.DMA,
         ],
-    )(state, base, col_map, row_map, lon_a, lon_b, got_lon_a, got_lon_b, lat_a, lat_b, got_lat_a,
-      got_lat_b, outgoing, ids)
+    )(state, base, col_map, row_map, coefs, side, top, lon_a, lon_b, got_lon_a, got_lon_b, north,
+      south, got_corner_a, got_corner_b, outgoing, ids)
     incoming = lax.all_to_all(
         outgoing.reshape(devices, slot_rows, 1, cols), ("lon", "lat"), 0, 0, tiled=True
     ).reshape(devices * slot_rows, cols)
@@ -712,7 +719,7 @@
     tr_out, ve_out = call(
         functools.partial(main_kernel, rows, levels, chunks),
         [shaped(flat, cols), shaped(flat, cols)],
-        in_specs=[vmem] * 2,
+        in_specs=[vmem] * 8,
         out_specs=[hbm] * 2,
         scratch_shapes=[
             pltpu.VMEM((fields * pitch, cols), F32),
@@ -724,7 +731,7 @@
         cost_estimate=pl.CostEstimate(
             flops=80 * fields * rows * cols, bytes_accessed=5 << 20, transcendentals=0
         ),
-    )(state, halo)
+    )(state, coefs, side, side_new, north, south, north_new, south_new)
     surface, cover = call(
         functools.partial(reduce_kernel, devices),
         [shaped(4, ATM_ROWS, cols), shaped(ATM_ROWS, cols)],

time: 34.4 us -> 33.8 us (0.983)
  starting transfers between devices: 14.9 us -> 13.6 us
  Pallas kernels: 10.7 us -> 11.1 us
    all_to_all x1, starting transfers between devices: 9.71 us -> 6.71 us  [local(): lax.all_to_all(outgoing.reshape(devices, slot_rows, 1, cols), ('lon', 'la...]
    ppermute x0 -> x2, waiting for transfers between devices: none -> 1.77 us  [the longest x1 1.27 us: local(): got_corner_b = lax.ppermute(corners, 'lon', swaps[1])]
    ppermute x0 -> x2, starting transfers between devices: none -> 1.64 us  [the longest x1 1.5 us: local(): got_corner_b = lax.ppermute(corners, 'lon', swaps[1])]
    ppermute x1, waiting for transfers between devices: 1.29 us -> 0.43 us  [local(): got_lon_b = lax.ppermute(lon_b, 'lon', swaps[1])]
    ppermute x1, waiting for transfers between devices: 0.57 us -> 0.01 us  [local(): got_lat_a = lax.ppermute(lat_a, ('lon', 'lat'), swaps[2])]
    ppermute x1, starting transfers between devices: 0.01 us -> 0.52 us  [local(): got_lat_a = lax.ppermute(lat_a, ('lon', 'lat'), swaps[2])]
    pallas_call x3 -> x5, Pallas kernels: 4.61 us -> 5.05 us  [the longest x1 1.93 us: local(): call(functools.partial(edge_kernel, rows, fields), [shaped(length, cols)]...]
    ppermute x1, starting transfers between devices: 3 us -> 2.58 us  [local(): got_lon_a = lax.ppermute(lon_a, 'lon', swaps[0])]
  transfers between devices with their start and end apart: 5 -> 7, of which waited for: 3 -> 4; matrix products, arithmetic and copies ran while one was open for 0% -> 0% of each run, Pallas kernels for 15% -> 20%
where the time goes in v4:
time: 33.8 us; the launch traced here: 33.3 us
  starting transfers between devices  13.6 us (40%)
  Pallas kernels  11.1 us (33%)
  waiting for transfers between devices  6.8 us (20%)
  local copies, waits for them, and re-layouts  1.07 us (3%)
  between operations  0.78 us (2%)
    all_to_all x1, starting transfers between devices, local(): lax.all_to_all(outgoing.reshape(devices, slot_rows, 1, cols), ('lon', 'la...  6.71 us
    all_to_all x1, waiting for transfers between devices, local(): lax.all_to_all(outgoing.reshape(devices, slot_rows, 1, cols), ('lon', 'la...  4.6 us
    pallas_call x1, Pallas kernels, local(): call(functools.partial(main_kernel, rows, levels, chunks), [shaped(flat,...  4 us
    ppermute x1, starting transfers between devices, local(): got_lon_a = lax.ppermute(lon_a, 'lon', swaps[0])  2.58 us
    pallas_call x1, Pallas kernels, local(): call(functools.partial(edge_kernel, rows, fields), [shaped(length, cols)]...  1.93 us
    pallas_call x1, Pallas kernels, local(): call(functools.partial(surface_kernel, rows, levels), [shaped(rows, cols)...  1.57 us
    ppermute x1, starting transfers between devices, local(): got_corner_b = lax.ppermute(corners, 'lon', swaps[1])  1.5 us
    ppermute x1, starting transfers between devices, local(): got_lon_b = lax.ppermute(lon_b, 'lon', swaps[1])  1.49 us
  transfers between devices with their start and end apart: 7, of which 4 were waited for; matrix products, arithmetic and copies ran while one was open for 0% of the time, Pallas kernels for 20%

profile of v4, /device:TPU:0, one launch (start us, length us, event | category | flops | bytes accessed | tf_op | source)
XLA Modules:
  0.0 33.3 jit_solution(245814362385904205)
XLA Ops:
  0.6 0.0 copy-start
  0.6 0.0 copy-start.3
  0.7 0.0 copy-start.4
  0.7 1.9 %shard_map.95 = (f32[136,128]{1,0:T(8,128)}, f32[136,128]{1,0:T(8,128)}) custom-call(f32[32,32,128]{2,1,0:T(8,128)} %bitcast.9, f32[32,32,128]{2,1,0:T(8,128)} %bitcast.12, s32[32,128]{1,0:T(8,128)} %mask_hbm.1, f32[32,128]{1,0:T(8,128)} %mix_hbm.1), custom_call_target="tpu_custom_call" | custom-call | tf_op jit(solution)/shard_map/pallas_call | solution.py:637
  2.6 0.5 %collective-permute-start.2 = (f32[136,128]{1,0:T(8,128)}, f32[136,128]{1,0:T(8,128)S(1)}, u32[]{:S(2)}, u32[]{:S(2)}) collective-permute-start(f32[136,128]{1,0:T(8,128)} %get-tuple-element.32), channel_id=1, source_target_pairs={{0,1},{1,0},{2,3},{3,2},{4,5},{5,4},{6,7},{7,6},{8,9},{9,8},{10,11... | collective-permute-start | bytes 208904 | tf_op jit(solution)/shard_map/ppermute | solution.py:651
  3.1 0.7 %collective-permute-start.3 = (f32[136,128]{1,0:T(8,128)}, f32[136,128]{1,0:T(8,128)S(1)}, u32[]{:S(2)}, u32[]{:S(2)}) collective-permute-start(f32[136,128]{1,0:T(8,128)} %get-tuple-element.33), channel_id=1, source_target_pairs={{1,2},{2,1},{3,4},{4,3},{5,6},{6,5},{7,31},{9,10},{10,9},{11,12},{... | collective-permute-start | bytes 208904 | tf_op jit(solution)/shard_map/ppermute | solution.py:650
  3.8 0.0 copy-done
  3.8 0.0 copy-done.3
  3.8 0.0 copy-done.4
  3.8 0.0 copy-start.1
  3.8 1.0 %copy-done.1 = f32[2,16,32,128]{3,2,1,0:T(8,128)S(1)} copy-done((f32[2,16,32,128]{3,2,1,0:T(8,128)S(1)}, f32[2,16,32,128]{3,2,1,0:T(8,128)}, u32[]{:S(2)}) %copy-start.1) | copy-done | bytes 524312
  4.9 0.0 copy-start.2
  4.9 1.2 %shard_map.94 = (f32[64,128]{1,0:T(8,128)S(1)}, f32[64,128]{1,0:T(8,128)S(1)}) custom-call(f32[1024,128]{1,0:T(8,128)S(1)} %bitcast.10, f32[1024,128]{1,0:T(8,128)S(1)} %bitcast.13, s32[32,128]{1,0:T(8,128)S(1)} %copy-done.3, f32[32,128]{1,0:T(8,128)S(1)} %copy-done.4), custom_call_target="tpu_custom_call" | custom-call | tf_op jit(solution)/shard_map/pallas_call | solution.py:654
  6.0 2.6 %collective-permute-start = (f32[64,128]{1,0:T(8,128)S(1)}, f32[64,128]{1,0:T(8,128)S(1)}, u32[]{:S(2)}, u32[]{:S(2)}) collective-permute-start(f32[64,128]{1,0:T(8,128)S(1)} %get-tuple-element.30.lon_a), channel_id=1, source_target_pairs={{0,8},{8,0},{16,24},{24,16},{1,9},{9,1},{17,25},{25,17},{2,10},{10... | collective-permute-start | bytes 98312 | tf_op jit(solution)/shard_map/ppermute | solution.py:659
  8.6 1.5 %collective-permute-start.1 = (f32[64,128]{1,0:T(8,128)S(1)}, f32[64,128]{1,0:T(8,128)S(1)}, u32[]{:S(2)}, u32[]{:S(2)}) collective-permute-start(f32[64,128]{1,0:T(8,128)S(1)} %get-tuple-element.31.lon_b), channel_id=1, source_target_pairs={{0,24},{8,16},{16,8},{24,0},{1,25},{9,17},{17,9},{25,1},{2,26},{10... | collective-permute-start | bytes 98312 | tf_op jit(solution)/shard_map/ppermute | solution.py:660
  10.1 0.0 collective-permute-done.2.got_a
  10.1 0.0 collective-permute-done.3.got_b
  10.1 0.2 shard_map.96
  10.3 0.0 copy-start.5
  10.3 0.0 copy-start.6
  10.3 1.5 %collective-permute-start.5 = (f32[8,128]{1,0:T(8,128)S(1)}, f32[8,128]{1,0:T(8,128)S(1)}, u32[]{:S(2)}, u32[]{:S(2)}) collective-permute-start(f32[8,128]{1,0:T(8,128)S(1)} %get-tuple-element.41), channel_id=1, source_target_pairs={{0,24},{8,16},{16,8},{24,0},{1,25},{9,17},{17,9},{25,1},{2,26},{10... | collective-permute-start | bytes 12296 | tf_op jit(solution)/shard_map/ppermute | solution.py:682
  11.8 0.1 collective-permute-start.4
  11.9 0.0 copy-done.2
  11.9 0.0 copy-done.5
  11.9 0.0 copy-done.6
  12.0 1.0 %shard_map.93 = (f32[2048,128]{1,0:T(8,128)S(1)}, f32[112,128]{1,0:T(8,128)S(1)}, f32[384,128]{1,0:T(8,128)S(1)}, f32[80,128]{1,0:T(8,128)S(1)}, f32[352,128]{1,0:T(8,128)S(1)}, /*index=5*/s32[8,128]{1,0:T(8,128)S(1)}) custom-call(f32[1024,128]{1,0:T(8,128)S(1)} %bitcast.11, f32[1024,128]{1,0:T(8,128)S(1)} %bitcast.14, s32[32,128]{1,0:T(8,128)S(1)} %copy-done.3, ...), custom_call_target="tpu_custom_call" | custom-call | tf_op jit(solution)/shard_map/pallas_call | solution.py:663
  13.0 0.0 collective-permute-done.got_lon_a
  13.0 0.4 %collective-permute-done.1.got_lon_b = f32[64,128]{1,0:T(8,128)S(1)} collective-permute-done((f32[64,128]{1,0:T(8,128)S(1)}, f32[64,128]{1,0:T(8,128)S(1)}, u32[]{:S(2)}, u32[]{:S(2)}) %collective-permute-start.1) | collective-permute-done | bytes 32800 | tf_op jit(solution)/shard_map/ppermute | solution.py:660
  13.4 0.2 shard_map.97
  13.6 1.3 %collective-permute-done.5.got_corner_b = f32[8,128]{1,0:T(8,128)S(1)} collective-permute-done((f32[8,128]{1,0:T(8,128)S(1)}, f32[8,128]{1,0:T(8,128)S(1)}, u32[]{:S(2)}, u32[]{:S(2)}) %collective-permute-start.5) | collective-permute-done | bytes 4128 | tf_op jit(solution)/shard_map/ppermute | solution.py:682
  14.9 0.5 %collective-permute-done.4.got_corner_a = f32[8,128]{1,0:T(8,128)S(1)} collective-permute-done((f32[8,128]{1,0:T(8,128)S(1)}, f32[8,128]{1,0:T(8,128)S(1)}, u32[]{:S(2)}, u32[]{:S(2)}) %collective-permute-start.4) | collective-permute-done | bytes 4128 | tf_op jit(solution)/shard_map/ppermute | solution.py:681
  15.4 1.6 %shard_map.98 = (f32[32,128]{1,0:T(8,128)S(1)}, f32[64,128]{1,0:T(8,128)S(1)}, f32[64,128]{1,0:T(8,128)S(1)}, f32[352,128]{1,0:T(8,128)}) custom-call(f32[2048,128]{1,0:T(8,128)S(1)} %get-tuple-element.28.state, f32[112,128]{1,0:T(8,128)S(1)} %get-tuple-element.29.base, f32[384,128]{1,0:T(8,128)S(1)} %get-tuple-element.38.col_map, ...), custom_call_target="tpu_custom_call" | custom-call | tf_op jit(solution)/shard_map/pallas_call | solution.py:698
  17.0 6.7 %all-to-all-start = ((f32[32,11,1,128]{3,2,1,0:T(1,128)}), f32[32,11,1,128]{3,2,1,0:T(1,128)S(1)}, u32[]{:S(2)}, u32[]{:S(2)}) async-start(f32[32,11,1,128]{3,2,1,0:T(1,128)} %bitcast.7), calls=%async_computation | async-start | bytes 360448 | tf_op jit(solution)/shard_map/all_to_all | solution.py:714
  23.7 4.0 %shard_map.99 = (f32[1024,128]{1,0:T(8,128)}, f32[1024,128]{1,0:T(8,128)}) custom-call(f32[2048,128]{1,0:T(8,128)S(1)} %get-tuple-element.28.state, f32[416,128]{1,0:T(8,128)S(1)} %get-tuple-element.36.coef.coefs, f32[32,128]{1,0:T(8,128)S(1)} %get-tuple-element.37.side, f32[32,128]{1,0:T(8,128)S(1)} %get-tuple-element.44.side_new, ...), custom_call_target="tpu_custom_call" | custom-call | flops 20971520 | bytes 5242880 | tf_op jit(solution)/shard_map/pallas_call | solution.py:719
  27.7 4.6 %all-to-all-done = f32[32,11,1,128]{3,2,1,0:T(1,128)S(1)} async-done(((f32[32,11,1,128]{3,2,1,0:T(1,128)}), f32[32,11,1,128]{3,2,1,0:T(1,128)S(1)}, u32[]{:S(2)}, u32[]{:S(2)}) %all-to-all-start) | async-done | bytes 180256 | tf_op jit(solution)/shard_map/all_to_all | solution.py:714
  32.3 1.0 %shard_map.100 = (f32[4,32,128]{2,1,0:T(8,128)}, f32[32,128]{1,0:T(8,128)}) custom-call(f32[352,128]{1,0:T(8,128)S(1)} %bitcast.15), custom_call_target="tpu_custom_call" | custom-call | tf_op jit(solution)/shard_map/pallas_call | solution.py:735
Async XLA Ops:
  0.6 3.1 %copy-start = (f32[2,16,32,128]{3,2,1,0:T(8,128)S(1)}, f32[2,16,32,128]{3,2,1,0:T(8,128)}, u32[]{:S(2)}) copy-start(f32[2,16,32,128]{3,2,1,0:T(8,128)} %param.6) | copy-start | bytes 1572868
  0.6 3.1 %copy-start.3 = (s32[32,128]{1,0:T(8,128)S(1)}, s32[32,128]{1,0:T(8,128)}, u32[]{:S(2)}) copy-start(s32[32,128]{1,0:T(8,128)} %mask_hbm.1) | copy-start | bytes 49156
  0.7 3.1 %copy-start.4 = (f32[32,128]{1,0:T(8,128)S(1)}, f32[32,128]{1,0:T(8,128)}, u32[]{:S(2)}) copy-start(f32[32,128]{1,0:T(8,128)} %mix_hbm.1) | copy-start | bytes 49156
  2.6 7.5 %collective-permute-start.2 = (f32[136,128]{1,0:T(8,128)}, f32[136,128]{1,0:T(8,128)S(1)}, u32[]{:S(2)}, u32[]{:S(2)}) collective-permute-start(f32[136,128]{1,0:T(8,128)} %get-tuple-element.32), channel_id=1, source_target_pairs={{0,1},{1,0},{2,3},{3,2},{4,5},{5,4},{6,7},{7,6},{8,9},{9,8},{10,11... | collective-permute-start | bytes 208904 | tf_op jit(solution)/shard_map/ppermute | solution.py:651
  3.1 7.0 %collective-permute-start.3 = (f32[136,128]{1,0:T(8,128)}, f32[136,128]{1,0:T(8,128)S(1)}, u32[]{:S(2)}, u32[]{:S(2)}) collective-permute-start(f32[136,128]{1,0:T(8,128)} %get-tuple-element.33), channel_id=1, source_target_pairs={{1,2},{2,1},{3,4},{4,3},{5,6},{6,5},{7,31},{9,10},{10,9},{11,12},{... | collective-permute-start | bytes 208904 | tf_op jit(solution)/shard_map/ppermute | solution.py:650
  3.8 1.0 %copy-start.1 = (f32[2,16,32,128]{3,2,1,0:T(8,128)S(1)}, f32[2,16,32,128]{3,2,1,0:T(8,128)}, u32[]{:S(2)}) copy-start(f32[2,16,32,128]{3,2,1,0:T(8,128)} %param.7) | copy-start | bytes 1572868
  4.9 7.1 %copy-start.2 = (f32[2,16,32,128]{3,2,1,0:T(8,128)S(1)}, f32[2,16,32,128]{3,2,1,0:T(8,128)}, u32[]{:S(2)}) copy-start(f32[2,16,32,128]{3,2,1,0:T(8,128)} %param.7) | copy-start | bytes 1572868
  6.0 7.0 %collective-permute-start = (f32[64,128]{1,0:T(8,128)S(1)}, f32[64,128]{1,0:T(8,128)S(1)}, u32[]{:S(2)}, u32[]{:S(2)}) collective-permute-start(f32[64,128]{1,0:T(8,128)S(1)} %get-tuple-element.30.lon_a), channel_id=1, source_target_pairs={{0,8},{8,0},{16,24},{24,16},{1,9},{9,1},{17,25},{25,17},{2,10},{10... | collective-permute-start | bytes 98312 | tf_op jit(solution)/shard_map/ppermute | solution.py:659
  8.6 4.8 %collective-permute-start.1 = (f32[64,128]{1,0:T(8,128)S(1)}, f32[64,128]{1,0:T(8,128)S(1)}, u32[]{:S(2)}, u32[]{:S(2)}) collective-permute-start(f32[64,128]{1,0:T(8,128)S(1)} %get-tuple-element.31.lon_b), channel_id=1, source_target_pairs={{0,24},{8,16},{16,8},{24,0},{1,25},{9,17},{17,9},{25,1},{2,26},{10... | collective-permute-start | bytes 98312 | tf_op jit(solution)/shard_map/ppermute | solution.py:660
  10.3 1.7 %copy-start.5 = (s32[32,1]{0,1:T(1,128)S(1)}, s32[32,1]{0,1:T(1,128)}, u32[]{:S(2)}) copy-start(s32[32,1]{0,1:T(1,128)} %param.10) | copy-start | bytes 388
  10.3 1.7 %copy-start.6 = (s32[32]{0:T(128)S(1)}, s32[32]{0:T(128)}, u32[]{:S(2)}) copy-start(s32[32]{0:T(128)} %atm_row.1) | copy-start | bytes 388
  10.3 4.6 %collective-permute-start.5 = (f32[8,128]{1,0:T(8,128)S(1)}, f32[8,128]{1,0:T(8,128)S(1)}, u32[]{:S(2)}, u32[]{:S(2)}) collective-permute-start(f32[8,128]{1,0:T(8,128)S(1)} %get-tuple-element.41), channel_id=1, source_target_pairs={{0,24},{8,16},{16,8},{24,0},{1,25},{9,17},{17,9},{25,1},{2,26},{10... | collective-permute-start | bytes 12296 | tf_op jit(solution)/shard_map/ppermute | solution.py:682
  11.8 3.6 %collective-permute-start.4 = (f32[8,128]{1,0:T(8,128)S(1)}, f32[8,128]{1,0:T(8,128)S(1)}, u32[]{:S(2)}, u32[]{:S(2)}) collective-permute-start(f32[8,128]{1,0:T(8,128)S(1)} %get-tuple-element.41), channel_id=1, source_target_pairs={{0,8},{8,0},{16,24},{24,16},{1,9},{9,1},{17,25},{25,17},{2,10},{10... | collective-permute-start | bytes 12296 | tf_op jit(solution)/shard_map/ppermute | solution.py:681
  17.0 15.3 %all-to-all-start = ((f32[32,11,1,128]{3,2,1,0:T(1,128)}), f32[32,11,1,128]{3,2,1,0:T(1,128)S(1)}, u32[]{:S(2)}, u32[]{:S(2)}) async-start(f32[32,11,1,128]{3,2,1,0:T(1,128)} %bitcast.7), calls=%async_computation | async-start | bytes 360448 | tf_op jit(solution)/shard_map/all_to_all | solution.py:714

commit v5 on v4

--- a/solution.py
+++ b/solution.py
@@ -24,7 +24,7 @@
 EXACT = lax.Precision.HIGHEST
 F32 = jnp.float32
 VMEM_LIMIT = 32 * 1024 * 1024
-VMEM_ALL = 63 * 1024 * 1024
+VMEM_ALL = 62 * 1024 * 1024
 
 
 def iota(shape, dim):
@@ -73,7 +73,7 @@
         buf[2 * fields + 2 : 2 * fields + 3, :] = mix[pl.ds(near, 1), :]
 
 
-def pack_kernel(rows, fields, tr, ve, mask, mix, lon_a, lon_b):
+def pack_kernel(rows, fields, tr, ve, mask, mix, cols):
     half = fields // 2
     wet = mask[...].astype(F32)
     lane = iota((rows, LANES), 1)
@@ -94,25 +94,20 @@
     carry = (jnp.zeros((rows, LANES), F32), jnp.zeros((rows, LANES), F32))
     for ref, base in ((tr, 0), (ve, half)):
         carry = lax.fori_loop(0, half, columns(ref, base), carry, unroll=8)
-    mixing = mix[...]
-    aux_east = jnp.where(
-        lane == 0,
-        pltpu.roll(wet, 1, 1),
-        jnp.where(lane == 1, pltpu.roll(wet, 3, 1), pltpu.roll(mixing, 3, 1)),
-    )
-    aux_west = jnp.where(lane <= 1, wet, pltpu.roll(mixing, 2, 1))
-
     def spread(x, i):
         return jnp.broadcast_to(x[:, i : i + 1], (rows, LANES))
 
     odd = (lane & 1) == 1
-    to_east = carry[0] * jnp.where(odd, spread(wet, LANES - 1), spread(wet, LANES - 2))
-    to_west = carry[1] * jnp.where(odd, spread(wet, 1), spread(wet, 0))
-    even = is_even("lon")
-    lon_a[0:rows, :] = jnp.where(even, to_east, to_west)
-    lon_b[0:rows, :] = jnp.where(even, to_west, to_east)
-    lon_a[rows : 2 * rows, :] = jnp.where(even, aux_east, aux_west)
-    lon_b[rows : 2 * rows, :] = jnp.where(even, aux_west, aux_east)
+    cols[0:rows, :] = carry[0] * jnp.where(odd, spread(wet, LANES - 1), spread(wet, LANES - 2))
+    cols[rows : 2 * rows, :] = carry[1] * jnp.where(odd, spread(wet, 1), spread(wet, 0))
+    cols[2 * rows :, :] = jnp.zeros((8, LANES), F32)
+    row = iota((rows, LANES), 0)
+    mixing = mix[...]
+    for i, (near, far) in enumerate(((LANES - 1, LANES - 2), (0, 1))):
+        line = jnp.zeros((rows, LANES), F32)
+        for part, column in enumerate((wet[:, near], wet[:, far], mixing[:, near])):
+            line = jnp.where(lane == part * rows + row, column[:, None], line)
+        cols[2 * rows + i : 2 * rows + i + 1, :] = jnp.sum(line, axis=0, keepdims=True)
 
 
 def prepare_kernel(
@@ -181,7 +176,7 @@
     ids[0:1, :] = places
 
 
-def corner_kernel(lat_count, fields, got_a, got_b, north, south, corners):
+def corner_kernel(lat_count, lon_count, rows, fields, got_a, got_b, cols, north, south, message):
     fold = lax.axis_index("lat") == lat_count - 1
     even = is_even("lat")
     a, b = got_a[...], got_b[...]
@@ -199,15 +194,62 @@
     north[...] = jnp.where(fold, flipped, straight)
     lane, field = iota((fields, LANES), 1), iota((fields, LANES), 0)
     lane1 = iota((1, LANES), 1)
-    corners[...] = jnp.zeros(corners.shape, F32)
-    for i, ref in enumerate((north, south)):
+    corners = []
+    for ref in (north, south):
         near = ref[0:fields, :]
         ends = jnp.where(
             lane == 2 * field, near[:, 0:1], jnp.where(lane == 2 * field + 1, near[:, LANES - 1 :], 0.0)
         )
-        corners[i : i + 1, :] = jnp.sum(ends, axis=0, keepdims=True)
+        corners.append(jnp.sum(ends, axis=0, keepdims=True))
+    for ref in (north, south):
         wet = ref[2 * fields : 2 * fields + 1, :]
-        corners[2 + i : 3 + i, :] = jnp.where(lane1 == 0, wet[:, 0:1], wet[:, LANES - 1 :])
+        corners.append(jnp.where(lane1 == 0, wet[:, 0:1], wet[:, LANES - 1 :]))
+    message[...] = jnp.zeros(message.shape, F32)
+    me = lax.axis_index("lon")
+    for i, step in enumerate((1, lon_count - 1)):
+        start = pl.multiple_of(lax.rem(me + step, lon_count) * (rows + 8), 8)
+        message[pl.ds(start, rows), :] = cols[i * rows : (i + 1) * rows, :]
+        extra = [*corners, cols[2 * rows + i : 2 * rows + i + 1, :], jnp.zeros((3, LANES), F32)]
+        message[pl.ds(start + rows, 8), :] = jnp.concatenate(extra, axis=0)
+
+
+class Sides:
+    def __init__(self, rows, lon_count, got, cols):
+        me = lax.axis_index("lon")
+        lane, row = iota((rows, LANES), 1), iota((rows, LANES), 0)
+        self.even = (lane & 1) == 0
+        self.even1 = (iota((1, LANES), 1) & 1) == 0
+        halves, extras = [], []
+        for step in (1, lon_count - 1):
+            start = pl.multiple_of(lax.rem(me + step, lon_count) * (rows + 8), 8)
+            halves.append(got[pl.ds(start, rows), :])
+            extras.append(got[pl.ds(start + rows, 8), :])
+        self.got, self.extras, self.cols, self.rows = halves, extras, cols, rows
+        self.columns = [
+            [
+                jnp.sum(jnp.where(lane == i * rows + row, x[4:5], 0.0), axis=1, keepdims=True)
+                for i in range(3)
+            ]
+            for x in extras
+        ]
+
+    def near(self):
+        return jnp.where(self.even, *self.got)
+
+    def far_and_inner(self):
+        east, west = self.got
+        mine_e, mine_w = self.cols[0 : self.rows, :], self.cols[self.rows : 2 * self.rows, :]
+        far = jnp.where(self.even, pltpu.roll(east, LANES - 1, 1), pltpu.roll(west, 1, 1))
+        inner = jnp.where(self.even, pltpu.roll(mine_e, LANES - 1, 1), pltpu.roll(mine_w, 1, 1))
+        return far, inner
+
+    def corner(self, i):
+        east, west = self.extras
+        wets = east[2 + i : 3 + i, 0:1], west[2 + i : 3 + i, 1:2]
+        return jnp.where(self.even1, east[i : i + 1], west[i : i + 1]), *wets
+
+    def lanes(self, i):
+        return jnp.where(self.even, self.columns[0][i], self.columns[1][i])
 
 
 def level_matrix(kind, levels, source, target):
@@ -223,25 +265,31 @@
     return jnp.where(group == 0, -THERMAL, jnp.where(group == 1, HALINE, 0.0)).astype(F32)
 
 
-def advance_columns(mid, outer, inner, corner_n, corner_s, wets, mixing, coriolis, level_map):
-    rows = mid.shape[0]
-    wet_mid, wet_out, wet_in, wet_corner_n, wet_corner_s = wets
+def advance_columns(sides, wet, coriolis, level_map):
+    rows = wet.shape[0]
+    mid = sides.near()
+    outer, inner = sides.far_and_inner()
+    (corner_n, wet_ne, wet_nw), (corner_s, wet_se, wet_sw) = sides.corner(0), sides.corner(1)
+    wet_mid, wet_out = sides.lanes(0), sides.lanes(1)
+    wet_in = jnp.where(sides.even, wet[:, LANES - 1 :], wet[:, 0:1])
+    wet_corner_n = jnp.where(sides.even1, wet_ne, wet_nw)
+    wet_corner_s = jnp.where(sides.even1, wet_se, wet_sw)
+    mixing = sides.lanes(2)
     lane = iota((rows, LANES), 1)
     row = iota((rows, LANES), 0)
-    even = (lane & 1) == 0
     span = LANES // 4
     group = lane // span
 
-    def sides(outside, inside):
-        return jnp.where(even, outside, inside), jnp.where(even, inside, outside)
+    def ends(outside, inside):
+        return jnp.where(sides.even, outside, inside), jnp.where(sides.even, inside, outside)
 
     def shifted(x, north, south):
         n = jnp.where(row == rows - 1, north, pltpu.roll(x, rows - 1, 0))
         s = jnp.where(row == 0, south, pltpu.roll(x, 1, 0))
         return n, s
 
-    e, w = sides(outer, inner)
-    wet_e, wet_w = sides(wet_out, wet_in)
+    e, w = ends(outer, inner)
+    wet_e, wet_w = ends(wet_out, wet_in)
     n, s = shifted(mid, corner_n, corner_s)
     wet_n, wet_s = shifted(wet_mid, wet_corner_n, wet_corner_s)
     lap = wet_e * (e - mid) + wet_w * (w - mid) + wet_n * (n - mid) + wet_s * (s - mid)
@@ -254,8 +302,14 @@
     u = pick(two, three, mid, one)
     v = pick(one, two, three, mid)
     adv = 0.5 * (u * de + v * dn)
-    linear = dot(jnp.concatenate([mid, de, dn], axis=1), level_map)
     zero = jnp.zeros_like(mid)
+    if level_map is None:
+        grad_x = HALINE * pltpu.roll(de, span, 1) - THERMAL * pltpu.roll(de, 2 * span, 1)
+        grad_y = HALINE * pltpu.roll(dn, 2 * span, 1) - THERMAL * pltpu.roll(dn, 3 * span, 1)
+        linear = VERTICAL_MIX * (pltpu.roll(mid, LANES - 2, 1) - mid)
+        linear = linear - (0.25 * GRAVITY) * pick(zero, zero, grad_x, grad_y)
+    else:
+        linear = dot(jnp.concatenate([mid, de, dn], axis=1), level_map)
     turn = pick(zero, zero, coriolis * v, -coriolis * u)
     kappa = jnp.where(group < 2, mixing, VISCOSITY)
     tend = turn - adv + kappa * lap + linear
@@ -370,158 +424,174 @@
     return new, (acc_x + dens_x, acc_y + dens_y)
 
 
-def ordered(flag, a, b):
-    return jnp.where(flag, a, b), jnp.where(flag, b, a)
-
-
-def padded(buf, count, levels, rows, q, k, value, north, south):
-    at = (q * count + k) * (rows + 2 * PAD) + PAD
-    field = q * levels + k
-    buf[at : at + rows, :] = value
-    buf[at + rows : at + rows + 1, :] = north[field : field + 1, :]
-    buf[at - 1 : at, :] = south[field : field + 1, :]
-
-
-def first_kernel(
-    rows, levels, state, base, got_lon_a, got_lon_b, north, south, coef, side, top, now, wet_pad
+def advance_top_rows(levels, sides, north, south, state, wet, rows, table):
+    fields = 4 * levels
+
+    def both(a, b):
+        return jnp.concatenate([a, b], axis=0)
+
+    def rows_at(first):
+        return both(
+            north[pl.ds(first, 4, stride=levels), :], south[pl.ds(first, 4, stride=levels), :]
+        )
+
+    lane, row = iota((8, LANES), 1), iota((8, LANES), 0)
+    upper = row < 4
+    field = row & 3
+    inside_n = state[pl.ds(rows - 1, 4, stride=levels * rows), :]
+    inside_s = state[pl.ds(0, 4, stride=levels * rows), :]
+    mid, below, outer = rows_at(0), rows_at(1), rows_at(fields)
+    n = both(outer[0:4], inside_s)
+    s = both(inside_n, outer[4:8])
+    (corner_n, wet_ne, wet_nw), (corner_s, wet_se, wet_sw) = sides.corner(0), sides.corner(1)
+    corner = jnp.where(upper, corner_n, corner_s)
+    at = 2 * levels * field
+
+    def end(parity):
+        return jnp.sum(jnp.where(lane == at + parity, corner, 0.0), axis=1, keepdims=True)
+
+    def west_east(x, east, west):
+        return (
+            jnp.where(lane == LANES - 1, east, pltpu.roll(x, LANES - 1, 1)),
+            jnp.where(lane == 0, west, pltpu.roll(x, 1, 1)),
+        )
+
+    def tail(i):
+        place = slice(2 * fields + i, 2 * fields + i + 1)
+        return north[place, :], south[place, :]
+
+    e, w = west_east(mid, end(0), end(1))
+    wet_mid = jnp.where(upper, *tail(0))
+    wet_e, wet_w = west_east(
+        wet_mid, jnp.where(upper, wet_ne, wet_se), jnp.where(upper, wet_nw, wet_sw)
+    )
+    out_n, out_s = tail(1)
+    wet_n = jnp.where(upper, out_n, wet[0:1])
+    wet_s = jnp.where(upper, wet[rows - 1 : rows], out_s)
+    lap = wet_e * (e - mid) + wet_w * (w - mid) + wet_n * (n - mid) + wet_s * (s - mid)
+    de, dn = e - w, n - s
+
+    def of(x, i):
+        return jnp.where(upper, x[i : i + 1], x[4 + i : 5 + i])
+
+    u, v = of(mid, 2), of(mid, 3)
+    coriolis = jnp.where(upper, table[PAD + rows : PAD + rows + 1], table[PAD - 1 : PAD])
+    grad_x = (0.25 * GRAVITY) * (HALINE * of(de, 1) - THERMAL * of(de, 0))
+    grad_y = (0.25 * GRAVITY) * (HALINE * of(dn, 1) - THERMAL * of(dn, 0))
+    turn = jnp.where(
+        field < 2, 0.0, jnp.where(field == 2, coriolis * v - grad_x, -coriolis * u - grad_y)
+    )
+    kappa = jnp.where(field < 2, jnp.where(upper, *tail(2)), VISCOSITY)
+    tend = turn - 0.5 * (u * de + v * dn) + kappa * lap + VERTICAL_MIX * (below - mid)
+    return wet_mid * (mid + TIMESTEP * tend)
+
+
+def surface_kernel(
+    rows, levels, lon_count,
+    state, base, cols, got, north, south, out_in, ids,
+    coef, side, out, now, later, wet_pad, stage, places, sem,
 ):
     fields = 4 * levels
-    even_lon = is_even("lon")
+    pitch = rows + 2 * PAD
+    to_scalars = pltpu.make_async_copy(ids, places, sem)
+    to_scalars.start()
+    out[...] = out_in[...]
     wet = base[0:rows, :]
     mixing = base[rows : 2 * rows, :]
-    coriolis = base[2 * rows + PAD : 3 * rows + PAD, :]
+    table = base[2 * rows :, :]
+    coriolis = table[PAD : PAD + rows]
     lane = iota((rows, LANES), 1)
+    sides = Sides(rows, lon_count, got, cols)
     wet_pad[PAD : PAD + rows, :] = wet
     wet_pad[PAD - 1 : PAD, :] = south[2 * fields : 2 * fields + 1, :]
     wet_pad[PAD + rows : PAD + rows + 1, :] = north[2 * fields : 2 * fields + 1, :]
     wet_n = wet_pad[PAD + 1 : PAD + 1 + rows, :]
     wet_s = wet_pad[PAD - 1 : PAD - 1 + rows, :]
-    aux_e, aux_w = ordered(even_lon, got_lon_a[rows:, :], got_lon_b[rows:, :])
-    wet_e = jnp.where(lane == LANES - 1, aux_e[:, 0:1], pltpu.roll(wet, LANES - 1, 1))
-    wet_w = jnp.where(lane == 0, aux_w[:, 0:1], pltpu.roll(wet, 1, 1))
+    wet_e = jnp.where(lane == LANES - 1, sides.columns[0][0], pltpu.roll(wet, LANES - 1, 1))
+    wet_w = jnp.where(lane == 0, sides.columns[1][0], pltpu.roll(wet, 1, 1))
     made = coefficients(wet, (wet_e, wet_w, wet_n, wet_s), mixing, coriolis)
     for name in COEFFICIENTS:
         coef[place_of(name, rows)] = made[name]
-    got_e, got_w = ordered(even_lon, got_lon_a[0:rows, :], got_lon_b[0:rows, :])
-    side[...] = jnp.where((lane & 1) == 0, got_e, got_w)
-
-    count = now.shape[0] // (4 * (rows + 2 * PAD))
+    near = sides.near()
+    side[...] = near
+
+    count = now.shape[0] // (4 * pitch)
     for q in range(4):
         for k in range(count):
             field = (q * levels + k) * rows
-            padded(now, count, levels, rows, q, k, state[field : field + rows, :], north, south)
+            at = (q * count + k) * pitch + PAD
+            now[at : at + rows, :] = state[field : field + rows, :]
+            now[at + rows : at + rows + 1, :] = north[q * levels + k : q * levels + k + 1, :]
+            now[at - 1 : at, :] = south[q * levels + k : q * levels + k + 1, :]
+
+    def read(name):
+        return coef[place_of(name, rows)]
+
     none = jnp.zeros((rows, LANES), F32)
     acc = (none, none)
+    edge_rows = advance_top_rows(levels, sides, north, south, state, wet, rows, table)
+    edge_cols = advance_columns(sides, wet, coriolis, None)
     for k in range(count - 1):
-        new, acc = advance_level(
-            k, count, levels, rows, now, side[...], lambda x: coef[place_of(x, rows)], acc
-        )
+        new, acc = advance_level(k, count, levels, rows, now, near, read, acc)
         for q in range(4):
-            at = (q * (count - 1) + k) * rows
-            top[at : at + rows, :] = new[q]
-
-
-def surface_kernel(
-    rows, levels,
-    state, base, col_map, row_map, coef, side, top, lon_a, lon_b, got_lon_a, got_lon_b, north, south,
-    got_corner_a, got_corner_b, out_in, ids,
-    side_new, north_new, south_new, out, later, stage, places, sem,
-):
+            at = (q * count + k) * pitch + PAD
+            later[at : at + rows, :] = new[q]
+            if k == 0:
+                later[at + rows : at + rows + 1, :] = edge_rows[q : q + 1]
+                later[at - 1 : at, :] = edge_rows[4 + q : 5 + q]
+    new, _ = advance_level(0, count, levels, rows, later, edge_cols, read, (none, none))
+    for q in range(4):
+        stage[pl.ds(q, rows, stride=4), :] = new[q]
+    to_scalars.wait()
+    for r in range(rows):
+        out[pl.ds(places[0, r], 4), :] = stage[4 * r : 4 * r + 4, :]
+
+
+def halo_after_first(rows, levels, sides, north, south, state, wet, table, col_map, row_map):
     fields = 4 * levels
-    to_scalars = pltpu.make_async_copy(ids, places, sem)
-    to_scalars.start()
-    out[...] = out_in[...]
-    even_lon = is_even("lon")
-    wet = base[0:rows, :]
-    table = base[2 * rows :, :]
-    lane = iota((rows, LANES), 1)
-    even = (lane & 1) == 0
-    lane1 = iota((1, LANES), 1)
-    even1 = (lane1 & 1) == 0
-
-    corner_e, corner_w = ordered(even_lon, got_corner_a[...], got_corner_b[...])
-
-    def corner(i):
-        wets = corner_e[2 + i : 3 + i, 0:1], corner_w[2 + i : 3 + i, 1:2]
-        return jnp.where(even1, corner_e[i : i + 1], corner_w[i : i + 1]), *wets
-
-    corner_n, wet_ne, wet_nw = corner(0)
-    corner_s, wet_se, wet_sw = corner(1)
-
-    def spread(x, i):
-        return jnp.broadcast_to(x[:, i : i + 1], (rows, LANES))
-
-    aux_e, aux_w = ordered(even_lon, got_lon_a[rows:, :], got_lon_b[rows:, :])
-    got_e, got_w = ordered(even_lon, got_lon_a[0:rows, :], got_lon_b[0:rows, :])
-    sent_e, sent_w = ordered(even_lon, lon_a[0:rows, :], lon_b[0:rows, :])
-    outer = jnp.where(even, pltpu.roll(got_e, LANES - 1, 1), pltpu.roll(got_w, 1, 1))
-    inner = jnp.where(even, pltpu.roll(sent_e, LANES - 1, 1), pltpu.roll(sent_w, 1, 1))
-    side_new[...] = advance_columns(
-        side[...], outer, inner, corner_n, corner_s,
-        (
-            jnp.where(even, spread(aux_e, 0), spread(aux_w, 0)),
-            jnp.where(even, spread(aux_e, 1), spread(aux_w, 1)),
-            jnp.where(even, spread(wet, LANES - 1), spread(wet, 0)),
-            jnp.where(even1, wet_ne, wet_nw),
-            jnp.where(even1, wet_se, wet_sw),
-        ),
-        jnp.where(even, spread(aux_e, 2), spread(aux_w, 2)),
-        table[PAD : PAD + rows], col_map[...],
-    )
-
-    field_lane = iota((fields, LANES), 1)
-    field_id = iota((fields, LANES), 0)
+    side_new = advance_columns(sides, wet, table[PAD : PAD + rows], col_map)
+    lane, field = iota((fields, LANES), 1), iota((fields, LANES), 0)
 
     def to_sublanes(x, parity):
-        here = field_lane == 2 * field_id + parity
+        here = lane == 2 * field + parity
         return jnp.sum(jnp.where(here, x, 0.0), axis=1, keepdims=True)
 
     parts = []
-    for north_side, ref, ends, corner_wets, line, lat_row in (
-        (True, north, corner_n, (wet_ne, wet_nw), rows - 1, PAD + rows),
-        (False, south, corner_s, (wet_se, wet_sw), 0, PAD - 1),
+    for north_side, ref, line, lat_row in (
+        (True, north, rows - 1, PAD + rows),
+        (False, south, 0, PAD - 1),
     ):
+        corner, *corner_wets = sides.corner(0 if north_side else 1)
         inside = state[pl.ds(line, fields, stride=rows), :]
         tail = ref[2 * fields :, :]
         pair = (ref[fields : 2 * fields, :], inside), (tail[1:2], wet[line : line + 1])
         (n, s), (wet_n, wet_s) = pair if north_side else [x[::-1] for x in pair]
         parts.append(
             (
-                ref[0:fields, :], n, s, (to_sublanes(ends, 0), to_sublanes(ends, 1)),
+                ref[0:fields, :], n, s, (to_sublanes(corner, 0), to_sublanes(corner, 1)),
                 (tail[0:1], wet_n, wet_s, *corner_wets),
                 tail[2:3], table[lat_row : lat_row + 1],
             )
         )
-    north_new[...], south_new[...] = advance_rows(levels, parts, row_map[...])
-
-    count = later.shape[0] // (4 * (rows + 2 * PAD))
-    for q in range(4):
-        for k in range(count):
-            at = (q * count + k) * rows
-            padded(
-                later, count, levels, rows, q, k, top[at : at + rows, :], north_new, south_new
-            )
-    none = jnp.zeros((rows, LANES), F32)
-    new, _ = advance_level(
-        0, count, levels, rows, later, side_new[...], lambda x: coef[place_of(x, rows)], (none, none)
-    )
-    for q in range(4):
-        stage[pl.ds(q, rows, stride=4), :] = new[q]
-    to_scalars.wait()
-    for r in range(rows):
-        out[pl.ds(places[0, r], 4), :] = stage[4 * r : 4 * r + 4, :]
+    return side_new, *advance_rows(levels, parts, row_map)
 
 
 def main_kernel(
-    rows, levels, chunks,
-    state, coefs, side, side_new, north, south, north_new, south_new,
-    tr_hbm, ve_hbm, now, later, tr_out, ve_out, sems,
+    rows, levels, lon_count, chunks,
+    state, base, cols, got, north, south, col_map, row_map, coefs, side,
+    tr_hbm, ve_hbm, now, later, side_new, tr_out, ve_out, sems,
 ):
     fields = 4 * levels
     pitch = rows + 2 * PAD
-    for buf, n, s in ((now, north, south), (later, north_new, south_new)):
-        buf[pl.ds(PAD - 1, fields, stride=pitch), :] = s[0:fields, :]
-        buf[pl.ds(PAD + rows, fields, stride=pitch), :] = n[0:fields, :]
+    sides = Sides(rows, lon_count, got, cols)
+    side_new[...], north_new, south_new = halo_after_first(
+        rows, levels, sides, north, south, state, base[0:rows, :], base[2 * rows :, :],
+        col_map[...], row_map[...],
+    )
+    edges = (now, north[0:fields, :], south[0:fields, :]), (later, north_new, south_new)
+    for buf, n, s in edges:
+        buf[pl.ds(PAD - 1, fields, stride=pitch), :] = s
+        buf[pl.ds(PAD + rows, fields, stride=pitch), :] = n
 
     def fill(f, carry):
         x = state[pl.ds(pl.multiple_of(f * rows, 8), rows), :]
@@ -603,19 +673,17 @@
     return jax.ShapeDtypeStruct(shape, dtype)
 
 
-def pairs_of(lon_count, lat_count):
-    lon_a = [(i, i ^ 1) for i in range(lon_count)]
-    lon_b = [(i, (i + 1 if i % 2 else i - 1) % lon_count) for i in range(lon_count)]
-    lat_a, lat_b = [], []
+def lat_swaps(lon_count, lat_count):
+    swap_a, swap_b = [], []
     for i in range(lon_count):
         for a in range(lat_count):
             here = i * lat_count + a
-            lat_a.append((here, i * lat_count + (a ^ 1)))
+            swap_a.append((here, i * lat_count + (a ^ 1)))
             if a == lat_count - 1:
-                lat_b.append((here, (lon_count - 1 - i) * lat_count + a))
+                swap_b.append((here, (lon_count - 1 - i) * lat_count + a))
             elif a > 0:
-                lat_b.append((here, here + 1 if a % 2 else here - 1))
-    return lon_a, lon_b, lat_a, lat_b
+                swap_b.append((here, here + 1 if a % 2 else here - 1))
+    return swap_a, swap_b
 
 
 def local(tracers, velocity, land_mask, mixing, owners, atm_row):
@@ -625,7 +693,7 @@
     lon_count, lat_count = lax.axis_size("lon"), lax.axis_size("lat")
     devices = lon_count * lat_count
     assert cols == LANES and rows % 8 == 0 and 2 * fields == LANES
-    assert lon_count % 2 == 0 and lat_count % 2 == 0
+    assert lon_count > 2 and lat_count % 2 == 0 and 3 * rows <= LANES
     length = 2 * fields + 8
     pitch = rows + 2 * PAD
     flat = 2 * levels * rows
@@ -646,18 +714,16 @@
             pltpu.SemaphoreType.DMA((6,)),
         ],
     )(tracers.reshape(deep), velocity.reshape(deep), land_mask, mixing)
-    swaps = pairs_of(lon_count, lat_count)
-    got_lat_b = lax.ppermute(lat_b, ("lon", "lat"), swaps[3])
-    got_lat_a = lax.ppermute(lat_a, ("lon", "lat"), swaps[2])
+    swap_a, swap_b = lat_swaps(lon_count, lat_count)
+    got_lat_b = lax.ppermute(lat_b, ("lon", "lat"), swap_b)
+    got_lat_a = lax.ppermute(lat_a, ("lon", "lat"), swap_a)
 
     tr, ve = tracers.reshape(flat, cols), velocity.reshape(flat, cols)
-    lon_a, lon_b = call(
+    columns = call(
         functools.partial(pack_kernel, rows, fields),
-        [shaped(2 * rows, cols)] * 2,
+        shaped(2 * rows + 8, cols),
         in_specs=[vmem] * 4,
     )(tr, ve, land_mask, mixing)
-    got_lon_a = lax.ppermute(lon_a, "lon", swaps[0])
-    got_lon_b = lax.ppermute(lon_b, "lon", swaps[1])
 
     slot_rows = 5 * CAP + 1
     state, base, col_map, row_map, outgoing, ids = call(
@@ -674,56 +740,46 @@
         scratch_shapes=[pltpu.SMEM((devices,), jnp.int32)],
     )(tr, ve, land_mask, mixing, owners.reshape(rows), atm_row)
 
-    north, south, corners = call(
-        functools.partial(corner_kernel, lat_count, fields),
-        [shaped(length, cols), shaped(length, cols), shaped(8, cols)],
-    )(got_lat_a, got_lat_b)
-    got_corner_a = lax.ppermute(corners, "lon", swaps[0])
-    got_corner_b = lax.ppermute(corners, "lon", swaps[1])
+    size = rows + 8
+    north, south, message = call(
+        functools.partial(corner_kernel, lat_count, lon_count, rows, fields),
+        [shaped(length, cols), shaped(length, cols), shaped(lon_count * size, cols)],
+    )(got_lat_a, got_lat_b, columns)
+    got = lax.all_to_all(
+        message.reshape(lon_count, size, cols), "lon", 0, 0, tiled=True
+    ).reshape(lon_count * size, cols)
 
     count = min(3, levels)
-    coefs, side, top = call(
-        functools.partial(first_kernel, rows, levels),
+    coefs, side, outgoing = call(
+        functools.partial(surface_kernel, rows, levels, lon_count),
         [
             shaped(len(COEFFICIENTS) * rows, cols),
             shaped(rows, cols),
-            shaped(4 * (count - 1) * rows, cols),
+            shaped(devices * slot_rows, cols),
         ],
         scratch_shapes=[
             pltpu.VMEM((4 * count * pitch, cols), F32),
+            pltpu.VMEM((4 * count * pitch, cols), F32),
             pltpu.VMEM((pitch, cols), F32),
-        ],
-    )(state, base, got_lon_a, got_lon_b, north, south)
-
-    side_new, north_new, south_new, outgoing = call(
-        functools.partial(surface_kernel, rows, levels),
-        [
-            shaped(rows, cols),
-            shaped(fields, cols),
-            shaped(fields, cols),
-            shaped(devices * slot_rows, cols),
-        ],
-        scratch_shapes=[
-            pltpu.VMEM((4 * (count - 1) * pitch, cols), F32),
             pltpu.VMEM((4 * rows, cols), F32),
             pltpu.SMEM((8, cols), jnp.int32),
             pltpu.SemaphoreType.DMA,
         ],
-    )(state, base, col_map, row_map, coefs, side, top, lon_a, lon_b, got_lon_a, got_lon_b, north,
-      south, got_corner_a, got_corner_b, outgoing, ids)
+    )(state, base, columns, got, north, south, outgoing, ids)
     incoming = lax.all_to_all(
         outgoing.reshape(devices, slot_rows, 1, cols), ("lon", "lat"), 0, 0, tiled=True
     ).reshape(devices * slot_rows, cols)
 
     chunks = 4
     tr_out, ve_out = call(
-        functools.partial(main_kernel, rows, levels, chunks),
+        functools.partial(main_kernel, rows, levels, lon_count, chunks),
         [shaped(flat, cols), shaped(flat, cols)],
-        in_specs=[vmem] * 8,
+        in_specs=[vmem] * 10,
         out_specs=[hbm] * 2,
         scratch_shapes=[
             pltpu.VMEM((fields * pitch, cols), F32),
             pltpu.VMEM((fields * pitch, cols), F32),
+            pltpu.VMEM((rows, cols), F32),
             pltpu.VMEM((flat, cols), F32),
             pltpu.VMEM((flat, cols), F32),
             pltpu.SemaphoreType.DMA((4 * chunks,)),
@@ -731,7 +787,7 @@
         cost_estimate=pl.CostEstimate(
             flops=80 * fields * rows * cols, bytes_accessed=5 << 20, transcendentals=0
         ),
-    )(state, coefs, side, side_new, north, south, north_new, south_new)
+    )(state, base, columns, got, north, south, col_map, row_map, coefs, side)
     surface, cover = call(
         functools.partial(reduce_kernel, devices),
         [shaped(4, ATM_ROWS, cols), shaped(ATM_ROWS, cols)],

time: 33.8 us -> 35.1 us (1.038)
  Pallas kernels: 11.1 us -> 12 us
  starting transfers between devices: 13.6 us -> 14 us
  local copies, waits for them, and re-layouts: 1.07 us -> 0.69 us
    ppermute x6 -> x2, starting transfers between devices: 6.87 us -> 1.17 us  [the longest x1 0.65 us: local(): got_lat_b = lax.ppermute(lat_b, ('lon', 'lat'), swap_b)]
    all_to_all x0 -> x1, starting transfers between devices: none -> 4.74 us  [local(): lax.all_to_all(message.reshape(lon_count, size, cols), 'lon', 0, 0, tiled...]
    all_to_all x0 -> x1, waiting for transfers between devices: none -> 3.19 us  [local(): lax.all_to_all(message.reshape(lon_count, size, cols), 'lon', 0, 0, tiled...]
    ppermute x6 -> x2, waiting for transfers between devices: 2.2 us -> 0.01 us  [the longest x1 0.01 us: local(): got_lat_a = lax.ppermute(lat_a, ('lon', 'lat'), swap_a)]
    all_to_all x1, starting transfers between devices: 6.71 us -> 8.11 us  [local(): lax.all_to_all(outgoing.reshape(devices, slot_rows, 1, cols), ('lon', 'la...]
    pallas_call x5 -> x4, Pallas kernels: 7.13 us -> 8.05 us  [the longest x1 4.7 us: local(): call(functools.partial(main_kernel, rows, levels, lon_count, chunks), [sh...]
    all_to_all x1, waiting for transfers between devices: 4.6 us -> 3.9 us  [local(): lax.all_to_all(outgoing.reshape(devices, slot_rows, 1, cols), ('lon', 'la...]
    unnamed x14 -> x12, local copies, waits for them, and re-layouts: 1.07 us -> 0.69 us
  transfers between devices with their start and end apart: 7 -> 4, of which waited for: 4 -> 2; matrix products, arithmetic and copies ran while one was open for 0% -> 0% of each run, Pallas kernels for 20% -> 20%
where the time goes in v5:
time: 35.1 us; the launch traced here: 34.6 us
  starting transfers between devices  14 us (40%)
  Pallas kernels  12 us (34%)
  waiting for transfers between devices  7.09 us (20%)
  between operations  0.77 us (2%)
  local copies, waits for them, and re-layouts  0.69 us (2%)
    all_to_all x1, starting transfers between devices, local(): lax.all_to_all(outgoing.reshape(devices, slot_rows, 1, cols), ('lon', 'la...  8.11 us
    all_to_all x1, starting transfers between devices, local(): lax.all_to_all(message.reshape(lon_count, size, cols), 'lon', 0, 0, tiled...  4.74 us
    pallas_call x1, Pallas kernels, local(): call(functools.partial(main_kernel, rows, levels, lon_count, chunks), [sh...  4.7 us
    all_to_all x1, waiting for transfers between devices, local(): lax.all_to_all(outgoing.reshape(devices, slot_rows, 1, cols), ('lon', 'la...  3.9 us
    all_to_all x1, waiting for transfers between devices, local(): lax.all_to_all(message.reshape(lon_count, size, cols), 'lon', 0, 0, tiled...  3.19 us
    pallas_call x1, Pallas kernels, local(): call(functools.partial(edge_kernel, rows, fields), [shaped(length, cols)]...  1.96 us
    pallas_call x1, Pallas kernels, local(): call(functools.partial(surface_kernel, rows, levels, lon_count), [shaped(...  1.35 us
    pallas_call x1, Pallas kernels, local(): call(functools.partial(pack_kernel, rows, fields), shaped(2 * rows + 8, c...  1.18 us
  transfers between devices with their start and end apart: 4, of which 2 were waited for; matrix products, arithmetic and copies ran while one was open for 0% of the time, Pallas kernels for 20%

profile of v5, /device:TPU:0, one launch (start us, length us, event | category | flops | bytes accessed | tf_op | source)
XLA Modules:
  0.0 34.6 jit_solution(7994905747449974511)
XLA Ops:
  0.6 0.0 copy-start
  0.6 0.0 copy-start.1
  0.7 0.0 copy-start.2
  0.7 0.0 copy-start.3
  0.7 2.0 %shard_map.95 = (f32[136,128]{1,0:T(8,128)}, f32[136,128]{1,0:T(8,128)}) custom-call(f32[32,32,128]{2,1,0:T(8,128)} %bitcast.11, f32[32,32,128]{2,1,0:T(8,128)} %bitcast.14, s32[32,128]{1,0:T(8,128)} %mask_hbm.1, f32[32,128]{1,0:T(8,128)} %mix_hbm.1), custom_call_target="tpu_custom_call" | custom-call | tf_op jit(solution)/shard_map/pallas_call | solution.py:705
  2.6 0.5 %collective-permute-start = (f32[136,128]{1,0:T(8,128)}, f32[136,128]{1,0:T(8,128)S(1)}, u32[]{:S(2)}, u32[]{:S(2)}) collective-permute-start(f32[136,128]{1,0:T(8,128)} %get-tuple-element.24), channel_id=1, source_target_pairs={{0,1},{1,0},{2,3},{3,2},{4,5},{5,4},{6,7},{7,6},{8,9},{9,8},{10,11... | collective-permute-start | bytes 208904 | tf_op jit(solution)/shard_map/ppermute | solution.py:719
  3.2 0.7 %collective-permute-start.1 = (f32[136,128]{1,0:T(8,128)}, f32[136,128]{1,0:T(8,128)S(1)}, u32[]{:S(2)}, u32[]{:S(2)}) collective-permute-start(f32[136,128]{1,0:T(8,128)} %get-tuple-element.25), channel_id=1, source_target_pairs={{1,2},{2,1},{3,4},{4,3},{5,6},{6,5},{7,31},{9,10},{10,9},{11,12},{... | collective-permute-start | bytes 208904 | tf_op jit(solution)/shard_map/ppermute | solution.py:718
  3.8 0.0 copy-done
  3.8 0.0 copy-done.1
  3.8 0.0 copy-done.2
  3.8 0.0 copy-done.3
  3.9 1.2 %shard_map.94.cols = f32[72,128]{1,0:T(8,128)S(1)} custom-call(f32[1024,128]{1,0:T(8,128)S(1)} %bitcast.12, f32[1024,128]{1,0:T(8,128)S(1)} %bitcast.15, s32[32,128]{1,0:T(8,128)S(1)} %copy-done.2, f32[32,128]{1,0:T(8,128)S(1)} %copy-done.3), custom_call_target="tpu_custom_call" | custom-call | tf_op jit(solution)/shard_map/pallas_call | solution.py:722
  5.0 0.0 collective-permute-done.got_a
  5.1 0.0 collective-permute-done.1.got_b
  5.1 0.8 %shard_map.96 = (f32[136,128]{1,0:T(8,128)S(1)}, f32[136,128]{1,0:T(8,128)S(1)}, f32[160,128]{1,0:T(8,128)}) custom-call(f32[136,128]{1,0:T(8,128)S(1)} %collective-permute-done.got_a, f32[136,128]{1,0:T(8,128)S(1)} %collective-permute-done.1.got_b, f32[72,128]{1,0:T(8,128)S(1)} %shard_map.94.cols), custom_call_target="tpu_custom_call" | custom-call | tf_op jit(solution)/shard_map/pallas_call | solution.py:744
  5.9 4.7 %all-to-all-start = ((f32[4,40,128]{2,1,0:T(8,128)}), f32[4,40,128]{2,1,0:T(8,128)S(1)}, u32[]{:S(2)}, u32[]{:S(2)}) async-start(f32[4,40,128]{2,1,0:T(8,128)} %bitcast.5), calls=%async_computation | async-start | bytes 163840 | tf_op jit(solution)/shard_map/all_to_all | solution.py:748
  10.6 0.0 copy-start.4
  10.6 0.0 copy-start.5
  10.6 0.7 %copy-done.4 = s32[32,1]{0,1:T(1,128)S(1)} copy-done((s32[32,1]{0,1:T(1,128)S(1)}, s32[32,1]{0,1:T(1,128)}, u32[]{:S(2)}) %copy-start.4) | copy-done | bytes 152
  11.3 0.0 copy-done.5
  11.3 1.0 %shard_map.93 = (f32[2048,128]{1,0:T(8,128)S(1)}, f32[112,128]{1,0:T(8,128)S(1)}, f32[384,128]{1,0:T(8,128)S(1)}, f32[80,128]{1,0:T(8,128)S(1)}, f32[352,128]{1,0:T(8,128)S(1)}, /*index=5*/s32[8,128]{1,0:T(8,128)S(1)}) custom-call(f32[1024,128]{1,0:T(8,128)S(1)} %bitcast.13, f32[1024,128]{1,0:T(8,128)S(1)} %bitcast.16, s32[32,128]{1,0:T(8,128)S(1)} %copy-done.2, ...), custom_call_target="tpu_custom_call" | custom-call | tf_op jit(solution)/shard_map/pallas_call | solution.py:729
  12.3 3.2 %all-to-all-done = f32[4,40,128]{2,1,0:T(8,128)S(1)} async-done(((f32[4,40,128]{2,1,0:T(8,128)}), f32[4,40,128]{2,1,0:T(8,128)S(1)}, u32[]{:S(2)}, u32[]{:S(2)}) %all-to-all-start) | async-done | bytes 81952 | tf_op jit(solution)/shard_map/all_to_all | solution.py:748
  15.5 1.4 %shard_map.97 = (f32[416,128]{1,0:T(8,128)S(1)}, f32[32,128]{1,0:T(8,128)S(1)}, f32[352,128]{1,0:T(8,128)}) custom-call(f32[2048,128]{1,0:T(8,128)S(1)} %get-tuple-element.22.state, f32[112,128]{1,0:T(8,128)S(1)} %get-tuple-element.23.base, f32[72,128]{1,0:T(8,128)S(1)} %shard_map.94.cols, f32[160,128]{1,0:T(8,128)S(1)} %bitcast.17, ...), custom_call_target="tpu_custom_call" | custom-call | tf_op jit(solution)/shard_map/pallas_call | solution.py:753
  16.9 8.1 %all-to-all-start.1 = ((f32[32,11,1,128]{3,2,1,0:T(1,128)}), f32[32,11,1,128]{3,2,1,0:T(1,128)S(1)}, u32[]{:S(2)}, u32[]{:S(2)}) async-start(f32[32,11,1,128]{3,2,1,0:T(1,128)} %bitcast.9), calls=%async_computation.1 | async-start | bytes 360448 | tf_op jit(solution)/shard_map/all_to_all | solution.py:769
  25.0 4.7 %shard_map.98 = (f32[1024,128]{1,0:T(8,128)}, f32[1024,128]{1,0:T(8,128)}) custom-call(f32[2048,128]{1,0:T(8,128)S(1)} %get-tuple-element.22.state, f32[112,128]{1,0:T(8,128)S(1)} %get-tuple-element.23.base, f32[72,128]{1,0:T(8,128)S(1)} %shard_map.94.cols, f32[160,128]{1,0:T(8,128)S(1)} %bitcast.18, f32[136,128]{1,0:T(8,128)S(1)} %get-tuple-element.27.north, ...), custom_call_target="tpu_custom_call" | custom-call | flops 20971520 | bytes 5242880 | tf_op jit(solution)/shard_map/pallas_call | solution.py:774
  29.7 3.9 %all-to-all-done.1 = f32[32,11,1,128]{3,2,1,0:T(1,128)S(1)} async-done(((f32[32,11,1,128]{3,2,1,0:T(1,128)}), f32[32,11,1,128]{3,2,1,0:T(1,128)S(1)}, u32[]{:S(2)}, u32[]{:S(2)}) %all-to-all-start.1) | async-done | bytes 180256 | tf_op jit(solution)/shard_map/all_to_all | solution.py:769
  33.6 1.0 %shard_map.99 = (f32[4,32,128]{2,1,0:T(8,128)}, f32[32,128]{1,0:T(8,128)}) custom-call(f32[352,128]{1,0:T(8,128)S(1)} %bitcast.19), custom_call_target="tpu_custom_call" | custom-call | tf_op jit(solution)/shard_map/pallas_call | solution.py:791
Async XLA Ops:
  0.6 3.2 %copy-start = (f32[2,16,32,128]{3,2,1,0:T(8,128)S(1)}, f32[2,16,32,128]{3,2,1,0:T(8,128)}, u32[]{:S(2)}) copy-start(f32[2,16,32,128]{3,2,1,0:T(8,128)} %param.6) | copy-start | bytes 1572868
  0.6 3.2 %copy-start.1 = (f32[2,16,32,128]{3,2,1,0:T(8,128)S(1)}, f32[2,16,32,128]{3,2,1,0:T(8,128)}, u32[]{:S(2)}) copy-start(f32[2,16,32,128]{3,2,1,0:T(8,128)} %param.7) | copy-start | bytes 1572868
  0.7 3.2 %copy-start.2 = (s32[32,128]{1,0:T(8,128)S(1)}, s32[32,128]{1,0:T(8,128)}, u32[]{:S(2)}) copy-start(s32[32,128]{1,0:T(8,128)} %mask_hbm.1) | copy-start | bytes 49156
  0.7 3.2 %copy-start.3 = (f32[32,128]{1,0:T(8,128)S(1)}, f32[32,128]{1,0:T(8,128)}, u32[]{:S(2)}) copy-start(f32[32,128]{1,0:T(8,128)} %mix_hbm.1) | copy-start | bytes 49156
  2.6 2.4 %collective-permute-start = (f32[136,128]{1,0:T(8,128)}, f32[136,128]{1,0:T(8,128)S(1)}, u32[]{:S(2)}, u32[]{:S(2)}) collective-permute-start(f32[136,128]{1,0:T(8,128)} %get-tuple-element.24), channel_id=1, source_target_pairs={{0,1},{1,0},{2,3},{3,2},{4,5},{5,4},{6,7},{7,6},{8,9},{9,8},{10,11... | collective-permute-start | bytes 208904 | tf_op jit(solution)/shard_map/ppermute | solution.py:719
  3.2 1.9 %collective-permute-start.1 = (f32[136,128]{1,0:T(8,128)}, f32[136,128]{1,0:T(8,128)S(1)}, u32[]{:S(2)}, u32[]{:S(2)}) collective-permute-start(f32[136,128]{1,0:T(8,128)} %get-tuple-element.25), channel_id=1, source_target_pairs={{1,2},{2,1},{3,4},{4,3},{5,6},{6,5},{7,31},{9,10},{10,9},{11,12},{... | collective-permute-start | bytes 208904 | tf_op jit(solution)/shard_map/ppermute | solution.py:718
  5.9 9.6 %all-to-all-start = ((f32[4,40,128]{2,1,0:T(8,128)}), f32[4,40,128]{2,1,0:T(8,128)S(1)}, u32[]{:S(2)}, u32[]{:S(2)}) async-start(f32[4,40,128]{2,1,0:T(8,128)} %bitcast.5), calls=%async_computation | async-start | bytes 163840 | tf_op jit(solution)/shard_map/all_to_all | solution.py:748
  10.6 0.7 %copy-start.4 = (s32[32,1]{0,1:T(1,128)S(1)}, s32[32,1]{0,1:T(1,128)}, u32[]{:S(2)}) copy-start(s32[32,1]{0,1:T(1,128)} %param.10) | copy-start | bytes 388
  10.6 0.7 %copy-start.5 = (s32[32]{0:T(128)S(1)}, s32[32]{0:T(128)}, u32[]{:S(2)}) copy-start(s32[32]{0:T(128)} %atm_row.1) | copy-start | bytes 388
  16.9 16.7 %all-to-all-start.1 = ((f32[32,11,1,128]{3,2,1,0:T(1,128)}), f32[32,11,1,128]{3,2,1,0:T(1,128)S(1)}, u32[]{:S(2)}, u32[]{:S(2)}) async-start(f32[32,11,1,128]{3,2,1,0:T(1,128)} %bitcast.9), calls=%async_computation.1 | async-start | bytes 360448 | tf_op jit(solution)/shard_map/all_to_all | solution.py:769

commit v6 on v5

--- a/solution.py
+++ b/solution.py
@@ -73,7 +73,7 @@
         buf[2 * fields + 2 : 2 * fields + 3, :] = mix[pl.ds(near, 1), :]
 
 
-def pack_kernel(rows, fields, tr, ve, mask, mix, cols):
+def pack_kernel(rows, fields, tr, ve, mask, mix, msg_a, msg_b):
     half = fields // 2
     wet = mask[...].astype(F32)
     lane = iota((rows, LANES), 1)
@@ -98,16 +98,21 @@
         return jnp.broadcast_to(x[:, i : i + 1], (rows, LANES))
 
     odd = (lane & 1) == 1
-    cols[0:rows, :] = carry[0] * jnp.where(odd, spread(wet, LANES - 1), spread(wet, LANES - 2))
-    cols[rows : 2 * rows, :] = carry[1] * jnp.where(odd, spread(wet, 1), spread(wet, 0))
-    cols[2 * rows :, :] = jnp.zeros((8, LANES), F32)
+    to_east = carry[0] * jnp.where(odd, spread(wet, LANES - 1), spread(wet, LANES - 2))
+    to_west = carry[1] * jnp.where(odd, spread(wet, 1), spread(wet, 0))
+    even = is_even("lon")
     row = iota((rows, LANES), 0)
     mixing = mix[...]
-    for i, (near, far) in enumerate(((LANES - 1, LANES - 2), (0, 1))):
+    lines = []
+    for near, far in ((LANES - 1, LANES - 2), (0, 1)):
         line = jnp.zeros((rows, LANES), F32)
         for part, column in enumerate((wet[:, near], wet[:, far], mixing[:, near])):
             line = jnp.where(lane == part * rows + row, column[:, None], line)
-        cols[2 * rows + i : 2 * rows + i + 1, :] = jnp.sum(line, axis=0, keepdims=True)
+        lines.append(jnp.sum(line, axis=0, keepdims=True))
+    for msg, flag in ((msg_a, even), (msg_b, jnp.logical_not(even))):
+        msg[0:rows, :] = jnp.where(flag, to_east, to_west)
+        msg[rows:, :] = jnp.zeros((8, LANES), F32)
+        msg[rows + 4 : rows + 5, :] = jnp.where(flag, *lines)
 
 
 def prepare_kernel(
@@ -176,7 +181,7 @@
     ids[0:1, :] = places
 
 
-def corner_kernel(lat_count, lon_count, rows, fields, got_a, got_b, cols, north, south, message):
+def corner_kernel(lat_count, fields, got_a, got_b, tail_a, tail_b, north, south, new_a, new_b):
     fold = lax.axis_index("lat") == lat_count - 1
     even = is_even("lat")
     a, b = got_a[...], got_b[...]
@@ -194,43 +199,40 @@
     north[...] = jnp.where(fold, flipped, straight)
     lane, field = iota((fields, LANES), 1), iota((fields, LANES), 0)
     lane1 = iota((1, LANES), 1)
-    corners = []
-    for ref in (north, south):
+    for old, new in ((tail_a, new_a), (tail_b, new_b)):
+        new[...] = old[...]
+    for i, ref in enumerate((north, south)):
         near = ref[0:fields, :]
         ends = jnp.where(
             lane == 2 * field, near[:, 0:1], jnp.where(lane == 2 * field + 1, near[:, LANES - 1 :], 0.0)
         )
-        corners.append(jnp.sum(ends, axis=0, keepdims=True))
-    for ref in (north, south):
+        corner = jnp.sum(ends, axis=0, keepdims=True)
         wet = ref[2 * fields : 2 * fields + 1, :]
-        corners.append(jnp.where(lane1 == 0, wet[:, 0:1], wet[:, LANES - 1 :]))
-    message[...] = jnp.zeros(message.shape, F32)
-    me = lax.axis_index("lon")
-    for i, step in enumerate((1, lon_count - 1)):
-        start = pl.multiple_of(lax.rem(me + step, lon_count) * (rows + 8), 8)
-        message[pl.ds(start, rows), :] = cols[i * rows : (i + 1) * rows, :]
-        extra = [*corners, cols[2 * rows + i : 2 * rows + i + 1, :], jnp.zeros((3, LANES), F32)]
-        message[pl.ds(start + rows, 8), :] = jnp.concatenate(extra, axis=0)
+        wet = jnp.where(lane1 == 0, wet[:, 0:1], wet[:, LANES - 1 :])
+        for new in (new_a, new_b):
+            new[i : i + 1, :] = corner
+            new[2 + i : 3 + i, :] = wet
 
 
 class Sides:
-    def __init__(self, rows, lon_count, got, cols):
-        me = lax.axis_index("lon")
+    def __init__(self, rows, got_a, got_b, msg_a, msg_b):
         lane, row = iota((rows, LANES), 1), iota((rows, LANES), 0)
         self.even = (lane & 1) == 0
         self.even1 = (iota((1, LANES), 1) & 1) == 0
-        halves, extras = [], []
-        for step in (1, lon_count - 1):
-            start = pl.multiple_of(lax.rem(me + step, lon_count) * (rows + 8), 8)
-            halves.append(got[pl.ds(start, rows), :])
-            extras.append(got[pl.ds(start + rows, 8), :])
-        self.got, self.extras, self.cols, self.rows = halves, extras, cols, rows
+        even = is_even("lon")
+
+        def ordered(a, b, place):
+            return jnp.where(even, a[place, :], b[place, :]), jnp.where(even, b[place, :], a[place, :])
+
+        self.got = ordered(got_a, got_b, slice(0, rows))
+        self.mine = ordered(msg_a, msg_b, slice(0, rows))
+        self.extras = ordered(got_a, got_b, slice(rows, rows + 8))
         self.columns = [
             [
                 jnp.sum(jnp.where(lane == i * rows + row, x[4:5], 0.0), axis=1, keepdims=True)
                 for i in range(3)
             ]
-            for x in extras
+            for x in self.extras
         ]
 
     def near(self):
@@ -238,7 +240,7 @@
 
     def far_and_inner(self):
         east, west = self.got
-        mine_e, mine_w = self.cols[0 : self.rows, :], self.cols[self.rows : 2 * self.rows, :]
+        mine_e, mine_w = self.mine
         far = jnp.where(self.even, pltpu.roll(east, LANES - 1, 1), pltpu.roll(west, 1, 1))
         inner = jnp.where(self.even, pltpu.roll(mine_e, LANES - 1, 1), pltpu.roll(mine_w, 1, 1))
         return far, inner
@@ -487,8 +489,8 @@
 
 
 def surface_kernel(
-    rows, levels, lon_count,
-    state, base, cols, got, north, south, out_in, ids,
+    rows, levels,
+    state, base, msg_a, msg_b, got_a, got_b, north, south, out_in, ids,
     coef, side, out, now, later, wet_pad, stage, places, sem,
 ):
     fields = 4 * levels
@@ -501,7 +503,7 @@
     table = base[2 * rows :, :]
     coriolis = table[PAD : PAD + rows]
     lane = iota((rows, LANES), 1)
-    sides = Sides(rows, lon_count, got, cols)
+    sides = Sides(rows, got_a, got_b, msg_a, msg_b)
     wet_pad[PAD : PAD + rows, :] = wet
     wet_pad[PAD - 1 : PAD, :] = south[2 * fields : 2 * fields + 1, :]
     wet_pad[PAD + rows : PAD + rows + 1, :] = north[2 * fields : 2 * fields + 1, :]
@@ -577,13 +579,13 @@
 
 
 def main_kernel(
-    rows, levels, lon_count, chunks,
-    state, base, cols, got, north, south, col_map, row_map, coefs, side,
+    rows, levels, chunks,
+    state, base, msg_a, msg_b, got_a, got_b, north, south, col_map, row_map, coefs, side,
     tr_hbm, ve_hbm, now, later, side_new, tr_out, ve_out, sems,
 ):
     fields = 4 * levels
     pitch = rows + 2 * PAD
-    sides = Sides(rows, lon_count, got, cols)
+    sides = Sides(rows, got_a, got_b, msg_a, msg_b)
     side_new[...], north_new, south_new = halo_after_first(
         rows, levels, sides, north, south, state, base[0:rows, :], base[2 * rows :, :],
         col_map[...], row_map[...],
@@ -693,7 +695,7 @@
     lon_count, lat_count = lax.axis_size("lon"), lax.axis_size("lat")
     devices = lon_count * lat_count
     assert cols == LANES and rows % 8 == 0 and 2 * fields == LANES
-    assert lon_count > 2 and lat_count % 2 == 0 and 3 * rows <= LANES
+    assert lon_count % 2 == 0 and lat_count % 2 == 0 and 3 * rows <= LANES
     length = 2 * fields + 8
     pitch = rows + 2 * PAD
     flat = 2 * levels * rows
@@ -719,9 +721,9 @@
     got_lat_a = lax.ppermute(lat_a, ("lon", "lat"), swap_a)
 
     tr, ve = tracers.reshape(flat, cols), velocity.reshape(flat, cols)
-    columns = call(
+    msg_a, msg_b = call(
         functools.partial(pack_kernel, rows, fields),
-        shaped(2 * rows + 8, cols),
+        [shaped(rows + 8, cols)] * 2,
         in_specs=[vmem] * 4,
     )(tr, ve, land_mask, mixing)
 
@@ -740,18 +742,26 @@
         scratch_shapes=[pltpu.SMEM((devices,), jnp.int32)],
     )(tr, ve, land_mask, mixing, owners.reshape(rows), atm_row)
 
-    size = rows + 8
-    north, south, message = call(
-        functools.partial(corner_kernel, lat_count, lon_count, rows, fields),
-        [shaped(length, cols), shaped(length, cols), shaped(lon_count * size, cols)],
-    )(got_lat_a, got_lat_b, columns)
-    got = lax.all_to_all(
-        message.reshape(lon_count, size, cols), "lon", 0, 0, tiled=True
-    ).reshape(lon_count * size, cols)
+    def full(n):
+        return pl.BlockSpec((n, cols), lambda i: (0, 0))
+
+    tail = pl.BlockSpec((8, cols), lambda i: (rows // 8, 0))
+    north, south, msg_a, msg_b = call(
+        functools.partial(corner_kernel, lat_count, fields),
+        [shaped(length, cols)] * 2 + [shaped(rows + 8, cols)] * 2,
+        grid=(1,),
+        in_specs=[full(length), full(length), tail, tail],
+        out_specs=[full(length), full(length), tail, tail],
+        input_output_aliases={2: 2, 3: 3},
+    )(got_lat_a, got_lat_b, msg_a, msg_b)
+    even_pairs = [(i, i ^ 1) for i in range(lon_count)]
+    odd_pairs = [(i, (i + 1 if i % 2 else i - 1) % lon_count) for i in range(lon_count)]
+    got_a = lax.ppermute(msg_a, "lon", even_pairs)
+    got_b = lax.ppermute(msg_b, "lon", odd_pairs)
 
     count = min(3, levels)
     coefs, side, outgoing = call(
-        functools.partial(surface_kernel, rows, levels, lon_count),
+        functools.partial(surface_kernel, rows, levels),
         [
             shaped(len(COEFFICIENTS) * rows, cols),
             shaped(rows, cols),
@@ -765,16 +775,16 @@
             pltpu.SMEM((8, cols), jnp.int32),
             pltpu.SemaphoreType.DMA,
         ],
-    )(state, base, columns, got, north, south, outgoing, ids)
+    )(state, base, msg_a, msg_b, got_a, got_b, north, south, outgoing, ids)
     incoming = lax.all_to_all(
         outgoing.reshape(devices, slot_rows, 1, cols), ("lon", "lat"), 0, 0, tiled=True
     ).reshape(devices * slot_rows, cols)
 
     chunks = 4
     tr_out, ve_out = call(
-        functools.partial(main_kernel, rows, levels, lon_count, chunks),
+        functools.partial(main_kernel, rows, levels, chunks),
         [shaped(flat, cols), shaped(flat, cols)],
-        in_specs=[vmem] * 10,
+        in_specs=[vmem] * 12,
         out_specs=[hbm] * 2,
         scratch_shapes=[
             pltpu.VMEM((fields * pitch, cols), F32),
@@ -787,7 +797,7 @@
         cost_estimate=pl.CostEstimate(
             flops=80 * fields * rows * cols, bytes_accessed=5 << 20, transcendentals=0
         ),
-    )(state, base, columns, got, north, south, col_map, row_map, coefs, side)
+    )(state, base, msg_a, msg_b, got_a, got_b, north, south, col_map, row_map, coefs, side)
     surface, cover = call(
         functools.partial(reduce_kernel, devices),
         [shaped(4, ATM_ROWS, cols), shaped(ATM_ROWS, cols)],

time: 35.1 us -> 32.7 us (0.932)
  Pallas kernels: 12 us -> 11.1 us
  waiting for transfers between devices: 7.09 us -> 6.3 us
  local copies, waits for them, and re-layouts: 0.69 us -> 0.02 us
    all_to_all x1 -> x0, starting transfers between devices: 4.74 us -> none  [local(): lax.all_to_all(message.reshape(lon_count, size, cols), 'lon', 0, 0, tiled...]
    ppermute x0 -> x2, starting transfers between devices: none -> 4.07 us  [the longest x1 2.58 us: local(): got_a = lax.ppermute(msg_a, 'lon', even_pairs)]
    all_to_all x1 -> x0, waiting for transfers between devices: 3.19 us -> none  [local(): lax.all_to_all(message.reshape(lon_count, size, cols), 'lon', 0, 0, tiled...]
    ppermute x0 -> x2, waiting for transfers between devices: none -> 2.15 us  [the longest x1 2.14 us: local(): got_b = lax.ppermute(msg_b, 'lon', odd_pairs)]
    pallas_call x4, Pallas kernels: 8.05 us -> 7.12 us  [the longest x1 4.45 us: local(): call(functools.partial(main_kernel, rows, levels, chunks), [shaped(flat,...]
    all_to_all x1, starting transfers between devices: 8.11 us -> 8.84 us  [local(): lax.all_to_all(outgoing.reshape(devices, slot_rows, 1, cols), ('lon', 'la...]
    unnamed x12, local copies, waits for them, and re-layouts: 0.69 us -> 0.02 us
  transfers between devices with their start and end apart: 4 -> 5, of which waited for: 2 -> 2; matrix products, arithmetic and copies ran while one was open for 0% -> 0% of each run, Pallas kernels for 20% -> 21%
where the time goes in v6:
time: 32.7 us; the launch traced here: 32.3 us
  starting transfers between devices  14.1 us (43%)
  Pallas kernels  11.1 us (34%)
  waiting for transfers between devices  6.3 us (19%)
  between operations  0.78 us (2%)
    all_to_all x1, starting transfers between devices, local(): lax.all_to_all(outgoing.reshape(devices, slot_rows, 1, cols), ('lon', 'la...  8.84 us
    pallas_call x1, Pallas kernels, local(): call(functools.partial(main_kernel, rows, levels, chunks), [shaped(flat,...  4.45 us
    all_to_all x1, waiting for transfers between devices, local(): lax.all_to_all(outgoing.reshape(devices, slot_rows, 1, cols), ('lon', 'la...  4.15 us
    ppermute x1, starting transfers between devices, local(): got_a = lax.ppermute(msg_a, 'lon', even_pairs)  2.58 us
    ppermute x1, waiting for transfers between devices, local(): got_b = lax.ppermute(msg_b, 'lon', odd_pairs)  2.14 us
    pallas_call x1, Pallas kernels, local(): call(functools.partial(edge_kernel, rows, fields), [shaped(length, cols)]...  1.96 us
    ppermute x1, starting transfers between devices, local(): got_b = lax.ppermute(msg_b, 'lon', odd_pairs)  1.49 us
    pallas_call x1, Pallas kernels, local(): call(functools.partial(surface_kernel, rows, levels), [shaped(len(COEFFIC...  1.31 us
  transfers between devices with their start and end apart: 5, of which 2 were waited for; matrix products, arithmetic and copies ran while one was open for 0% of the time, Pallas kernels for 21%

profile of v6, /device:TPU:0, one launch (start us, length us, event | category | flops | bytes accessed | tf_op | source)
XLA Modules:
  0.0 32.3 jit_solution(273370239317709252)
XLA Ops:
  0.6 0.0 copy-start
  0.6 0.0 copy-start.1
  0.7 0.0 copy-start.2
  0.7 0.0 copy-start.3
  0.7 2.0 %shard_map.94 = (f32[136,128]{1,0:T(8,128)}, f32[136,128]{1,0:T(8,128)}) custom-call(f32[32,32,128]{2,1,0:T(8,128)} %bitcast.9, f32[32,32,128]{2,1,0:T(8,128)} %bitcast.12, s32[32,128]{1,0:T(8,128)} %mask.3, f32[32,128]{1,0:T(8,128)} %mix.3), custom_call_target="tpu_custom_call" | custom-call | tf_op jit(solution)/shard_map/pallas_call | solution.py:707
  2.6 0.5 %collective-permute-start = (f32[136,128]{1,0:T(8,128)}, f32[136,128]{1,0:T(8,128)S(1)}, u32[]{:S(2)}, u32[]{:S(2)}) collective-permute-start(f32[136,128]{1,0:T(8,128)} %get-tuple-element.27), channel_id=1, source_target_pairs={{0,1},{1,0},{2,3},{3,2},{4,5},{5,4},{6,7},{7,6},{8,9},{9,8},{10,11... | collective-permute-start | bytes 208904 | tf_op jit(solution)/shard_map/ppermute | solution.py:721
  3.2 0.7 %collective-permute-start.1 = (f32[136,128]{1,0:T(8,128)}, f32[136,128]{1,0:T(8,128)S(1)}, u32[]{:S(2)}, u32[]{:S(2)}) collective-permute-start(f32[136,128]{1,0:T(8,128)} %get-tuple-element.28), channel_id=1, source_target_pairs={{1,2},{2,1},{3,4},{4,3},{5,6},{6,5},{7,31},{9,10},{10,9},{11,12},{... | collective-permute-start | bytes 208904 | tf_op jit(solution)/shard_map/ppermute | solution.py:720
  3.8 0.0 copy-done
  3.8 0.0 copy-done.1
  3.8 0.0 copy-done.2
  3.8 0.0 copy-done.3
  3.9 1.2 %shard_map.95 = (f32[40,128]{1,0:T(8,128)S(1)}, f32[40,128]{1,0:T(8,128)S(1)}) custom-call(f32[1024,128]{1,0:T(8,128)S(1)} %bitcast.10, f32[1024,128]{1,0:T(8,128)S(1)} %bitcast.13, s32[32,128]{1,0:T(8,128)S(1)} %copy-done.2, f32[32,128]{1,0:T(8,128)S(1)} %copy-done.3), custom_call_target="tpu_custom_call" | custom-call | tf_op jit(solution)/shard_map/pallas_call | solution.py:724
  5.0 0.0 collective-permute-done.got_a
  5.1 0.0 collective-permute-done.1.got_b
  5.1 0.2 shard_map.96
  5.2 2.6 %collective-permute-start.2 = (f32[40,128]{1,0:T(8,128)S(1)}, f32[40,128]{1,0:T(8,128)S(1)}, u32[]{:S(2)}, u32[]{:S(2)}) collective-permute-start(f32[40,128]{1,0:T(8,128)S(1)} %get-tuple-element.31.msg_a), channel_id=1, source_target_pairs={{0,8},{8,0},{16,24},{24,16},{1,9},{9,1},{17,25},{25,17},{2,10},{10... | collective-permute-start | bytes 61448 | tf_op jit(solution)/shard_map/ppermute | solution.py:759
  7.8 0.0 copy-start.4
  7.8 0.0 copy-start.5
  7.8 1.5 %collective-permute-start.3 = (f32[40,128]{1,0:T(8,128)S(1)}, f32[40,128]{1,0:T(8,128)S(1)}, u32[]{:S(2)}, u32[]{:S(2)}) collective-permute-start(f32[40,128]{1,0:T(8,128)S(1)} %get-tuple-element.32.msg_b), channel_id=1, source_target_pairs={{0,24},{8,16},{16,8},{24,0},{1,25},{9,17},{17,9},{25,1},{2,26},{10... | collective-permute-start | bytes 61448 | tf_op jit(solution)/shard_map/ppermute | solution.py:760
  9.3 0.0 copy-done.4
  9.3 0.0 copy-done.5
  9.3 1.0 %shard_map.93 = (f32[2048,128]{1,0:T(8,128)S(1)}, f32[112,128]{1,0:T(8,128)S(1)}, f32[384,128]{1,0:T(8,128)S(1)}, f32[80,128]{1,0:T(8,128)S(1)}, f32[352,128]{1,0:T(8,128)S(1)}, /*index=5*/s32[8,128]{1,0:T(8,128)S(1)}) custom-call(f32[1024,128]{1,0:T(8,128)S(1)} %bitcast.11, f32[1024,128]{1,0:T(8,128)S(1)} %bitcast.14, s32[32,128]{1,0:T(8,128)S(1)} %copy-done.2, ...), custom_call_target="tpu_custom_call" | custom-call | tf_op jit(solution)/shard_map/pallas_call | solution.py:731
  10.4 0.0 collective-permute-done.2.got_a
  10.4 2.1 %collective-permute-done.3.got_b = f32[40,128]{1,0:T(8,128)S(1)} collective-permute-done((f32[40,128]{1,0:T(8,128)S(1)}, f32[40,128]{1,0:T(8,128)S(1)}, u32[]{:S(2)}, u32[]{:S(2)}) %collective-permute-start.3) | collective-permute-done | bytes 20512 | tf_op jit(solution)/shard_map/ppermute | solution.py:760
  12.5 1.3 %shard_map.97 = (f32[416,128]{1,0:T(8,128)S(1)}, f32[32,128]{1,0:T(8,128)S(1)}, f32[352,128]{1,0:T(8,128)}) custom-call(f32[2048,128]{1,0:T(8,128)S(1)} %get-tuple-element.25.state, f32[112,128]{1,0:T(8,128)S(1)} %get-tuple-element.26.base, f32[40,128]{1,0:T(8,128)S(1)} %get-tuple-element.31.msg_a, f32[40,128]{1,0:T(8,128)S(1)} %get-tuple-element.32.msg_b, ...), custom_call_target="tpu_custom_call" | custom-call | tf_op jit(solution)/shard_map/pallas_call | solution.py:763
  13.8 8.8 %all-to-all-start = ((f32[32,11,1,128]{3,2,1,0:T(1,128)}), f32[32,11,1,128]{3,2,1,0:T(1,128)S(1)}, u32[]{:S(2)}, u32[]{:S(2)}) async-start(f32[32,11,1,128]{3,2,1,0:T(1,128)} %bitcast.7), calls=%async_computation | async-start | bytes 360448 | tf_op jit(solution)/shard_map/all_to_all | solution.py:779
  22.7 4.5 %shard_map.98 = (f32[1024,128]{1,0:T(8,128)}, f32[1024,128]{1,0:T(8,128)}) custom-call(f32[2048,128]{1,0:T(8,128)S(1)} %get-tuple-element.25.state, f32[112,128]{1,0:T(8,128)S(1)} %get-tuple-element.26.base, f32[40,128]{1,0:T(8,128)S(1)} %get-tuple-element.31.msg_a, f32[40,128]{1,0:T(8,128)S(1)} %get-tuple-element.32.msg_b, ...), custom_call_target="tpu_custom_call" | custom-call | flops 20971520 | bytes 5242880 | tf_op jit(solution)/shard_map/pallas_call | solution.py:784
  27.1 4.1 %all-to-all-done = f32[32,11,1,128]{3,2,1,0:T(1,128)S(1)} async-done(((f32[32,11,1,128]{3,2,1,0:T(1,128)}), f32[32,11,1,128]{3,2,1,0:T(1,128)S(1)}, u32[]{:S(2)}, u32[]{:S(2)}) %all-to-all-start) | async-done | bytes 180256 | tf_op jit(solution)/shard_map/all_to_all | solution.py:779
  31.3 1.0 %shard_map.99 = (f32[4,32,128]{2,1,0:T(8,128)}, f32[32,128]{1,0:T(8,128)}) custom-call(f32[352,128]{1,0:T(8,128)S(1)} %bitcast.15), custom_call_target="tpu_custom_call" | custom-call | tf_op jit(solution)/shard_map/pallas_call | solution.py:801
Async XLA Ops:
  0.6 3.2 %copy-start = (f32[2,16,32,128]{3,2,1,0:T(8,128)S(1)}, f32[2,16,32,128]{3,2,1,0:T(8,128)}, u32[]{:S(2)}) copy-start(f32[2,16,32,128]{3,2,1,0:T(8,128)} %param.6) | copy-start | bytes 1572868
  0.6 3.2 %copy-start.1 = (f32[2,16,32,128]{3,2,1,0:T(8,128)S(1)}, f32[2,16,32,128]{3,2,1,0:T(8,128)}, u32[]{:S(2)}) copy-start(f32[2,16,32,128]{3,2,1,0:T(8,128)} %param.7) | copy-start | bytes 1572868
  0.7 3.2 %copy-start.2 = (s32[32,128]{1,0:T(8,128)S(1)}, s32[32,128]{1,0:T(8,128)}, u32[]{:S(2)}) copy-start(s32[32,128]{1,0:T(8,128)} %mask.3) | copy-start | bytes 49156
  0.7 3.2 %copy-start.3 = (f32[32,128]{1,0:T(8,128)S(1)}, f32[32,128]{1,0:T(8,128)}, u32[]{:S(2)}) copy-start(f32[32,128]{1,0:T(8,128)} %mix.3) | copy-start | bytes 49156
  2.6 2.4 %collective-permute-start = (f32[136,128]{1,0:T(8,128)}, f32[136,128]{1,0:T(8,128)S(1)}, u32[]{:S(2)}, u32[]{:S(2)}) collective-permute-start(f32[136,128]{1,0:T(8,128)} %get-tuple-element.27), channel_id=1, source_target_pairs={{0,1},{1,0},{2,3},{3,2},{4,5},{5,4},{6,7},{7,6},{8,9},{9,8},{10,11... | collective-permute-start | bytes 208904 | tf_op jit(solution)/shard_map/ppermute | solution.py:721
  3.2 1.9 %collective-permute-start.1 = (f32[136,128]{1,0:T(8,128)}, f32[136,128]{1,0:T(8,128)S(1)}, u32[]{:S(2)}, u32[]{:S(2)}) collective-permute-start(f32[136,128]{1,0:T(8,128)} %get-tuple-element.28), channel_id=1, source_target_pairs={{1,2},{2,1},{3,4},{4,3},{5,6},{6,5},{7,31},{9,10},{10,9},{11,12},{... | collective-permute-start | bytes 208904 | tf_op jit(solution)/shard_map/ppermute | solution.py:720
  5.2 5.1 %collective-permute-start.2 = (f32[40,128]{1,0:T(8,128)S(1)}, f32[40,128]{1,0:T(8,128)S(1)}, u32[]{:S(2)}, u32[]{:S(2)}) collective-permute-start(f32[40,128]{1,0:T(8,128)S(1)} %get-tuple-element.31.msg_a), channel_id=1, source_target_pairs={{0,8},{8,0},{16,24},{24,16},{1,9},{9,1},{17,25},{25,17},{2,10},{10... | collective-permute-start | bytes 61448 | tf_op jit(solution)/shard_map/ppermute | solution.py:759
  7.8 1.5 %copy-start.4 = (s32[32,1]{0,1:T(1,128)S(1)}, s32[32,1]{0,1:T(1,128)}, u32[]{:S(2)}) copy-start(s32[32,1]{0,1:T(1,128)} %param.10) | copy-start | bytes 388
  7.8 1.5 %copy-start.5 = (s32[32]{0:T(128)S(1)}, s32[32]{0:T(128)}, u32[]{:S(2)}) copy-start(s32[32]{0:T(128)} %atm_row.1) | copy-start | bytes 388
  7.8 4.7 %collective-permute-start.3 = (f32[40,128]{1,0:T(8,128)S(1)}, f32[40,128]{1,0:T(8,128)S(1)}, u32[]{:S(2)}, u32[]{:S(2)}) collective-permute-start(f32[40,128]{1,0:T(8,128)S(1)} %get-tuple-element.32.msg_b), channel_id=1, source_target_pairs={{0,24},{8,16},{16,8},{24,0},{1,25},{9,17},{17,9},{25,1},{2,26},{10... | collective-permute-start | bytes 61448 | tf_op jit(solution)/shard_map/ppermute | solution.py:760
  13.8 17.5 %all-to-all-start = ((f32[32,11,1,128]{3,2,1,0:T(1,128)}), f32[32,11,1,128]{3,2,1,0:T(1,128)S(1)}, u32[]{:S(2)}, u32[]{:S(2)}) async-start(f32[32,11,1,128]{3,2,1,0:T(1,128)} %bitcast.7), calls=%async_computation | async-start | bytes 360448 | tf_op jit(solution)/shard_map/all_to_all | solution.py:779

commit v7 on v6

--- a/solution.py
+++ b/solution.py
@@ -109,7 +109,7 @@
         for part, column in enumerate((wet[:, near], wet[:, far], mixing[:, near])):
             line = jnp.where(lane == part * rows + row, column[:, None], line)
         lines.append(jnp.sum(line, axis=0, keepdims=True))
-    for msg, flag in ((msg_a, even), (msg_b, jnp.logical_not(even))):
+    for msg, flag in ((msg_a, jnp.logical_not(even)), (msg_b, even)):
         msg[0:rows, :] = jnp.where(flag, to_east, to_west)
         msg[rows:, :] = jnp.zeros((8, LANES), F32)
         msg[rows + 4 : rows + 5, :] = jnp.where(flag, *lines)
@@ -158,6 +158,7 @@
     row_map[fields:, 0:fields] = press
 
     slot_rows = out.shape[0] // devices
+    lon_count, lat_count = lax.axis_size("lon"), lax.axis_size("lat")
 
     def clear(d, carry):
         used[d] = 0
@@ -171,7 +172,7 @@
         owner = own[r]
         slot = used[owner]
         used[owner] = slot + 1
-        start = owner * slot_rows
+        start = (lax.rem(owner, lat_count) * lon_count + owner // lat_count) * slot_rows
         places = jnp.where(lane1 == r, start + 4 * slot, places)
         out[pl.ds(start + 4 * CAP + slot, 1), :] = base[r : r + 1, :]
         line = out[pl.ds(start + 5 * CAP, 1), :]
@@ -181,7 +182,7 @@
     ids[0:1, :] = places
 
 
-def corner_kernel(lat_count, fields, got_a, got_b, tail_a, tail_b, north, south, new_a, new_b):
+def corner_kernel(lat_count, fields, got_b, got_a, tail_a, tail_b, north, south, new_a, new_b):
     fold = lax.axis_index("lat") == lat_count - 1
     even = is_even("lat")
     a, b = got_a[...], got_b[...]
@@ -222,7 +223,7 @@
         even = is_even("lon")
 
         def ordered(a, b, place):
-            return jnp.where(even, a[place, :], b[place, :]), jnp.where(even, b[place, :], a[place, :])
+            return jnp.where(even, b[place, :], a[place, :]), jnp.where(even, a[place, :], b[place, :])
 
         self.got = ordered(got_a, got_b, slice(0, rows))
         self.mine = ordered(msg_a, msg_b, slice(0, rows))
@@ -753,11 +754,11 @@
         in_specs=[full(length), full(length), tail, tail],
         out_specs=[full(length), full(length), tail, tail],
         input_output_aliases={2: 2, 3: 3},
-    )(got_lat_a, got_lat_b, msg_a, msg_b)
+    )(got_lat_b, got_lat_a, msg_a, msg_b)
     even_pairs = [(i, i ^ 1) for i in range(lon_count)]
     odd_pairs = [(i, (i + 1 if i % 2 else i - 1) % lon_count) for i in range(lon_count)]
-    got_a = lax.ppermute(msg_a, "lon", even_pairs)
-    got_b = lax.ppermute(msg_b, "lon", odd_pairs)
+    got_b = lax.ppermute(msg_b, "lon", even_pairs)
+    got_a = lax.ppermute(msg_a, "lon", odd_pairs)
 
     count = min(3, levels)
     coefs, side, outgoing = call(
@@ -777,7 +778,7 @@
         ],
     )(state, base, msg_a, msg_b, got_a, got_b, north, south, outgoing, ids)
     incoming = lax.all_to_all(
-        outgoing.reshape(devices, slot_rows, 1, cols), ("lon", "lat"), 0, 0, tiled=True
+        outgoing.reshape(devices, slot_rows, 1, cols), ("lat", "lon"), 0, 0, tiled=True
     ).reshape(devices * slot_rows, cols)
 
     chunks = 4

time: 32.7 us -> 32.3 us (0.988)
  starting transfers between devices: 14.1 us -> 13.4 us
  waiting for transfers between devices: 6.3 us -> 6.63 us
    ppermute x1, starting transfers between devices: 0.52 us -> 4.45 us  [local(): got_lat_a = lax.ppermute(lat_a, ('lon', 'lat'), swap_a)]
    all_to_all x1, starting transfers between devices: 8.84 us -> 5.25 us  [local(): lax.all_to_all(outgoing.reshape(devices, slot_rows, 1, cols), ('lat', 'lo...]
    ppermute x2, starting transfers between devices: 4.07 us -> 3.05 us  [the longest x1 2.51 us: local(): got_a = lax.ppermute(msg_a, 'lon', odd_pairs)]
    all_to_all x1, waiting for transfers between devices: 4.15 us -> 4.64 us  [local(): lax.all_to_all(outgoing.reshape(devices, slot_rows, 1, cols), ('lat', 'lo...]
  transfers between devices with their start and end apart: 5 -> 5, of which waited for: 2 -> 3; matrix products, arithmetic and copies ran while one was open for 0% -> 0% of each run, Pallas kernels for 21% -> 21%
where the time goes in v7:
time: 32.3 us; the launch traced here: 32.1 us
  starting transfers between devices  13.4 us (41%)
  Pallas kernels  11.2 us (35%)
  waiting for transfers between devices  6.63 us (21%)
  between operations  0.75 us (2%)
    all_to_all x1, starting transfers between devices, local(): lax.all_to_all(outgoing.reshape(devices, slot_rows, 1, cols), ('lat', 'lo...  5.25 us
    all_to_all x1, waiting for transfers between devices, local(): lax.all_to_all(outgoing.reshape(devices, slot_rows, 1, cols), ('lat', 'lo...  4.64 us
    pallas_call x1, Pallas kernels, local(): call(functools.partial(main_kernel, rows, levels, chunks), [shaped(flat,...  4.45 us
    ppermute x1, starting transfers between devices, local(): got_lat_a = lax.ppermute(lat_a, ('lon', 'lat'), swap_a)  4.45 us
    ppermute x1, starting transfers between devices, local(): got_a = lax.ppermute(msg_a, 'lon', odd_pairs)  2.51 us
    pallas_call x1, Pallas kernels, local(): call(functools.partial(edge_kernel, rows, fields), [shaped(length, cols)]...  1.96 us
    ppermute x1, waiting for transfers between devices, local(): got_b = lax.ppermute(msg_b, 'lon', even_pairs)  1.4 us
    pallas_call x1, Pallas kernels, local(): call(functools.partial(surface_kernel, rows, levels), [shaped(len(COEFFIC...  1.31 us
  transfers between devices with their start and end apart: 5, of which 3 were waited for; matrix products, arithmetic and copies ran while one was open for 0% of the time, Pallas kernels for 21%

profile of v7, /device:TPU:0, one launch (start us, length us, event | category | flops | bytes accessed | tf_op | source)
XLA Modules:
  0.0 32.1 jit_solution(2688892367610273655)
XLA Ops:
  0.6 0.0 copy-start
  0.6 0.0 copy-start.1
  0.7 0.0 copy-start.2
  0.7 0.0 copy-start.3
  0.7 2.0 %shard_map.94 = (f32[136,128]{1,0:T(8,128)}, f32[136,128]{1,0:T(8,128)}) custom-call(f32[32,32,128]{2,1,0:T(8,128)} %bitcast.9, f32[32,32,128]{2,1,0:T(8,128)} %bitcast.12, s32[32,128]{1,0:T(8,128)} %mask.3, f32[32,128]{1,0:T(8,128)} %mix.3), custom_call_target="tpu_custom_call" | custom-call | tf_op jit(solution)/shard_map/pallas_call | solution.py:708
  2.6 0.7 %collective-permute-start = (f32[136,128]{1,0:T(8,128)}, f32[136,128]{1,0:T(8,128)S(1)}, u32[]{:S(2)}, u32[]{:S(2)}) collective-permute-start(f32[136,128]{1,0:T(8,128)} %get-tuple-element.27), channel_id=1, source_target_pairs={{1,2},{2,1},{3,4},{4,3},{5,6},{6,5},{7,31},{9,10},{10,9},{11,12},{... | collective-permute-start | bytes 208904 | tf_op jit(solution)/shard_map/ppermute | solution.py:721
  3.3 4.4 %collective-permute-start.1 = (f32[136,128]{1,0:T(8,128)}, f32[136,128]{1,0:T(8,128)S(1)}, u32[]{:S(2)}, u32[]{:S(2)}) collective-permute-start(f32[136,128]{1,0:T(8,128)} %get-tuple-element.28), channel_id=1, source_target_pairs={{0,1},{1,0},{2,3},{3,2},{4,5},{5,4},{6,7},{7,6},{8,9},{9,8},{10,11... | collective-permute-start | bytes 208904 | tf_op jit(solution)/shard_map/ppermute | solution.py:722
  7.8 0.0 copy-done
  7.8 0.0 copy-done.1
  7.8 0.0 copy-done.2
  7.8 0.0 copy-done.3
  7.8 1.2 %shard_map.95 = (f32[40,128]{1,0:T(8,128)S(1)}, f32[40,128]{1,0:T(8,128)S(1)}) custom-call(f32[1024,128]{1,0:T(8,128)S(1)} %bitcast.10, f32[1024,128]{1,0:T(8,128)S(1)} %bitcast.13, s32[32,128]{1,0:T(8,128)S(1)} %copy-done.2, f32[32,128]{1,0:T(8,128)S(1)} %copy-done.3), custom_call_target="tpu_custom_call" | custom-call | tf_op jit(solution)/shard_map/pallas_call | solution.py:725
  9.0 0.0 collective-permute-done.got_b
  9.0 0.0 collective-permute-done.1.got_a
  9.0 0.2 shard_map.96
  9.2 2.5 %collective-permute-start.2 = (f32[40,128]{1,0:T(8,128)S(1)}, f32[40,128]{1,0:T(8,128)S(1)}, u32[]{:S(2)}, u32[]{:S(2)}) collective-permute-start(f32[40,128]{1,0:T(8,128)S(1)} %get-tuple-element.31.msg_a), channel_id=1, source_target_pairs={{0,24},{8,16},{16,8},{24,0},{1,25},{9,17},{17,9},{25,1},{2,26},{10... | collective-permute-start | bytes 61448 | tf_op jit(solution)/shard_map/ppermute | solution.py:761
  11.7 0.0 copy-start.4
  11.7 0.0 copy-start.5
  11.7 0.5 %collective-permute-start.3 = (f32[40,128]{1,0:T(8,128)S(1)}, f32[40,128]{1,0:T(8,128)S(1)}, u32[]{:S(2)}, u32[]{:S(2)}) collective-permute-start(f32[40,128]{1,0:T(8,128)S(1)} %get-tuple-element.32.msg_b), channel_id=1, source_target_pairs={{0,8},{8,0},{16,24},{24,16},{1,9},{9,1},{17,25},{25,17},{2,10},{10... | collective-permute-start | bytes 61448 | tf_op jit(solution)/shard_map/ppermute | solution.py:760
  12.2 0.1 copy-done.4
  12.3 0.0 copy-done.5
  12.3 1.1 %shard_map.93 = (f32[2048,128]{1,0:T(8,128)S(1)}, f32[112,128]{1,0:T(8,128)S(1)}, f32[384,128]{1,0:T(8,128)S(1)}, f32[80,128]{1,0:T(8,128)S(1)}, f32[352,128]{1,0:T(8,128)S(1)}, /*index=5*/s32[8,128]{1,0:T(8,128)S(1)}) custom-call(f32[1024,128]{1,0:T(8,128)S(1)} %bitcast.11, f32[1024,128]{1,0:T(8,128)S(1)} %bitcast.14, s32[32,128]{1,0:T(8,128)S(1)} %copy-done.2, ...), custom_call_target="tpu_custom_call" | custom-call | tf_op jit(solution)/shard_map/pallas_call | solution.py:732
  13.5 0.6 %collective-permute-done.2.got_a = f32[40,128]{1,0:T(8,128)S(1)} collective-permute-done((f32[40,128]{1,0:T(8,128)S(1)}, f32[40,128]{1,0:T(8,128)S(1)}, u32[]{:S(2)}, u32[]{:S(2)}) %collective-permute-start.2) | collective-permute-done | bytes 20512 | tf_op jit(solution)/shard_map/ppermute | solution.py:761
  14.1 1.4 %collective-permute-done.3.got_b = f32[40,128]{1,0:T(8,128)S(1)} collective-permute-done((f32[40,128]{1,0:T(8,128)S(1)}, f32[40,128]{1,0:T(8,128)S(1)}, u32[]{:S(2)}, u32[]{:S(2)}) %collective-permute-start.3) | collective-permute-done | bytes 20512 | tf_op jit(solution)/shard_map/ppermute | solution.py:760
  15.5 1.3 %shard_map.97 = (f32[416,128]{1,0:T(8,128)S(1)}, f32[32,128]{1,0:T(8,128)S(1)}, f32[352,128]{1,0:T(8,128)}) custom-call(f32[2048,128]{1,0:T(8,128)S(1)} %get-tuple-element.25.state, f32[112,128]{1,0:T(8,128)S(1)} %get-tuple-element.26.base, f32[40,128]{1,0:T(8,128)S(1)} %get-tuple-element.31.msg_a, f32[40,128]{1,0:T(8,128)S(1)} %get-tuple-element.32.msg_b, ...), custom_call_target="tpu_custom_call" | custom-call | tf_op jit(solution)/shard_map/pallas_call | solution.py:764
  16.8 5.3 %all-to-all-start = ((f32[32,11,1,128]{3,2,1,0:T(1,128)}), f32[32,11,1,128]{3,2,1,0:T(1,128)S(1)}, u32[]{:S(2)}, u32[]{:S(2)}) async-start(f32[32,11,1,128]{3,2,1,0:T(1,128)} %bitcast.7), calls=%async_computation | async-start | bytes 360448 | tf_op jit(solution)/shard_map/all_to_all | solution.py:780
  22.0 4.5 %shard_map.98 = (f32[1024,128]{1,0:T(8,128)}, f32[1024,128]{1,0:T(8,128)}) custom-call(f32[2048,128]{1,0:T(8,128)S(1)} %get-tuple-element.25.state, f32[112,128]{1,0:T(8,128)S(1)} %get-tuple-element.26.base, f32[40,128]{1,0:T(8,128)S(1)} %get-tuple-element.31.msg_a, f32[40,128]{1,0:T(8,128)S(1)} %get-tuple-element.32.msg_b, ...), custom_call_target="tpu_custom_call" | custom-call | flops 20971520 | bytes 5242880 | tf_op jit(solution)/shard_map/pallas_call | solution.py:785
  26.5 4.6 %all-to-all-done = f32[32,11,1,128]{3,2,1,0:T(1,128)S(1)} async-done(((f32[32,11,1,128]{3,2,1,0:T(1,128)}), f32[32,11,1,128]{3,2,1,0:T(1,128)S(1)}, u32[]{:S(2)}, u32[]{:S(2)}) %all-to-all-start) | async-done | bytes 180256 | tf_op jit(solution)/shard_map/all_to_all | solution.py:780
  31.1 1.0 %shard_map.99 = (f32[4,32,128]{2,1,0:T(8,128)}, f32[32,128]{1,0:T(8,128)}) custom-call(f32[352,128]{1,0:T(8,128)S(1)} %bitcast.15), custom_call_target="tpu_custom_call" | custom-call | tf_op jit(solution)/shard_map/pallas_call | solution.py:802
Async XLA Ops:
  0.6 7.1 %copy-start = (f32[2,16,32,128]{3,2,1,0:T(8,128)S(1)}, f32[2,16,32,128]{3,2,1,0:T(8,128)}, u32[]{:S(2)}) copy-start(f32[2,16,32,128]{3,2,1,0:T(8,128)} %param.6) | copy-start | bytes 1572868
  0.6 7.1 %copy-start.1 = (f32[2,16,32,128]{3,2,1,0:T(8,128)S(1)}, f32[2,16,32,128]{3,2,1,0:T(8,128)}, u32[]{:S(2)}) copy-start(f32[2,16,32,128]{3,2,1,0:T(8,128)} %param.7) | copy-start | bytes 1572868
  0.7 7.1 %copy-start.2 = (s32[32,128]{1,0:T(8,128)S(1)}, s32[32,128]{1,0:T(8,128)}, u32[]{:S(2)}) copy-start(s32[32,128]{1,0:T(8,128)} %mask.3) | copy-start | bytes 49156
  0.7 7.1 %copy-start.3 = (f32[32,128]{1,0:T(8,128)S(1)}, f32[32,128]{1,0:T(8,128)}, u32[]{:S(2)}) copy-start(f32[32,128]{1,0:T(8,128)} %mix.3) | copy-start | bytes 49156
  2.6 6.3 %collective-permute-start = (f32[136,128]{1,0:T(8,128)}, f32[136,128]{1,0:T(8,128)S(1)}, u32[]{:S(2)}, u32[]{:S(2)}) collective-permute-start(f32[136,128]{1,0:T(8,128)} %get-tuple-element.27), channel_id=1, source_target_pairs={{1,2},{2,1},{3,4},{4,3},{5,6},{6,5},{7,31},{9,10},{10,9},{11,12},{... | collective-permute-start | bytes 208904 | tf_op jit(solution)/shard_map/ppermute | solution.py:721
  3.3 5.7 %collective-permute-start.1 = (f32[136,128]{1,0:T(8,128)}, f32[136,128]{1,0:T(8,128)S(1)}, u32[]{:S(2)}, u32[]{:S(2)}) collective-permute-start(f32[136,128]{1,0:T(8,128)} %get-tuple-element.28), channel_id=1, source_target_pairs={{0,1},{1,0},{2,3},{3,2},{4,5},{5,4},{6,7},{7,6},{8,9},{9,8},{10,11... | collective-permute-start | bytes 208904 | tf_op jit(solution)/shard_map/ppermute | solution.py:722
  9.2 4.9 %collective-permute-start.2 = (f32[40,128]{1,0:T(8,128)S(1)}, f32[40,128]{1,0:T(8,128)S(1)}, u32[]{:S(2)}, u32[]{:S(2)}) collective-permute-start(f32[40,128]{1,0:T(8,128)S(1)} %get-tuple-element.31.msg_a), channel_id=1, source_target_pairs={{0,24},{8,16},{16,8},{24,0},{1,25},{9,17},{17,9},{25,1},{2,26},{10... | collective-permute-start | bytes 61448 | tf_op jit(solution)/shard_map/ppermute | solution.py:761
  11.7 0.7 %copy-start.4 = (s32[32,1]{0,1:T(1,128)S(1)}, s32[32,1]{0,1:T(1,128)}, u32[]{:S(2)}) copy-start(s32[32,1]{0,1:T(1,128)} %param.10) | copy-start | bytes 388
  11.7 0.7 %copy-start.5 = (s32[32]{0:T(128)S(1)}, s32[32]{0:T(128)}, u32[]{:S(2)}) copy-start(s32[32]{0:T(128)} %atm_row.1) | copy-start | bytes 388
  11.7 3.8 %collective-permute-start.3 = (f32[40,128]{1,0:T(8,128)S(1)}, f32[40,128]{1,0:T(8,128)S(1)}, u32[]{:S(2)}, u32[]{:S(2)}) collective-permute-start(f32[40,128]{1,0:T(8,128)S(1)} %get-tuple-element.32.msg_b), channel_id=1, source_target_pairs={{0,8},{8,0},{16,24},{24,16},{1,9},{9,1},{17,25},{25,17},{2,10},{10... | collective-permute-start | bytes 61448 | tf_op jit(solution)/shard_map/ppermute | solution.py:760
  16.8 14.4 %all-to-all-start = ((f32[32,11,1,128]{3,2,1,0:T(1,128)}), f32[32,11,1,128]{3,2,1,0:T(1,128)S(1)}, u32[]{:S(2)}, u32[]{:S(2)}) async-start(f32[32,11,1,128]{3,2,1,0:T(1,128)} %bitcast.7), calls=%async_computation | async-start | bytes 360448 | tf_op jit(solution)/shard_map/all_to_all | solution.py:780

commit v8 on v7

--- a/solution.py
+++ b/solution.py
@@ -158,7 +158,6 @@
     row_map[fields:, 0:fields] = press
 
     slot_rows = out.shape[0] // devices
-    lon_count, lat_count = lax.axis_size("lon"), lax.axis_size("lat")
 
     def clear(d, carry):
         used[d] = 0
@@ -172,7 +171,7 @@
         owner = own[r]
         slot = used[owner]
         used[owner] = slot + 1
-        start = (lax.rem(owner, lat_count) * lon_count + owner // lat_count) * slot_rows
+        start = (devices - 1 - owner) * slot_rows
         places = jnp.where(lane1 == r, start + 4 * slot, places)
         out[pl.ds(start + 4 * CAP + slot, 1), :] = base[r : r + 1, :]
         line = out[pl.ds(start + 5 * CAP, 1), :]
@@ -778,7 +777,12 @@
         ],
     )(state, base, msg_a, msg_b, got_a, got_b, north, south, outgoing, ids)
     incoming = lax.all_to_all(
-        outgoing.reshape(devices, slot_rows, 1, cols), ("lat", "lon"), 0, 0, tiled=True
+        outgoing.reshape(devices, slot_rows, 1, cols),
+        ("lon", "lat"),
+        0,
+        0,
+        axis_index_groups=[list(range(devices))[::-1]],
+        tiled=True,
     ).reshape(devices * slot_rows, cols)
 
     chunks = 4

time: 32.3 us -> 32.2 us (level)
  no operation moved by 1% of the time
where the time goes in v8:
time: 32.2 us; the launch traced here: 31.9 us
  starting transfers between devices  13.4 us (42%)
  Pallas kernels  11.1 us (34%)
  waiting for transfers between devices  6.54 us (20%)
  between operations  0.75 us (2%)
    all_to_all x1, starting transfers between devices, local(): lax.all_to_all(outgoing.reshape(devices, slot_rows, 1, cols), ('lon', 'la...  5.25 us
    pallas_call x1, Pallas kernels, local(): call(functools.partial(main_kernel, rows, levels, chunks), [shaped(flat,...  4.45 us
    all_to_all x1, waiting for transfers between devices, local(): lax.all_to_all(outgoing.reshape(devices, slot_rows, 1, cols), ('lon', 'la...  4.45 us
    ppermute x1, starting transfers between devices, local(): got_lat_a = lax.ppermute(lat_a, ('lon', 'lat'), swap_a)  4.45 us
    ppermute x1, starting transfers between devices, local(): got_a = lax.ppermute(msg_a, 'lon', odd_pairs)  2.51 us
    pallas_call x1, Pallas kernels, local(): call(functools.partial(edge_kernel, rows, fields), [shaped(length, cols)]...  1.96 us
    ppermute x1, waiting for transfers between devices, local(): got_b = lax.ppermute(msg_b, 'lon', even_pairs)  1.4 us
    pallas_call x1, Pallas kernels, local(): call(functools.partial(surface_kernel, rows, levels), [shaped(len(COEFFIC...  1.31 us
  transfers between devices with their start and end apart: 5, of which 3 were waited for; matrix products, arithmetic and copies ran while one was open for 0% of the time, Pallas kernels for 21%

profile of v8, /device:TPU:0, one launch (start us, length us, event | category | flops | bytes accessed | tf_op | source)
XLA Modules:
  0.0 31.9 jit_solution(4903394821229090395)
XLA Ops:
  0.6 0.0 copy-start
  0.6 0.0 copy-start.1
  0.7 0.0 copy-start.2
  0.7 0.0 copy-start.3
  0.7 2.0 %shard_map.94 = (f32[136,128]{1,0:T(8,128)}, f32[136,128]{1,0:T(8,128)}) custom-call(f32[32,32,128]{2,1,0:T(8,128)} %bitcast.9, f32[32,32,128]{2,1,0:T(8,128)} %bitcast.12, s32[32,128]{1,0:T(8,128)} %mask.3, f32[32,128]{1,0:T(8,128)} %mix.3), custom_call_target="tpu_custom_call" | custom-call | tf_op jit(solution)/shard_map/pallas_call | solution.py:707
  2.6 0.7 %collective-permute-start = (f32[136,128]{1,0:T(8,128)}, f32[136,128]{1,0:T(8,128)S(1)}, u32[]{:S(2)}, u32[]{:S(2)}) collective-permute-start(f32[136,128]{1,0:T(8,128)} %get-tuple-element.27), channel_id=1, source_target_pairs={{1,2},{2,1},{3,4},{4,3},{5,6},{6,5},{7,31},{9,10},{10,9},{11,12},{... | collective-permute-start | bytes 208904 | tf_op jit(solution)/shard_map/ppermute | solution.py:720
  3.3 4.4 %collective-permute-start.1 = (f32[136,128]{1,0:T(8,128)}, f32[136,128]{1,0:T(8,128)S(1)}, u32[]{:S(2)}, u32[]{:S(2)}) collective-permute-start(f32[136,128]{1,0:T(8,128)} %get-tuple-element.28), channel_id=1, source_target_pairs={{0,1},{1,0},{2,3},{3,2},{4,5},{5,4},{6,7},{7,6},{8,9},{9,8},{10,11... | collective-permute-start | bytes 208904 | tf_op jit(solution)/shard_map/ppermute | solution.py:721
  7.8 0.0 copy-done
  7.8 0.0 copy-done.1
  7.8 0.0 copy-done.2
  7.8 0.0 copy-done.3
  7.8 1.2 %shard_map.95 = (f32[40,128]{1,0:T(8,128)S(1)}, f32[40,128]{1,0:T(8,128)S(1)}) custom-call(f32[1024,128]{1,0:T(8,128)S(1)} %bitcast.10, f32[1024,128]{1,0:T(8,128)S(1)} %bitcast.13, s32[32,128]{1,0:T(8,128)S(1)} %copy-done.2, f32[32,128]{1,0:T(8,128)S(1)} %copy-done.3), custom_call_target="tpu_custom_call" | custom-call | tf_op jit(solution)/shard_map/pallas_call | solution.py:724
  9.0 0.0 collective-permute-done.got_b
  9.0 0.0 collective-permute-done.1.got_a
  9.0 0.2 shard_map.96
  9.2 2.5 %collective-permute-start.2 = (f32[40,128]{1,0:T(8,128)S(1)}, f32[40,128]{1,0:T(8,128)S(1)}, u32[]{:S(2)}, u32[]{:S(2)}) collective-permute-start(f32[40,128]{1,0:T(8,128)S(1)} %get-tuple-element.31.msg_a), channel_id=1, source_target_pairs={{0,24},{8,16},{16,8},{24,0},{1,25},{9,17},{17,9},{25,1},{2,26},{10... | collective-permute-start | bytes 61448 | tf_op jit(solution)/shard_map/ppermute | solution.py:760
  11.7 0.0 copy-start.4
  11.7 0.0 copy-start.5
  11.7 0.5 %collective-permute-start.3 = (f32[40,128]{1,0:T(8,128)S(1)}, f32[40,128]{1,0:T(8,128)S(1)}, u32[]{:S(2)}, u32[]{:S(2)}) collective-permute-start(f32[40,128]{1,0:T(8,128)S(1)} %get-tuple-element.32.msg_b), channel_id=1, source_target_pairs={{0,8},{8,0},{16,24},{24,16},{1,9},{9,1},{17,25},{25,17},{2,10},{10... | collective-permute-start | bytes 61448 | tf_op jit(solution)/shard_map/ppermute | solution.py:759
  12.2 0.1 copy-done.4
  12.3 0.0 copy-done.5
  12.3 1.0 %shard_map.93 = (f32[2048,128]{1,0:T(8,128)S(1)}, f32[112,128]{1,0:T(8,128)S(1)}, f32[384,128]{1,0:T(8,128)S(1)}, f32[80,128]{1,0:T(8,128)S(1)}, f32[352,128]{1,0:T(8,128)S(1)}, /*index=5*/s32[8,128]{1,0:T(8,128)S(1)}) custom-call(f32[1024,128]{1,0:T(8,128)S(1)} %bitcast.11, f32[1024,128]{1,0:T(8,128)S(1)} %bitcast.14, s32[32,128]{1,0:T(8,128)S(1)} %copy-done.2, ...), custom_call_target="tpu_custom_call" | custom-call | tf_op jit(solution)/shard_map/pallas_call | solution.py:731
  13.4 0.7 %collective-permute-done.2.got_a = f32[40,128]{1,0:T(8,128)S(1)} collective-permute-done((f32[40,128]{1,0:T(8,128)S(1)}, f32[40,128]{1,0:T(8,128)S(1)}, u32[]{:S(2)}, u32[]{:S(2)}) %collective-permute-start.2) | collective-permute-done | bytes 20512 | tf_op jit(solution)/shard_map/ppermute | solution.py:760
  14.1 1.4 %collective-permute-done.3.got_b = f32[40,128]{1,0:T(8,128)S(1)} collective-permute-done((f32[40,128]{1,0:T(8,128)S(1)}, f32[40,128]{1,0:T(8,128)S(1)}, u32[]{:S(2)}, u32[]{:S(2)}) %collective-permute-start.3) | collective-permute-done | bytes 20512 | tf_op jit(solution)/shard_map/ppermute | solution.py:759
  15.5 1.3 %shard_map.97 = (f32[416,128]{1,0:T(8,128)S(1)}, f32[32,128]{1,0:T(8,128)S(1)}, f32[352,128]{1,0:T(8,128)}) custom-call(f32[2048,128]{1,0:T(8,128)S(1)} %get-tuple-element.25.state, f32[112,128]{1,0:T(8,128)S(1)} %get-tuple-element.26.base, f32[40,128]{1,0:T(8,128)S(1)} %get-tuple-element.31.msg_a, f32[40,128]{1,0:T(8,128)S(1)} %get-tuple-element.32.msg_b, ...), custom_call_target="tpu_custom_call" | custom-call | tf_op jit(solution)/shard_map/pallas_call | solution.py:763
  16.8 5.3 %all-to-all-start = ((f32[32,11,1,128]{3,2,1,0:T(1,128)}), f32[32,11,1,128]{3,2,1,0:T(1,128)S(1)}, u32[]{:S(2)}, u32[]{:S(2)}) async-start(f32[32,11,1,128]{3,2,1,0:T(1,128)} %bitcast.7), calls=%async_computation | async-start | bytes 360448 | tf_op jit(solution)/shard_map/all_to_all | solution.py:779
  22.0 4.5 %shard_map.98 = (f32[1024,128]{1,0:T(8,128)}, f32[1024,128]{1,0:T(8,128)}) custom-call(f32[2048,128]{1,0:T(8,128)S(1)} %get-tuple-element.25.state, f32[112,128]{1,0:T(8,128)S(1)} %get-tuple-element.26.base, f32[40,128]{1,0:T(8,128)S(1)} %get-tuple-element.31.msg_a, f32[40,128]{1,0:T(8,128)S(1)} %get-tuple-element.32.msg_b, ...), custom_call_target="tpu_custom_call" | custom-call | flops 20971520 | bytes 5242880 | tf_op jit(solution)/shard_map/pallas_call | solution.py:789
  26.5 4.5 %all-to-all-done = f32[32,11,1,128]{3,2,1,0:T(1,128)S(1)} async-done(((f32[32,11,1,128]{3,2,1,0:T(1,128)}), f32[32,11,1,128]{3,2,1,0:T(1,128)S(1)}, u32[]{:S(2)}, u32[]{:S(2)}) %all-to-all-start) | async-done | bytes 180256 | tf_op jit(solution)/shard_map/all_to_all | solution.py:779
  31.0 1.0 %shard_map.99 = (f32[4,32,128]{2,1,0:T(8,128)}, f32[32,128]{1,0:T(8,128)}) custom-call(f32[352,128]{1,0:T(8,128)S(1)} %bitcast.15), custom_call_target="tpu_custom_call" | custom-call | tf_op jit(solution)/shard_map/pallas_call | solution.py:806
Async XLA Ops:
  0.6 7.1 %copy-start = (f32[2,16,32,128]{3,2,1,0:T(8,128)S(1)}, f32[2,16,32,128]{3,2,1,0:T(8,128)}, u32[]{:S(2)}) copy-start(f32[2,16,32,128]{3,2,1,0:T(8,128)} %param.6) | copy-start | bytes 1572868
  0.6 7.1 %copy-start.1 = (f32[2,16,32,128]{3,2,1,0:T(8,128)S(1)}, f32[2,16,32,128]{3,2,1,0:T(8,128)}, u32[]{:S(2)}) copy-start(f32[2,16,32,128]{3,2,1,0:T(8,128)} %param.7) | copy-start | bytes 1572868
  0.7 7.1 %copy-start.2 = (s32[32,128]{1,0:T(8,128)S(1)}, s32[32,128]{1,0:T(8,128)}, u32[]{:S(2)}) copy-start(s32[32,128]{1,0:T(8,128)} %mask.3) | copy-start | bytes 49156
  0.7 7.1 %copy-start.3 = (f32[32,128]{1,0:T(8,128)S(1)}, f32[32,128]{1,0:T(8,128)}, u32[]{:S(2)}) copy-start(f32[32,128]{1,0:T(8,128)} %mix.3) | copy-start | bytes 49156
  2.6 6.3 %collective-permute-start = (f32[136,128]{1,0:T(8,128)}, f32[136,128]{1,0:T(8,128)S(1)}, u32[]{:S(2)}, u32[]{:S(2)}) collective-permute-start(f32[136,128]{1,0:T(8,128)} %get-tuple-element.27), channel_id=1, source_target_pairs={{1,2},{2,1},{3,4},{4,3},{5,6},{6,5},{7,31},{9,10},{10,9},{11,12},{... | collective-permute-start | bytes 208904 | tf_op jit(solution)/shard_map/ppermute | solution.py:720
  3.3 5.7 %collective-permute-start.1 = (f32[136,128]{1,0:T(8,128)}, f32[136,128]{1,0:T(8,128)S(1)}, u32[]{:S(2)}, u32[]{:S(2)}) collective-permute-start(f32[136,128]{1,0:T(8,128)} %get-tuple-element.28), channel_id=1, source_target_pairs={{0,1},{1,0},{2,3},{3,2},{4,5},{5,4},{6,7},{7,6},{8,9},{9,8},{10,11... | collective-permute-start | bytes 208904 | tf_op jit(solution)/shard_map/ppermute | solution.py:721
  9.2 4.9 %collective-permute-start.2 = (f32[40,128]{1,0:T(8,128)S(1)}, f32[40,128]{1,0:T(8,128)S(1)}, u32[]{:S(2)}, u32[]{:S(2)}) collective-permute-start(f32[40,128]{1,0:T(8,128)S(1)} %get-tuple-element.31.msg_a), channel_id=1, source_target_pairs={{0,24},{8,16},{16,8},{24,0},{1,25},{9,17},{17,9},{25,1},{2,26},{10... | collective-permute-start | bytes 61448 | tf_op jit(solution)/shard_map/ppermute | solution.py:760
  11.7 0.7 %copy-start.4 = (s32[32,1]{0,1:T(1,128)S(1)}, s32[32,1]{0,1:T(1,128)}, u32[]{:S(2)}) copy-start(s32[32,1]{0,1:T(1,128)} %param.10) | copy-start | bytes 388
  11.7 0.7 %copy-start.5 = (s32[32]{0:T(128)S(1)}, s32[32]{0:T(128)}, u32[]{:S(2)}) copy-start(s32[32]{0:T(128)} %atm_row.1) | copy-start | bytes 388
  11.7 3.8 %collective-permute-start.3 = (f32[40,128]{1,0:T(8,128)S(1)}, f32[40,128]{1,0:T(8,128)S(1)}, u32[]{:S(2)}, u32[]{:S(2)}) collective-permute-start(f32[40,128]{1,0:T(8,128)S(1)} %get-tuple-element.32.msg_b), channel_id=1, source_target_pairs={{0,8},{8,0},{16,24},{24,16},{1,9},{9,1},{17,25},{25,17},{2,10},{10... | collective-permute-start | bytes 61448 | tf_op jit(solution)/shard_map/ppermute | solution.py:759
  16.8 14.2 %all-to-all-start = ((f32[32,11,1,128]{3,2,1,0:T(1,128)}), f32[32,11,1,128]{3,2,1,0:T(1,128)S(1)}, u32[]{:S(2)}, u32[]{:S(2)}) async-start(f32[32,11,1,128]{3,2,1,0:T(1,128)} %bitcast.7), calls=%async_computation | async-start | bytes 360448 | tf_op jit(solution)/shard_map/all_to_all | solution.py:779

commit v9 on v8

--- a/solution.py
+++ b/solution.py
@@ -652,8 +652,18 @@
         to_rows.append(named[:, slot * width : slot * width + ATM_ROWS])
         parts = [rows_of(4 * slot + q) for q in range(4)] + [rows_of(4 * CAP + slot)]
         values.append(jnp.concatenate(parts, axis=1))
-    totals = dot(
-        jnp.concatenate(to_rows, axis=0), jnp.concatenate(values, axis=0), (((0,), (0,)), ((), ()))
+    rest = jnp.concatenate(values, axis=0)
+    pieces = []
+    for _ in range(3):
+        piece = rest.astype(jnp.bfloat16)
+        pieces.append(piece)
+        rest = rest - piece.astype(F32)
+    one = jnp.concatenate(to_rows, axis=0).astype(jnp.bfloat16)
+    totals = lax.dot_general(
+        jnp.concatenate([one] * 3, axis=0),
+        jnp.concatenate(pieces, axis=0),
+        (((0,), (0,)), ((), ())),
+        preferred_element_type=F32,
     )
     ocean = totals[:, 4 * LANES :]
     cover[...] = ocean
@@ -706,7 +716,7 @@
     deep = (2 * levels, rows, cols)
     lat_a, lat_b = call(
         functools.partial(edge_kernel, rows, fields),
-        [shaped(length, cols)] * 2,
+        [pltpu.VMEM((length, cols), F32)] * 2,
         limit=VMEM_ALL,
         in_specs=[hbm] * 4,
         scratch_shapes=[
@@ -765,7 +775,7 @@
         [
             shaped(len(COEFFICIENTS) * rows, cols),
             shaped(rows, cols),
-            shaped(devices * slot_rows, cols),
+            pltpu.VMEM((devices * slot_rows, cols), F32),
         ],
         scratch_shapes=[
             pltpu.VMEM((4 * count * pitch, cols), F32),

time: 32.2 us -> 31.2 us (0.969)
  Pallas kernels: 11.1 us -> 10.4 us
    pallas_call x1, Pallas kernels: 1.96 us -> 1.31 us  [local(): call(functools.partial(edge_kernel, rows, fields), [pltpu.VMEM((length, c...]
where the time goes in v9:
time: 31.2 us; the launch traced here: 31 us
  starting transfers between devices  13.2 us (42%)
  Pallas kernels  10.4 us (33%)
  waiting for transfers between devices  6.54 us (21%)
  between operations  0.75 us (2%)
    all_to_all x1, starting transfers between devices, local(): lax.all_to_all(outgoing.reshape(devices, slot_rows, 1, cols), ('lon', 'la...  5.04 us
    pallas_call x1, Pallas kernels, local(): call(functools.partial(main_kernel, rows, levels, chunks), [shaped(flat,...  4.45 us
    all_to_all x1, waiting for transfers between devices, local(): lax.all_to_all(outgoing.reshape(devices, slot_rows, 1, cols), ('lon', 'la...  4.45 us
    ppermute x1, starting transfers between devices, local(): got_lat_a = lax.ppermute(lat_a, ('lon', 'lat'), swap_a)  4.45 us
    ppermute x1, starting transfers between devices, local(): got_a = lax.ppermute(msg_a, 'lon', odd_pairs)  2.51 us
    ppermute x1, waiting for transfers between devices, local(): got_b = lax.ppermute(msg_b, 'lon', even_pairs)  1.55 us
    pallas_call x1, Pallas kernels, local(): call(functools.partial(surface_kernel, rows, levels), [shaped(len(COEFFIC...  1.31 us
    pallas_call x1, Pallas kernels, local(): call(functools.partial(edge_kernel, rows, fields), [pltpu.VMEM((length, c...  1.31 us
  transfers between devices with their start and end apart: 5, of which 3 were waited for; matrix products, arithmetic and copies ran while one was open for 0% of the time, Pallas kernels for 21%

profile of v9, /device:TPU:0, one launch (start us, length us, event | category | flops | bytes accessed | tf_op | source)
XLA Modules:
  0.0 31.0 jit_solution(6492762439632466272)
XLA Ops:
  0.6 0.0 copy-start
  0.6 0.0 copy-start.1
  0.7 0.0 copy-start.2
  0.7 0.0 copy-start.3
  0.7 1.3 %shard_map.94 = (f32[136,128]{1,0:T(8,128)S(1)}, f32[136,128]{1,0:T(8,128)S(1)}) custom-call(f32[32,32,128]{2,1,0:T(8,128)} %bitcast.9, f32[32,32,128]{2,1,0:T(8,128)} %bitcast.12, s32[32,128]{1,0:T(8,128)} %mask.3, f32[32,128]{1,0:T(8,128)} %mix.3), custom_call_target="tpu_custom_call" | custom-call | tf_op jit(solution)/shard_map/pallas_call | solution.py:717
  2.0 0.7 %collective-permute-start = (f32[136,128]{1,0:T(8,128)S(1)}, f32[136,128]{1,0:T(8,128)S(1)}, u32[]{:S(2)}, u32[]{:S(2)}) collective-permute-start(f32[136,128]{1,0:T(8,128)S(1)} %get-tuple-element.27), channel_id=1, source_target_pairs={{1,2},{2,1},{3,4},{4,3},{5,6},{6,5},{7,31},{9,10},{10,9},{11,12},{... | collective-permute-start | bytes 208904 | tf_op jit(solution)/shard_map/ppermute | solution.py:730
  2.7 4.4 %collective-permute-start.1 = (f32[136,128]{1,0:T(8,128)S(1)}, f32[136,128]{1,0:T(8,128)S(1)}, u32[]{:S(2)}, u32[]{:S(2)}) collective-permute-start(f32[136,128]{1,0:T(8,128)S(1)} %get-tuple-element.28), channel_id=1, source_target_pairs={{0,1},{1,0},{2,3},{3,2},{4,5},{5,4},{6,7},{7,6},{8,9},{9,8},{10,11... | collective-permute-start | bytes 208904 | tf_op jit(solution)/shard_map/ppermute | solution.py:731
  7.1 0.0 copy-done
  7.1 0.0 copy-done.1
  7.1 0.0 copy-done.2
  7.1 0.0 copy-done.3
  7.1 1.2 %shard_map.95 = (f32[40,128]{1,0:T(8,128)S(1)}, f32[40,128]{1,0:T(8,128)S(1)}) custom-call(f32[1024,128]{1,0:T(8,128)S(1)} %bitcast.10, f32[1024,128]{1,0:T(8,128)S(1)} %bitcast.13, s32[32,128]{1,0:T(8,128)S(1)} %copy-done.2, f32[32,128]{1,0:T(8,128)S(1)} %copy-done.3), custom_call_target="tpu_custom_call" | custom-call | tf_op jit(solution)/shard_map/pallas_call | solution.py:734
  8.3 0.0 collective-permute-done.got_b
  8.3 0.0 collective-permute-done.1.got_a
  8.3 0.2 shard_map.96
  8.5 2.5 %collective-permute-start.2 = (f32[40,128]{1,0:T(8,128)S(1)}, f32[40,128]{1,0:T(8,128)S(1)}, u32[]{:S(2)}, u32[]{:S(2)}) collective-permute-start(f32[40,128]{1,0:T(8,128)S(1)} %get-tuple-element.31.msg_a), channel_id=1, source_target_pairs={{0,24},{8,16},{16,8},{24,0},{1,25},{9,17},{17,9},{25,1},{2,26},{10... | collective-permute-start | bytes 61448 | tf_op jit(solution)/shard_map/ppermute | solution.py:770
  11.0 0.0 copy-start.4
  11.0 0.0 copy-start.5
  11.0 0.5 %collective-permute-start.3 = (f32[40,128]{1,0:T(8,128)S(1)}, f32[40,128]{1,0:T(8,128)S(1)}, u32[]{:S(2)}, u32[]{:S(2)}) collective-permute-start(f32[40,128]{1,0:T(8,128)S(1)} %get-tuple-element.32.msg_b), channel_id=1, source_target_pairs={{0,8},{8,0},{16,24},{24,16},{1,9},{9,1},{17,25},{25,17},{2,10},{10... | collective-permute-start | bytes 61448 | tf_op jit(solution)/shard_map/ppermute | solution.py:769
  11.6 0.1 copy-done.4
  11.7 0.0 copy-done.5
  11.7 1.0 %shard_map.93 = (f32[2048,128]{1,0:T(8,128)S(1)}, f32[112,128]{1,0:T(8,128)S(1)}, f32[384,128]{1,0:T(8,128)S(1)}, f32[80,128]{1,0:T(8,128)S(1)}, f32[352,128]{1,0:T(8,128)S(1)}, /*index=5*/s32[8,128]{1,0:T(8,128)S(1)}) custom-call(f32[1024,128]{1,0:T(8,128)S(1)} %bitcast.11, f32[1024,128]{1,0:T(8,128)S(1)} %bitcast.14, s32[32,128]{1,0:T(8,128)S(1)} %copy-done.2, ...), custom_call_target="tpu_custom_call" | custom-call | tf_op jit(solution)/shard_map/pallas_call | solution.py:741
  12.7 0.5 %collective-permute-done.2.got_a = f32[40,128]{1,0:T(8,128)S(1)} collective-permute-done((f32[40,128]{1,0:T(8,128)S(1)}, f32[40,128]{1,0:T(8,128)S(1)}, u32[]{:S(2)}, u32[]{:S(2)}) %collective-permute-start.2) | collective-permute-done | bytes 20512 | tf_op jit(solution)/shard_map/ppermute | solution.py:770
  13.3 1.6 %collective-permute-done.3.got_b = f32[40,128]{1,0:T(8,128)S(1)} collective-permute-done((f32[40,128]{1,0:T(8,128)S(1)}, f32[40,128]{1,0:T(8,128)S(1)}, u32[]{:S(2)}, u32[]{:S(2)}) %collective-permute-start.3) | collective-permute-done | bytes 20512 | tf_op jit(solution)/shard_map/ppermute | solution.py:769
  14.8 1.3 %shard_map.97 = (f32[416,128]{1,0:T(8,128)S(1)}, f32[32,128]{1,0:T(8,128)S(1)}, f32[352,128]{1,0:T(8,128)}) custom-call(f32[2048,128]{1,0:T(8,128)S(1)} %get-tuple-element.25.state, f32[112,128]{1,0:T(8,128)S(1)} %get-tuple-element.26.base, f32[40,128]{1,0:T(8,128)S(1)} %get-tuple-element.31.msg_a, f32[40,128]{1,0:T(8,128)S(1)} %get-tuple-element.32.msg_b, ...), custom_call_target="tpu_custom_call" | custom-call | tf_op jit(solution)/shard_map/pallas_call | solution.py:773
  16.1 5.0 %all-to-all-start = ((f32[32,11,1,128]{3,2,1,0:T(1,128)}), f32[32,11,1,128]{3,2,1,0:T(1,128)S(1)}, u32[]{:S(2)}, u32[]{:S(2)}) async-start(f32[32,11,1,128]{3,2,1,0:T(1,128)} %bitcast.7), calls=%async_computation | async-start | bytes 360448 | tf_op jit(solution)/shard_map/all_to_all | solution.py:789
  21.2 4.5 %shard_map.98 = (f32[1024,128]{1,0:T(8,128)}, f32[1024,128]{1,0:T(8,128)}) custom-call(f32[2048,128]{1,0:T(8,128)S(1)} %get-tuple-element.25.state, f32[112,128]{1,0:T(8,128)S(1)} %get-tuple-element.26.base, f32[40,128]{1,0:T(8,128)S(1)} %get-tuple-element.31.msg_a, f32[40,128]{1,0:T(8,128)S(1)} %get-tuple-element.32.msg_b, ...), custom_call_target="tpu_custom_call" | custom-call | flops 20971520 | bytes 5242880 | tf_op jit(solution)/shard_map/pallas_call | solution.py:799
  25.6 4.5 %all-to-all-done = f32[32,11,1,128]{3,2,1,0:T(1,128)S(1)} async-done(((f32[32,11,1,128]{3,2,1,0:T(1,128)}), f32[32,11,1,128]{3,2,1,0:T(1,128)S(1)}, u32[]{:S(2)}, u32[]{:S(2)}) %all-to-all-start) | async-done | bytes 180256 | tf_op jit(solution)/shard_map/all_to_all | solution.py:789
  30.1 0.9 %shard_map.99 = (f32[4,32,128]{2,1,0:T(8,128)}, f32[32,128]{1,0:T(8,128)}) custom-call(f32[352,128]{1,0:T(8,128)S(1)} %bitcast.15), custom_call_target="tpu_custom_call" | custom-call | tf_op jit(solution)/shard_map/pallas_call | solution.py:816
Async XLA Ops:
  0.6 6.5 %copy-start = (f32[2,16,32,128]{3,2,1,0:T(8,128)S(1)}, f32[2,16,32,128]{3,2,1,0:T(8,128)}, u32[]{:S(2)}) copy-start(f32[2,16,32,128]{3,2,1,0:T(8,128)} %param.6) | copy-start | bytes 1572868
  0.6 6.5 %copy-start.1 = (f32[2,16,32,128]{3,2,1,0:T(8,128)S(1)}, f32[2,16,32,128]{3,2,1,0:T(8,128)}, u32[]{:S(2)}) copy-start(f32[2,16,32,128]{3,2,1,0:T(8,128)} %param.7) | copy-start | bytes 1572868
  0.7 6.5 %copy-start.2 = (s32[32,128]{1,0:T(8,128)S(1)}, s32[32,128]{1,0:T(8,128)}, u32[]{:S(2)}) copy-start(s32[32,128]{1,0:T(8,128)} %mask.3) | copy-start | bytes 49156
  0.7 6.5 %copy-start.3 = (f32[32,128]{1,0:T(8,128)S(1)}, f32[32,128]{1,0:T(8,128)}, u32[]{:S(2)}) copy-start(f32[32,128]{1,0:T(8,128)} %mix.3) | copy-start | bytes 49156
  2.0 6.3 %collective-permute-start = (f32[136,128]{1,0:T(8,128)S(1)}, f32[136,128]{1,0:T(8,128)S(1)}, u32[]{:S(2)}, u32[]{:S(2)}) collective-permute-start(f32[136,128]{1,0:T(8,128)S(1)} %get-tuple-element.27), channel_id=1, source_target_pairs={{1,2},{2,1},{3,4},{4,3},{5,6},{6,5},{7,31},{9,10},{10,9},{11,12},{... | collective-permute-start | bytes 208904 | tf_op jit(solution)/shard_map/ppermute | solution.py:730
  2.7 5.7 %collective-permute-start.1 = (f32[136,128]{1,0:T(8,128)S(1)}, f32[136,128]{1,0:T(8,128)S(1)}, u32[]{:S(2)}, u32[]{:S(2)}) collective-permute-start(f32[136,128]{1,0:T(8,128)S(1)} %get-tuple-element.28), channel_id=1, source_target_pairs={{0,1},{1,0},{2,3},{3,2},{4,5},{5,4},{6,7},{7,6},{8,9},{9,8},{10,11... | collective-permute-start | bytes 208904 | tf_op jit(solution)/shard_map/ppermute | solution.py:731
  8.5 4.7 %collective-permute-start.2 = (f32[40,128]{1,0:T(8,128)S(1)}, f32[40,128]{1,0:T(8,128)S(1)}, u32[]{:S(2)}, u32[]{:S(2)}) collective-permute-start(f32[40,128]{1,0:T(8,128)S(1)} %get-tuple-element.31.msg_a), channel_id=1, source_target_pairs={{0,24},{8,16},{16,8},{24,0},{1,25},{9,17},{17,9},{25,1},{2,26},{10... | collective-permute-start | bytes 61448 | tf_op jit(solution)/shard_map/ppermute | solution.py:770
  11.0 0.7 %copy-start.4 = (s32[32,1]{0,1:T(1,128)S(1)}, s32[32,1]{0,1:T(1,128)}, u32[]{:S(2)}) copy-start(s32[32,1]{0,1:T(1,128)} %param.10) | copy-start | bytes 388
  11.0 0.7 %copy-start.5 = (s32[32]{0:T(128)S(1)}, s32[32]{0:T(128)}, u32[]{:S(2)}) copy-start(s32[32]{0:T(128)} %atm_row.1) | copy-start | bytes 388
  11.0 3.8 %collective-permute-start.3 = (f32[40,128]{1,0:T(8,128)S(1)}, f32[40,128]{1,0:T(8,128)S(1)}, u32[]{:S(2)}, u32[]{:S(2)}) collective-permute-start(f32[40,128]{1,0:T(8,128)S(1)} %get-tuple-element.32.msg_b), channel_id=1, source_target_pairs={{0,8},{8,0},{16,24},{24,16},{1,9},{9,1},{17,25},{25,17},{2,10},{10... | collective-permute-start | bytes 61448 | tf_op jit(solution)/shard_map/ppermute | solution.py:769
  16.1 14.0 %all-to-all-start = ((f32[32,11,1,128]{3,2,1,0:T(1,128)}), f32[32,11,1,128]{3,2,1,0:T(1,128)S(1)}, u32[]{:S(2)}, u32[]{:S(2)}) async-start(f32[32,11,1,128]{3,2,1,0:T(1,128)} %bitcast.7), calls=%async_computation | async-start | bytes 360448 | tf_op jit(solution)/shard_map/all_to_all | solution.py:789

commit v10 on v9

--- a/solution.py
+++ b/solution.py
@@ -37,6 +37,10 @@
 
 def is_even(axis):
     return lax.rem(lax.axis_index(axis), 2) == 0
+
+
+def is_east_first():
+    return lax.rem(lax.axis_index("lon") + lax.axis_index("lat"), 2) == 1
 
 
 def start_copies(pairs, sems):
@@ -100,7 +104,7 @@
     odd = (lane & 1) == 1
     to_east = carry[0] * jnp.where(odd, spread(wet, LANES - 1), spread(wet, LANES - 2))
     to_west = carry[1] * jnp.where(odd, spread(wet, 1), spread(wet, 0))
-    even = is_even("lon")
+    east_first = is_east_first()
     row = iota((rows, LANES), 0)
     mixing = mix[...]
     lines = []
@@ -109,7 +113,7 @@
         for part, column in enumerate((wet[:, near], wet[:, far], mixing[:, near])):
             line = jnp.where(lane == part * rows + row, column[:, None], line)
         lines.append(jnp.sum(line, axis=0, keepdims=True))
-    for msg, flag in ((msg_a, jnp.logical_not(even)), (msg_b, even)):
+    for msg, flag in ((msg_a, east_first), (msg_b, jnp.logical_not(east_first))):
         msg[0:rows, :] = jnp.where(flag, to_east, to_west)
         msg[rows:, :] = jnp.zeros((8, LANES), F32)
         msg[rows + 4 : rows + 5, :] = jnp.where(flag, *lines)
@@ -219,10 +223,11 @@
         lane, row = iota((rows, LANES), 1), iota((rows, LANES), 0)
         self.even = (lane & 1) == 0
         self.even1 = (iota((1, LANES), 1) & 1) == 0
-        even = is_even("lon")
+        first = is_east_first()
 
         def ordered(a, b, place):
-            return jnp.where(even, b[place, :], a[place, :]), jnp.where(even, a[place, :], b[place, :])
+            a, b = a[place, :], b[place, :]
+            return jnp.where(first, a, b), jnp.where(first, b, a)
 
         self.got = ordered(got_a, got_b, slice(0, rows))
         self.mine = ordered(msg_a, msg_b, slice(0, rows))
@@ -698,6 +703,15 @@
     return swap_a, swap_b
 
 
+def lon_swaps(lon_count, lat_count):
+    swaps = [], []
+    for i in range(lon_count):
+        for a in range(lat_count):
+            for swap, step in zip(swaps, (1, -1) if (i + a) % 2 else (-1, 1)):
+                swap.append((i * lat_count + a, (i + step) % lon_count * lat_count + a))
+    return swaps
+
+
 def local(tracers, velocity, land_mask, mixing, owners, atm_row):
     levels = tracers.shape[1]
     rows, cols = land_mask.shape
@@ -764,10 +778,9 @@
         out_specs=[full(length), full(length), tail, tail],
         input_output_aliases={2: 2, 3: 3},
     )(got_lat_b, got_lat_a, msg_a, msg_b)
-    even_pairs = [(i, i ^ 1) for i in range(lon_count)]
-    odd_pairs = [(i, (i + 1 if i % 2 else i - 1) % lon_count) for i in range(lon_count)]
-    got_b = lax.ppermute(msg_b, "lon", even_pairs)
-    got_a = lax.ppermute(msg_a, "lon", odd_pairs)
+    swap_a, swap_b = lon_swaps(lon_count, lat_count)
+    got_b = lax.ppermute(msg_b, ("lon", "lat"), swap_b)
+    got_a = lax.ppermute(msg_a, ("lon", "lat"), swap_a)
 
     count = min(3, levels)
     coefs, side, outgoing = call(

time: 31.2 us -> 31.2 us (level)
  no operation moved by 1% of the time
where the time goes in v10:
time: 31.2 us; the launch traced here: 31 us
  starting transfers between devices  13.2 us (42%)
  Pallas kernels  10.4 us (33%)
  waiting for transfers between devices  6.54 us (21%)
  between operations  0.75 us (2%)
    all_to_all x1, starting transfers between devices, local(): lax.all_to_all(outgoing.reshape(devices, slot_rows, 1, cols), ('lon', 'la...  5.04 us
    pallas_call x1, Pallas kernels, local(): call(functools.partial(main_kernel, rows, levels, chunks), [shaped(flat,...  4.45 us
    all_to_all x1, waiting for transfers between devices, local(): lax.all_to_all(outgoing.reshape(devices, slot_rows, 1, cols), ('lon', 'la...  4.45 us
    ppermute x1, starting transfers between devices, local(): got_lat_a = lax.ppermute(lat_a, ('lon', 'lat'), swap_a)  4.45 us
    ppermute x1, starting transfers between devices, local(): got_a = lax.ppermute(msg_a, ('lon', 'lat'), swap_a)  2.51 us
    ppermute x1, waiting for transfers between devices, local(): got_b = lax.ppermute(msg_b, ('lon', 'lat'), swap_b)  1.55 us
    pallas_call x1, Pallas kernels, local(): call(functools.partial(surface_kernel, rows, levels), [shaped(len(COEFFIC...  1.31 us
    pallas_call x1, Pallas kernels, local(): call(functools.partial(edge_kernel, rows, fields), [pltpu.VMEM((length, c...  1.31 us
  transfers between devices with their start and end apart: 5, of which 3 were waited for; matrix products, arithmetic and copies ran while one was open for 0% of the time, Pallas kernels for 21%

profile of v10, /device:TPU:0, one launch (start us, length us, event | category | flops | bytes accessed | tf_op | source)
XLA Modules:
  0.0 31.0 jit_solution(8466338614568688781)
XLA Ops:
  0.6 0.0 copy-start
  0.6 0.0 copy-start.1
  0.7 0.0 copy-start.2
  0.7 0.0 copy-start.3
  0.7 1.3 %shard_map.94 = (f32[136,128]{1,0:T(8,128)S(1)}, f32[136,128]{1,0:T(8,128)S(1)}) custom-call(f32[32,32,128]{2,1,0:T(8,128)} %bitcast.9, f32[32,32,128]{2,1,0:T(8,128)} %bitcast.12, s32[32,128]{1,0:T(8,128)} %mask.3, f32[32,128]{1,0:T(8,128)} %mix.3), custom_call_target="tpu_custom_call" | custom-call | tf_op jit(solution)/shard_map/pallas_call | solution.py:731
  2.0 0.7 %collective-permute-start = (f32[136,128]{1,0:T(8,128)S(1)}, f32[136,128]{1,0:T(8,128)S(1)}, u32[]{:S(2)}, u32[]{:S(2)}) collective-permute-start(f32[136,128]{1,0:T(8,128)S(1)} %get-tuple-element.27), channel_id=1, source_target_pairs={{1,2},{2,1},{3,4},{4,3},{5,6},{6,5},{7,31},{9,10},{10,9},{11,12},{... | collective-permute-start | bytes 208904 | tf_op jit(solution)/shard_map/ppermute | solution.py:744
  2.7 4.4 %collective-permute-start.1 = (f32[136,128]{1,0:T(8,128)S(1)}, f32[136,128]{1,0:T(8,128)S(1)}, u32[]{:S(2)}, u32[]{:S(2)}) collective-permute-start(f32[136,128]{1,0:T(8,128)S(1)} %get-tuple-element.28), channel_id=1, source_target_pairs={{0,1},{1,0},{2,3},{3,2},{4,5},{5,4},{6,7},{7,6},{8,9},{9,8},{10,11... | collective-permute-start | bytes 208904 | tf_op jit(solution)/shard_map/ppermute | solution.py:745
  7.1 0.0 copy-done
  7.1 0.0 copy-done.1
  7.1 0.0 copy-done.2
  7.1 0.0 copy-done.3
  7.1 1.2 %shard_map.95 = (f32[40,128]{1,0:T(8,128)S(1)}, f32[40,128]{1,0:T(8,128)S(1)}) custom-call(f32[1024,128]{1,0:T(8,128)S(1)} %bitcast.10, f32[1024,128]{1,0:T(8,128)S(1)} %bitcast.13, s32[32,128]{1,0:T(8,128)S(1)} %copy-done.2, f32[32,128]{1,0:T(8,128)S(1)} %copy-done.3), custom_call_target="tpu_custom_call" | custom-call | tf_op jit(solution)/shard_map/pallas_call | solution.py:748
  8.3 0.0 collective-permute-done.got_b
  8.3 0.0 collective-permute-done.1.got_a
  8.3 0.2 shard_map.96
  8.5 2.5 %collective-permute-start.2 = (f32[40,128]{1,0:T(8,128)S(1)}, f32[40,128]{1,0:T(8,128)S(1)}, u32[]{:S(2)}, u32[]{:S(2)}) collective-permute-start(f32[40,128]{1,0:T(8,128)S(1)} %get-tuple-element.31.msg_a), channel_id=1, source_target_pairs={{0,24},{1,9},{2,26},{3,11},{4,28},{5,13},{6,30},{7,15},{8,16},{9,1... | collective-permute-start | bytes 61448 | tf_op jit(solution)/shard_map/ppermute | solution.py:783
  11.0 0.0 copy-start.4
  11.0 0.0 copy-start.5
  11.0 0.5 %collective-permute-start.3 = (f32[40,128]{1,0:T(8,128)S(1)}, f32[40,128]{1,0:T(8,128)S(1)}, u32[]{:S(2)}, u32[]{:S(2)}) collective-permute-start(f32[40,128]{1,0:T(8,128)S(1)} %get-tuple-element.32.msg_b), channel_id=1, source_target_pairs={{0,8},{1,25},{2,10},{3,27},{4,12},{5,29},{6,14},{7,31},{8,0},{9,17... | collective-permute-start | bytes 61448 | tf_op jit(solution)/shard_map/ppermute | solution.py:782
  11.6 0.1 copy-done.4
  11.7 0.0 copy-done.5
  11.7 1.0 %shard_map.93 = (f32[2048,128]{1,0:T(8,128)S(1)}, f32[112,128]{1,0:T(8,128)S(1)}, f32[384,128]{1,0:T(8,128)S(1)}, f32[80,128]{1,0:T(8,128)S(1)}, f32[352,128]{1,0:T(8,128)S(1)}, /*index=5*/s32[8,128]{1,0:T(8,128)S(1)}) custom-call(f32[1024,128]{1,0:T(8,128)S(1)} %bitcast.11, f32[1024,128]{1,0:T(8,128)S(1)} %bitcast.14, s32[32,128]{1,0:T(8,128)S(1)} %copy-done.2, ...), custom_call_target="tpu_custom_call" | custom-call | tf_op jit(solution)/shard_map/pallas_call | solution.py:755
  12.7 0.5 %collective-permute-done.2.got_a = f32[40,128]{1,0:T(8,128)S(1)} collective-permute-done((f32[40,128]{1,0:T(8,128)S(1)}, f32[40,128]{1,0:T(8,128)S(1)}, u32[]{:S(2)}, u32[]{:S(2)}) %collective-permute-start.2) | collective-permute-done | bytes 20512 | tf_op jit(solution)/shard_map/ppermute | solution.py:783
  13.3 1.6 %collective-permute-done.3.got_b = f32[40,128]{1,0:T(8,128)S(1)} collective-permute-done((f32[40,128]{1,0:T(8,128)S(1)}, f32[40,128]{1,0:T(8,128)S(1)}, u32[]{:S(2)}, u32[]{:S(2)}) %collective-permute-start.3) | collective-permute-done | bytes 20512 | tf_op jit(solution)/shard_map/ppermute | solution.py:782
  14.8 1.3 %shard_map.97 = (f32[416,128]{1,0:T(8,128)S(1)}, f32[32,128]{1,0:T(8,128)S(1)}, f32[352,128]{1,0:T(8,128)}) custom-call(f32[2048,128]{1,0:T(8,128)S(1)} %get-tuple-element.25.state, f32[112,128]{1,0:T(8,128)S(1)} %get-tuple-element.26.base, f32[40,128]{1,0:T(8,128)S(1)} %get-tuple-element.31.msg_a, f32[40,128]{1,0:T(8,128)S(1)} %get-tuple-element.32.msg_b, ...), custom_call_target="tpu_custom_call" | custom-call | tf_op jit(solution)/shard_map/pallas_call | solution.py:786
  16.1 5.0 %all-to-all-start = ((f32[32,11,1,128]{3,2,1,0:T(1,128)}), f32[32,11,1,128]{3,2,1,0:T(1,128)S(1)}, u32[]{:S(2)}, u32[]{:S(2)}) async-start(f32[32,11,1,128]{3,2,1,0:T(1,128)} %bitcast.7), calls=%async_computation | async-start | bytes 360448 | tf_op jit(solution)/shard_map/all_to_all | solution.py:802
  21.2 4.5 %shard_map.98 = (f32[1024,128]{1,0:T(8,128)}, f32[1024,128]{1,0:T(8,128)}) custom-call(f32[2048,128]{1,0:T(8,128)S(1)} %get-tuple-element.25.state, f32[112,128]{1,0:T(8,128)S(1)} %get-tuple-element.26.base, f32[40,128]{1,0:T(8,128)S(1)} %get-tuple-element.31.msg_a, f32[40,128]{1,0:T(8,128)S(1)} %get-tuple-element.32.msg_b, ...), custom_call_target="tpu_custom_call" | custom-call | flops 20971520 | bytes 5242880 | tf_op jit(solution)/shard_map/pallas_call | solution.py:812
  25.6 4.5 %all-to-all-done = f32[32,11,1,128]{3,2,1,0:T(1,128)S(1)} async-done(((f32[32,11,1,128]{3,2,1,0:T(1,128)}), f32[32,11,1,128]{3,2,1,0:T(1,128)S(1)}, u32[]{:S(2)}, u32[]{:S(2)}) %all-to-all-start) | async-done | bytes 180256 | tf_op jit(solution)/shard_map/all_to_all | solution.py:802
  30.1 0.9 %shard_map.99 = (f32[4,32,128]{2,1,0:T(8,128)}, f32[32,128]{1,0:T(8,128)}) custom-call(f32[352,128]{1,0:T(8,128)S(1)} %bitcast.15), custom_call_target="tpu_custom_call" | custom-call | tf_op jit(solution)/shard_map/pallas_call | solution.py:829
Async XLA Ops:
  0.6 6.5 %copy-start = (f32[2,16,32,128]{3,2,1,0:T(8,128)S(1)}, f32[2,16,32,128]{3,2,1,0:T(8,128)}, u32[]{:S(2)}) copy-start(f32[2,16,32,128]{3,2,1,0:T(8,128)} %param.6) | copy-start | bytes 1572868
  0.6 6.5 %copy-start.1 = (f32[2,16,32,128]{3,2,1,0:T(8,128)S(1)}, f32[2,16,32,128]{3,2,1,0:T(8,128)}, u32[]{:S(2)}) copy-start(f32[2,16,32,128]{3,2,1,0:T(8,128)} %param.7) | copy-start | bytes 1572868
  0.7 6.5 %copy-start.2 = (s32[32,128]{1,0:T(8,128)S(1)}, s32[32,128]{1,0:T(8,128)}, u32[]{:S(2)}) copy-start(s32[32,128]{1,0:T(8,128)} %mask.3) | copy-start | bytes 49156
  0.7 6.5 %copy-start.3 = (f32[32,128]{1,0:T(8,128)S(1)}, f32[32,128]{1,0:T(8,128)}, u32[]{:S(2)}) copy-start(f32[32,128]{1,0:T(8,128)} %mix.3) | copy-start | bytes 49156
  2.0 6.3 %collective-permute-start = (f32[136,128]{1,0:T(8,128)S(1)}, f32[136,128]{1,0:T(8,128)S(1)}, u32[]{:S(2)}, u32[]{:S(2)}) collective-permute-start(f32[136,128]{1,0:T(8,128)S(1)} %get-tuple-element.27), channel_id=1, source_target_pairs={{1,2},{2,1},{3,4},{4,3},{5,6},{6,5},{7,31},{9,10},{10,9},{11,12},{... | collective-permute-start | bytes 208904 | tf_op jit(solution)/shard_map/ppermute | solution.py:744
  2.7 5.7 %collective-permute-start.1 = (f32[136,128]{1,0:T(8,128)S(1)}, f32[136,128]{1,0:T(8,128)S(1)}, u32[]{:S(2)}, u32[]{:S(2)}) collective-permute-start(f32[136,128]{1,0:T(8,128)S(1)} %get-tuple-element.28), channel_id=1, source_target_pairs={{0,1},{1,0},{2,3},{3,2},{4,5},{5,4},{6,7},{7,6},{8,9},{9,8},{10,11... | collective-permute-start | bytes 208904 | tf_op jit(solution)/shard_map/ppermute | solution.py:745
  8.5 4.7 %collective-permute-start.2 = (f32[40,128]{1,0:T(8,128)S(1)}, f32[40,128]{1,0:T(8,128)S(1)}, u32[]{:S(2)}, u32[]{:S(2)}) collective-permute-start(f32[40,128]{1,0:T(8,128)S(1)} %get-tuple-element.31.msg_a), channel_id=1, source_target_pairs={{0,24},{1,9},{2,26},{3,11},{4,28},{5,13},{6,30},{7,15},{8,16},{9,1... | collective-permute-start | bytes 61448 | tf_op jit(solution)/shard_map/ppermute | solution.py:783
  11.0 0.7 %copy-start.4 = (s32[32,1]{0,1:T(1,128)S(1)}, s32[32,1]{0,1:T(1,128)}, u32[]{:S(2)}) copy-start(s32[32,1]{0,1:T(1,128)} %param.10) | copy-start | bytes 388
  11.0 0.7 %copy-start.5 = (s32[32]{0:T(128)S(1)}, s32[32]{0:T(128)}, u32[]{:S(2)}) copy-start(s32[32]{0:T(128)} %atm_row.1) | copy-start | bytes 388
  11.0 3.8 %collective-permute-start.3 = (f32[40,128]{1,0:T(8,128)S(1)}, f32[40,128]{1,0:T(8,128)S(1)}, u32[]{:S(2)}, u32[]{:S(2)}) collective-permute-start(f32[40,128]{1,0:T(8,128)S(1)} %get-tuple-element.32.msg_b), channel_id=1, source_target_pairs={{0,8},{1,25},{2,10},{3,27},{4,12},{5,29},{6,14},{7,31},{8,0},{9,17... | collective-permute-start | bytes 61448 | tf_op jit(solution)/shard_map/ppermute | solution.py:782
  16.1 14.0 %all-to-all-start = ((f32[32,11,1,128]{3,2,1,0:T(1,128)}), f32[32,11,1,128]{3,2,1,0:T(1,128)S(1)}, u32[]{:S(2)}, u32[]{:S(2)}) async-start(f32[32,11,1,128]{3,2,1,0:T(1,128)} %bitcast.7), calls=%async_computation | async-start | bytes 360448 | tf_op jit(solution)/shard_map/all_to_all | solution.py:802

commit v11 on v9

--- a/solution.py
+++ b/solution.py
@@ -488,35 +488,24 @@
     return wet_mid * (mid + TIMESTEP * tend)
 
 
-def surface_kernel(
-    rows, levels,
-    state, base, msg_a, msg_b, got_a, got_b, north, south, out_in, ids,
-    coef, side, out, now, later, wet_pad, stage, places, sem,
-):
+def inside_kernel(rows, levels, state, base, north, south, coef, part, now, wet_pad):
     fields = 4 * levels
     pitch = rows + 2 * PAD
-    to_scalars = pltpu.make_async_copy(ids, places, sem)
-    to_scalars.start()
-    out[...] = out_in[...]
     wet = base[0:rows, :]
-    mixing = base[rows : 2 * rows, :]
-    table = base[2 * rows :, :]
-    coriolis = table[PAD : PAD + rows]
     lane = iota((rows, LANES), 1)
-    sides = Sides(rows, got_a, got_b, msg_a, msg_b)
     wet_pad[PAD : PAD + rows, :] = wet
     wet_pad[PAD - 1 : PAD, :] = south[2 * fields : 2 * fields + 1, :]
     wet_pad[PAD + rows : PAD + rows + 1, :] = north[2 * fields : 2 * fields + 1, :]
     wet_n = wet_pad[PAD + 1 : PAD + 1 + rows, :]
     wet_s = wet_pad[PAD - 1 : PAD - 1 + rows, :]
-    wet_e = jnp.where(lane == LANES - 1, sides.columns[0][0], pltpu.roll(wet, LANES - 1, 1))
-    wet_w = jnp.where(lane == 0, sides.columns[1][0], pltpu.roll(wet, 1, 1))
-    made = coefficients(wet, (wet_e, wet_w, wet_n, wet_s), mixing, coriolis)
+    wet_e = jnp.where(lane == LANES - 1, 0.0, pltpu.roll(wet, LANES - 1, 1))
+    wet_w = jnp.where(lane == 0, 0.0, pltpu.roll(wet, 1, 1))
+    made = coefficients(
+        wet, (wet_e, wet_w, wet_n, wet_s), base[rows : 2 * rows, :],
+        base[2 * rows + PAD : 3 * rows + PAD, :],
+    )
     for name in COEFFICIENTS:
         coef[place_of(name, rows)] = made[name]
-    near = sides.near()
-    side[...] = near
-
     count = now.shape[0] // (4 * pitch)
     for q in range(4):
         for k in range(count):
@@ -525,22 +514,77 @@
             now[at : at + rows, :] = state[field : field + rows, :]
             now[at + rows : at + rows + 1, :] = north[q * levels + k : q * levels + k + 1, :]
             now[at - 1 : at, :] = south[q * levels + k : q * levels + k + 1, :]
+    none = jnp.zeros((rows, LANES), F32)
+    acc = (none, none)
+    for k in range(count - 1):
+        new, acc = advance_level(
+            k, count, levels, rows, now, none, lambda x: coef[place_of(x, rows)], acc
+        )
+        for q in range(4):
+            at = (q * (count - 1) + k) * rows
+            part[at : at + rows, :] = new[q]
+
+
+def surface_kernel(
+    rows, levels,
+    state, base, inner, part, msg_a, msg_b, got_b, got_a, north, south, out_in, ids,
+    coef, side, out, later, stage, places, sem,
+):
+    pitch = rows + 2 * PAD
+    to_scalars = pltpu.make_async_copy(ids, places, sem)
+    to_scalars.start()
+    out[...] = out_in[...]
+    wet = base[0:rows, :]
+    table = base[2 * rows :, :]
+    lane = iota((rows, LANES), 1)
+    sides = Sides(rows, got_a, got_b, msg_a, msg_b)
+    near = sides.near()
+    side[...] = near
+    edge_rows = advance_top_rows(levels, sides, north, south, state, wet, rows, table)
+    edge_cols = advance_columns(sides, wet, table[PAD : PAD + rows], None)
+
+    east, west = lane == LANES - 1, lane == 0
+    wet_out = jnp.where(east, sides.columns[0][0], jnp.where(west, sides.columns[1][0], 0.0))
+    sign = jnp.where(east, -1.0, jnp.where(west, 1.0, 0.0))
+    take_v = (TIMESTEP * VISCOSITY) * wet * wet_out
+    take = {"t": TIMESTEP * base[rows : 2 * rows, :] * wet * wet_out, "v": take_v}
+    coef[...] = inner[...]
+    for kind, more in take.items():
+        for name, change in (
+            ("e", jnp.where(east, more, 0.0)), ("w", jnp.where(west, more, 0.0)), ("c", -more)
+        ):
+            place = place_of(kind + name, rows)
+            coef[place] = inner[place] + change
 
     def read(name):
         return coef[place_of(name, rows)]
 
-    none = jnp.zeros((rows, LANES), F32)
-    acc = (none, none)
-    edge_rows = advance_top_rows(levels, sides, north, south, state, wet, rows, table)
-    edge_cols = advance_columns(sides, wet, coriolis, None)
-    for k in range(count - 1):
-        new, acc = advance_level(k, count, levels, rows, now, near, read, acc)
+    count = later.shape[0] // (4 * pitch)
+    scale = 0.5 * GRAVITY / VERTICAL_MIX
+    acc = jnp.zeros((rows, LANES), F32)
+    for k in range(count):
+        edges = [
+            pltpu.roll(near, (LANES - 1 - 2 * (q * levels + k)) & (LANES - 1), 1) for q in range(4)
+        ]
+        center = [
+            state[(q * levels + k) * rows : (q * levels + k + 1) * rows, :] for q in range(4)
+        ]
+        u = sign * inner[place_of("adv", rows)] * center[2]
+        dens = (scale * HALINE) * edges[1] - (scale * THERMAL) * edges[0]
+        grad = sign * inner[place_of("mix", rows)] * (acc + 0.5 * dens)
+        acc = acc + dens
         for q in range(4):
+            more = take["t" if q < 2 else "v"] * (edges[q] - center[q]) + u * edges[q]
+            if q == 2:
+                more = more + grad
+            at = (q * count + k) * rows
+            new = part[at : at + rows, :] + more
             at = (q * count + k) * pitch + PAD
-            later[at : at + rows, :] = new[q]
+            later[at : at + rows, :] = new
             if k == 0:
                 later[at + rows : at + rows + 1, :] = edge_rows[q : q + 1]
                 later[at - 1 : at, :] = edge_rows[4 + q : 5 + q]
+    none = jnp.zeros((rows, LANES), F32)
     new, _ = advance_level(0, count, levels, rows, later, edge_cols, read, (none, none))
     for q in range(4):
         stage[pl.ds(q, rows, stride=4), :] = new[q]
@@ -770,6 +814,14 @@
     got_a = lax.ppermute(msg_a, "lon", odd_pairs)
 
     count = min(3, levels)
+    inner, part = call(
+        functools.partial(inside_kernel, rows, levels),
+        [shaped(len(COEFFICIENTS) * rows, cols), shaped(4 * (count - 1) * rows, cols)],
+        scratch_shapes=[
+            pltpu.VMEM((4 * count * pitch, cols), F32),
+            pltpu.VMEM((pitch, cols), F32),
+        ],
+    )(state, base, north, south)
     coefs, side, outgoing = call(
         functools.partial(surface_kernel, rows, levels),
         [
@@ -778,14 +830,12 @@
             pltpu.VMEM((devices * slot_rows, cols), F32),
         ],
         scratch_shapes=[
-            pltpu.VMEM((4 * count * pitch, cols), F32),
-            pltpu.VMEM((4 * count * pitch, cols), F32),
-            pltpu.VMEM((pitch, cols), F32),
+            pltpu.VMEM((4 * (count - 1) * pitch, cols), F32),
             pltpu.VMEM((4 * rows, cols), F32),
             pltpu.SMEM((8, cols), jnp.int32),
             pltpu.SemaphoreType.DMA,
         ],
-    )(state, base, msg_a, msg_b, got_a, got_b, north, south, outgoing, ids)
+    )(state, base, inner, part, msg_a, msg_b, got_b, got_a, north, south, outgoing, ids)
     incoming = lax.all_to_all(
         outgoing.reshape(devices, slot_rows, 1, cols),
         ("lon", "lat"),

time: 31.2 us -> 31.5 us (level)
  Pallas kernels: 10.4 us -> 10.8 us
  transfers between devices with their start and end apart: 5 -> 5, of which waited for: 3 -> 3; matrix products, arithmetic and copies ran while one was open for 0% -> 0% of each run, Pallas kernels for 21% -> 22%
where the time goes in v11:
time: 31.5 us; the launch traced here: 31.3 us
  starting transfers between devices  13.2 us (42%)
  Pallas kernels  10.8 us (34%)
  waiting for transfers between devices  6.34 us (20%)
  between operations  0.75 us (2%)
    all_to_all x1, starting transfers between devices, local(): lax.all_to_all(outgoing.reshape(devices, slot_rows, 1, cols), ('lon', 'la...  5.04 us
    pallas_call x1, Pallas kernels, local(): call(functools.partial(main_kernel, rows, levels, chunks), [shaped(flat,...  4.45 us
    all_to_all x1, waiting for transfers between devices, local(): lax.all_to_all(outgoing.reshape(devices, slot_rows, 1, cols), ('lon', 'la...  4.45 us
    ppermute x1, starting transfers between devices, local(): got_lat_a = lax.ppermute(lat_a, ('lon', 'lat'), swap_a)  4.45 us
    ppermute x1, starting transfers between devices, local(): got_a = lax.ppermute(msg_a, 'lon', odd_pairs)  2.51 us
    pallas_call x1, Pallas kernels, local(): call(functools.partial(surface_kernel, rows, levels), [shaped(len(COEFFIC...  1.58 us
    ppermute x1, waiting for transfers between devices, local(): got_b = lax.ppermute(msg_b, 'lon', even_pairs)  1.55 us
    pallas_call x1, Pallas kernels, local(): call(functools.partial(edge_kernel, rows, fields), [pltpu.VMEM((length, c...  1.31 us
  transfers between devices with their start and end apart: 5, of which 3 were waited for; matrix products, arithmetic and copies ran while one was open for 0% of the time, Pallas kernels for 22%

profile of v11, /device:TPU:0, one launch (start us, length us, event | category | flops | bytes accessed | tf_op | source)
XLA Modules:
  0.0 31.3 jit_solution(15979135141201170675)
XLA Ops:
  0.6 0.0 copy-start
  0.6 0.0 copy-start.1
  0.7 0.0 copy-start.2
  0.7 0.0 copy-start.3
  0.7 1.3 %shard_map.94 = (f32[136,128]{1,0:T(8,128)S(1)}, f32[136,128]{1,0:T(8,128)S(1)}) custom-call(f32[32,32,128]{2,1,0:T(8,128)} %bitcast.9, f32[32,32,128]{2,1,0:T(8,128)} %bitcast.12, s32[32,128]{1,0:T(8,128)} %mask.3, f32[32,128]{1,0:T(8,128)} %mix.3), custom_call_target="tpu_custom_call" | custom-call | tf_op jit(solution)/shard_map/pallas_call | solution.py:761
  2.0 0.7 %collective-permute-start = (f32[136,128]{1,0:T(8,128)S(1)}, f32[136,128]{1,0:T(8,128)S(1)}, u32[]{:S(2)}, u32[]{:S(2)}) collective-permute-start(f32[136,128]{1,0:T(8,128)S(1)} %get-tuple-element.29), channel_id=1, source_target_pairs={{1,2},{2,1},{3,4},{4,3},{5,6},{6,5},{7,31},{9,10},{10,9},{11,12},{... | collective-permute-start | bytes 208904 | tf_op jit(solution)/shard_map/ppermute | solution.py:774
  2.7 4.4 %collective-permute-start.1 = (f32[136,128]{1,0:T(8,128)S(1)}, f32[136,128]{1,0:T(8,128)S(1)}, u32[]{:S(2)}, u32[]{:S(2)}) collective-permute-start(f32[136,128]{1,0:T(8,128)S(1)} %get-tuple-element.30), channel_id=1, source_target_pairs={{0,1},{1,0},{2,3},{3,2},{4,5},{5,4},{6,7},{7,6},{8,9},{9,8},{10,11... | collective-permute-start | bytes 208904 | tf_op jit(solution)/shard_map/ppermute | solution.py:775
  7.1 0.0 copy-done
  7.1 0.0 copy-done.1
  7.1 0.0 copy-done.2
  7.1 0.0 copy-done.3
  7.1 1.2 %shard_map.95 = (f32[40,128]{1,0:T(8,128)S(1)}, f32[40,128]{1,0:T(8,128)S(1)}) custom-call(f32[1024,128]{1,0:T(8,128)S(1)} %bitcast.10, f32[1024,128]{1,0:T(8,128)S(1)} %bitcast.13, s32[32,128]{1,0:T(8,128)S(1)} %copy-done.2, f32[32,128]{1,0:T(8,128)S(1)} %copy-done.3), custom_call_target="tpu_custom_call" | custom-call | tf_op jit(solution)/shard_map/pallas_call | solution.py:778
  8.3 0.0 collective-permute-done.got_b
  8.3 0.0 collective-permute-done.1.got_a
  8.3 0.2 shard_map.96
  8.5 2.5 %collective-permute-start.2 = (f32[40,128]{1,0:T(8,128)S(1)}, f32[40,128]{1,0:T(8,128)S(1)}, u32[]{:S(2)}, u32[]{:S(2)}) collective-permute-start(f32[40,128]{1,0:T(8,128)S(1)} %get-tuple-element.33.msg_a), channel_id=1, source_target_pairs={{0,24},{8,16},{16,8},{24,0},{1,25},{9,17},{17,9},{25,1},{2,26},{10... | collective-permute-start | bytes 61448 | tf_op jit(solution)/shard_map/ppermute | solution.py:814
  11.0 0.0 copy-start.4
  11.0 0.0 copy-start.5
  11.0 0.5 %collective-permute-start.3 = (f32[40,128]{1,0:T(8,128)S(1)}, f32[40,128]{1,0:T(8,128)S(1)}, u32[]{:S(2)}, u32[]{:S(2)}) collective-permute-start(f32[40,128]{1,0:T(8,128)S(1)} %get-tuple-element.34.msg_b), channel_id=1, source_target_pairs={{0,8},{8,0},{16,24},{24,16},{1,9},{9,1},{17,25},{25,17},{2,10},{10... | collective-permute-start | bytes 61448 | tf_op jit(solution)/shard_map/ppermute | solution.py:813
  11.6 0.1 copy-done.4
  11.7 0.0 copy-done.5
  11.7 1.0 %shard_map.93 = (f32[2048,128]{1,0:T(8,128)S(1)}, f32[112,128]{1,0:T(8,128)S(1)}, f32[384,128]{1,0:T(8,128)S(1)}, f32[80,128]{1,0:T(8,128)S(1)}, f32[352,128]{1,0:T(8,128)S(1)}, /*index=5*/s32[8,128]{1,0:T(8,128)S(1)}) custom-call(f32[1024,128]{1,0:T(8,128)S(1)} %bitcast.11, f32[1024,128]{1,0:T(8,128)S(1)} %bitcast.14, s32[32,128]{1,0:T(8,128)S(1)} %copy-done.2, ...), custom_call_target="tpu_custom_call" | custom-call | tf_op jit(solution)/shard_map/pallas_call | solution.py:785
  12.7 0.2 shard_map.97
  12.9 0.3 %collective-permute-done.2.got_a = f32[40,128]{1,0:T(8,128)S(1)} collective-permute-done((f32[40,128]{1,0:T(8,128)S(1)}, f32[40,128]{1,0:T(8,128)S(1)}, u32[]{:S(2)}, u32[]{:S(2)}) %collective-permute-start.2) | collective-permute-done | bytes 20512 | tf_op jit(solution)/shard_map/ppermute | solution.py:814
  13.3 1.6 %collective-permute-done.3.got_b = f32[40,128]{1,0:T(8,128)S(1)} collective-permute-done((f32[40,128]{1,0:T(8,128)S(1)}, f32[40,128]{1,0:T(8,128)S(1)}, u32[]{:S(2)}, u32[]{:S(2)}) %collective-permute-start.3) | collective-permute-done | bytes 20512 | tf_op jit(solution)/shard_map/ppermute | solution.py:813
  14.8 1.6 %shard_map.98 = (f32[416,128]{1,0:T(8,128)S(1)}, f32[32,128]{1,0:T(8,128)S(1)}, f32[352,128]{1,0:T(8,128)}) custom-call(f32[2048,128]{1,0:T(8,128)S(1)} %get-tuple-element.27.state, f32[112,128]{1,0:T(8,128)S(1)} %get-tuple-element.28.base, f32[416,128]{1,0:T(8,128)S(1)} %get-tuple-element.39.inner, f32[256,128]{1,0:T(8,128)S(1)} %get-tuple-element.40.part, ...), custom_call_target="tpu_custom_call" | custom-call | tf_op jit(solution)/shard_map/pallas_call | solution.py:825
  16.4 5.0 %all-to-all-start = ((f32[32,11,1,128]{3,2,1,0:T(1,128)}), f32[32,11,1,128]{3,2,1,0:T(1,128)S(1)}, u32[]{:S(2)}, u32[]{:S(2)}) async-start(f32[32,11,1,128]{3,2,1,0:T(1,128)} %bitcast.7), calls=%async_computation | async-start | bytes 360448 | tf_op jit(solution)/shard_map/all_to_all | solution.py:839
  21.5 4.5 %shard_map.99 = (f32[1024,128]{1,0:T(8,128)}, f32[1024,128]{1,0:T(8,128)}) custom-call(f32[2048,128]{1,0:T(8,128)S(1)} %get-tuple-element.27.state, f32[112,128]{1,0:T(8,128)S(1)} %get-tuple-element.28.base, f32[40,128]{1,0:T(8,128)S(1)} %get-tuple-element.33.msg_a, f32[40,128]{1,0:T(8,128)S(1)} %get-tuple-element.34.msg_b, ...), custom_call_target="tpu_custom_call" | custom-call | flops 20971520 | bytes 5242880 | tf_op jit(solution)/shard_map/pallas_call | solution.py:849
  25.9 4.5 %all-to-all-done = f32[32,11,1,128]{3,2,1,0:T(1,128)S(1)} async-done(((f32[32,11,1,128]{3,2,1,0:T(1,128)}), f32[32,11,1,128]{3,2,1,0:T(1,128)S(1)}, u32[]{:S(2)}, u32[]{:S(2)}) %all-to-all-start) | async-done | bytes 180256 | tf_op jit(solution)/shard_map/all_to_all | solution.py:839
  30.4 0.9 %shard_map.100 = (f32[4,32,128]{2,1,0:T(8,128)}, f32[32,128]{1,0:T(8,128)}) custom-call(f32[352,128]{1,0:T(8,128)S(1)} %bitcast.15), custom_call_target="tpu_custom_call" | custom-call | tf_op jit(solution)/shard_map/pallas_call | solution.py:866
Async XLA Ops:
  0.6 6.5 %copy-start = (f32[2,16,32,128]{3,2,1,0:T(8,128)S(1)}, f32[2,16,32,128]{3,2,1,0:T(8,128)}, u32[]{:S(2)}) copy-start(f32[2,16,32,128]{3,2,1,0:T(8,128)} %param.6) | copy-start | bytes 1572868
  0.6 6.5 %copy-start.1 = (f32[2,16,32,128]{3,2,1,0:T(8,128)S(1)}, f32[2,16,32,128]{3,2,1,0:T(8,128)}, u32[]{:S(2)}) copy-start(f32[2,16,32,128]{3,2,1,0:T(8,128)} %param.7) | copy-start | bytes 1572868
  0.7 6.5 %copy-start.2 = (s32[32,128]{1,0:T(8,128)S(1)}, s32[32,128]{1,0:T(8,128)}, u32[]{:S(2)}) copy-start(s32[32,128]{1,0:T(8,128)} %mask.3) | copy-start | bytes 49156
  0.7 6.5 %copy-start.3 = (f32[32,128]{1,0:T(8,128)S(1)}, f32[32,128]{1,0:T(8,128)}, u32[]{:S(2)}) copy-start(f32[32,128]{1,0:T(8,128)} %mix.3) | copy-start | bytes 49156
  2.0 6.3 %collective-permute-start = (f32[136,128]{1,0:T(8,128)S(1)}, f32[136,128]{1,0:T(8,128)S(1)}, u32[]{:S(2)}, u32[]{:S(2)}) collective-permute-start(f32[136,128]{1,0:T(8,128)S(1)} %get-tuple-element.29), channel_id=1, source_target_pairs={{1,2},{2,1},{3,4},{4,3},{5,6},{6,5},{7,31},{9,10},{10,9},{11,12},{... | collective-permute-start | bytes 208904 | tf_op jit(solution)/shard_map/ppermute | solution.py:774
  2.7 5.7 %collective-permute-start.1 = (f32[136,128]{1,0:T(8,128)S(1)}, f32[136,128]{1,0:T(8,128)S(1)}, u32[]{:S(2)}, u32[]{:S(2)}) collective-permute-start(f32[136,128]{1,0:T(8,128)S(1)} %get-tuple-element.30), channel_id=1, source_target_pairs={{0,1},{1,0},{2,3},{3,2},{4,5},{5,4},{6,7},{7,6},{8,9},{9,8},{10,11... | collective-permute-start | bytes 208904 | tf_op jit(solution)/shard_map/ppermute | solution.py:775
  8.5 4.7 %collective-permute-start.2 = (f32[40,128]{1,0:T(8,128)S(1)}, f32[40,128]{1,0:T(8,128)S(1)}, u32[]{:S(2)}, u32[]{:S(2)}) collective-permute-start(f32[40,128]{1,0:T(8,128)S(1)} %get-tuple-element.33.msg_a), channel_id=1, source_target_pairs={{0,24},{8,16},{16,8},{24,0},{1,25},{9,17},{17,9},{25,1},{2,26},{10... | collective-permute-start | bytes 61448 | tf_op jit(solution)/shard_map/ppermute | solution.py:814
  11.0 0.7 %copy-start.4 = (s32[32,1]{0,1:T(1,128)S(1)}, s32[32,1]{0,1:T(1,128)}, u32[]{:S(2)}) copy-start(s32[32,1]{0,1:T(1,128)} %param.10) | copy-start | bytes 388
  11.0 0.7 %copy-start.5 = (s32[32]{0:T(128)S(1)}, s32[32]{0:T(128)}, u32[]{:S(2)}) copy-start(s32[32]{0:T(128)} %atm_row.1) | copy-start | bytes 388
  11.0 3.8 %collective-permute-start.3 = (f32[40,128]{1,0:T(8,128)S(1)}, f32[40,128]{1,0:T(8,128)S(1)}, u32[]{:S(2)}, u32[]{:S(2)}) collective-permute-start(f32[40,128]{1,0:T(8,128)S(1)} %get-tuple-element.34.msg_b), channel_id=1, source_target_pairs={{0,8},{8,0},{16,24},{24,16},{1,9},{9,1},{17,25},{25,17},{2,10},{10... | collective-permute-start | bytes 61448 | tf_op jit(solution)/shard_map/ppermute | solution.py:813
  16.4 14.0 %all-to-all-start = ((f32[32,11,1,128]{3,2,1,0:T(1,128)}), f32[32,11,1,128]{3,2,1,0:T(1,128)S(1)}, u32[]{:S(2)}, u32[]{:S(2)}) async-start(f32[32,11,1,128]{3,2,1,0:T(1,128)} %bitcast.7), calls=%async_computation | async-start | bytes 360448 | tf_op jit(solution)/shard_map/all_to_all | solution.py:839

commit v12 on v9

--- a/solution.py
+++ b/solution.py
@@ -33,6 +33,14 @@
 
 def dot(a, b, dims=(((1,), (0,)), ((), ()))):
     return lax.dot_general(a, b, dims, precision=EXACT, preferred_element_type=F32)
+
+
+def exact_parts(x):
+    parts = []
+    for _ in range(3):
+        parts.append(x.astype(jnp.bfloat16))
+        x = x - parts[-1].astype(F32)
+    return parts
 
 
 def is_even(axis):
@@ -172,13 +180,13 @@
         slot = used[owner]
         used[owner] = slot + 1
         start = (devices - 1 - owner) * slot_rows
-        places = jnp.where(lane1 == r, start + 4 * slot, places)
+        places = jnp.where(lane1 % rows == r, start + 4 * slot, places)
         out[pl.ds(start + 4 * CAP + slot, 1), :] = base[r : r + 1, :]
         line = out[pl.ds(start + 5 * CAP, 1), :]
         target = jnp.full((1, LANES), atm_row[r], jnp.int32).astype(F32)
         out[pl.ds(start + 5 * CAP, 1), :] = jnp.where(lane1 // (LANES // CAP) == slot, target, line)
     ids[...] = jnp.zeros(ids.shape, jnp.int32)
-    ids[0:1, :] = places
+    ids[0:1, :] = places + lane1 // rows
 
 
 def corner_kernel(lat_count, fields, got_b, got_a, tail_a, tail_b, north, south, new_a, new_b):
@@ -491,13 +499,10 @@
 def surface_kernel(
     rows, levels,
     state, base, msg_a, msg_b, got_a, got_b, north, south, out_in, ids,
-    coef, side, out, now, later, wet_pad, stage, places, sem,
+    coef, side, out, now, later, wet_pad,
 ):
     fields = 4 * levels
     pitch = rows + 2 * PAD
-    to_scalars = pltpu.make_async_copy(ids, places, sem)
-    to_scalars.start()
-    out[...] = out_in[...]
     wet = base[0:rows, :]
     mixing = base[rows : 2 * rows, :]
     table = base[2 * rows :, :]
@@ -542,11 +547,13 @@
                 later[at + rows : at + rows + 1, :] = edge_rows[q : q + 1]
                 later[at - 1 : at, :] = edge_rows[4 + q : 5 + q]
     new, _ = advance_level(0, count, levels, rows, later, edge_cols, read, (none, none))
-    for q in range(4):
-        stage[pl.ds(q, rows, stride=4), :] = new[q]
-    to_scalars.wait()
-    for r in range(rows):
-        out[pl.ds(places[0, r], 4), :] = stage[4 * r : 4 * r + 4, :]
+    length = out.shape[0]
+    here = (iota((length, LANES), 0) == ids[0:1, :]).astype(F32).astype(jnp.bfloat16)
+    out[...] = out_in[...] + jnp.dot(
+        jnp.concatenate([here] * 3, axis=1),
+        jnp.concatenate(exact_parts(jnp.concatenate(new, axis=0)), axis=0),
+        preferred_element_type=F32,
+    )
 
 
 def halo_after_first(rows, levels, sides, north, south, state, wet, table, col_map, row_map):
@@ -653,11 +660,7 @@
         parts = [rows_of(4 * slot + q) for q in range(4)] + [rows_of(4 * CAP + slot)]
         values.append(jnp.concatenate(parts, axis=1))
     rest = jnp.concatenate(values, axis=0)
-    pieces = []
-    for _ in range(3):
-        piece = rest.astype(jnp.bfloat16)
-        pieces.append(piece)
-        rest = rest - piece.astype(F32)
+    pieces = exact_parts(rest)
     one = jnp.concatenate(to_rows, axis=0).astype(jnp.bfloat16)
     totals = lax.dot_general(
         jnp.concatenate([one] * 3, axis=0),
@@ -704,7 +707,7 @@
     fields = 4 * levels
     lon_count, lat_count = lax.axis_size("lon"), lax.axis_size("lat")
     devices = lon_count * lat_count
-    assert cols == LANES and rows % 8 == 0 and 2 * fields == LANES
+    assert cols == LANES and 4 * rows == LANES and 2 * fields == LANES
     assert lon_count % 2 == 0 and lat_count % 2 == 0 and 3 * rows <= LANES
     length = 2 * fields + 8
     pitch = rows + 2 * PAD
@@ -781,9 +784,6 @@
             pltpu.VMEM((4 * count * pitch, cols), F32),
             pltpu.VMEM((4 * count * pitch, cols), F32),
             pltpu.VMEM((pitch, cols), F32),
-            pltpu.VMEM((4 * rows, cols), F32),
-            pltpu.SMEM((8, cols), jnp.int32),
-            pltpu.SemaphoreType.DMA,
         ],
     )(state, base, msg_a, msg_b, got_a, got_b, north, south, outgoing, ids)
     incoming = lax.all_to_all(

time: 31.2 us -> 31.3 us (level)
  no operation moved by 1% of the time
where the time goes in v12:
time: 31.3 us; the launch traced here: 31.1 us
  starting transfers between devices  13.2 us (42%)
  Pallas kernels  10.5 us (34%)
  waiting for transfers between devices  6.54 us (21%)
  between operations  0.74 us (2%)
    all_to_all x1, starting transfers between devices, local(): lax.all_to_all(outgoing.reshape(devices, slot_rows, 1, cols), ('lon', 'la...  5.03 us
    pallas_call x1, Pallas kernels, local(): call(functools.partial(main_kernel, rows, levels, chunks), [shaped(flat,...  4.45 us
    all_to_all x1, waiting for transfers between devices, local(): lax.all_to_all(outgoing.reshape(devices, slot_rows, 1, cols), ('lon', 'la...  4.45 us
    ppermute x1, starting transfers between devices, local(): got_lat_a = lax.ppermute(lat_a, ('lon', 'lat'), swap_a)  4.45 us
    ppermute x1, starting transfers between devices, local(): got_a = lax.ppermute(msg_a, 'lon', odd_pairs)  2.51 us
    ppermute x1, waiting for transfers between devices, local(): got_b = lax.ppermute(msg_b, 'lon', even_pairs)  1.55 us
    pallas_call x1, Pallas kernels, local(): call(functools.partial(surface_kernel, rows, levels), [shaped(len(COEFFIC...  1.4 us
    pallas_call x1, Pallas kernels, local(): call(functools.partial(edge_kernel, rows, fields), [pltpu.VMEM((length, c...  1.31 us
  transfers between devices with their start and end apart: 5, of which 3 were waited for; matrix products, arithmetic and copies ran while one was open for 0% of the time, Pallas kernels for 21%

profile of v12, /device:TPU:0, one launch (start us, length us, event | category | flops | bytes accessed | tf_op | source)
XLA Modules:
  0.0 31.1 jit_solution(9882421647032068182)
XLA Ops:
  0.6 0.0 copy-start
  0.6 0.0 copy-start.1
  0.7 0.0 copy-start.2
  0.7 0.0 copy-start.3
  0.7 1.3 %shard_map.94 = (f32[136,128]{1,0:T(8,128)S(1)}, f32[136,128]{1,0:T(8,128)S(1)}) custom-call(f32[32,32,128]{2,1,0:T(8,128)} %bitcast.9, f32[32,32,128]{2,1,0:T(8,128)} %bitcast.12, s32[32,128]{1,0:T(8,128)} %mask.3, f32[32,128]{1,0:T(8,128)} %mix.3), custom_call_target="tpu_custom_call" | custom-call | tf_op jit(solution)/shard_map/pallas_call | solution.py:720
  2.0 0.7 %collective-permute-start = (f32[136,128]{1,0:T(8,128)S(1)}, f32[136,128]{1,0:T(8,128)S(1)}, u32[]{:S(2)}, u32[]{:S(2)}) collective-permute-start(f32[136,128]{1,0:T(8,128)S(1)} %get-tuple-element.27), channel_id=1, source_target_pairs={{1,2},{2,1},{3,4},{4,3},{5,6},{6,5},{7,31},{9,10},{10,9},{11,12},{... | collective-permute-start | bytes 208904 | tf_op jit(solution)/shard_map/ppermute | solution.py:733
  2.7 4.4 %collective-permute-start.1 = (f32[136,128]{1,0:T(8,128)S(1)}, f32[136,128]{1,0:T(8,128)S(1)}, u32[]{:S(2)}, u32[]{:S(2)}) collective-permute-start(f32[136,128]{1,0:T(8,128)S(1)} %get-tuple-element.28), channel_id=1, source_target_pairs={{0,1},{1,0},{2,3},{3,2},{4,5},{5,4},{6,7},{7,6},{8,9},{9,8},{10,11... | collective-permute-start | bytes 208904 | tf_op jit(solution)/shard_map/ppermute | solution.py:734
  7.1 0.0 copy-done
  7.1 0.0 copy-done.1
  7.1 0.0 copy-done.2
  7.1 0.0 copy-done.3
  7.1 1.2 %shard_map.95 = (f32[40,128]{1,0:T(8,128)S(1)}, f32[40,128]{1,0:T(8,128)S(1)}) custom-call(f32[1024,128]{1,0:T(8,128)S(1)} %bitcast.10, f32[1024,128]{1,0:T(8,128)S(1)} %bitcast.13, s32[32,128]{1,0:T(8,128)S(1)} %copy-done.2, f32[32,128]{1,0:T(8,128)S(1)} %copy-done.3), custom_call_target="tpu_custom_call" | custom-call | tf_op jit(solution)/shard_map/pallas_call | solution.py:737
  8.3 0.0 collective-permute-done.got_b
  8.3 0.0 collective-permute-done.1.got_a
  8.3 0.2 shard_map.96
  8.5 2.5 %collective-permute-start.2 = (f32[40,128]{1,0:T(8,128)S(1)}, f32[40,128]{1,0:T(8,128)S(1)}, u32[]{:S(2)}, u32[]{:S(2)}) collective-permute-start(f32[40,128]{1,0:T(8,128)S(1)} %get-tuple-element.31.msg_a), channel_id=1, source_target_pairs={{0,24},{8,16},{16,8},{24,0},{1,25},{9,17},{17,9},{25,1},{2,26},{10... | collective-permute-start | bytes 61448 | tf_op jit(solution)/shard_map/ppermute | solution.py:773
  11.0 0.0 copy-start.4
  11.0 0.0 copy-start.5
  11.0 0.5 %collective-permute-start.3 = (f32[40,128]{1,0:T(8,128)S(1)}, f32[40,128]{1,0:T(8,128)S(1)}, u32[]{:S(2)}, u32[]{:S(2)}) collective-permute-start(f32[40,128]{1,0:T(8,128)S(1)} %get-tuple-element.32.msg_b), channel_id=1, source_target_pairs={{0,8},{8,0},{16,24},{24,16},{1,9},{9,1},{17,25},{25,17},{2,10},{10... | collective-permute-start | bytes 61448 | tf_op jit(solution)/shard_map/ppermute | solution.py:772
  11.6 0.1 copy-done.4
  11.7 0.0 copy-done.5
  11.7 1.0 %shard_map.93 = (f32[2048,128]{1,0:T(8,128)S(1)}, f32[112,128]{1,0:T(8,128)S(1)}, f32[384,128]{1,0:T(8,128)S(1)}, f32[80,128]{1,0:T(8,128)S(1)}, f32[352,128]{1,0:T(8,128)S(1)}, /*index=5*/s32[8,128]{1,0:T(8,128)S(1)}) custom-call(f32[1024,128]{1,0:T(8,128)S(1)} %bitcast.11, f32[1024,128]{1,0:T(8,128)S(1)} %bitcast.14, s32[32,128]{1,0:T(8,128)S(1)} %copy-done.2, ...), custom_call_target="tpu_custom_call" | custom-call | tf_op jit(solution)/shard_map/pallas_call | solution.py:744
  12.7 0.5 %collective-permute-done.2.got_a = f32[40,128]{1,0:T(8,128)S(1)} collective-permute-done((f32[40,128]{1,0:T(8,128)S(1)}, f32[40,128]{1,0:T(8,128)S(1)}, u32[]{:S(2)}, u32[]{:S(2)}) %collective-permute-start.2) | collective-permute-done | bytes 20512 | tf_op jit(solution)/shard_map/ppermute | solution.py:773
  13.3 1.6 %collective-permute-done.3.got_b = f32[40,128]{1,0:T(8,128)S(1)} collective-permute-done((f32[40,128]{1,0:T(8,128)S(1)}, f32[40,128]{1,0:T(8,128)S(1)}, u32[]{:S(2)}, u32[]{:S(2)}) %collective-permute-start.3) | collective-permute-done | bytes 20512 | tf_op jit(solution)/shard_map/ppermute | solution.py:772
  14.8 1.4 %shard_map.97 = (f32[416,128]{1,0:T(8,128)S(1)}, f32[32,128]{1,0:T(8,128)S(1)}, f32[352,128]{1,0:T(8,128)}) custom-call(f32[2048,128]{1,0:T(8,128)S(1)} %get-tuple-element.25.state, f32[112,128]{1,0:T(8,128)S(1)} %get-tuple-element.26.base, f32[40,128]{1,0:T(8,128)S(1)} %get-tuple-element.31.msg_a, f32[40,128]{1,0:T(8,128)S(1)} %get-tuple-element.32.msg_b, ...), custom_call_target="tpu_custom_call" | custom-call | tf_op jit(solution)/shard_map/pallas_call | solution.py:776
  16.2 5.0 %all-to-all-start = ((f32[32,11,1,128]{3,2,1,0:T(1,128)}), f32[32,11,1,128]{3,2,1,0:T(1,128)S(1)}, u32[]{:S(2)}, u32[]{:S(2)}) async-start(f32[32,11,1,128]{3,2,1,0:T(1,128)} %bitcast.7), calls=%async_computation | async-start | bytes 360448 | tf_op jit(solution)/shard_map/all_to_all | solution.py:789
  21.2 4.5 %shard_map.98 = (f32[1024,128]{1,0:T(8,128)}, f32[1024,128]{1,0:T(8,128)}) custom-call(f32[2048,128]{1,0:T(8,128)S(1)} %get-tuple-element.25.state, f32[112,128]{1,0:T(8,128)S(1)} %get-tuple-element.26.base, f32[40,128]{1,0:T(8,128)S(1)} %get-tuple-element.31.msg_a, f32[40,128]{1,0:T(8,128)S(1)} %get-tuple-element.32.msg_b, ...), custom_call_target="tpu_custom_call" | custom-call | flops 20971520 | bytes 5242880 | tf_op jit(solution)/shard_map/pallas_call | solution.py:799
  25.7 4.5 %all-to-all-done = f32[32,11,1,128]{3,2,1,0:T(1,128)S(1)} async-done(((f32[32,11,1,128]{3,2,1,0:T(1,128)}), f32[32,11,1,128]{3,2,1,0:T(1,128)S(1)}, u32[]{:S(2)}, u32[]{:S(2)}) %all-to-all-start) | async-done | bytes 180256 | tf_op jit(solution)/shard_map/all_to_all | solution.py:789
  30.2 0.9 %shard_map.99 = (f32[4,32,128]{2,1,0:T(8,128)}, f32[32,128]{1,0:T(8,128)}) custom-call(f32[352,128]{1,0:T(8,128)S(1)} %bitcast.15), custom_call_target="tpu_custom_call" | custom-call | tf_op jit(solution)/shard_map/pallas_call | solution.py:816
Async XLA Ops:
  0.6 6.5 %copy-start = (f32[2,16,32,128]{3,2,1,0:T(8,128)S(1)}, f32[2,16,32,128]{3,2,1,0:T(8,128)}, u32[]{:S(2)}) copy-start(f32[2,16,32,128]{3,2,1,0:T(8,128)} %param.6) | copy-start | bytes 1572868
  0.6 6.5 %copy-start.1 = (f32[2,16,32,128]{3,2,1,0:T(8,128)S(1)}, f32[2,16,32,128]{3,2,1,0:T(8,128)}, u32[]{:S(2)}) copy-start(f32[2,16,32,128]{3,2,1,0:T(8,128)} %param.7) | copy-start | bytes 1572868
  0.7 6.5 %copy-start.2 = (s32[32,128]{1,0:T(8,128)S(1)}, s32[32,128]{1,0:T(8,128)}, u32[]{:S(2)}) copy-start(s32[32,128]{1,0:T(8,128)} %mask.3) | copy-start | bytes 49156
  0.7 6.5 %copy-start.3 = (f32[32,128]{1,0:T(8,128)S(1)}, f32[32,128]{1,0:T(8,128)}, u32[]{:S(2)}) copy-start(f32[32,128]{1,0:T(8,128)} %mix.3) | copy-start | bytes 49156
  2.0 6.3 %collective-permute-start = (f32[136,128]{1,0:T(8,128)S(1)}, f32[136,128]{1,0:T(8,128)S(1)}, u32[]{:S(2)}, u32[]{:S(2)}) collective-permute-start(f32[136,128]{1,0:T(8,128)S(1)} %get-tuple-element.27), channel_id=1, source_target_pairs={{1,2},{2,1},{3,4},{4,3},{5,6},{6,5},{7,31},{9,10},{10,9},{11,12},{... | collective-permute-start | bytes 208904 | tf_op jit(solution)/shard_map/ppermute | solution.py:733
  2.7 5.7 %collective-permute-start.1 = (f32[136,128]{1,0:T(8,128)S(1)}, f32[136,128]{1,0:T(8,128)S(1)}, u32[]{:S(2)}, u32[]{:S(2)}) collective-permute-start(f32[136,128]{1,0:T(8,128)S(1)} %get-tuple-element.28), channel_id=1, source_target_pairs={{0,1},{1,0},{2,3},{3,2},{4,5},{5,4},{6,7},{7,6},{8,9},{9,8},{10,11... | collective-permute-start | bytes 208904 | tf_op jit(solution)/shard_map/ppermute | solution.py:734
  8.5 4.7 %collective-permute-start.2 = (f32[40,128]{1,0:T(8,128)S(1)}, f32[40,128]{1,0:T(8,128)S(1)}, u32[]{:S(2)}, u32[]{:S(2)}) collective-permute-start(f32[40,128]{1,0:T(8,128)S(1)} %get-tuple-element.31.msg_a), channel_id=1, source_target_pairs={{0,24},{8,16},{16,8},{24,0},{1,25},{9,17},{17,9},{25,1},{2,26},{10... | collective-permute-start | bytes 61448 | tf_op jit(solution)/shard_map/ppermute | solution.py:773
  11.0 0.7 %copy-start.4 = (s32[32,1]{0,1:T(1,128)S(1)}, s32[32,1]{0,1:T(1,128)}, u32[]{:S(2)}) copy-start(s32[32,1]{0,1:T(1,128)} %param.10) | copy-start | bytes 388
  11.0 0.7 %copy-start.5 = (s32[32]{0:T(128)S(1)}, s32[32]{0:T(128)}, u32[]{:S(2)}) copy-start(s32[32]{0:T(128)} %atm_row.1) | copy-start | bytes 388
  11.0 3.8 %collective-permute-start.3 = (f32[40,128]{1,0:T(8,128)S(1)}, f32[40,128]{1,0:T(8,128)S(1)}, u32[]{:S(2)}, u32[]{:S(2)}) collective-permute-start(f32[40,128]{1,0:T(8,128)S(1)} %get-tuple-element.32.msg_b), channel_id=1, source_target_pairs={{0,8},{8,0},{16,24},{24,16},{1,9},{9,1},{17,25},{25,17},{2,10},{10... | collective-permute-start | bytes 61448 | tf_op jit(solution)/shard_map/ppermute | solution.py:772
  16.2 14.0 %all-to-all-start = ((f32[32,11,1,128]{3,2,1,0:T(1,128)}), f32[32,11,1,128]{3,2,1,0:T(1,128)S(1)}, u32[]{:S(2)}, u32[]{:S(2)}) async-start(f32[32,11,1,128]{3,2,1,0:T(1,128)} %bitcast.7), calls=%async_computation | async-start | bytes 360448 | tf_op jit(solution)/shard_map/all_to_all | solution.py:789

commit v13 on v9

--- a/solution.py
+++ b/solution.py
@@ -216,7 +216,7 @@
 
 class Sides:
     def __init__(self, rows, got_a, got_b, msg_a, msg_b):
-        lane, row = iota((rows, LANES), 1), iota((rows, LANES), 0)
+        lane = iota((rows, LANES), 1)
         self.even = (lane & 1) == 0
         self.even1 = (iota((1, LANES), 1) & 1) == 0
         even = is_even("lon")
@@ -227,13 +227,9 @@
         self.got = ordered(got_a, got_b, slice(0, rows))
         self.mine = ordered(msg_a, msg_b, slice(0, rows))
         self.extras = ordered(got_a, got_b, slice(rows, rows + 8))
-        self.columns = [
-            [
-                jnp.sum(jnp.where(lane == i * rows + row, x[4:5], 0.0), axis=1, keepdims=True)
-                for i in range(3)
-            ]
-            for x in self.extras
-        ]
+        both = jnp.where((iota((LANES, LANES), 0) & 1) == 0, *[x[4:5] for x in self.extras])
+        turned = jnp.transpose(both)
+        self.columns = [turned[i * rows : (i + 1) * rows] for i in range(3)]
 
     def near(self):
         return jnp.where(self.even, *self.got)
@@ -251,7 +247,7 @@
         return jnp.where(self.even1, east[i : i + 1], west[i : i + 1]), *wets
 
     def lanes(self, i):
-        return jnp.where(self.even, self.columns[0][i], self.columns[1][i])
+        return self.columns[i]
 
 
 def level_matrix(kind, levels, source, target):
@@ -509,8 +505,9 @@
     wet_pad[PAD + rows : PAD + rows + 1, :] = north[2 * fields : 2 * fields + 1, :]
     wet_n = wet_pad[PAD + 1 : PAD + 1 + rows, :]
     wet_s = wet_pad[PAD - 1 : PAD - 1 + rows, :]
-    wet_e = jnp.where(lane == LANES - 1, sides.columns[0][0], pltpu.roll(wet, LANES - 1, 1))
-    wet_w = jnp.where(lane == 0, sides.columns[1][0], pltpu.roll(wet, 1, 1))
+    ends = pltpu.roll(sides.lanes(0), LANES - 1, 1)
+    wet_e = jnp.where(lane == LANES - 1, ends, pltpu.roll(wet, LANES - 1, 1))
+    wet_w = jnp.where(lane == 0, ends, pltpu.roll(wet, 1, 1))
     made = coefficients(wet, (wet_e, wet_w, wet_n, wet_s), mixing, coriolis)
     for name in COEFFICIENTS:
         coef[place_of(name, rows)] = made[name]

time: 31.2 us -> 31.3 us (level)
  no operation moved by 1% of the time
where the time goes in v13:
time: 31.3 us; the launch traced here: 31.1 us
  starting transfers between devices  13.2 us (42%)
  Pallas kernels  10.4 us (33%)
  waiting for transfers between devices  6.53 us (21%)
  between operations  0.75 us (2%)
    all_to_all x1, starting transfers between devices, local(): lax.all_to_all(outgoing.reshape(devices, slot_rows, 1, cols), ('lon', 'la...  5.04 us
    pallas_call x1, Pallas kernels, local(): call(functools.partial(main_kernel, rows, levels, chunks), [shaped(flat,...  4.46 us
    ppermute x1, starting transfers between devices, local(): got_lat_a = lax.ppermute(lat_a, ('lon', 'lat'), swap_a)  4.45 us
    all_to_all x1, waiting for transfers between devices, local(): lax.all_to_all(outgoing.reshape(devices, slot_rows, 1, cols), ('lon', 'la...  4.44 us
    ppermute x1, starting transfers between devices, local(): got_a = lax.ppermute(msg_a, 'lon', odd_pairs)  2.51 us
    ppermute x1, waiting for transfers between devices, local(): got_b = lax.ppermute(msg_b, 'lon', even_pairs)  1.55 us
    pallas_call x1, Pallas kernels, local(): call(functools.partial(surface_kernel, rows, levels), [shaped(len(COEFFIC...  1.37 us
    pallas_call x1, Pallas kernels, local(): call(functools.partial(edge_kernel, rows, fields), [pltpu.VMEM((length, c...  1.31 us
  transfers between devices with their start and end apart: 5, of which 3 were waited for; matrix products, arithmetic and copies ran while one was open for 0% of the time, Pallas kernels for 21%

profile of v13, /device:TPU:0, one launch (start us, length us, event | category | flops | bytes accessed | tf_op | source)
XLA Modules:
  0.0 31.1 jit_solution(15490328534484000515)
XLA Ops:
  0.6 0.0 copy-start
  0.6 0.0 copy-start.1
  0.7 0.0 copy-start.2
  0.7 0.0 copy-start.3
  0.7 1.3 %shard_map.94 = (f32[136,128]{1,0:T(8,128)S(1)}, f32[136,128]{1,0:T(8,128)S(1)}) custom-call(f32[32,32,128]{2,1,0:T(8,128)} %bitcast.9, f32[32,32,128]{2,1,0:T(8,128)} %bitcast.12, s32[32,128]{1,0:T(8,128)} %mask.3, f32[32,128]{1,0:T(8,128)} %mix.3), custom_call_target="tpu_custom_call" | custom-call | tf_op jit(solution)/shard_map/pallas_call | solution.py:714
  2.0 0.7 %collective-permute-start = (f32[136,128]{1,0:T(8,128)S(1)}, f32[136,128]{1,0:T(8,128)S(1)}, u32[]{:S(2)}, u32[]{:S(2)}) collective-permute-start(f32[136,128]{1,0:T(8,128)S(1)} %get-tuple-element.27), channel_id=1, source_target_pairs={{1,2},{2,1},{3,4},{4,3},{5,6},{6,5},{7,31},{9,10},{10,9},{11,12},{... | collective-permute-start | bytes 208904 | tf_op jit(solution)/shard_map/ppermute | solution.py:727
  2.7 4.4 %collective-permute-start.1 = (f32[136,128]{1,0:T(8,128)S(1)}, f32[136,128]{1,0:T(8,128)S(1)}, u32[]{:S(2)}, u32[]{:S(2)}) collective-permute-start(f32[136,128]{1,0:T(8,128)S(1)} %get-tuple-element.28), channel_id=1, source_target_pairs={{0,1},{1,0},{2,3},{3,2},{4,5},{5,4},{6,7},{7,6},{8,9},{9,8},{10,11... | collective-permute-start | bytes 208904 | tf_op jit(solution)/shard_map/ppermute | solution.py:728
  7.1 0.0 copy-done
  7.1 0.0 copy-done.1
  7.1 0.0 copy-done.2
  7.1 0.0 copy-done.3
  7.1 1.2 %shard_map.95 = (f32[40,128]{1,0:T(8,128)S(1)}, f32[40,128]{1,0:T(8,128)S(1)}) custom-call(f32[1024,128]{1,0:T(8,128)S(1)} %bitcast.10, f32[1024,128]{1,0:T(8,128)S(1)} %bitcast.13, s32[32,128]{1,0:T(8,128)S(1)} %copy-done.2, f32[32,128]{1,0:T(8,128)S(1)} %copy-done.3), custom_call_target="tpu_custom_call" | custom-call | tf_op jit(solution)/shard_map/pallas_call | solution.py:731
  8.3 0.0 collective-permute-done.got_b
  8.3 0.0 collective-permute-done.1.got_a
  8.3 0.2 shard_map.96
  8.5 2.5 %collective-permute-start.2 = (f32[40,128]{1,0:T(8,128)S(1)}, f32[40,128]{1,0:T(8,128)S(1)}, u32[]{:S(2)}, u32[]{:S(2)}) collective-permute-start(f32[40,128]{1,0:T(8,128)S(1)} %get-tuple-element.31.msg_a), channel_id=1, source_target_pairs={{0,24},{8,16},{16,8},{24,0},{1,25},{9,17},{17,9},{25,1},{2,26},{10... | collective-permute-start | bytes 61448 | tf_op jit(solution)/shard_map/ppermute | solution.py:767
  11.0 0.0 copy-start.4
  11.0 0.0 copy-start.5
  11.0 0.5 %collective-permute-start.3 = (f32[40,128]{1,0:T(8,128)S(1)}, f32[40,128]{1,0:T(8,128)S(1)}, u32[]{:S(2)}, u32[]{:S(2)}) collective-permute-start(f32[40,128]{1,0:T(8,128)S(1)} %get-tuple-element.32.msg_b), channel_id=1, source_target_pairs={{0,8},{8,0},{16,24},{24,16},{1,9},{9,1},{17,25},{25,17},{2,10},{10... | collective-permute-start | bytes 61448 | tf_op jit(solution)/shard_map/ppermute | solution.py:766
  11.6 0.1 copy-done.4
  11.7 0.0 copy-done.5
  11.7 1.0 %shard_map.93 = (f32[2048,128]{1,0:T(8,128)S(1)}, f32[112,128]{1,0:T(8,128)S(1)}, f32[384,128]{1,0:T(8,128)S(1)}, f32[80,128]{1,0:T(8,128)S(1)}, f32[352,128]{1,0:T(8,128)S(1)}, /*index=5*/s32[8,128]{1,0:T(8,128)S(1)}) custom-call(f32[1024,128]{1,0:T(8,128)S(1)} %bitcast.11, f32[1024,128]{1,0:T(8,128)S(1)} %bitcast.14, s32[32,128]{1,0:T(8,128)S(1)} %copy-done.2, ...), custom_call_target="tpu_custom_call" | custom-call | tf_op jit(solution)/shard_map/pallas_call | solution.py:738
  12.7 0.5 %collective-permute-done.2.got_a = f32[40,128]{1,0:T(8,128)S(1)} collective-permute-done((f32[40,128]{1,0:T(8,128)S(1)}, f32[40,128]{1,0:T(8,128)S(1)}, u32[]{:S(2)}, u32[]{:S(2)}) %collective-permute-start.2) | collective-permute-done | bytes 20512 | tf_op jit(solution)/shard_map/ppermute | solution.py:767
  13.3 1.6 %collective-permute-done.3.got_b = f32[40,128]{1,0:T(8,128)S(1)} collective-permute-done((f32[40,128]{1,0:T(8,128)S(1)}, f32[40,128]{1,0:T(8,128)S(1)}, u32[]{:S(2)}, u32[]{:S(2)}) %collective-permute-start.3) | collective-permute-done | bytes 20512 | tf_op jit(solution)/shard_map/ppermute | solution.py:766
  14.8 1.4 %shard_map.97 = (f32[416,128]{1,0:T(8,128)S(1)}, f32[32,128]{1,0:T(8,128)S(1)}, f32[352,128]{1,0:T(8,128)}) custom-call(f32[2048,128]{1,0:T(8,128)S(1)} %get-tuple-element.25.state, f32[112,128]{1,0:T(8,128)S(1)} %get-tuple-element.26.base, f32[40,128]{1,0:T(8,128)S(1)} %get-tuple-element.31.msg_a, f32[40,128]{1,0:T(8,128)S(1)} %get-tuple-element.32.msg_b, ...), custom_call_target="tpu_custom_call" | custom-call | tf_op jit(solution)/shard_map/pallas_call | solution.py:770
  16.2 5.0 %all-to-all-start = ((f32[32,11,1,128]{3,2,1,0:T(1,128)}), f32[32,11,1,128]{3,2,1,0:T(1,128)S(1)}, u32[]{:S(2)}, u32[]{:S(2)}) async-start(f32[32,11,1,128]{3,2,1,0:T(1,128)} %bitcast.7), calls=%async_computation | async-start | bytes 360448 | tf_op jit(solution)/shard_map/all_to_all | solution.py:786
  21.2 4.5 %shard_map.98 = (f32[1024,128]{1,0:T(8,128)}, f32[1024,128]{1,0:T(8,128)}) custom-call(f32[2048,128]{1,0:T(8,128)S(1)} %get-tuple-element.25.state, f32[112,128]{1,0:T(8,128)S(1)} %get-tuple-element.26.base, f32[40,128]{1,0:T(8,128)S(1)} %get-tuple-element.31.msg_a, f32[40,128]{1,0:T(8,128)S(1)} %get-tuple-element.32.msg_b, ...), custom_call_target="tpu_custom_call" | custom-call | flops 20971520 | bytes 5242880 | tf_op jit(solution)/shard_map/pallas_call | solution.py:796
  25.7 4.4 %all-to-all-done = f32[32,11,1,128]{3,2,1,0:T(1,128)S(1)} async-done(((f32[32,11,1,128]{3,2,1,0:T(1,128)}), f32[32,11,1,128]{3,2,1,0:T(1,128)S(1)}, u32[]{:S(2)}, u32[]{:S(2)}) %all-to-all-start) | async-done | bytes 180256 | tf_op jit(solution)/shard_map/all_to_all | solution.py:786
  30.1 0.9 %shard_map.99 = (f32[4,32,128]{2,1,0:T(8,128)}, f32[32,128]{1,0:T(8,128)}) custom-call(f32[352,128]{1,0:T(8,128)S(1)} %bitcast.15), custom_call_target="tpu_custom_call" | custom-call | tf_op jit(solution)/shard_map/pallas_call | solution.py:813
Async XLA Ops:
  0.6 6.5 %copy-start = (f32[2,16,32,128]{3,2,1,0:T(8,128)S(1)}, f32[2,16,32,128]{3,2,1,0:T(8,128)}, u32[]{:S(2)}) copy-start(f32[2,16,32,128]{3,2,1,0:T(8,128)} %param.6) | copy-start | bytes 1572868
  0.6 6.5 %copy-start.1 = (f32[2,16,32,128]{3,2,1,0:T(8,128)S(1)}, f32[2,16,32,128]{3,2,1,0:T(8,128)}, u32[]{:S(2)}) copy-start(f32[2,16,32,128]{3,2,1,0:T(8,128)} %param.7) | copy-start | bytes 1572868
  0.7 6.5 %copy-start.2 = (s32[32,128]{1,0:T(8,128)S(1)}, s32[32,128]{1,0:T(8,128)}, u32[]{:S(2)}) copy-start(s32[32,128]{1,0:T(8,128)} %mask.3) | copy-start | bytes 49156
  0.7 6.5 %copy-start.3 = (f32[32,128]{1,0:T(8,128)S(1)}, f32[32,128]{1,0:T(8,128)}, u32[]{:S(2)}) copy-start(f32[32,128]{1,0:T(8,128)} %mix.3) | copy-start | bytes 49156
  2.0 6.3 %collective-permute-start = (f32[136,128]{1,0:T(8,128)S(1)}, f32[136,128]{1,0:T(8,128)S(1)}, u32[]{:S(2)}, u32[]{:S(2)}) collective-permute-start(f32[136,128]{1,0:T(8,128)S(1)} %get-tuple-element.27), channel_id=1, source_target_pairs={{1,2},{2,1},{3,4},{4,3},{5,6},{6,5},{7,31},{9,10},{10,9},{11,12},{... | collective-permute-start | bytes 208904 | tf_op jit(solution)/shard_map/ppermute | solution.py:727
  2.7 5.7 %collective-permute-start.1 = (f32[136,128]{1,0:T(8,128)S(1)}, f32[136,128]{1,0:T(8,128)S(1)}, u32[]{:S(2)}, u32[]{:S(2)}) collective-permute-start(f32[136,128]{1,0:T(8,128)S(1)} %get-tuple-element.28), channel_id=1, source_target_pairs={{0,1},{1,0},{2,3},{3,2},{4,5},{5,4},{6,7},{7,6},{8,9},{9,8},{10,11... | collective-permute-start | bytes 208904 | tf_op jit(solution)/shard_map/ppermute | solution.py:728
  8.5 4.7 %collective-permute-start.2 = (f32[40,128]{1,0:T(8,128)S(1)}, f32[40,128]{1,0:T(8,128)S(1)}, u32[]{:S(2)}, u32[]{:S(2)}) collective-permute-start(f32[40,128]{1,0:T(8,128)S(1)} %get-tuple-element.31.msg_a), channel_id=1, source_target_pairs={{0,24},{8,16},{16,8},{24,0},{1,25},{9,17},{17,9},{25,1},{2,26},{10... | collective-permute-start | bytes 61448 | tf_op jit(solution)/shard_map/ppermute | solution.py:767
  11.0 0.7 %copy-start.4 = (s32[32,1]{0,1:T(1,128)S(1)}, s32[32,1]{0,1:T(1,128)}, u32[]{:S(2)}) copy-start(s32[32,1]{0,1:T(1,128)} %param.10) | copy-start | bytes 388
  11.0 0.7 %copy-start.5 = (s32[32]{0:T(128)S(1)}, s32[32]{0:T(128)}, u32[]{:S(2)}) copy-start(s32[32]{0:T(128)} %atm_row.1) | copy-start | bytes 388
  11.0 3.8 %collective-permute-start.3 = (f32[40,128]{1,0:T(8,128)S(1)}, f32[40,128]{1,0:T(8,128)S(1)}, u32[]{:S(2)}, u32[]{:S(2)}) collective-permute-start(f32[40,128]{1,0:T(8,128)S(1)} %get-tuple-element.32.msg_b), channel_id=1, source_target_pairs={{0,8},{8,0},{16,24},{24,16},{1,9},{9,1},{17,25},{25,17},{2,10},{10... | collective-permute-start | bytes 61448 | tf_op jit(solution)/shard_map/ppermute | solution.py:766
  16.2 14.0 %all-to-all-start = ((f32[32,11,1,128]{3,2,1,0:T(1,128)}), f32[32,11,1,128]{3,2,1,0:T(1,128)S(1)}, u32[]{:S(2)}, u32[]{:S(2)}) async-start(f32[32,11,1,128]{3,2,1,0:T(1,128)} %bitcast.7), calls=%async_computation | async-start | bytes 360448 | tf_op jit(solution)/shard_map/all_to_all | solution.py:786

commit v14 on v9

--- a/solution.py
+++ b/solution.py
@@ -171,7 +171,7 @@
         owner = own[r]
         slot = used[owner]
         used[owner] = slot + 1
-        start = (devices - 1 - owner) * slot_rows
+        start = owner * slot_rows
         places = jnp.where(lane1 == r, start + 4 * slot, places)
         out[pl.ds(start + 4 * CAP + slot, 1), :] = base[r : r + 1, :]
         line = out[pl.ds(start + 5 * CAP, 1), :]
@@ -621,12 +621,12 @@
         return acc
 
     none = jnp.zeros((rows, LANES), F32)
-    lax.fori_loop(0, levels, first, (none, none), unroll=2)
+    lax.fori_loop(0, levels, first, (none, none), unroll=4)
     acc = (none, none)
     size = levels // chunks
     copies = []
     for i in range(chunks):
-        acc = lax.fori_loop(i * size, (i + 1) * size, second, acc, unroll=2)
+        acc = lax.fori_loop(i * size, (i + 1) * size, second, acc, unroll=4)
         for src, dst in ((tr_out, tr_hbm), (ve_out, ve_hbm)):
             for q in range(2):
                 start = (q * levels + i * size) * rows
@@ -791,7 +791,6 @@
         ("lon", "lat"),
         0,
         0,
-        axis_index_groups=[list(range(devices))[::-1]],
         tiled=True,
     ).reshape(devices * slot_rows, cols)
 

time: 31.2 us -> 31.1 us (level)
  Pallas kernels: 10.4 us -> 9.61 us
  waiting for transfers between devices: 6.54 us -> 6.99 us
    pallas_call x1, Pallas kernels: 4.45 us -> 3.7 us  [local(): call(functools.partial(main_kernel, rows, levels, chunks), [shaped(flat,...]
    all_to_all x1, waiting for transfers between devices: 4.45 us -> 4.9 us  [local(): lax.all_to_all(outgoing.reshape(devices, slot_rows, 1, cols), ('lon', 'la...]
  transfers between devices with their start and end apart: 5 -> 5, of which waited for: 3 -> 3; matrix products, arithmetic and copies ran while one was open for 0% -> 0% of each run, Pallas kernels for 21% -> 19%
where the time goes in v14:
time: 31.1 us; the launch traced here: 30.7 us
  starting transfers between devices  13.2 us (42%)
  Pallas kernels  9.61 us (31%)
  waiting for transfers between devices  6.99 us (22%)
  between operations  0.75 us (2%)
    all_to_all x1, starting transfers between devices, local(): lax.all_to_all(outgoing.reshape(devices, slot_rows, 1, cols), ('lon', 'la...  5.04 us
    all_to_all x1, waiting for transfers between devices, local(): lax.all_to_all(outgoing.reshape(devices, slot_rows, 1, cols), ('lon', 'la...  4.9 us
    ppermute x1, starting transfers between devices, local(): got_lat_a = lax.ppermute(lat_a, ('lon', 'lat'), swap_a)  4.45 us
    pallas_call x1, Pallas kernels, local(): call(functools.partial(main_kernel, rows, levels, chunks), [shaped(flat,...  3.7 us
    ppermute x1, starting transfers between devices, local(): got_a = lax.ppermute(msg_a, 'lon', odd_pairs)  2.51 us
    ppermute x1, waiting for transfers between devices, local(): got_b = lax.ppermute(msg_b, 'lon', even_pairs)  1.55 us
    pallas_call x1, Pallas kernels, local(): call(functools.partial(surface_kernel, rows, levels), [shaped(len(COEFFIC...  1.31 us
    pallas_call x1, Pallas kernels, local(): call(functools.partial(edge_kernel, rows, fields), [pltpu.VMEM((length, c...  1.31 us
  transfers between devices with their start and end apart: 5, of which 3 were waited for; matrix products, arithmetic and copies ran while one was open for 0% of the time, Pallas kernels for 19%

profile of v14, /device:TPU:0, one launch (start us, length us, event | category | flops | bytes accessed | tf_op | source)
XLA Modules:
  0.0 30.7 jit_solution(12404548931551675910)
XLA Ops:
  0.6 0.0 copy-start
  0.6 0.0 copy-start.1
  0.7 0.0 copy-start.2
  0.7 0.0 copy-start.3
  0.7 1.3 %shard_map.94 = (f32[136,128]{1,0:T(8,128)S(1)}, f32[136,128]{1,0:T(8,128)S(1)}) custom-call(f32[32,32,128]{2,1,0:T(8,128)} %bitcast.9, f32[32,32,128]{2,1,0:T(8,128)} %bitcast.12, s32[32,128]{1,0:T(8,128)} %mask.3, f32[32,128]{1,0:T(8,128)} %mix.3), custom_call_target="tpu_custom_call" | custom-call | tf_op jit(solution)/shard_map/pallas_call | solution.py:717
  2.0 0.7 %collective-permute-start = (f32[136,128]{1,0:T(8,128)S(1)}, f32[136,128]{1,0:T(8,128)S(1)}, u32[]{:S(2)}, u32[]{:S(2)}) collective-permute-start(f32[136,128]{1,0:T(8,128)S(1)} %get-tuple-element.27), channel_id=1, source_target_pairs={{1,2},{2,1},{3,4},{4,3},{5,6},{6,5},{7,31},{9,10},{10,9},{11,12},{... | collective-permute-start | bytes 208904 | tf_op jit(solution)/shard_map/ppermute | solution.py:730
  2.7 4.4 %collective-permute-start.1 = (f32[136,128]{1,0:T(8,128)S(1)}, f32[136,128]{1,0:T(8,128)S(1)}, u32[]{:S(2)}, u32[]{:S(2)}) collective-permute-start(f32[136,128]{1,0:T(8,128)S(1)} %get-tuple-element.28), channel_id=1, source_target_pairs={{0,1},{1,0},{2,3},{3,2},{4,5},{5,4},{6,7},{7,6},{8,9},{9,8},{10,11... | collective-permute-start | bytes 208904 | tf_op jit(solution)/shard_map/ppermute | solution.py:731
  7.1 0.0 copy-done
  7.1 0.0 copy-done.1
  7.1 0.0 copy-done.2
  7.1 0.0 copy-done.3
  7.1 1.2 %shard_map.95 = (f32[40,128]{1,0:T(8,128)S(1)}, f32[40,128]{1,0:T(8,128)S(1)}) custom-call(f32[1024,128]{1,0:T(8,128)S(1)} %bitcast.10, f32[1024,128]{1,0:T(8,128)S(1)} %bitcast.13, s32[32,128]{1,0:T(8,128)S(1)} %copy-done.2, f32[32,128]{1,0:T(8,128)S(1)} %copy-done.3), custom_call_target="tpu_custom_call" | custom-call | tf_op jit(solution)/shard_map/pallas_call | solution.py:734
  8.3 0.0 collective-permute-done.got_b
  8.3 0.0 collective-permute-done.1.got_a
  8.3 0.2 shard_map.96
  8.5 2.5 %collective-permute-start.2 = (f32[40,128]{1,0:T(8,128)S(1)}, f32[40,128]{1,0:T(8,128)S(1)}, u32[]{:S(2)}, u32[]{:S(2)}) collective-permute-start(f32[40,128]{1,0:T(8,128)S(1)} %get-tuple-element.31.msg_a), channel_id=1, source_target_pairs={{0,24},{8,16},{16,8},{24,0},{1,25},{9,17},{17,9},{25,1},{2,26},{10... | collective-permute-start | bytes 61448 | tf_op jit(solution)/shard_map/ppermute | solution.py:770
  11.0 0.0 copy-start.4
  11.0 0.0 copy-start.5
  11.0 0.5 %collective-permute-start.3 = (f32[40,128]{1,0:T(8,128)S(1)}, f32[40,128]{1,0:T(8,128)S(1)}, u32[]{:S(2)}, u32[]{:S(2)}) collective-permute-start(f32[40,128]{1,0:T(8,128)S(1)} %get-tuple-element.32.msg_b), channel_id=1, source_target_pairs={{0,8},{8,0},{16,24},{24,16},{1,9},{9,1},{17,25},{25,17},{2,10},{10... | collective-permute-start | bytes 61448 | tf_op jit(solution)/shard_map/ppermute | solution.py:769
  11.6 0.1 copy-done.4
  11.7 0.0 copy-done.5
  11.7 1.0 %shard_map.93 = (f32[2048,128]{1,0:T(8,128)S(1)}, f32[112,128]{1,0:T(8,128)S(1)}, f32[384,128]{1,0:T(8,128)S(1)}, f32[80,128]{1,0:T(8,128)S(1)}, f32[352,128]{1,0:T(8,128)S(1)}, /*index=5*/s32[8,128]{1,0:T(8,128)S(1)}) custom-call(f32[1024,128]{1,0:T(8,128)S(1)} %bitcast.11, f32[1024,128]{1,0:T(8,128)S(1)} %bitcast.14, s32[32,128]{1,0:T(8,128)S(1)} %copy-done.2, ...), custom_call_target="tpu_custom_call" | custom-call | tf_op jit(solution)/shard_map/pallas_call | solution.py:741
  12.7 0.5 %collective-permute-done.2.got_a = f32[40,128]{1,0:T(8,128)S(1)} collective-permute-done((f32[40,128]{1,0:T(8,128)S(1)}, f32[40,128]{1,0:T(8,128)S(1)}, u32[]{:S(2)}, u32[]{:S(2)}) %collective-permute-start.2) | collective-permute-done | bytes 20512 | tf_op jit(solution)/shard_map/ppermute | solution.py:770
  13.3 1.6 %collective-permute-done.3.got_b = f32[40,128]{1,0:T(8,128)S(1)} collective-permute-done((f32[40,128]{1,0:T(8,128)S(1)}, f32[40,128]{1,0:T(8,128)S(1)}, u32[]{:S(2)}, u32[]{:S(2)}) %collective-permute-start.3) | collective-permute-done | bytes 20512 | tf_op jit(solution)/shard_map/ppermute | solution.py:769
  14.8 1.3 %shard_map.97 = (f32[416,128]{1,0:T(8,128)S(1)}, f32[32,128]{1,0:T(8,128)S(1)}, f32[352,128]{1,0:T(8,128)}) custom-call(f32[2048,128]{1,0:T(8,128)S(1)} %get-tuple-element.25.state, f32[112,128]{1,0:T(8,128)S(1)} %get-tuple-element.26.base, f32[40,128]{1,0:T(8,128)S(1)} %get-tuple-element.31.msg_a, f32[40,128]{1,0:T(8,128)S(1)} %get-tuple-element.32.msg_b, ...), custom_call_target="tpu_custom_call" | custom-call | tf_op jit(solution)/shard_map/pallas_call | solution.py:773
  16.1 5.0 %all-to-all-start = ((f32[32,11,1,128]{3,2,1,0:T(1,128)}), f32[32,11,1,128]{3,2,1,0:T(1,128)S(1)}, u32[]{:S(2)}, u32[]{:S(2)}) async-start(f32[32,11,1,128]{3,2,1,0:T(1,128)} %bitcast.7), calls=%async_computation | async-start | bytes 360448 | tf_op jit(solution)/shard_map/all_to_all | solution.py:789
  21.2 3.7 %shard_map.98 = (f32[1024,128]{1,0:T(8,128)}, f32[1024,128]{1,0:T(8,128)}) custom-call(f32[2048,128]{1,0:T(8,128)S(1)} %get-tuple-element.25.state, f32[112,128]{1,0:T(8,128)S(1)} %get-tuple-element.26.base, f32[40,128]{1,0:T(8,128)S(1)} %get-tuple-element.31.msg_a, f32[40,128]{1,0:T(8,128)S(1)} %get-tuple-element.32.msg_b, ...), custom_call_target="tpu_custom_call" | custom-call | flops 20971520 | bytes 5242880 | tf_op jit(solution)/shard_map/pallas_call | solution.py:798
  24.9 4.9 %all-to-all-done = f32[32,11,1,128]{3,2,1,0:T(1,128)S(1)} async-done(((f32[32,11,1,128]{3,2,1,0:T(1,128)}), f32[32,11,1,128]{3,2,1,0:T(1,128)S(1)}, u32[]{:S(2)}, u32[]{:S(2)}) %all-to-all-start) | async-done | bytes 180256 | tf_op jit(solution)/shard_map/all_to_all | solution.py:789
  29.8 0.9 %shard_map.99 = (f32[4,32,128]{2,1,0:T(8,128)}, f32[32,128]{1,0:T(8,128)}) custom-call(f32[352,128]{1,0:T(8,128)S(1)} %bitcast.15), custom_call_target="tpu_custom_call" | custom-call | tf_op jit(solution)/shard_map/pallas_call | solution.py:815
Async XLA Ops:
  0.6 6.5 %copy-start = (f32[2,16,32,128]{3,2,1,0:T(8,128)S(1)}, f32[2,16,32,128]{3,2,1,0:T(8,128)}, u32[]{:S(2)}) copy-start(f32[2,16,32,128]{3,2,1,0:T(8,128)} %param.6) | copy-start | bytes 1572868
  0.6 6.5 %copy-start.1 = (f32[2,16,32,128]{3,2,1,0:T(8,128)S(1)}, f32[2,16,32,128]{3,2,1,0:T(8,128)}, u32[]{:S(2)}) copy-start(f32[2,16,32,128]{3,2,1,0:T(8,128)} %param.7) | copy-start | bytes 1572868
  0.7 6.5 %copy-start.2 = (s32[32,128]{1,0:T(8,128)S(1)}, s32[32,128]{1,0:T(8,128)}, u32[]{:S(2)}) copy-start(s32[32,128]{1,0:T(8,128)} %mask.3) | copy-start | bytes 49156
  0.7 6.5 %copy-start.3 = (f32[32,128]{1,0:T(8,128)S(1)}, f32[32,128]{1,0:T(8,128)}, u32[]{:S(2)}) copy-start(f32[32,128]{1,0:T(8,128)} %mix.3) | copy-start | bytes 49156
  2.0 6.3 %collective-permute-start = (f32[136,128]{1,0:T(8,128)S(1)}, f32[136,128]{1,0:T(8,128)S(1)}, u32[]{:S(2)}, u32[]{:S(2)}) collective-permute-start(f32[136,128]{1,0:T(8,128)S(1)} %get-tuple-element.27), channel_id=1, source_target_pairs={{1,2},{2,1},{3,4},{4,3},{5,6},{6,5},{7,31},{9,10},{10,9},{11,12},{... | collective-permute-start | bytes 208904 | tf_op jit(solution)/shard_map/ppermute | solution.py:730
  2.7 5.7 %collective-permute-start.1 = (f32[136,128]{1,0:T(8,128)S(1)}, f32[136,128]{1,0:T(8,128)S(1)}, u32[]{:S(2)}, u32[]{:S(2)}) collective-permute-start(f32[136,128]{1,0:T(8,128)S(1)} %get-tuple-element.28), channel_id=1, source_target_pairs={{0,1},{1,0},{2,3},{3,2},{4,5},{5,4},{6,7},{7,6},{8,9},{9,8},{10,11... | collective-permute-start | bytes 208904 | tf_op jit(solution)/shard_map/ppermute | solution.py:731
  8.5 4.7 %collective-permute-start.2 = (f32[40,128]{1,0:T(8,128)S(1)}, f32[40,128]{1,0:T(8,128)S(1)}, u32[]{:S(2)}, u32[]{:S(2)}) collective-permute-start(f32[40,128]{1,0:T(8,128)S(1)} %get-tuple-element.31.msg_a), channel_id=1, source_target_pairs={{0,24},{8,16},{16,8},{24,0},{1,25},{9,17},{17,9},{25,1},{2,26},{10... | collective-permute-start | bytes 61448 | tf_op jit(solution)/shard_map/ppermute | solution.py:770
  11.0 0.7 %copy-start.4 = (s32[32,1]{0,1:T(1,128)S(1)}, s32[32,1]{0,1:T(1,128)}, u32[]{:S(2)}) copy-start(s32[32,1]{0,1:T(1,128)} %param.10) | copy-start | bytes 388
  11.0 0.7 %copy-start.5 = (s32[32]{0:T(128)S(1)}, s32[32]{0:T(128)}, u32[]{:S(2)}) copy-start(s32[32]{0:T(128)} %atm_row.1) | copy-start | bytes 388
  11.0 3.8 %collective-permute-start.3 = (f32[40,128]{1,0:T(8,128)S(1)}, f32[40,128]{1,0:T(8,128)S(1)}, u32[]{:S(2)}, u32[]{:S(2)}) collective-permute-start(f32[40,128]{1,0:T(8,128)S(1)} %get-tuple-element.32.msg_b), channel_id=1, source_target_pairs={{0,8},{8,0},{16,24},{24,16},{1,9},{9,1},{17,25},{25,17},{2,10},{10... | collective-permute-start | bytes 61448 | tf_op jit(solution)/shard_map/ppermute | solution.py:769
  16.1 13.7 %all-to-all-start = ((f32[32,11,1,128]{3,2,1,0:T(1,128)}), f32[32,11,1,128]{3,2,1,0:T(1,128)S(1)}, u32[]{:S(2)}, u32[]{:S(2)}) async-start(f32[32,11,1,128]{3,2,1,0:T(1,128)} %bitcast.7), calls=%async_computation | async-start | bytes 360448 | tf_op jit(solution)/shard_map/all_to_all | solution.py:789
